TPU v7x, 32 devices: a whole 2x2x4 slice. The times are simulated.
32 devices in a mesh: groups: 2 (over y), dp: 4 (over x, core), prefix: 4 (over z).
Axes of the slice: x: 2, y: 2, z: 4, core: 2. Of those that a mesh axis runs over, the one named last changes fastest.
Arguments:
- queries: bfloat16 [16, 512, 4096], P(('groups', 'dp'), None, 'prefix'), parts along dimension 0, may hold values from -4.5 to 4.5
- resp_kv: bfloat16 [16, 512, 2048], P(('groups', 'dp'), None, 'prefix'), parts along dimension 0, may hold values from -4.5 to 4.5
- prompt_kv: bfloat16 [4, 1024, 2048], P('groups', 'dp', 'prefix'), parts along dimension 0, may hold values from -4.5 to 4.5
- prompt_of: int32 [16], P(('groups', 'dp')), parts along dimension 0, may hold values from 0 to 1, as said below
- d_out: bfloat16 [16, 512, 4096], P(('groups', 'dp'), None, 'prefix'), parts along dimension 0, may hold values from -6 to 6
Outputs:
- attended: bfloat16 [16, 512, 4096], P(('groups', 'dp'), None, 'prefix'), parts along dimension 0
- d_queries: bfloat16 [16, 512, 4096], P(('groups', 'dp'), None, 'prefix'), parts along dimension 0
- d_resp_kv: bfloat16 [16, 512, 2048], P(('groups', 'dp'), None, 'prefix'), parts along dimension 0
- d_prompt_kv: float32 [4, 1024, 2048], P('groups', 'dp', 'prefix'), parts along dimension 0
There are 2 independent parts, one for each index of `groups`. A program takes and returns all parts, laid end to end along the dimension named above; each array names one. Nothing has to cross between parts.
Inputs may be any that keep to these rules, and one draw needn't show every extreme that they name: `prompt_of`: each prompt has at least 2 responses; responses of the two prompts may stand in any order.
All inputs are finite; a program needn't handle non-finite values.
Results may differ from a plain program's by a relative error of at most 0.011.
Values may be sent and summed in bfloat16 or wider, within the bound.
No kernel may reach another device: no remote copies, remote signals or barrier semaphores. Data moves between devices by JAX's collectives and lax.ppermute only.
A program may use at most 192 MiB of HBM per device.

v0:
```python
import functools

import jax
import jax.numpy as jnp
from jax import lax
from jax.experimental import pallas as pl
from jax.experimental.pallas import tpu as pltpu
from jax.sharding import PartitionSpec as P

H = 32
KVH = 8
HD = 128
P_SIZE = 2
GROUP = H // KVH
BLOCK = 256
MASKED = -1e30
SCALE = HD ** (-0.5)
LOG2E = 1.4426950408889634

NT = (((1,), (1,)), ((), ()))
NN = (((1,), (0,)), ((), ()))
TN = (((0,), (0,)), ((), ()))


def dot(a, b, dims):
    return lax.dot_general(a, b, dims, preferred_element_type=jnp.float32)


def swap(block, axis, bit):
    count = lax.axis_size(axis)
    route = [(i, i ^ (1 << bit)) for i in range(count)]
    return lax.ppermute(block, axis, route)


def attend_kernel(sizes, scalars, *refs):
    pieces, rows, n_keep, heads = sizes
    refs = list(refs)
    q_ref, do_ref, ra_ref, rb_ref = refs[:4]
    pa_refs = refs[4 : 4 + pieces]
    pb_refs = refs[4 + pieces : 4 + 2 * pieces]
    rest = refs[4 + 2 * pieces :]
    n_out = 5 + (1 if pieces > n_keep else 0)
    out_ref, dq_ref, dra_ref, drb_ref, dkeep_ref = rest[:5]
    dsend_ref = rest[5] if n_out == 6 else None
    k_all, v_all, probs, dscores, acc_k, acc_v, res_k, res_v = rest[n_out:]

    r = pl.program_id(0)
    head = pl.program_id(1)
    prompt = scalars[r]
    even = scalars[pl.num_programs(0)] == 0
    n_prompt = pieces * rows
    n_query = q_ref.shape[1]

    @pl.when((r == 0) & (head == 0))
    def _():
        acc_k[...] = jnp.zeros_like(acc_k)
        acc_v[...] = jnp.zeros_like(acc_v)

    def gather(dst, piece_refs, resp_ref):
        for i, ref in enumerate(piece_refs):
            dst[i * rows : (i + 1) * rows, :] = ref[0]
        dst[n_prompt:, :] = resp_ref[0]

    @pl.when((head == 0) & even)
    def _():
        gather(k_all, pa_refs, ra_ref)
        gather(v_all, pb_refs, rb_ref)

    @pl.when((head == 0) & jnp.logical_not(even))
    def _():
        gather(k_all, pb_refs, rb_ref)
        gather(v_all, pa_refs, ra_ref)

    @pl.when(head == 0)
    def _():
        res_k[...] = jnp.zeros_like(res_k)
        res_v[...] = jnp.zeros_like(res_v)

    n_blocks = n_query // BLOCK
    for i in range(n_blocks):
        t0 = i * BLOCK
        seen = n_prompt + t0 + BLOCK
        q = q_ref[0, t0 : t0 + BLOCK, :]
        do = do_ref[0, t0 : t0 + BLOCK, :]
        keys = k_all[:seen, :]
        values = v_all[:seen, :]
        s = dot(q, keys, NT)
        diag = s[:, seen - BLOCK :]
        row = lax.broadcasted_iota(jnp.int32, (BLOCK, BLOCK), 0)
        col = lax.broadcasted_iota(jnp.int32, (BLOCK, BLOCK), 1)
        diag = jnp.where(col <= row, diag, MASKED)
        s = jnp.concatenate([s[:, : seen - BLOCK], diag], axis=1)
        top = jnp.max(s, axis=1, keepdims=True)
        w = jnp.exp2(s * (SCALE * LOG2E) - top * (SCALE * LOG2E))
        p = w * (1.0 / jnp.sum(w, axis=1, keepdims=True))
        p16 = p.astype(jnp.bfloat16)
        probs[t0 : t0 + BLOCK, :seen] = p16
        o = dot(p16, values, NN)
        out_ref[0, t0 : t0 + BLOCK, :] = o.astype(jnp.bfloat16)
        delta = jnp.sum(o * do.astype(jnp.float32), axis=1, keepdims=True)
        dp = dot(do, values, NT)
        ds = (p * (dp - delta)).astype(jnp.bfloat16)
        dscores[t0 : t0 + BLOCK, :seen] = ds
        dq_ref[0, t0 : t0 + BLOCK, :] = (dot(ds, keys, NN) * SCALE).astype(jnp.bfloat16)

    q_all = q_ref[0]
    do_all = do_ref[0]
    acc_k[prompt] += dot(dscores[:, :n_prompt], q_all, TN)
    acc_v[prompt] += dot(probs[:, :n_prompt], do_all, TN)
    for i in range(n_blocks):
        t0 = i * BLOCK
        u0 = n_prompt + t0
        res_k[t0 : t0 + BLOCK, :] += dot(dscores[t0:, u0 : u0 + BLOCK], q_all[t0:], TN)
        res_v[t0 : t0 + BLOCK, :] += dot(probs[t0:, u0 : u0 + BLOCK], do_all[t0:], TN)

    last = head == heads - 1

    @pl.when(last & even)
    def _():
        dra_ref[0] = (res_k[...] * SCALE).astype(jnp.bfloat16)
        drb_ref[0] = res_v[...].astype(jnp.bfloat16)

    @pl.when(last & jnp.logical_not(even))
    def _():
        dra_ref[0] = res_v[...].astype(jnp.bfloat16)
        drb_ref[0] = (res_k[...] * SCALE).astype(jnp.bfloat16)

    done = last & (r == pl.num_programs(0) - 1)

    def scatter(slot, acc, factor):
        for i in range(pieces):
            for p_id in range(P_SIZE):
                val = acc[p_id, i * rows : (i + 1) * rows, :]
                if factor != 1.0:
                    val = val * factor
                if i < n_keep:
                    dkeep_ref[i, p_id, :, slot * HD : (slot + 1) * HD] = val
                else:
                    dsend_ref[i - n_keep, p_id, :, slot * HD : (slot + 1) * HD] = val.astype(jnp.bfloat16)

    @pl.when(done & even)
    def _():
        scatter(0, acc_k, SCALE)
        scatter(1, acc_v, 1.0)

    @pl.when(done & jnp.logical_not(even))
    def _():
        scatter(0, acc_v, 1.0)
        scatter(1, acc_k, SCALE)


def attend(scalars, queries, d_out, resp_a, resp_b, prompt_a, prompt_b, n_keep, chunk, heads):
    n_resp, n_query, _ = queries.shape
    pieces = len(prompt_a)
    rows = prompt_a[0][0].shape[1]
    n_prompt = pieces * rows
    n_keys = n_prompt + n_query
    n_send = pieces - n_keep

    def query_map(r, j, sc):
        return (r, 0, chunk * heads + j)

    def resp_map(column):
        return lambda r, j, sc: (r, 0, column(sc[n_resp]))

    def prompt_map(column):
        return lambda r, j, sc: (sc[r], 0, column(sc[n_resp]))

    q_spec = pl.BlockSpec((1, n_query, HD), query_map)
    in_specs = [q_spec, q_spec]
    in_specs += [pl.BlockSpec((1, n_query, HD), resp_map(c)) for _, c in (resp_a, resp_b)]
    in_specs += [pl.BlockSpec((1, rows, HD), prompt_map(c)) for _, c in (*prompt_a, *prompt_b)]
    own_map = lambda r, j, sc: (r, 0, j)
    out_specs = [
        pl.BlockSpec((1, n_query, HD), own_map),
        pl.BlockSpec((1, n_query, HD), own_map),
        pl.BlockSpec((1, n_query, HD), lambda r, j, sc: (r, 0, 0)),
        pl.BlockSpec((1, n_query, HD), lambda r, j, sc: (r, 0, 0)),
        pl.BlockSpec((n_keep, P_SIZE, rows, 2 * HD), lambda r, j, sc: (0, 0, 0, 0)),
    ]
    shape = jax.ShapeDtypeStruct
    out_shape = [
        shape((n_resp, n_query, heads * HD), jnp.bfloat16),
        shape((n_resp, n_query, heads * HD), jnp.bfloat16),
        shape((n_resp, n_query, HD), jnp.bfloat16),
        shape((n_resp, n_query, HD), jnp.bfloat16),
        shape((n_keep, P_SIZE, rows, 2 * HD), jnp.float32),
    ]
    if n_send:
        out_specs.append(pl.BlockSpec((n_send, P_SIZE, rows, 2 * HD), lambda r, j, sc: (0, 0, 0, 0)))
        out_shape.append(shape((n_send, P_SIZE, rows, 2 * HD), jnp.bfloat16))
    scratch = [
        pltpu.VMEM((n_keys, HD), jnp.bfloat16),
        pltpu.VMEM((n_keys, HD), jnp.bfloat16),
        pltpu.VMEM((n_query, n_keys), jnp.bfloat16),
        pltpu.VMEM((n_query, n_keys), jnp.bfloat16),
        pltpu.VMEM((P_SIZE, n_prompt, HD), jnp.float32),
        pltpu.VMEM((P_SIZE, n_prompt, HD), jnp.float32),
        pltpu.VMEM((n_query, HD), jnp.float32),
        pltpu.VMEM((n_query, HD), jnp.float32),
    ]
    flops = 12 * n_resp * heads * n_query * n_keys * HD
    return pl.pallas_call(
        functools.partial(attend_kernel, (pieces, rows, n_keep, heads)),
        grid_spec=pltpu.PrefetchScalarGridSpec(
            num_scalar_prefetch=1,
            grid=(n_resp, heads),
            in_specs=in_specs,
            out_specs=out_specs,
            scratch_shapes=scratch,
        ),
        out_shape=out_shape,
        compiler_params=pltpu.CompilerParams(vmem_limit_bytes=48 * 2**20),
        cost_estimate=pl.CostEstimate(flops=2 * flops, bytes_accessed=8 * 2**20, transcendentals=0),
    )(scalars, queries, d_out, resp_a[0], resp_b[0], *[a for a, _ in (*prompt_a, *prompt_b)])


def per_device(queries, resp_kv, prompt_kv, prompt_of, d_out):
    n_resp, n_query, width = queries.shape
    pair_heads = prompt_kv.shape[2] // HD
    parity = lax.axis_index("prefix") % 2
    scalars = jnp.concatenate([prompt_of, parity[None].astype(jnp.int32)])
    if lax.axis_size("dp") == 4 and pair_heads % 2 == 0:
        return whole_heads(queries, resp_kv, prompt_kv, scalars, parity, d_out)
    return shared_head(queries, resp_kv, prompt_kv, scalars, parity, d_out)


def whole_heads(queries, resp_kv, prompt_kv, scalars, parity, d_out):
    n_own = prompt_kv.shape[2] // HD // 2

    def column(array, which):
        return lax.dynamic_slice_in_dim(array, which * HD, HD, axis=array.ndim - 1)

    attended, d_queries, d_resp, d_prompt = [], [], [], []
    for h in range(n_own):
        own = lambda par, h=h: par * n_own + h
        theirs = (1 - parity) * n_own + h
        first = lambda par: 0
        pa0 = column(prompt_kv, own(parity))
        pb0 = swap(column(prompt_kv, theirs), "prefix", 0)
        rb = swap(column(resp_kv, theirs), "prefix", 0)
        pa2 = swap(pa0, "dp", 1)
        pb2 = swap(pb0, "dp", 1)
        pa1 = swap(pa0, "dp", 0)
        pb1 = swap(pb0, "dp", 0)
        pa3 = swap(pa2, "dp", 0)
        pb3 = swap(pb2, "dp", 0)
        att, dq, dra, drb, dkeep, dsend = attend(
            scalars,
            queries,
            d_out,
            (resp_kv, own),
            (rb, first),
            [(prompt_kv, own), (pa2, first), (pa1, first), (pa3, first)],
            [(pb0, first), (pb2, first), (pb1, first), (pb3, first)],
            2,
            h,
            GROUP,
        )
        attended.append(att)
        d_queries.append(dq)
        d_resp.append((dra, swap(drb, "prefix", 0)))
        part = swap(dsend, "dp", 0)
        sums = dkeep + part.astype(jnp.float32)
        across = swap(sums[1].astype(jnp.bfloat16), "dp", 1)
        total = sums[0] + across.astype(jnp.float32)
        mine = total[:, :, :HD]
        other = swap(total[:, :, HD:].astype(jnp.bfloat16), "prefix", 0)
        d_prompt.append((mine, other.astype(jnp.float32)))

    def place(parts):
        mine = jnp.concatenate([a for a, _ in parts], axis=-1)
        other = jnp.concatenate([b for _, b in parts], axis=-1)
        even = parity == 0
        return jnp.concatenate([jnp.where(even, mine, other), jnp.where(even, other, mine)], axis=-1)

    return (
        jnp.concatenate(attended, axis=-1),
        jnp.concatenate(d_queries, axis=-1),
        place(d_resp),
        place(d_prompt),
    )


def shared_head(queries, resp_kv, prompt_kv, scalars, parity, d_out):
    pair_heads = prompt_kv.shape[2] // HD
    local_heads = queries.shape[2] // HD
    prompt_a = lax.all_gather(prompt_kv, "dp", axis=1, tiled=True)
    prompt_b = swap(prompt_a, "prefix", 0)
    resp_b = swap(resp_kv, "prefix", 0)
    first = lambda par: 0
    att, dq, dra, drb, dkeep = attend(
        scalars,
        queries,
        d_out,
        (resp_kv, first),
        (resp_b, first),
        [(prompt_a, first)],
        [(prompt_b, first)],
        1,
        0,
        local_heads,
    )
    d_resp = (dra.astype(jnp.float32) + swap(drb, "prefix", 0).astype(jnp.float32)).astype(jnp.bfloat16)
    other = swap(dkeep[0, :, :, HD:].astype(jnp.bfloat16), "prefix", 0)
    paired = dkeep[0, :, :, :HD] + other.astype(jnp.float32)
    d_prompt = lax.psum_scatter(paired, "dp", scatter_dimension=1, tiled=True)
    return att, dq, d_resp, d_prompt


def solution(mesh):
    in_specs = (
        P(("groups", "dp"), None, "prefix"),
        P(("groups", "dp"), None, "prefix"),
        P("groups", "dp", "prefix"),
        P(("groups", "dp")),
        P(("groups", "dp"), None, "prefix"),
    )
    out_specs = (
        P(("groups", "dp"), None, "prefix"),
        P(("groups", "dp"), None, "prefix"),
        P(("groups", "dp"), None, "prefix"),
        P("groups", "dp", "prefix"),
    )
    return jax.shard_map(
        per_device, mesh=mesh, in_specs=in_specs, out_specs=out_specs, check_vma=False
    )
```

profile of v0, /device:TPU:0, one launch (start us, length us, event | category | flops | bytes accessed | tf_op | source)
XLA Modules:
  0.0 116.4 jit_solution(10938705018134192524)
XLA Ops:
  0.7 1.2 %constant_dynamic-slice_fusion.3 = (bf16[2,256,128]{2,1,0:T(8,128)(2,1)S(1)}, bf16[2,256,128]{2,1,0:T(8,128)(2,1)S(1)}, bf16[2,256,128]{2,1,0:T(8,128)(2,1)S(1)}, bf16[2,256,128]{2,1,0:T(8,128)(2,1)S(1)}) fusion(bf16[2,256,512]{2,1,0:T(8,128)(2,1)} %refs_4_.3, s32[]{:T(128)S(6)} %select_n.46, s32[]{:T(128)S(6)} %select_n.49, s32[]{:T(128)S(6)} %select_n.47, ...), kind=kLoop, calls=%fused_computation.29 | loop fusion | bytes 1048592 | tf_op jit(solution)/shard_map/dynamic_slice | solution.py:232
  1.9 3.1 %collective-permute-start.4 = (bf16[2,256,128]{2,1,0:T(8,128)(2,1)S(1)}, bf16[2,256,128]{2,1,0:T(8,128)(2,1)S(1)}, u32[]{:S(2)}, u32[]{:S(2)}) collective-permute-start(bf16[2,256,128]{2,1,0:T(8,128)(2,1)S(1)} %get-tuple-element.34), channel_id=1, source_target_pairs={{0,1},{1,0},{2,3},{3,2},{4,5},{5,4},{6,7},{7,6},{8,9},{9,8},{10,11... | collective-permute-start | bytes 393224 | tf_op jit(solution)/shard_map/ppermute | solution.py:32
  5.0 1.5 %collective-permute-start.1 = (bf16[2,256,128]{2,1,0:T(8,128)(2,1)S(1)}, bf16[2,256,128]{2,1,0:T(8,128)(2,1)S(1)}, u32[]{:S(2)}, u32[]{:S(2)}) collective-permute-start(bf16[2,256,128]{2,1,0:T(8,128)(2,1)S(1)} %get-tuple-element.36), channel_id=1, source_target_pairs={{0,8},{4,12},{8,0},{12,4},{1,9},{5,13},{9,1},{13,5},{2,10},{6,14},... | collective-permute-start | bytes 393224 | tf_op jit(solution)/shard_map/ppermute | solution.py:32
  6.9 1.1 constant_dynamic-slice_fusion.5
  8.0 1.6 %collective-permute-start = (bf16[2,512,128]{2,1,0:T(8,128)(2,1)S(1)}, bf16[2,512,128]{2,1,0:T(8,128)(2,1)S(1)}, u32[]{:S(2)}, u32[]{:S(2)}) collective-permute-start(bf16[2,512,128]{2,1,0:T(8,128)(2,1)S(1)} %get-tuple-element.30), channel_id=1, source_target_pairs={{0,1},{1,0},{2,3},{3,2},{4,5},{5,4},{6,7},{7,6},{8,9},{9,8},{10,11... | collective-permute-start | bytes 786440 | tf_op jit(solution)/shard_map/ppermute | solution.py:32
  10.4 1.3 %collective-permute-start.5 = (bf16[2,256,128]{2,1,0:T(8,128)(2,1)S(1)}, bf16[2,256,128]{2,1,0:T(8,128)(2,1)S(1)}, u32[]{:S(2)}, u32[]{:S(2)}) collective-permute-start(bf16[2,256,128]{2,1,0:T(8,128)(2,1)S(1)} %collective-permute-done.4.refs_8_), channel_id=1, source_target_pairs={{0,8},{4,12},{8,0},{12,4},{1,9},{5,13},{9,1},{13,5},{2,10},{6,14},... | collective-permute-start | bytes 393224 | tf_op jit(solution)/shard_map/ppermute | solution.py:32
  11.7 1.1 collective-permute-done.12.refs_8_
  12.8 3.2 %collective-permute-done.9.refs_5_ = bf16[2,256,128]{2,1,0:T(8,128)(2,1)S(1)} collective-permute-done((bf16[2,256,128]{2,1,0:T(8,128)(2,1)S(1)}, bf16[2,256,128]{2,1,0:T(8,128)(2,1)S(1)}, u32[]{:S(2)}, u32[]{:S(2)}) %collective-permute-start.9) | collective-permute-done | bytes 131104 | tf_op jit(solution)/shard_map/ppermute | solution.py:32
  16.8 2.1 %collective-permute-done.5.refs_9_ = bf16[2,256,128]{2,1,0:T(8,128)(2,1)S(1)} collective-permute-done((bf16[2,256,128]{2,1,0:T(8,128)(2,1)S(1)}, bf16[2,256,128]{2,1,0:T(8,128)(2,1)S(1)}, u32[]{:S(2)}, u32[]{:S(2)}) %collective-permute-start.5) | collective-permute-done | bytes 131104 | tf_op jit(solution)/shard_map/ppermute | solution.py:32
  20.0 1.0 collective-permute-done.13.refs_9_
  21.5 30.3 %shard_map.84 = (bf16[2,512,512]{2,1,0:T(8,128)(2,1)S(1)}, bf16[2,512,512]{2,1,0:T(8,128)(2,1)S(1)}, bf16[2,512,128]{2,1,0:T(8,128)(2,1)S(1)}, bf16[2,512,128]{2...) custom-call(s32[3]{0:T(128)S(1)} %pad_add_fusion.scalars, ...), custom_call_target="tpu_custom_call" | custom-call | flops 19327352832 | bytes 8388608 | tf_op jit(solution)/shard_map/pallas_call | solution.py:203
  51.9 30.3 %shard_map.85 = (bf16[2,512,512]{2,1,0:T(8,128)(2,1)S(1)}, bf16[2,512,512]{2,1,0:T(8,128)(2,1)S(1)}, bf16[2,512,128]{2,1,0:T(8,128)(2,1)S(1)}, bf16[2,512,128]{2...) custom-call(s32[3]{0:T(128)S(1)} %pad_add_fusion.scalars, ...), custom_call_target="tpu_custom_call" | custom-call | flops 19327352832 | bytes 8388608 | tf_op jit(solution)/shard_map/pallas_call | solution.py:203
  83.6 1.2 %collective-permute-start.17 = (bf16[2,512,128]{2,1,0:T(8,128)(2,1)S(1)}, bf16[2,512,128]{2,1,0:T(8,128)(2,1)S(1)}, u32[]{:S(2)}, u32[]{:S(2)}) collective-permute-start(bf16[2,512,128]{2,1,0:T(8,128)(2,1)S(1)} %get-tuple-element.23), channel_id=1, source_target_pairs={{0,1},{1,0},{2,3},{3,2},{4,5},{5,4},{6,7},{7,6},{8,9},{9,8},{10,11... | collective-permute-start | bytes 786440 | tf_op jit(solution)/shard_map/ppermute | solution.py:32
  84.8 2.5 %pad_maximum_fusion = (bf16[2,512,1024]{2,1,0:T(8,128)(2,1)}, bf16[2,512,1024]{2,1,0:T(8,128)(2,1)}) fusion(bf16[2,512,512]{2,1,0:T(8,128)(2,1)S(1)} %get-tuple-element.17, bf16[2,512,512]{2,1,0:T(8,128)(2,1)S(1)} %get-tuple-element.16, bf16[2,512,512]{2,1,0:T(8,128)(2,1)S(1)} %get-tuple-element.19, bf16[2,512,512]{2,1,0:T(8,128)(2,1)S(1)} %get-tuple-element.18), kind=kLoop, calls=%fused_computation | loop fusion | flops 8388608 | bytes 8388608 | tf_op jit(solution)/shard_map/concatenate | solution.py:278
  87.5 4.5 %collective-permute-done.16 = bf16[2,512,128]{2,1,0:T(8,128)(2,1)S(1)} collective-permute-done((bf16[2,512,128]{2,1,0:T(8,128)(2,1)S(1)}, bf16[2,512,128]{2,1,0:T(8,128)(2,1)S(1)}, u32[]{:S(2)}, u32[]{:S(2)}) %collective-permute-start.16) | collective-permute-done | bytes 262176 | tf_op jit(solution)/shard_map/ppermute | solution.py:32
  92.0 4.7 %collective-permute-done.17 = bf16[2,512,128]{2,1,0:T(8,128)(2,1)S(1)} collective-permute-done((bf16[2,512,128]{2,1,0:T(8,128)(2,1)S(1)}, bf16[2,512,128]{2,1,0:T(8,128)(2,1)S(1)}, u32[]{:S(2)}, u32[]{:S(2)}) %collective-permute-start.17) | collective-permute-done | bytes 262176 | tf_op jit(solution)/shard_map/ppermute | solution.py:32
  97.8 1.4 %collective-permute-start.21 = (bf16[2,256,256]{2,1,0:T(8,128)(2,1)S(1)}, bf16[2,256,256]{2,1,0:T(8,128)(2,1)S(1)}, u32[]{:S(2)}, u32[]{:S(2)}) collective-permute-start(bf16[2,256,256]{2,1,0:T(8,128)(2,1)S(1)} %fusion.3), channel_id=1, source_target_pairs={{0,8},{4,12},{8,0},{12,4},{1,9},{5,13},{9,1},{13,5},{2,10},{6,14},... | collective-permute-start | bytes 786440 | tf_op jit(solution)/shard_map/ppermute | solution.py:32
  99.3 6.9 %collective-permute-done.19 = bf16[2,256,256]{2,1,0:T(8,128)(2,1)S(1)} collective-permute-done((bf16[2,256,256]{2,1,0:T(8,128)(2,1)S(1)}, bf16[2,256,256]{2,1,0:T(8,128)(2,1)S(1)}, u32[]{:S(2)}, u32[]{:S(2)}) %collective-permute-start.19) | collective-permute-done | bytes 262176 | tf_op jit(solution)/shard_map/ppermute | solution.py:32
  106.3 0.9 collective-permute-start.22
  107.3 2.8 %collective-permute-done.21 = bf16[2,256,256]{2,1,0:T(8,128)(2,1)S(1)} collective-permute-done((bf16[2,256,256]{2,1,0:T(8,128)(2,1)S(1)}, bf16[2,256,256]{2,1,0:T(8,128)(2,1)S(1)}, u32[]{:S(2)}, u32[]{:S(2)}) %collective-permute-start.21) | collective-permute-done | bytes 262176 | tf_op jit(solution)/shard_map/ppermute | solution.py:32
  110.2 1.0 collective-permute-start.23
  111.2 1.1 pad_maximum_fusion.2
  112.3 2.9 %collective-permute-done.23 = bf16[2,256,128]{2,1,0:T(8,128)(2,1)S(1)} collective-permute-done((bf16[2,256,128]{2,1,0:T(8,128)(2,1)S(1)}, bf16[2,256,128]{2,1,0:T(8,128)(2,1)S(1)}, u32[]{:S(2)}, u32[]{:S(2)}) %collective-permute-start.23) | collective-permute-done | bytes 131104 | tf_op jit(solution)/shard_map/ppermute | solution.py:32
  115.3 1.1 pad_maximum_fusion.3
  (52 shorter events, 6.7 us)
Async XLA Ops:
  1.9 7.8 %collective-permute-start.4 = (bf16[2,256,128]{2,1,0:T(8,128)(2,1)S(1)}, bf16[2,256,128]{2,1,0:T(8,128)(2,1)S(1)}, u32[]{:S(2)}, u32[]{:S(2)}) collective-permute-start(bf16[2,256,128]{2,1,0:T(8,128)(2,1)S(1)} %get-tuple-element.34), channel_id=1, source_target_pairs={{0,1},{1,0},{2,3},{3,2},{4,5},{5,4},{6,7},{7,6},{8,9},{9,8},{10,11... | collective-permute-start | bytes 393224 | tf_op jit(solution)/shard_map/ppermute | solution.py:32
  5.0 5.4 %collective-permute-start.1 = (bf16[2,256,128]{2,1,0:T(8,128)(2,1)S(1)}, bf16[2,256,128]{2,1,0:T(8,128)(2,1)S(1)}, u32[]{:S(2)}, u32[]{:S(2)}) collective-permute-start(bf16[2,256,128]{2,1,0:T(8,128)(2,1)S(1)} %get-tuple-element.36), channel_id=1, source_target_pairs={{0,8},{4,12},{8,0},{12,4},{1,9},{5,13},{9,1},{13,5},{2,10},{6,14},... | collective-permute-start | bytes 393224 | tf_op jit(solution)/shard_map/ppermute | solution.py:32
  6.5 5.2 %collective-permute-start.2 = (bf16[2,256,128]{2,1,0:T(8,128)(2,1)S(1)}, bf16[2,256,128]{2,1,0:T(8,128)(2,1)S(1)}, u32[]{:S(2)}, u32[]{:S(2)}) collective-permute-start(bf16[2,256,128]{2,1,0:T(8,128)(2,1)S(1)} %get-tuple-element.36), channel_id=1, source_target_pairs={{0,4},{4,0},{8,12},{12,8},{1,5},{5,1},{9,13},{13,9},{2,6},{6,2},{1... | collective-permute-start | bytes 393224 | tf_op jit(solution)/shard_map/ppermute | solution.py:32
  6.5 6.3 %collective-permute-start.12 = (bf16[2,256,128]{2,1,0:T(8,128)(2,1)S(1)}, bf16[2,256,128]{2,1,0:T(8,128)(2,1)S(1)}, u32[]{:S(2)}, u32[]{:S(2)}) collective-permute-start(bf16[2,256,128]{2,1,0:T(8,128)(2,1)S(1)} %get-tuple-element.37), channel_id=1, source_target_pairs={{0,1},{1,0},{2,3},{3,2},{4,5},{5,4},{6,7},{7,6},{8,9},{9,8},{10,11... | collective-permute-start | bytes 393224 | tf_op jit(solution)/shard_map/ppermute | solution.py:32
  8.0 12.0 %collective-permute-start = (bf16[2,512,128]{2,1,0:T(8,128)(2,1)S(1)}, bf16[2,512,128]{2,1,0:T(8,128)(2,1)S(1)}, u32[]{:S(2)}, u32[]{:S(2)}) collective-permute-start(bf16[2,512,128]{2,1,0:T(8,128)(2,1)S(1)} %get-tuple-element.30), channel_id=1, source_target_pairs={{0,1},{1,0},{2,3},{3,2},{4,5},{5,4},{6,7},{7,6},{8,9},{9,8},{10,11... | collective-permute-start | bytes 786440 | tf_op jit(solution)/shard_map/ppermute | solution.py:32
  9.6 6.4 %collective-permute-start.9 = (bf16[2,256,128]{2,1,0:T(8,128)(2,1)S(1)}, bf16[2,256,128]{2,1,0:T(8,128)(2,1)S(1)}, u32[]{:S(2)}, u32[]{:S(2)}) collective-permute-start(bf16[2,256,128]{2,1,0:T(8,128)(2,1)S(1)} %get-tuple-element.35), channel_id=1, source_target_pairs={{0,8},{4,12},{8,0},{12,4},{1,9},{5,13},{9,1},{13,5},{2,10},{6,14},... | collective-permute-start | bytes 393224 | tf_op jit(solution)/shard_map/ppermute | solution.py:32
  10.4 8.5 %collective-permute-start.5 = (bf16[2,256,128]{2,1,0:T(8,128)(2,1)S(1)}, bf16[2,256,128]{2,1,0:T(8,128)(2,1)S(1)}, u32[]{:S(2)}, u32[]{:S(2)}) collective-permute-start(bf16[2,256,128]{2,1,0:T(8,128)(2,1)S(1)} %collective-permute-done.4.refs_8_), channel_id=1, source_target_pairs={{0,8},{4,12},{8,0},{12,4},{1,9},{5,13},{9,1},{13,5},{2,10},{6,14},... | collective-permute-start | bytes 393224 | tf_op jit(solution)/shard_map/ppermute | solution.py:32
  11.7 7.2 %collective-permute-start.3 = (bf16[2,256,128]{2,1,0:T(8,128)(2,1)S(1)}, bf16[2,256,128]{2,1,0:T(8,128)(2,1)S(1)}, u32[]{:S(2)}, u32[]{:S(2)}) collective-permute-start(bf16[2,256,128]{2,1,0:T(8,128)(2,1)S(1)} %collective-permute-done.1.refs_5_), channel_id=1, source_target_pairs={{0,4},{4,0},{8,12},{12,8},{1,5},{5,1},{9,13},{13,9},{2,6},{6,2},{1... | collective-permute-start | bytes 393224 | tf_op jit(solution)/shard_map/ppermute | solution.py:32
  12.8 6.7 %collective-permute-start.6 = (bf16[2,256,128]{2,1,0:T(8,128)(2,1)S(1)}, bf16[2,256,128]{2,1,0:T(8,128)(2,1)S(1)}, u32[]{:S(2)}, u32[]{:S(2)}) collective-permute-start(bf16[2,256,128]{2,1,0:T(8,128)(2,1)S(1)} %collective-permute-done.4.refs_8_), channel_id=1, source_target_pairs={{0,4},{4,0},{8,12},{12,8},{1,5},{5,1},{9,13},{13,9},{2,6},{6,2},{1... | collective-permute-start | bytes 393224 | tf_op jit(solution)/shard_map/ppermute | solution.py:32
  16.0 5.0 %collective-permute-start.13 = (bf16[2,256,128]{2,1,0:T(8,128)(2,1)S(1)}, bf16[2,256,128]{2,1,0:T(8,128)(2,1)S(1)}, u32[]{:S(2)}, u32[]{:S(2)}) collective-permute-start(bf16[2,256,128]{2,1,0:T(8,128)(2,1)S(1)} %collective-permute-done.12.refs_8_), channel_id=1, source_target_pairs={{0,8},{4,12},{8,0},{12,4},{1,9},{5,13},{9,1},{13,5},{2,10},{6,14},... | collective-permute-start | bytes 393224 | tf_op jit(solution)/shard_map/ppermute | solution.py:32
  18.8 2.2 %collective-permute-start.7 = (bf16[2,256,128]{2,1,0:T(8,128)(2,1)S(1)}, bf16[2,256,128]{2,1,0:T(8,128)(2,1)S(1)}, u32[]{:S(2)}, u32[]{:S(2)}) collective-permute-start(bf16[2,256,128]{2,1,0:T(8,128)(2,1)S(1)} %collective-permute-done.5.refs_9_), channel_id=1, source_target_pairs={{0,4},{4,0},{8,12},{12,8},{1,5},{5,1},{9,13},{13,9},{2,6},{6,2},{1... | collective-permute-start | bytes 393224 | tf_op jit(solution)/shard_map/ppermute | solution.py:32
  18.9 32.9 %collective-permute-start.10 = (bf16[2,256,128]{2,1,0:T(8,128)(2,1)S(1)}, bf16[2,256,128]{2,1,0:T(8,128)(2,1)S(1)}, u32[]{:S(2)}, u32[]{:S(2)}) collective-permute-start(bf16[2,256,128]{2,1,0:T(8,128)(2,1)S(1)} %get-tuple-element.35), channel_id=1, source_target_pairs={{0,4},{4,0},{8,12},{12,8},{1,5},{5,1},{9,13},{13,9},{2,6},{6,2},{1... | collective-permute-start | bytes 393224 | tf_op jit(solution)/shard_map/ppermute | solution.py:32
  19.4 32.5 %collective-permute-start.8 = (bf16[2,512,128]{2,1,0:T(8,128)(2,1)S(1)}, bf16[2,512,128]{2,1,0:T(8,128)(2,1)S(1)}, u32[]{:S(2)}, u32[]{:S(2)}) collective-permute-start(bf16[2,512,128]{2,1,0:T(8,128)(2,1)S(1)} %get-tuple-element.31), channel_id=1, source_target_pairs={{0,1},{1,0},{2,3},{3,2},{4,5},{5,4},{6,7},{7,6},{8,9},{9,8},{10,11... | collective-permute-start | bytes 786440 | tf_op jit(solution)/shard_map/ppermute | solution.py:32
  20.0 31.9 %collective-permute-start.14 = (bf16[2,256,128]{2,1,0:T(8,128)(2,1)S(1)}, bf16[2,256,128]{2,1,0:T(8,128)(2,1)S(1)}, u32[]{:S(2)}, u32[]{:S(2)}) collective-permute-start(bf16[2,256,128]{2,1,0:T(8,128)(2,1)S(1)} %collective-permute-done.12.refs_8_), channel_id=1, source_target_pairs={{0,4},{4,0},{8,12},{12,8},{1,5},{5,1},{9,13},{13,9},{2,6},{6,2},{1... | collective-permute-start | bytes 393224 | tf_op jit(solution)/shard_map/ppermute | solution.py:32
  21.0 30.9 %collective-permute-start.11 = (bf16[2,256,128]{2,1,0:T(8,128)(2,1)S(1)}, bf16[2,256,128]{2,1,0:T(8,128)(2,1)S(1)}, u32[]{:S(2)}, u32[]{:S(2)}) collective-permute-start(bf16[2,256,128]{2,1,0:T(8,128)(2,1)S(1)} %collective-permute-done.9.refs_5_), channel_id=1, source_target_pairs={{0,4},{4,0},{8,12},{12,8},{1,5},{5,1},{9,13},{13,9},{2,6},{6,2},{1... | collective-permute-start | bytes 393224 | tf_op jit(solution)/shard_map/ppermute | solution.py:32
  21.0 30.9 %collective-permute-start.15 = (bf16[2,256,128]{2,1,0:T(8,128)(2,1)S(1)}, bf16[2,256,128]{2,1,0:T(8,128)(2,1)S(1)}, u32[]{:S(2)}, u32[]{:S(2)}) collective-permute-start(bf16[2,256,128]{2,1,0:T(8,128)(2,1)S(1)} %collective-permute-done.13.refs_9_), channel_id=1, source_target_pairs={{0,4},{4,0},{8,12},{12,8},{1,5},{5,1},{9,13},{13,9},{2,6},{6,2},{1... | collective-permute-start | bytes 393224 | tf_op jit(solution)/shard_map/ppermute | solution.py:32
  51.8 45.0 %collective-permute-start.18 = (bf16[2,2,256,256]{3,2,1,0:T(8,128)(2,1)S(1)}, bf16[2,2,256,256]{3,2,1,0:T(8,128)(2,1)S(1)}, u32[]{:S(2)}, u32[]{:S(2)}) collective-permute-start(bf16[2,2,256,256]{3,2,1,0:T(8,128)(2,1)S(1)} %get-tuple-element.25), channel_id=1, source_target_pairs={{0,4},{4,0},{8,12},{12,8},{1,5},{5,1},{9,13},{13,9},{2,6},{6,2},{1... | collective-permute-start | bytes 1572872 | tf_op jit(solution)/shard_map/ppermute | solution.py:32
  82.3 15.4 %collective-permute-start.20 = (bf16[2,2,256,256]{3,2,1,0:T(8,128)(2,1)S(1)}, bf16[2,2,256,256]{3,2,1,0:T(8,128)(2,1)S(1)}, u32[]{:S(2)}, u32[]{:S(2)}) collective-permute-start(bf16[2,2,256,256]{3,2,1,0:T(8,128)(2,1)S(1)} %get-tuple-element.27), channel_id=1, source_target_pairs={{0,4},{4,0},{8,12},{12,8},{1,5},{5,1},{9,13},{13,9},{2,6},{6,2},{1... | collective-permute-start | bytes 1572872 | tf_op jit(solution)/shard_map/ppermute | solution.py:32
  82.8 9.2 %collective-permute-start.16 = (bf16[2,512,128]{2,1,0:T(8,128)(2,1)S(1)}, bf16[2,512,128]{2,1,0:T(8,128)(2,1)S(1)}, u32[]{:S(2)}, u32[]{:S(2)}) collective-permute-start(bf16[2,512,128]{2,1,0:T(8,128)(2,1)S(1)} %get-tuple-element.22), channel_id=1, source_target_pairs={{0,1},{1,0},{2,3},{3,2},{4,5},{5,4},{6,7},{7,6},{8,9},{9,8},{10,11... | collective-permute-start | bytes 786440 | tf_op jit(solution)/shard_map/ppermute | solution.py:32
  83.6 13.1 %collective-permute-start.17 = (bf16[2,512,128]{2,1,0:T(8,128)(2,1)S(1)}, bf16[2,512,128]{2,1,0:T(8,128)(2,1)S(1)}, u32[]{:S(2)}, u32[]{:S(2)}) collective-permute-start(bf16[2,512,128]{2,1,0:T(8,128)(2,1)S(1)} %get-tuple-element.23), channel_id=1, source_target_pairs={{0,1},{1,0},{2,3},{3,2},{4,5},{5,4},{6,7},{7,6},{8,9},{9,8},{10,11... | collective-permute-start | bytes 786440 | tf_op jit(solution)/shard_map/ppermute | solution.py:32
  97.0 9.3 %collective-permute-start.19 = (bf16[2,256,256]{2,1,0:T(8,128)(2,1)S(1)}, bf16[2,256,256]{2,1,0:T(8,128)(2,1)S(1)}, u32[]{:S(2)}, u32[]{:S(2)}) collective-permute-start(bf16[2,256,256]{2,1,0:T(8,128)(2,1)S(1)} %fusion.2), channel_id=1, source_target_pairs={{0,8},{4,12},{8,0},{12,4},{1,9},{5,13},{9,1},{13,5},{2,10},{6,14},... | collective-permute-start | bytes 786440 | tf_op jit(solution)/shard_map/ppermute | solution.py:32
  97.8 12.3 %collective-permute-start.21 = (bf16[2,256,256]{2,1,0:T(8,128)(2,1)S(1)}, bf16[2,256,256]{2,1,0:T(8,128)(2,1)S(1)}, u32[]{:S(2)}, u32[]{:S(2)}) collective-permute-start(bf16[2,256,256]{2,1,0:T(8,128)(2,1)S(1)} %fusion.3), channel_id=1, source_target_pairs={{0,8},{4,12},{8,0},{12,4},{1,9},{5,13},{9,1},{13,5},{2,10},{6,14},... | collective-permute-start | bytes 786440 | tf_op jit(solution)/shard_map/ppermute | solution.py:32
  106.3 5.9 %collective-permute-start.22 = (bf16[2,256,128]{2,1,0:T(8,128)(2,1)S(1)}, bf16[2,256,128]{2,1,0:T(8,128)(2,1)S(1)}, u32[]{:S(2)}, u32[]{:S(2)}) collective-permute-start(bf16[2,256,128]{2,1,0:T(8,128)(2,1)S(1)} %slice.59), channel_id=1, source_target_pairs={{0,1},{1,0},{2,3},{3,2},{4,5},{5,4},{6,7},{7,6},{8,9},{9,8},{10,11... | collective-permute-start | bytes 393224 | tf_op jit(solution)/shard_map/ppermute | solution.py:32
  110.2 5.0 %collective-permute-start.23 = (bf16[2,256,128]{2,1,0:T(8,128)(2,1)S(1)}, bf16[2,256,128]{2,1,0:T(8,128)(2,1)S(1)}, u32[]{:S(2)}, u32[]{:S(2)}) collective-permute-start(bf16[2,256,128]{2,1,0:T(8,128)(2,1)S(1)} %slice.58), channel_id=1, source_target_pairs={{0,1},{1,0},{2,3},{3,2},{4,5},{5,4},{6,7},{7,6},{8,9},{9,8},{10,11... | collective-permute-start | bytes 393224 | tf_op jit(solution)/shard_map/ppermute | solution.py:32
  (2 other events, 39.1 us)
where the time goes:
time: 117 us; the launch traced here: 116 us
  Pallas kernels  60.6 us (52%)
  waiting for transfers between devices  29.2 us (25%)
  starting transfers between devices  17.8 us (15%)
  other arithmetic  5.29 us (5%)
  local copies, waits for them, and re-layouts  2.63 us (2%)
    pallas_call x2, Pallas kernels, attend(): pl.pallas_call(functools.partial(attend_kernel, (pieces, rows, n_keep, he...  60.6 us
    ppermute x24, waiting for transfers between devices, swap(): return lax.ppermute(block, axis, route)  29.2 us
    ppermute x24, starting transfers between devices, swap(): return lax.ppermute(block, axis, route)  17.8 us
    concatenate x1, other arithmetic, whole_heads(): jnp.concatenate(attended, axis=-1)  2.54 us
  transfers between devices with their start and end apart: 24, of which 9 were waited for; matrix products, arithmetic and copies ran while one was open for 5% of the time, Pallas kernels for 52%

commit v1 on v0

--- a/solution.py
+++ b/solution.py
@@ -33,16 +33,16 @@
 
 
 def attend_kernel(sizes, scalars, *refs):
-    pieces, rows, n_keep, heads = sizes
+    pieces, rows, n_keep, heads, aliased = sizes
     refs = list(refs)
     q_ref, do_ref, ra_ref, rb_ref = refs[:4]
     pa_refs = refs[4 : 4 + pieces]
     pb_refs = refs[4 + pieces : 4 + 2 * pieces]
-    rest = refs[4 + 2 * pieces :]
+    rest = refs[4 + 2 * pieces + (2 if aliased else 0) :]
     n_out = 5 + (1 if pieces > n_keep else 0)
     out_ref, dq_ref, dra_ref, drb_ref, dkeep_ref = rest[:5]
     dsend_ref = rest[5] if n_out == 6 else None
-    k_all, v_all, probs, dscores, acc_k, acc_v, res_k, res_v = rest[n_out:]
+    k_all, v_all, k_t, v_t, weights, probs, dscores, acc_k, acc_v, res_k, res_v = rest[n_out:]
 
     r = pl.program_id(0)
     head = pl.program_id(1)
@@ -75,64 +75,102 @@
     def _():
         res_k[...] = jnp.zeros_like(res_k)
         res_v[...] = jnp.zeros_like(res_v)
+        k_t[...] = k_all[...].T
+        v_t[...] = v_all[...].T
 
     n_blocks = n_query // BLOCK
-    for i in range(n_blocks):
-        t0 = i * BLOCK
-        seen = n_prompt + t0 + BLOCK
-        q = q_ref[0, t0 : t0 + BLOCK, :]
-        do = do_ref[0, t0 : t0 + BLOCK, :]
-        keys = k_all[:seen, :]
-        values = v_all[:seen, :]
-        s = dot(q, keys, NT)
-        diag = s[:, seen - BLOCK :]
-        row = lax.broadcasted_iota(jnp.int32, (BLOCK, BLOCK), 0)
-        col = lax.broadcasted_iota(jnp.int32, (BLOCK, BLOCK), 1)
-        diag = jnp.where(col <= row, diag, MASKED)
-        s = jnp.concatenate([s[:, : seen - BLOCK], diag], axis=1)
-        top = jnp.max(s, axis=1, keepdims=True)
-        w = jnp.exp2(s * (SCALE * LOG2E) - top * (SCALE * LOG2E))
-        p = w * (1.0 / jnp.sum(w, axis=1, keepdims=True))
-        p16 = p.astype(jnp.bfloat16)
-        probs[t0 : t0 + BLOCK, :seen] = p16
-        o = dot(p16, values, NN)
-        out_ref[0, t0 : t0 + BLOCK, :] = o.astype(jnp.bfloat16)
-        delta = jnp.sum(o * do.astype(jnp.float32), axis=1, keepdims=True)
-        dp = dot(do, values, NT)
-        ds = (p * (dp - delta)).astype(jnp.bfloat16)
-        dscores[t0 : t0 + BLOCK, :seen] = ds
-        dq_ref[0, t0 : t0 + BLOCK, :] = (dot(ds, keys, NN) * SCALE).astype(jnp.bfloat16)
+    state = [dict() for _ in range(n_blocks)]
+
+    def span(c):
+        return slice(c * BLOCK, (c + 1) * BLOCK)
+
+    def fold(x, op):
+        return op(x.reshape(-1, 8, x.shape[-1]), axis=0)
+
+    def stages(i):
+        st = state[i]
+        t = span(i)
+        n_chunks = n_prompt // BLOCK + i + 1
+        seen = n_chunks * BLOCK
+        q = q_ref[0, t, :]
+        do = do_ref[0, t, :]
+
+        def score(c):
+            s = dot(k_all[span(c), :], q, NT)
+            if c == n_chunks - 1:
+                row = lax.broadcasted_iota(jnp.int32, (BLOCK, BLOCK), 0)
+                col = lax.broadcasted_iota(jnp.int32, (BLOCK, BLOCK), 1)
+                s = jnp.where(row <= col, s, MASKED)
+            weights[span(c), t] = s
+            top = fold(s, jnp.max)
+            st["top"] = top if c == 0 else jnp.maximum(st["top"], top)
+            if c == n_chunks - 1:
+                st["top"] = jnp.max(st["top"], axis=0, keepdims=True) * (SCALE * LOG2E)
+
+        def weigh(c):
+            w = jnp.exp2(weights[span(c), t] * (SCALE * LOG2E) - st["top"])
+            weights[span(c), t] = w
+            total = fold(w, jnp.sum)
+            st["sum"] = total if c == 0 else st["sum"] + total
+            if c == n_chunks - 1:
+                st["inv"] = 1.0 / jnp.sum(st["sum"], axis=0, keepdims=True)
+
+        def norm(c):
+            probs[span(c), t] = (weights[span(c), t] * st["inv"]).astype(jnp.bfloat16)
+            if c == n_chunks - 1:
+                o = dot(v_t[:, :seen], probs[:seen, t], NN)
+                out_ref[0, t, :] = o.T.astype(jnp.bfloat16)
+                do_t = do.astype(jnp.float32).T
+                st["delta"] = jnp.sum(o * do_t, axis=0, keepdims=True)
+                st["inv"] = st["inv"] * SCALE
+
+        def grad(c):
+            dp = dot(v_all[span(c), :], do, NT)
+            ds = (weights[span(c), t] * st["inv"]) * (dp - st["delta"])
+            dscores[span(c), t] = ds.astype(jnp.bfloat16)
+            if c == n_chunks - 1:
+                dq = dot(k_t[:, :seen], dscores[:seen, t], NN)
+                dq_ref[0, t, :] = dq.T.astype(jnp.bfloat16)
+
+        return [[functools.partial(f, c) for c in range(n_chunks)] for f in (score, weigh, norm, grad)]
+
+    plan = [stages(i) for i in range(n_blocks)]
+    for slot in range(4 + n_blocks - 1):
+        groups = [plan[i][slot - i] for i in reversed(range(n_blocks)) if 0 <= slot - i < 4]
+        for c in range(max(len(g) for g in groups)):
+            for g in groups:
+                if c < len(g):
+                    g[c]()
 
     q_all = q_ref[0]
     do_all = do_ref[0]
-    acc_k[prompt] += dot(dscores[:, :n_prompt], q_all, TN)
-    acc_v[prompt] += dot(probs[:, :n_prompt], do_all, TN)
+    for c in range(n_prompt // BLOCK):
+        acc_v[prompt, span(c), :] += dot(probs[span(c), :], do_all, NN)
+        acc_k[prompt, span(c), :] += dot(dscores[span(c), :], q_all, NN)
     for i in range(n_blocks):
+        u = span(n_prompt // BLOCK + i)
         t0 = i * BLOCK
-        u0 = n_prompt + t0
-        res_k[t0 : t0 + BLOCK, :] += dot(dscores[t0:, u0 : u0 + BLOCK], q_all[t0:], TN)
-        res_v[t0 : t0 + BLOCK, :] += dot(probs[t0:, u0 : u0 + BLOCK], do_all[t0:], TN)
+        res_v[span(i), :] += dot(probs[u, t0:], do_all[t0:], NN)
+        res_k[span(i), :] += dot(dscores[u, t0:], q_all[t0:], NN)
 
     last = head == heads - 1
 
     @pl.when(last & even)
     def _():
-        dra_ref[0] = (res_k[...] * SCALE).astype(jnp.bfloat16)
+        dra_ref[0] = res_k[...].astype(jnp.bfloat16)
         drb_ref[0] = res_v[...].astype(jnp.bfloat16)
 
     @pl.when(last & jnp.logical_not(even))
     def _():
         dra_ref[0] = res_v[...].astype(jnp.bfloat16)
-        drb_ref[0] = (res_k[...] * SCALE).astype(jnp.bfloat16)
+        drb_ref[0] = res_k[...].astype(jnp.bfloat16)
 
     done = last & (r == pl.num_programs(0) - 1)
 
-    def scatter(slot, acc, factor):
+    def scatter(slot, acc):
         for i in range(pieces):
             for p_id in range(P_SIZE):
                 val = acc[p_id, i * rows : (i + 1) * rows, :]
-                if factor != 1.0:
-                    val = val * factor
                 if i < n_keep:
                     dkeep_ref[i, p_id, :, slot * HD : (slot + 1) * HD] = val
                 else:
@@ -140,16 +178,16 @@
 
     @pl.when(done & even)
     def _():
-        scatter(0, acc_k, SCALE)
-        scatter(1, acc_v, 1.0)
+        scatter(0, acc_k)
+        scatter(1, acc_v)
 
     @pl.when(done & jnp.logical_not(even))
     def _():
-        scatter(0, acc_v, 1.0)
-        scatter(1, acc_k, SCALE)
-
-
-def attend(scalars, queries, d_out, resp_a, resp_b, prompt_a, prompt_b, n_keep, chunk, heads):
+        scatter(0, acc_v)
+        scatter(1, acc_k)
+
+
+def attend(scalars, queries, d_out, resp_a, resp_b, prompt_a, prompt_b, n_keep, chunk, heads, before=None):
     n_resp, n_query, _ = queries.shape
     pieces = len(prompt_a)
     rows = prompt_a[0][0].shape[1]
@@ -170,18 +208,19 @@
     in_specs = [q_spec, q_spec]
     in_specs += [pl.BlockSpec((1, n_query, HD), resp_map(c)) for _, c in (resp_a, resp_b)]
     in_specs += [pl.BlockSpec((1, rows, HD), prompt_map(c)) for _, c in (*prompt_a, *prompt_b)]
-    own_map = lambda r, j, sc: (r, 0, j)
+    if before is not None:
+        in_specs += [pl.BlockSpec(memory_space=pl.ANY)] * 2
     out_specs = [
-        pl.BlockSpec((1, n_query, HD), own_map),
-        pl.BlockSpec((1, n_query, HD), own_map),
+        q_spec,
+        q_spec,
         pl.BlockSpec((1, n_query, HD), lambda r, j, sc: (r, 0, 0)),
         pl.BlockSpec((1, n_query, HD), lambda r, j, sc: (r, 0, 0)),
         pl.BlockSpec((n_keep, P_SIZE, rows, 2 * HD), lambda r, j, sc: (0, 0, 0, 0)),
     ]
     shape = jax.ShapeDtypeStruct
     out_shape = [
-        shape((n_resp, n_query, heads * HD), jnp.bfloat16),
-        shape((n_resp, n_query, heads * HD), jnp.bfloat16),
+        shape(queries.shape, jnp.bfloat16),
+        shape(queries.shape, jnp.bfloat16),
         shape((n_resp, n_query, HD), jnp.bfloat16),
         shape((n_resp, n_query, HD), jnp.bfloat16),
         shape((n_keep, P_SIZE, rows, 2 * HD), jnp.float32),
@@ -192,16 +231,22 @@
     scratch = [
         pltpu.VMEM((n_keys, HD), jnp.bfloat16),
         pltpu.VMEM((n_keys, HD), jnp.bfloat16),
-        pltpu.VMEM((n_query, n_keys), jnp.bfloat16),
-        pltpu.VMEM((n_query, n_keys), jnp.bfloat16),
+        pltpu.VMEM((HD, n_keys), jnp.bfloat16),
+        pltpu.VMEM((HD, n_keys), jnp.bfloat16),
+        pltpu.VMEM((n_keys, n_query), jnp.float32),
+        pltpu.VMEM((n_keys, n_query), jnp.bfloat16),
+        pltpu.VMEM((n_keys, n_query), jnp.bfloat16),
         pltpu.VMEM((P_SIZE, n_prompt, HD), jnp.float32),
         pltpu.VMEM((P_SIZE, n_prompt, HD), jnp.float32),
         pltpu.VMEM((n_query, HD), jnp.float32),
         pltpu.VMEM((n_query, HD), jnp.float32),
     ]
+    extra = () if before is None else before
+    n_in = 5 + 2 * pieces
+    aliases = {} if before is None else {n_in: 0, n_in + 1: 1}
     flops = 12 * n_resp * heads * n_query * n_keys * HD
     return pl.pallas_call(
-        functools.partial(attend_kernel, (pieces, rows, n_keep, heads)),
+        functools.partial(attend_kernel, (pieces, rows, n_keep, heads, before is not None)),
         grid_spec=pltpu.PrefetchScalarGridSpec(
             num_scalar_prefetch=1,
             grid=(n_resp, heads),
@@ -210,9 +255,10 @@
             scratch_shapes=scratch,
         ),
         out_shape=out_shape,
+        input_output_aliases=aliases,
         compiler_params=pltpu.CompilerParams(vmem_limit_bytes=48 * 2**20),
         cost_estimate=pl.CostEstimate(flops=2 * flops, bytes_accessed=8 * 2**20, transcendentals=0),
-    )(scalars, queries, d_out, resp_a[0], resp_b[0], *[a for a, _ in (*prompt_a, *prompt_b)])
+    )(scalars, queries, d_out, resp_a[0], resp_b[0], *[a for a, _ in (*prompt_a, *prompt_b)], *extra)
 
 
 def per_device(queries, resp_kv, prompt_kv, prompt_of, d_out):
@@ -231,7 +277,7 @@
     def column(array, which):
         return lax.dynamic_slice_in_dim(array, which * HD, HD, axis=array.ndim - 1)
 
-    attended, d_queries, d_resp, d_prompt = [], [], [], []
+    d_resp, d_prompt, before = [], [], None
     for h in range(n_own):
         own = lambda par, h=h: par * n_own + h
         theirs = (1 - parity) * n_own + h
@@ -256,9 +302,9 @@
             2,
             h,
             GROUP,
+            before,
         )
-        attended.append(att)
-        d_queries.append(dq)
+        before = (att, dq)
         d_resp.append((dra, swap(drb, "prefix", 0)))
         part = swap(dsend, "dp", 0)
         sums = dkeep + part.astype(jnp.float32)
@@ -275,8 +321,7 @@
         return jnp.concatenate([jnp.where(even, mine, other), jnp.where(even, other, mine)], axis=-1)
 
     return (
-        jnp.concatenate(attended, axis=-1),
-        jnp.concatenate(d_queries, axis=-1),
+        *before,
         place(d_resp),
         place(d_prompt),
     )

time: 117 us -> 106 us (0.906)
  Pallas kernels: 60.6 us -> 53.5 us
  other arithmetic: 5.29 us -> 2.76 us
  waiting for transfers between devices: 29.2 us -> 27.5 us
    pallas_call x2, Pallas kernels: 60.6 us -> 53.5 us  [attend(): pl.pallas_call(functools.partial(attend_kernel, (pieces, rows, n_keep, he...]
    concatenate x1 -> x0, other arithmetic: 2.54 us -> none  [whole_heads(): jnp.concatenate(attended, axis=-1)]
    ppermute x24, waiting for transfers between devices: 29.2 us -> 27.5 us  [swap(): return lax.ppermute(block, axis, route)]
  transfers between devices with their start and end apart: 24 -> 24, of which waited for: 9 -> 8; matrix products, arithmetic and copies ran while one was open for 5% -> 3% of each run, Pallas kernels for 52% -> 51%
where the time goes in v1:
time: 106 us
  Pallas kernels  53.5 us (50%)
  waiting for transfers between devices  27.5 us (26%)
  starting transfers between devices  17.6 us (17%)
  local copies, waits for them, and re-layouts  3.4 us (3%)
  other arithmetic  2.76 us (3%)
    pallas_call x2, Pallas kernels, attend(): pl.pallas_call(functools.partial(attend_kernel, (pieces, rows, n_keep, he...  53.5 us
    ppermute x24, waiting for transfers between devices, swap(): return lax.ppermute(block, axis, route)  27.5 us
    ppermute x24, starting transfers between devices, swap(): return lax.ppermute(block, axis, route)  17.6 us
    dynamic_slice x2, local copies, waits for them, and re-layouts, column(): return lax.dynamic_slice_in_dim(array, which * HD, HD, axis=array.ndim - 1)  3.03 us
    concatenate x2, other arithmetic, place(): jnp.concatenate([jnp.where(even, mine, other), jnp.where(even, other, min...  2.18 us
  transfers between devices with their start and end apart: 24, of which 8 were waited for; matrix products, arithmetic and copies ran while one was open for 3% of the time, Pallas kernels for 51%

profile of v1, /device:TPU:0, one launch (start us, length us, event | category | flops | bytes accessed | tf_op | source)
XLA Modules:
  0.0 105.7 jit_solution(6420241537952152946)
XLA Ops:
  0.7 1.3 %constant_dynamic-slice_fusion = (bf16[2,256,128]{2,1,0:T(8,128)(2,1)S(1)}, bf16[2,256,128]{2,1,0:T(8,128)(2,1)S(1)}, bf16[2,256,128]{2,1,0:T(8,128)(2,1)S(1)}, bf16[2,256,128]{2,1,0:T(8,128)(2,1)S(1)}) fusion(bf16[2,256,512]{2,1,0:T(8,128)(2,1)} %refs_4_.3, s32[]{:T(128)S(6)} %select_n.48, s32[]{:T(128)S(6)} %select_n.49, s32[]{:T(128)S(6)} %select_n.46, ...), kind=kLoop, calls=%fused_computation.24 | loop fusion | bytes 1048592 | tf_op jit(solution)/shard_map/dynamic_slice | solution.py:278
  2.0 3.1 %collective-permute-start.12 = (bf16[2,256,128]{2,1,0:T(8,128)(2,1)S(1)}, bf16[2,256,128]{2,1,0:T(8,128)(2,1)S(1)}, u32[]{:S(2)}, u32[]{:S(2)}) collective-permute-start(bf16[2,256,128]{2,1,0:T(8,128)(2,1)S(1)} %get-tuple-element.34), channel_id=1, source_target_pairs={{0,1},{1,0},{2,3},{3,2},{4,5},{5,4},{6,7},{7,6},{8,9},{9,8},{10,11... | collective-permute-start | bytes 393224 | tf_op jit(solution)/shard_map/ppermute | solution.py:32
  5.0 1.5 %collective-permute-start.9 = (bf16[2,256,128]{2,1,0:T(8,128)(2,1)S(1)}, bf16[2,256,128]{2,1,0:T(8,128)(2,1)S(1)}, u32[]{:S(2)}, u32[]{:S(2)}) collective-permute-start(bf16[2,256,128]{2,1,0:T(8,128)(2,1)S(1)} %get-tuple-element.35), channel_id=1, source_target_pairs={{0,8},{4,12},{8,0},{12,4},{1,9},{5,13},{9,1},{13,5},{2,10},{6,14},... | collective-permute-start | bytes 393224 | tf_op jit(solution)/shard_map/ppermute | solution.py:32
  7.0 1.8 %constant_dynamic-slice_fusion.2 = (bf16[2,512,128]{2,1,0:T(8,128)(2,1)}, bf16[2,512,128]{2,1,0:T(8,128)(2,1)S(1)}) fusion(bf16[2,512,512]{2,1,0:T(8,128)(2,1)} %refs_2_.3, s32[]{:T(128)S(6)} %select_n.48, s32[]{:T(128)S(6)} %select_n.46), kind=kLoop, calls=%fused_computation.26 | loop fusion | bytes 1048584 | tf_op jit(solution)/shard_map/dynamic_slice | solution.py:278
  8.8 1.6 %collective-permute-start.8 = (bf16[2,512,128]{2,1,0:T(8,128)(2,1)}, bf16[2,512,128]{2,1,0:T(8,128)(2,1)S(1)}, u32[]{:S(2)}, u32[]{:S(2)}) collective-permute-start(bf16[2,512,128]{2,1,0:T(8,128)(2,1)} %get-tuple-element.30), channel_id=1, source_target_pairs={{0,1},{1,0},{2,3},{3,2},{4,5},{5,4},{6,7},{7,6},{8,9},{9,8},{10,11... | collective-permute-start | bytes 786440 | tf_op jit(solution)/shard_map/ppermute | solution.py:32
  10.9 1.5 %collective-permute-start.13 = (bf16[2,256,128]{2,1,0:T(8,128)(2,1)S(1)}, bf16[2,256,128]{2,1,0:T(8,128)(2,1)S(1)}, u32[]{:S(2)}, u32[]{:S(2)}) collective-permute-start(bf16[2,256,128]{2,1,0:T(8,128)(2,1)S(1)} %collective-permute-done.12.refs_8_), channel_id=1, source_target_pairs={{0,8},{4,12},{8,0},{12,4},{1,9},{5,13},{9,1},{13,5},{2,10},{6,14},... | collective-permute-start | bytes 393224 | tf_op jit(solution)/shard_map/ppermute | solution.py:32
  12.9 3.8 %collective-permute-done.1.refs_5_ = bf16[2,256,128]{2,1,0:T(8,128)(2,1)S(1)} collective-permute-done((bf16[2,256,128]{2,1,0:T(8,128)(2,1)S(1)}, bf16[2,256,128]{2,1,0:T(8,128)(2,1)S(1)}, u32[]{:S(2)}, u32[]{:S(2)}) %collective-permute-start.1) | collective-permute-done | bytes 131104 | tf_op jit(solution)/shard_map/ppermute | solution.py:32
  17.3 2.3 %collective-permute-done.13.refs_9_ = bf16[2,256,128]{2,1,0:T(8,128)(2,1)S(1)} collective-permute-done((bf16[2,256,128]{2,1,0:T(8,128)(2,1)S(1)}, bf16[2,256,128]{2,1,0:T(8,128)(2,1)S(1)}, u32[]{:S(2)}, u32[]{:S(2)}) %collective-permute-start.13) | collective-permute-done | bytes 131104 | tf_op jit(solution)/shard_map/ppermute | solution.py:32
  20.1 0.6 collective-permute-start
  20.7 1.0 collective-permute-done.5.refs_9_
  22.2 26.8 %shard_map.84 = (bf16[2,512,1024]{2,1,0:T(8,128)(2,1)}, bf16[2,512,1024]{2,1,0:T(8,128)(2,1)}, bf16[2,512,128]{2,1,0:T(8,128)(2,1)S(1)}, bf16[2,512,128]{2,1,0:T...) custom-call(s32[3]{0:T(128)S(1)} %pad_add_fusion.scalars, ...), custom_call_target="tpu_custom_call" | custom-call | flops 19327352832 | bytes 8388608 | tf_op jit(solution)/shard_map/pallas_call | solution.py:248
  49.0 1.0 collective-permute-start.16
  50.0 26.8 %shard_map.85 = (bf16[2,512,1024]{2,1,0:T(8,128)(2,1)}, bf16[2,512,1024]{2,1,0:T(8,128)(2,1)}, bf16[2,512,128]{2,1,0:T(8,128)(2,1)S(1)}, bf16[2,512,128]{2,1,0:T...) custom-call(s32[3]{0:T(128)S(1)} %pad_add_fusion.scalars, ...), custom_call_target="tpu_custom_call", output_to_operand_aliasing={{0}: (13, {}), {1}: (14, {})} | custom-call | flops 19327352832 | bytes 8388608 | tf_op jit(solution)/shard_map/pallas_call | solution.py:248
  76.8 1.3 %collective-permute-start.17 = (bf16[2,512,128]{2,1,0:T(8,128)(2,1)S(1)}, bf16[2,512,128]{2,1,0:T(8,128)(2,1)S(1)}, u32[]{:S(2)}, u32[]{:S(2)}) collective-permute-start(bf16[2,512,128]{2,1,0:T(8,128)(2,1)S(1)} %get-tuple-element.23), channel_id=1, source_target_pairs={{0,1},{1,0},{2,3},{3,2},{4,5},{5,4},{6,7},{7,6},{8,9},{9,8},{10,11... | collective-permute-start | bytes 786440 | tf_op jit(solution)/shard_map/ppermute | solution.py:32
  78.3 7.2 %collective-permute-done.17 = bf16[2,512,128]{2,1,0:T(8,128)(2,1)S(1)} collective-permute-done((bf16[2,512,128]{2,1,0:T(8,128)(2,1)S(1)}, bf16[2,512,128]{2,1,0:T(8,128)(2,1)S(1)}, u32[]{:S(2)}, u32[]{:S(2)}) %collective-permute-start.17) | collective-permute-done | bytes 262176 | tf_op jit(solution)/shard_map/ppermute | solution.py:32
  85.8 0.6 collective-permute-start.19
  86.6 1.5 %collective-permute-start.21 = (bf16[2,256,256]{2,1,0:T(8,128)(2,1)S(1)}, bf16[2,256,256]{2,1,0:T(8,128)(2,1)S(1)}, u32[]{:S(2)}, u32[]{:S(2)}) collective-permute-start(bf16[2,256,256]{2,1,0:T(8,128)(2,1)S(1)} %fusion.3), channel_id=1, source_target_pairs={{0,8},{4,12},{8,0},{12,4},{1,9},{5,13},{9,1},{13,5},{2,10},{6,14},... | collective-permute-start | bytes 786440 | tf_op jit(solution)/shard_map/ppermute | solution.py:32
  88.2 6.9 %collective-permute-done.19 = bf16[2,256,256]{2,1,0:T(8,128)(2,1)S(1)} collective-permute-done((bf16[2,256,256]{2,1,0:T(8,128)(2,1)S(1)}, bf16[2,256,256]{2,1,0:T(8,128)(2,1)S(1)}, u32[]{:S(2)}, u32[]{:S(2)}) %collective-permute-start.19) | collective-permute-done | bytes 262176 | tf_op jit(solution)/shard_map/ppermute | solution.py:32
  95.1 1.2 %collective-permute-start.22 = (bf16[2,256,128]{2,1,0:T(8,128)(2,1)S(1)}, bf16[2,256,128]{2,1,0:T(8,128)(2,1)S(1)}, u32[]{:S(2)}, u32[]{:S(2)}) collective-permute-start(bf16[2,256,128]{2,1,0:T(8,128)(2,1)S(1)} %slice.59), channel_id=1, source_target_pairs={{0,1},{1,0},{2,3},{3,2},{4,5},{5,4},{6,7},{7,6},{8,9},{9,8},{10,11... | collective-permute-start | bytes 393224 | tf_op jit(solution)/shard_map/ppermute | solution.py:32
  96.4 3.0 %collective-permute-done.21 = bf16[2,256,256]{2,1,0:T(8,128)(2,1)S(1)} collective-permute-done((bf16[2,256,256]{2,1,0:T(8,128)(2,1)S(1)}, bf16[2,256,256]{2,1,0:T(8,128)(2,1)S(1)}, u32[]{:S(2)}, u32[]{:S(2)}) %collective-permute-start.21) | collective-permute-done | bytes 262176 | tf_op jit(solution)/shard_map/ppermute | solution.py:32
  99.4 1.1 %collective-permute-start.23 = (bf16[2,256,128]{2,1,0:T(8,128)(2,1)S(1)}, bf16[2,256,128]{2,1,0:T(8,128)(2,1)S(1)}, u32[]{:S(2)}, u32[]{:S(2)}) collective-permute-start(bf16[2,256,128]{2,1,0:T(8,128)(2,1)S(1)} %slice.58), channel_id=1, source_target_pairs={{0,1},{1,0},{2,3},{3,2},{4,5},{5,4},{6,7},{7,6},{8,9},{9,8},{10,11... | collective-permute-start | bytes 393224 | tf_op jit(solution)/shard_map/ppermute | solution.py:32
  100.5 1.1 pad_maximum_fusion
  101.6 2.8 %collective-permute-done.23 = bf16[2,256,128]{2,1,0:T(8,128)(2,1)S(1)} collective-permute-done((bf16[2,256,128]{2,1,0:T(8,128)(2,1)S(1)}, bf16[2,256,128]{2,1,0:T(8,128)(2,1)S(1)}, u32[]{:S(2)}, u32[]{:S(2)}) %collective-permute-start.23) | collective-permute-done | bytes 131104 | tf_op jit(solution)/shard_map/ppermute | solution.py:32
  104.5 1.1 %pad_maximum_fusion.1 = f32[2,256,512]{2,1,0:T(8,128)} fusion(f32[2,256,256]{2,1,0:T(8,128)S(1)} %get-tuple-element.33, f32[2,256,256]{2,1,0:T(8,128)S(1)} %get-tuple-element.32), kind=kLoop, calls=%fused_computation.1 | loop fusion | flops 262144 | bytes 2097152 | tf_op jit(solution)/shard_map/concatenate | solution.py:321
  (53 shorter events, 4.1 us)
Async XLA Ops:
  2.0 8.4 %collective-permute-start.12 = (bf16[2,256,128]{2,1,0:T(8,128)(2,1)S(1)}, bf16[2,256,128]{2,1,0:T(8,128)(2,1)S(1)}, u32[]{:S(2)}, u32[]{:S(2)}) collective-permute-start(bf16[2,256,128]{2,1,0:T(8,128)(2,1)S(1)} %get-tuple-element.34), channel_id=1, source_target_pairs={{0,1},{1,0},{2,3},{3,2},{4,5},{5,4},{6,7},{7,6},{8,9},{9,8},{10,11... | collective-permute-start | bytes 393224 | tf_op jit(solution)/shard_map/ppermute | solution.py:32
  5.0 5.8 %collective-permute-start.9 = (bf16[2,256,128]{2,1,0:T(8,128)(2,1)S(1)}, bf16[2,256,128]{2,1,0:T(8,128)(2,1)S(1)}, u32[]{:S(2)}, u32[]{:S(2)}) collective-permute-start(bf16[2,256,128]{2,1,0:T(8,128)(2,1)S(1)} %get-tuple-element.35), channel_id=1, source_target_pairs={{0,8},{4,12},{8,0},{12,4},{1,9},{5,13},{9,1},{13,5},{2,10},{6,14},... | collective-permute-start | bytes 393224 | tf_op jit(solution)/shard_map/ppermute | solution.py:32
  6.5 5.8 %collective-permute-start.10 = (bf16[2,256,128]{2,1,0:T(8,128)(2,1)S(1)}, bf16[2,256,128]{2,1,0:T(8,128)(2,1)S(1)}, u32[]{:S(2)}, u32[]{:S(2)}) collective-permute-start(bf16[2,256,128]{2,1,0:T(8,128)(2,1)S(1)} %get-tuple-element.35), channel_id=1, source_target_pairs={{0,4},{4,0},{8,12},{12,8},{1,5},{5,1},{9,13},{13,9},{2,6},{6,2},{1... | collective-permute-start | bytes 393224 | tf_op jit(solution)/shard_map/ppermute | solution.py:32
  6.5 6.3 %collective-permute-start.4 = (bf16[2,256,128]{2,1,0:T(8,128)(2,1)S(1)}, bf16[2,256,128]{2,1,0:T(8,128)(2,1)S(1)}, u32[]{:S(2)}, u32[]{:S(2)}) collective-permute-start(bf16[2,256,128]{2,1,0:T(8,128)(2,1)S(1)} %get-tuple-element.36), channel_id=1, source_target_pairs={{0,1},{1,0},{2,3},{3,2},{4,5},{5,4},{6,7},{7,6},{8,9},{9,8},{10,11... | collective-permute-start | bytes 393224 | tf_op jit(solution)/shard_map/ppermute | solution.py:32
  8.8 11.9 %collective-permute-start.8 = (bf16[2,512,128]{2,1,0:T(8,128)(2,1)}, bf16[2,512,128]{2,1,0:T(8,128)(2,1)S(1)}, u32[]{:S(2)}, u32[]{:S(2)}) collective-permute-start(bf16[2,512,128]{2,1,0:T(8,128)(2,1)} %get-tuple-element.30), channel_id=1, source_target_pairs={{0,1},{1,0},{2,3},{3,2},{4,5},{5,4},{6,7},{7,6},{8,9},{9,8},{10,11... | collective-permute-start | bytes 786440 | tf_op jit(solution)/shard_map/ppermute | solution.py:32
  10.3 6.4 %collective-permute-start.1 = (bf16[2,256,128]{2,1,0:T(8,128)(2,1)S(1)}, bf16[2,256,128]{2,1,0:T(8,128)(2,1)S(1)}, u32[]{:S(2)}, u32[]{:S(2)}) collective-permute-start(bf16[2,256,128]{2,1,0:T(8,128)(2,1)S(1)} %get-tuple-element.37), channel_id=1, source_target_pairs={{0,8},{4,12},{8,0},{12,4},{1,9},{5,13},{9,1},{13,5},{2,10},{6,14},... | collective-permute-start | bytes 393224 | tf_op jit(solution)/shard_map/ppermute | solution.py:32
  10.9 8.6 %collective-permute-start.13 = (bf16[2,256,128]{2,1,0:T(8,128)(2,1)S(1)}, bf16[2,256,128]{2,1,0:T(8,128)(2,1)S(1)}, u32[]{:S(2)}, u32[]{:S(2)}) collective-permute-start(bf16[2,256,128]{2,1,0:T(8,128)(2,1)S(1)} %collective-permute-done.12.refs_8_), channel_id=1, source_target_pairs={{0,8},{4,12},{8,0},{12,4},{1,9},{5,13},{9,1},{13,5},{2,10},{6,14},... | collective-permute-start | bytes 393224 | tf_op jit(solution)/shard_map/ppermute | solution.py:32
  12.4 7.2 %collective-permute-start.11 = (bf16[2,256,128]{2,1,0:T(8,128)(2,1)S(1)}, bf16[2,256,128]{2,1,0:T(8,128)(2,1)S(1)}, u32[]{:S(2)}, u32[]{:S(2)}) collective-permute-start(bf16[2,256,128]{2,1,0:T(8,128)(2,1)S(1)} %collective-permute-done.9.refs_5_), channel_id=1, source_target_pairs={{0,4},{4,0},{8,12},{12,8},{1,5},{5,1},{9,13},{13,9},{2,6},{6,2},{1... | collective-permute-start | bytes 393224 | tf_op jit(solution)/shard_map/ppermute | solution.py:32
  12.8 7.3 %collective-permute-start.14 = (bf16[2,256,128]{2,1,0:T(8,128)(2,1)S(1)}, bf16[2,256,128]{2,1,0:T(8,128)(2,1)S(1)}, u32[]{:S(2)}, u32[]{:S(2)}) collective-permute-start(bf16[2,256,128]{2,1,0:T(8,128)(2,1)S(1)} %collective-permute-done.12.refs_8_), channel_id=1, source_target_pairs={{0,4},{4,0},{8,12},{12,8},{1,5},{5,1},{9,13},{13,9},{2,6},{6,2},{1... | collective-permute-start | bytes 393224 | tf_op jit(solution)/shard_map/ppermute | solution.py:32
  16.7 5.0 %collective-permute-start.5 = (bf16[2,256,128]{2,1,0:T(8,128)(2,1)S(1)}, bf16[2,256,128]{2,1,0:T(8,128)(2,1)S(1)}, u32[]{:S(2)}, u32[]{:S(2)}) collective-permute-start(bf16[2,256,128]{2,1,0:T(8,128)(2,1)S(1)} %collective-permute-done.4.refs_8_), channel_id=1, source_target_pairs={{0,8},{4,12},{8,0},{12,4},{1,9},{5,13},{9,1},{13,5},{2,10},{6,14},... | collective-permute-start | bytes 393224 | tf_op jit(solution)/shard_map/ppermute | solution.py:32
  19.5 2.2 %collective-permute-start.15 = (bf16[2,256,128]{2,1,0:T(8,128)(2,1)S(1)}, bf16[2,256,128]{2,1,0:T(8,128)(2,1)S(1)}, u32[]{:S(2)}, u32[]{:S(2)}) collective-permute-start(bf16[2,256,128]{2,1,0:T(8,128)(2,1)S(1)} %collective-permute-done.13.refs_9_), channel_id=1, source_target_pairs={{0,4},{4,0},{8,12},{12,8},{1,5},{5,1},{9,13},{13,9},{2,6},{6,2},{1... | collective-permute-start | bytes 393224 | tf_op jit(solution)/shard_map/ppermute | solution.py:32
  19.6 29.4 %collective-permute-start.2 = (bf16[2,256,128]{2,1,0:T(8,128)(2,1)S(1)}, bf16[2,256,128]{2,1,0:T(8,128)(2,1)S(1)}, u32[]{:S(2)}, u32[]{:S(2)}) collective-permute-start(bf16[2,256,128]{2,1,0:T(8,128)(2,1)S(1)} %get-tuple-element.37), channel_id=1, source_target_pairs={{0,4},{4,0},{8,12},{12,8},{1,5},{5,1},{9,13},{13,9},{2,6},{6,2},{1... | collective-permute-start | bytes 393224 | tf_op jit(solution)/shard_map/ppermute | solution.py:32
  20.1 29.9 %collective-permute-start = (bf16[2,512,128]{2,1,0:T(8,128)(2,1)S(1)}, bf16[2,512,128]{2,1,0:T(8,128)(2,1)S(1)}, u32[]{:S(2)}, u32[]{:S(2)}) collective-permute-start(bf16[2,512,128]{2,1,0:T(8,128)(2,1)S(1)} %get-tuple-element.31), channel_id=1, source_target_pairs={{0,1},{1,0},{2,3},{3,2},{4,5},{5,4},{6,7},{7,6},{8,9},{9,8},{10,11... | collective-permute-start | bytes 786440 | tf_op jit(solution)/shard_map/ppermute | solution.py:32
  20.7 29.3 %collective-permute-start.6 = (bf16[2,256,128]{2,1,0:T(8,128)(2,1)S(1)}, bf16[2,256,128]{2,1,0:T(8,128)(2,1)S(1)}, u32[]{:S(2)}, u32[]{:S(2)}) collective-permute-start(bf16[2,256,128]{2,1,0:T(8,128)(2,1)S(1)} %collective-permute-done.4.refs_8_), channel_id=1, source_target_pairs={{0,4},{4,0},{8,12},{12,8},{1,5},{5,1},{9,13},{13,9},{2,6},{6,2},{1... | collective-permute-start | bytes 393224 | tf_op jit(solution)/shard_map/ppermute | solution.py:32
  21.7 27.4 %collective-permute-start.3 = (bf16[2,256,128]{2,1,0:T(8,128)(2,1)S(1)}, bf16[2,256,128]{2,1,0:T(8,128)(2,1)S(1)}, u32[]{:S(2)}, u32[]{:S(2)}) collective-permute-start(bf16[2,256,128]{2,1,0:T(8,128)(2,1)S(1)} %collective-permute-done.1.refs_5_), channel_id=1, source_target_pairs={{0,4},{4,0},{8,12},{12,8},{1,5},{5,1},{9,13},{13,9},{2,6},{6,2},{1... | collective-permute-start | bytes 393224 | tf_op jit(solution)/shard_map/ppermute | solution.py:32
  21.7 28.3 %collective-permute-start.7 = (bf16[2,256,128]{2,1,0:T(8,128)(2,1)S(1)}, bf16[2,256,128]{2,1,0:T(8,128)(2,1)S(1)}, u32[]{:S(2)}, u32[]{:S(2)}) collective-permute-start(bf16[2,256,128]{2,1,0:T(8,128)(2,1)S(1)} %collective-permute-done.5.refs_9_), channel_id=1, source_target_pairs={{0,4},{4,0},{8,12},{12,8},{1,5},{5,1},{9,13},{13,9},{2,6},{6,2},{1... | collective-permute-start | bytes 393224 | tf_op jit(solution)/shard_map/ppermute | solution.py:32
  49.0 36.6 %collective-permute-start.18 = (bf16[2,2,256,256]{3,2,1,0:T(8,128)(2,1)S(1)}, bf16[2,2,256,256]{3,2,1,0:T(8,128)(2,1)S(1)}, u32[]{:S(2)}, u32[]{:S(2)}) collective-permute-start(bf16[2,2,256,256]{3,2,1,0:T(8,128)(2,1)S(1)} %get-tuple-element.25), channel_id=1, source_target_pairs={{0,4},{4,0},{8,12},{12,8},{1,5},{5,1},{9,13},{13,9},{2,6},{6,2},{1... | collective-permute-start | bytes 1572872 | tf_op jit(solution)/shard_map/ppermute | solution.py:32
  49.0 29.2 %collective-permute-start.16 = (bf16[2,512,128]{2,1,0:T(8,128)(2,1)S(1)}, bf16[2,512,128]{2,1,0:T(8,128)(2,1)S(1)}, u32[]{:S(2)}, u32[]{:S(2)}) collective-permute-start(bf16[2,512,128]{2,1,0:T(8,128)(2,1)S(1)} %get-tuple-element.22), channel_id=1, source_target_pairs={{0,1},{1,0},{2,3},{3,2},{4,5},{5,4},{6,7},{7,6},{8,9},{9,8},{10,11... | collective-permute-start | bytes 786440 | tf_op jit(solution)/shard_map/ppermute | solution.py:32
  76.8 9.6 %collective-permute-start.20 = (bf16[2,2,256,256]{3,2,1,0:T(8,128)(2,1)S(1)}, bf16[2,2,256,256]{3,2,1,0:T(8,128)(2,1)S(1)}, u32[]{:S(2)}, u32[]{:S(2)}) collective-permute-start(bf16[2,2,256,256]{3,2,1,0:T(8,128)(2,1)S(1)} %get-tuple-element.27), channel_id=1, source_target_pairs={{0,4},{4,0},{8,12},{12,8},{1,5},{5,1},{9,13},{13,9},{2,6},{6,2},{1... | collective-permute-start | bytes 1572872 | tf_op jit(solution)/shard_map/ppermute | solution.py:32
  76.8 8.7 %collective-permute-start.17 = (bf16[2,512,128]{2,1,0:T(8,128)(2,1)S(1)}, bf16[2,512,128]{2,1,0:T(8,128)(2,1)S(1)}, u32[]{:S(2)}, u32[]{:S(2)}) collective-permute-start(bf16[2,512,128]{2,1,0:T(8,128)(2,1)S(1)} %get-tuple-element.23), channel_id=1, source_target_pairs={{0,1},{1,0},{2,3},{3,2},{4,5},{5,4},{6,7},{7,6},{8,9},{9,8},{10,11... | collective-permute-start | bytes 786440 | tf_op jit(solution)/shard_map/ppermute | solution.py:32
  85.8 9.3 %collective-permute-start.19 = (bf16[2,256,256]{2,1,0:T(8,128)(2,1)S(1)}, bf16[2,256,256]{2,1,0:T(8,128)(2,1)S(1)}, u32[]{:S(2)}, u32[]{:S(2)}) collective-permute-start(bf16[2,256,256]{2,1,0:T(8,128)(2,1)S(1)} %fusion.2), channel_id=1, source_target_pairs={{0,8},{4,12},{8,0},{12,4},{1,9},{5,13},{9,1},{13,5},{2,10},{6,14},... | collective-permute-start | bytes 786440 | tf_op jit(solution)/shard_map/ppermute | solution.py:32
  86.6 12.8 %collective-permute-start.21 = (bf16[2,256,256]{2,1,0:T(8,128)(2,1)S(1)}, bf16[2,256,256]{2,1,0:T(8,128)(2,1)S(1)}, u32[]{:S(2)}, u32[]{:S(2)}) collective-permute-start(bf16[2,256,256]{2,1,0:T(8,128)(2,1)S(1)} %fusion.3), channel_id=1, source_target_pairs={{0,8},{4,12},{8,0},{12,4},{1,9},{5,13},{9,1},{13,5},{2,10},{6,14},... | collective-permute-start | bytes 786440 | tf_op jit(solution)/shard_map/ppermute | solution.py:32
  95.1 6.5 %collective-permute-start.22 = (bf16[2,256,128]{2,1,0:T(8,128)(2,1)S(1)}, bf16[2,256,128]{2,1,0:T(8,128)(2,1)S(1)}, u32[]{:S(2)}, u32[]{:S(2)}) collective-permute-start(bf16[2,256,128]{2,1,0:T(8,128)(2,1)S(1)} %slice.59), channel_id=1, source_target_pairs={{0,1},{1,0},{2,3},{3,2},{4,5},{5,4},{6,7},{7,6},{8,9},{9,8},{10,11... | collective-permute-start | bytes 393224 | tf_op jit(solution)/shard_map/ppermute | solution.py:32
  99.4 5.0 %collective-permute-start.23 = (bf16[2,256,128]{2,1,0:T(8,128)(2,1)S(1)}, bf16[2,256,128]{2,1,0:T(8,128)(2,1)S(1)}, u32[]{:S(2)}, u32[]{:S(2)}) collective-permute-start(bf16[2,256,128]{2,1,0:T(8,128)(2,1)S(1)} %slice.58), channel_id=1, source_target_pairs={{0,1},{1,0},{2,3},{3,2},{4,5},{5,4},{6,7},{7,6},{8,9},{9,8},{10,11... | collective-permute-start | bytes 393224 | tf_op jit(solution)/shard_map/ppermute | solution.py:32
  (3 other events, 62.0 us)

commit v2 on v1

v2 whole, which is shorter than its diff:
```python
import functools

import jax
import jax.numpy as jnp
from jax import lax
from jax.experimental import pallas as pl
from jax.experimental.pallas import tpu as pltpu
from jax.sharding import PartitionSpec as P

H = 32
KVH = 8
HD = 128
P_SIZE = 2
GROUP = H // KVH
BLOCK = 256
MASKED = -1e30
SCALE = HD ** (-0.5)

NT = (((1,), (1,)), ((), ()))
NN = (((1,), (0,)), ((), ()))


def dot(a, b, dims):
    return lax.dot_general(a, b, dims, preferred_element_type=jnp.float32)


def swap(block, axis, step):
    return lax.ppermute(block, axis, [(i, i ^ step) for i in range(lax.axis_size(axis))])


def attend_kernel(sizes, scalars, *refs):
    pieces, rows, n_keep, heads, turn, n_resp, n_pass = sizes
    refs = list(refs)
    q_ref, do_ref, ra_ref, rb_ref = refs[:4]
    pa_refs = refs[4 : 4 + pieces]
    pb_refs = refs[4 + pieces : 4 + 2 * pieces]
    prior_ref = refs[4 + 2 * pieces] if turn > 0 else None
    rest = refs[4 + 2 * pieces + (1 if turn > 0 else 0) + n_pass :]
    out_ref, dq_ref, dra_ref, drb_ref = rest[:4]
    final = turn == n_resp - 1
    n_out = 4 + (1 if not final or pieces == n_keep else 2)
    grads = rest[4:n_out]
    k_all, v_all, k_t, v_t, weights, probs, dscores, acc_k, acc_v, res_k, res_v = rest[n_out:]

    head = pl.program_id(0)
    prompt = scalars[turn]
    even = scalars[n_resp] == 0
    n_prompt = pieces * rows
    n_query = q_ref.shape[1]

    @pl.when(head == 0)
    def _():
        if turn == 0:
            acc_k[...] = jnp.zeros_like(acc_k)
            acc_v[...] = jnp.zeros_like(acc_v)
        elif turn == 1:
            before = scalars[0]
            acc_k[1 - before] = jnp.zeros(acc_k.shape[1:], jnp.float32)
            acc_v[1 - before] = jnp.zeros(acc_v.shape[1:], jnp.float32)
            acc_k[before] = prior_ref[0, 0]
            acc_v[before] = prior_ref[1, 0]
        else:
            acc_k[...] = prior_ref[0]
            acc_v[...] = prior_ref[1]

    def gather(dst, piece_refs, resp_ref):
        for i, ref in enumerate(piece_refs):
            dst[i * rows : (i + 1) * rows, :] = ref[0]
        dst[n_prompt:, :] = resp_ref[0]

    @pl.when((head == 0) & even)
    def _():
        gather(k_all, pa_refs, ra_ref)
        gather(v_all, pb_refs, rb_ref)

    @pl.when((head == 0) & jnp.logical_not(even))
    def _():
        gather(k_all, pb_refs, rb_ref)
        gather(v_all, pa_refs, ra_ref)

    @pl.when(head == 0)
    def _():
        res_k[...] = jnp.zeros_like(res_k)
        res_v[...] = jnp.zeros_like(res_v)
        k_t[...] = k_all[...].T
        v_t[...] = v_all[...].T

    n_blocks = n_query // BLOCK
    state = [dict() for _ in range(n_blocks)]

    def span(c):
        return slice(c * BLOCK, (c + 1) * BLOCK)

    def fold(x, op):
        return op(x.reshape(-1, 8, x.shape[-1]), axis=0)

    def stages(i):
        st = state[i]
        t = span(i)
        n_chunks = n_prompt // BLOCK + i + 1
        seen = n_chunks * BLOCK
        q = q_ref[0, t, :]
        do = do_ref[0, t, :]

        def score(c):
            if c == 0:
                st["s"] = dot(k_all[:seen, :], q, NT)
            s = st["s"][span(c), :]
            if c == n_chunks - 1:
                row = lax.broadcasted_iota(jnp.int32, (BLOCK, BLOCK), 0)
                col = lax.broadcasted_iota(jnp.int32, (BLOCK, BLOCK), 1)
                s = jnp.where(row <= col, s, MASKED)
            weights[span(c), t] = s
            top = fold(s, jnp.max)
            st["top"] = top if c == 0 else jnp.maximum(st["top"], top)
            if c == n_chunks - 1:
                st["top"] = jnp.max(st["top"], axis=0, keepdims=True) * SCALE

        def weigh(c):
            w = jnp.exp(weights[span(c), t] * SCALE - st["top"])
            weights[span(c), t] = w
            total = fold(w, jnp.sum)
            st["sum"] = total if c == 0 else st["sum"] + total
            if c == n_chunks - 1:
                st["inv"] = 1.0 / jnp.sum(st["sum"], axis=0, keepdims=True)

        def norm(c):
            probs[span(c), t] = (weights[span(c), t] * st["inv"]).astype(jnp.bfloat16)
            if c == n_chunks - 1:
                o = dot(v_t[:, :seen], probs[:seen, t], NN)
                out_ref[0, t, :] = o.T.astype(jnp.bfloat16)
                do_t = do.astype(jnp.float32).T
                st["delta"] = jnp.sum(o * do_t, axis=0, keepdims=True)
                st["inv"] = st["inv"] * SCALE

        def grad(c):
            if c == 0:
                st["dp"] = dot(v_all[:seen, :], do, NT)
            dp = st["dp"][span(c), :]
            ds = (weights[span(c), t] * st["inv"]) * (dp - st["delta"])
            dscores[span(c), t] = ds.astype(jnp.bfloat16)
            if c == n_chunks - 1:
                dq = dot(k_t[:, :seen], dscores[:seen, t], NN)
                dq_ref[0, t, :] = dq.T.astype(jnp.bfloat16)

        return [[functools.partial(f, c) for c in range(n_chunks)] for f in (score, weigh, norm, grad)]

    plan = [stages(i) for i in range(n_blocks)]
    for slot in range(4 + n_blocks - 1):
        groups = [plan[i][slot - i] for i in reversed(range(n_blocks)) if 0 <= slot - i < 4]
        for c in range(max(len(g) for g in groups)):
            for g in groups:
                if c < len(g):
                    g[c]()

    q_all = q_ref[0]
    do_all = do_ref[0]
    acc_v[prompt] += dot(probs[:n_prompt, :], do_all, NN)
    acc_k[prompt] += dot(dscores[:n_prompt, :], q_all, NN)
    for i in range(n_blocks):
        u = span(n_prompt // BLOCK + i)
        t0 = i * BLOCK
        res_v[span(i), :] += dot(probs[u, t0:], do_all[t0:], NN)
        res_k[span(i), :] += dot(dscores[u, t0:], q_all[t0:], NN)

    last = head == heads - 1

    @pl.when(last & even)
    def _():
        dra_ref[0] = res_k[...].astype(jnp.bfloat16)
        drb_ref[0] = res_v[...].astype(jnp.bfloat16)

    @pl.when(last & jnp.logical_not(even))
    def _():
        dra_ref[0] = res_v[...].astype(jnp.bfloat16)
        drb_ref[0] = res_k[...].astype(jnp.bfloat16)

    if not final:

        @pl.when(last)
        def _():
            if turn == 0:
                grads[0][0, 0] = acc_k[prompt]
                grads[0][1, 0] = acc_v[prompt]
            else:
                grads[0][0] = acc_k[...]
                grads[0][1] = acc_v[...]

        return

    def scatter(slot, acc):
        for i in range(pieces):
            for p_id in range(P_SIZE):
                val = acc[p_id, i * rows : (i + 1) * rows, :]
                if i < n_keep:
                    grads[0][i, p_id, :, slot * HD : (slot + 1) * HD] = val
                else:
                    grads[1][i - n_keep, p_id, :, slot * HD : (slot + 1) * HD] = val.astype(jnp.bfloat16)

    @pl.when(last & even)
    def _():
        scatter(0, acc_k)
        scatter(1, acc_v)

    @pl.when(last & jnp.logical_not(even))
    def _():
        scatter(0, acc_v)
        scatter(1, acc_k)


def attend(scalars, queries, d_out, resp_a, resp_b, prompt_a, prompt_b, n_keep, chunk, heads, turn, prior, shared, after=()):
    n_resp, n_query, _ = queries.shape
    pieces = len(prompt_a)
    rows = prompt_a[0][0].shape[1]
    n_prompt = pieces * rows
    n_keys = n_prompt + n_query
    n_send = pieces - n_keep
    final = turn == n_resp - 1
    shape = jax.ShapeDtypeStruct

    def resp_map(place):
        return lambda j, sc: (turn if place[0] else 0, 0, place[1](sc[n_resp]))

    def prompt_map(place):
        return lambda j, sc: (sc[turn], 0, place[1](sc[n_resp]))

    q_spec = pl.BlockSpec((1, n_query, HD), lambda j, sc: (turn, 0, chunk * heads + j))
    in_specs = [q_spec, q_spec]
    in_specs += [pl.BlockSpec((1, n_query, HD), resp_map(c)) for _, c in (resp_a, resp_b)]
    in_specs += [pl.BlockSpec((1, rows, HD), prompt_map(c)) for _, c in (*prompt_a, *prompt_b)]
    args = [queries, d_out, resp_a[0], resp_b[0], *[a for a, _ in (*prompt_a, *prompt_b)]]
    if turn > 0:
        in_specs.append(pl.BlockSpec(prior.shape, lambda j, sc: (0, 0, 0, 0)))
        args.append(prior)
    aliases = {}
    if shared is not None:
        aliases = {1 + len(args) + i: i for i in range(3)}
        args += list(shared)
    args += list(after)
    n_pass = len(args) - len(in_specs)
    in_specs += [pl.BlockSpec(memory_space=pl.ANY)] * n_pass
    out_specs = [
        q_spec,
        q_spec,
        pl.BlockSpec((1, n_query, HD), lambda j, sc: (turn, 0, resp_a[1][1](sc[n_resp]))),
        pl.BlockSpec((1, n_query, HD), lambda j, sc: (0, 0, 0)),
    ]
    out_shape = [
        shape(queries.shape, jnp.bfloat16),
        shape(queries.shape, jnp.bfloat16),
        shape(resp_a[0].shape, jnp.bfloat16),
        shape((1, n_query, HD), jnp.bfloat16),
    ]
    if final:
        grads = [shape((n_keep, P_SIZE, rows, 2 * HD), jnp.float32)]
        if n_send:
            grads.append(shape((n_send, P_SIZE, rows, 2 * HD), jnp.bfloat16))
    else:
        grads = [shape((2, 1 if turn == 0 else P_SIZE, n_prompt, HD), jnp.float32)]
    out_shape += grads
    out_specs += [pl.BlockSpec(g.shape, lambda j, sc: (0, 0, 0, 0)) for g in grads]
    scratch = [
        pltpu.VMEM((n_keys, HD), jnp.bfloat16),
        pltpu.VMEM((n_keys, HD), jnp.bfloat16),
        pltpu.VMEM((HD, n_keys), jnp.bfloat16),
        pltpu.VMEM((HD, n_keys), jnp.bfloat16),
        pltpu.VMEM((n_keys, n_query), jnp.float32),
        pltpu.VMEM((n_keys, n_query), jnp.bfloat16),
        pltpu.VMEM((n_keys, n_query), jnp.bfloat16),
        pltpu.VMEM((P_SIZE, n_prompt, HD), jnp.float32),
        pltpu.VMEM((P_SIZE, n_prompt, HD), jnp.float32),
        pltpu.VMEM((n_query, HD), jnp.float32),
        pltpu.VMEM((n_query, HD), jnp.float32),
    ]
    flops = 12 * heads * n_query * n_keys * HD
    return pl.pallas_call(
        functools.partial(attend_kernel, (pieces, rows, n_keep, heads, turn, n_resp, n_pass)),
        grid_spec=pltpu.PrefetchScalarGridSpec(
            num_scalar_prefetch=1,
            grid=(heads,),
            in_specs=in_specs,
            out_specs=out_specs,
            scratch_shapes=scratch,
        ),
        out_shape=out_shape,
        input_output_aliases=aliases,
        compiler_params=pltpu.CompilerParams(vmem_limit_bytes=40 * 2**20),
        cost_estimate=pl.CostEstimate(flops=2 * flops, bytes_accessed=4 * 2**20, transcendentals=0),
    )(scalars, *args)


def first(par):
    return 0


def per_device(queries, resp_kv, prompt_kv, prompt_of, d_out):
    pair_heads = prompt_kv.shape[2] // HD
    parity = lax.axis_index("prefix") % 2
    scalars = jnp.concatenate([prompt_of, parity[None].astype(jnp.int32)])
    if lax.axis_size("dp") == 4 and pair_heads % 2 == 0:
        return whole_heads(queries, resp_kv, prompt_kv, scalars, parity, d_out)
    return shared_head(queries, resp_kv, prompt_kv, scalars, parity, d_out)


def whole_heads(queries, resp_kv, prompt_kv, scalars, parity, d_out):
    n_own = prompt_kv.shape[2] // HD // 2
    n_resp, n_query, _ = queries.shape
    z = functools.partial(swap, axis="prefix", step=1)
    core, x, both = [functools.partial(swap, axis="dp", step=k) for k in (1, 2, 3)]
    own = [lambda par, h=h: par * n_own + h for h in range(n_own)]
    theirs = [(1 - parity) * n_own + h for h in range(n_own)]

    def resp_column(r, h):
        return lax.dynamic_slice(resp_kv, (r, 0, theirs[h] * HD), (1, n_query, HD))

    def prompt_column(which):
        return lax.dynamic_slice_in_dim(prompt_kv, which * HD, HD, axis=2)

    def order(values, done):
        return lax.optimization_barrier((tuple(values), tuple(done)))[0]

    pa, pb, resp_b = [], [], {}
    a0 = prompt_column(own[0](parity))
    b0 = z(prompt_column(theirs[0]))
    a2 = x(a0)
    resp_b[0, 0] = z(resp_column(0, 0))
    (b0,) = order([b0], [a2])
    b2 = x(b0)
    pa.append([a2, core(a0), core(a2)])
    pb.append([b0, b2, core(b0), core(b2)])

    shared, ready = None, ()
    d_resp, d_prompt = {}, []
    for h in range(n_own):
        prior = None
        if h + 1 < n_own:
            a0, b0, *rest = order(
                [prompt_column(own[h + 1](parity)), prompt_column(theirs[h + 1])]
                + [resp_column(r, h) for r in range(1, n_resp)],
                [pb[h][1]],
            )
            b0 = z(b0)
            for r in range(1, n_resp):
                resp_b[r, h] = z(rest[r - 1])
            a2 = x(a0)
        here = (True, own[h])
        for r in range(n_resp):
            att, dq, dra, drb, *grads = attend(
                scalars,
                queries,
                d_out,
                (resp_kv, here),
                (resp_b[r, h], (False, first)),
                [(prompt_kv, here)] + [(a, (False, first)) for a in pa[h]],
                [(a, (False, first)) for a in pb[h]],
                2,
                h,
                GROUP,
                r,
                prior,
                shared,
                ready if r == n_resp - 1 else (),
            )
            prior = grads[0]
            shared = (att, dq, dra)
            if r == 0 and h + 1 < n_own:
                a0, b0, *rest = order([a0, b0] + [resp_column(i, h + 1) for i in range(n_resp)], [drb])
                pb.append([b0, x(b0), core(b0), both(b0)])
                pa.append([a2, core(a0), core(a2)])
                for i in range(n_resp):
                    resp_b[i, h + 1] = z(rest[i])
            if (r, h) != (n_resp - 1, n_own - 1):
                d_resp[r, h] = z(drb)
        keep, send = grads
        if h == n_own - 1:
            (send, drb) = order([send, drb], [across, d_resp[0, h]])
            d_resp[n_resp - 1, h] = z(drb)
        sums = keep + core(send).astype(jnp.float32)
        part = sums[1].astype(jnp.bfloat16)
        across = x(part)
        ready = (part, *[d_resp[r, h] for r in range(n_resp)])
        total = sums[0] + across.astype(jnp.float32)
        other = z(total[:, :, HD:].astype(jnp.bfloat16))
        d_prompt.append((total[:, :, :HD], other.astype(jnp.float32)))

    even = parity == 0
    mine = jnp.concatenate([a for a, _ in d_prompt], axis=-1)
    other = jnp.concatenate([b for _, b in d_prompt], axis=-1)
    d_prompt = jnp.concatenate([jnp.where(even, mine, other), jnp.where(even, other, mine)], axis=-1)
    att, dq, d_resp_kv = shared
    received = jnp.concatenate(
        [jnp.concatenate([d_resp[r, h] for r in range(n_resp)], axis=0) for h in range(n_own)], axis=-1
    )
    d_resp_kv = lax.dynamic_update_slice_in_dim(d_resp_kv, received, (1 - parity) * n_own * HD, axis=2)
    return att, dq, d_resp_kv, d_prompt


def shared_head(queries, resp_kv, prompt_kv, scalars, parity, d_out):
    n_resp = queries.shape[0]
    local_heads = queries.shape[2] // HD
    prompt_a = lax.all_gather(prompt_kv, "dp", axis=1, tiled=True)
    prompt_b = swap(prompt_a, "prefix", 1)
    resp_b = swap(resp_kv, "prefix", 1)
    shared, prior, d_resp = None, None, []
    for r in range(n_resp):
        att, dq, dra, drb, prior = attend(
            scalars,
            queries,
            d_out,
            (resp_kv, (True, first)),
            (resp_b, (True, first)),
            [(prompt_a, (True, first))],
            [(prompt_b, (True, first))],
            1,
            0,
            local_heads,
            r,
            prior,
            shared,
        )
        shared = (att, dq, dra)
        d_resp.append(swap(drb, "prefix", 1))
    att, dq, dra = shared
    d_resp = (dra.astype(jnp.float32) + jnp.concatenate(d_resp, axis=0).astype(jnp.float32)).astype(jnp.bfloat16)
    other = swap(prior[0, :, :, HD:].astype(jnp.bfloat16), "prefix", 1)
    paired = prior[0, :, :, :HD] + other.astype(jnp.float32)
    d_prompt = lax.psum_scatter(paired, "dp", scatter_dimension=1, tiled=True)
    return att, dq, d_resp, d_prompt


def solution(mesh):
    in_specs = (
        P(("groups", "dp"), None, "prefix"),
        P(("groups", "dp"), None, "prefix"),
        P("groups", "dp", "prefix"),
        P(("groups", "dp")),
        P(("groups", "dp"), None, "prefix"),
    )
    out_specs = (
        P(("groups", "dp"), None, "prefix"),
        P(("groups", "dp"), None, "prefix"),
        P(("groups", "dp"), None, "prefix"),
        P("groups", "dp", "prefix"),
    )
    return jax.shard_map(
        per_device, mesh=mesh, in_specs=in_specs, out_specs=out_specs, check_vma=False
    )
```

time: 106 us -> 113 us (1.066)
  Pallas kernels: 53.5 us -> 64.4 us
  waiting for transfers between devices: 27.5 us -> 16.7 us
  starting transfers between devices: 17.6 us -> 23.8 us
  local copies, waits for them, and re-layouts: 3.4 us -> 5.74 us
    pallas_call x2 -> x4, Pallas kernels: 53.5 us -> 64.4 us  [attend(): pl.pallas_call(functools.partial(attend_kernel, (pieces, rows, n_keep, he...]
    ppermute x24 -> x28, waiting for transfers between devices: 27.5 us -> 16.7 us  [swap(): lax.ppermute(block, axis, [(i, i ^ step) for i in range(lax.axis_size(axi...]
    ppermute x24 -> x28, starting transfers between devices: 17.6 us -> 23.8 us  [swap(): lax.ppermute(block, axis, [(i, i ^ step) for i in range(lax.axis_size(axi...]
    unnamed x8 -> x14, local copies, waits for them, and re-layouts: 0.11 us -> 3.2 us
  transfers between devices with their start and end apart: 24 -> 28, of which waited for: 8 -> 7; matrix products, arithmetic and copies ran while one was open for 3% -> 1% of each run, Pallas kernels for 51% -> 57%
where the time goes in v2:
time: 113 us
  Pallas kernels  64.4 us (57%)
  starting transfers between devices  23.8 us (21%)
  waiting for transfers between devices  16.7 us (15%)
  local copies, waits for them, and re-layouts  5.74 us (5%)
  other arithmetic  1.76 us (2%)
    pallas_call x4, Pallas kernels, attend(): pl.pallas_call(functools.partial(attend_kernel, (pieces, rows, n_keep, he...  64.4 us
    ppermute x28, starting transfers between devices, swap(): lax.ppermute(block, axis, [(i, i ^ step) for i in range(lax.axis_size(axi...  23.8 us
    ppermute x28, waiting for transfers between devices, swap(): lax.ppermute(block, axis, [(i, i ^ step) for i in range(lax.axis_size(axi...  16.7 us
    unnamed x14, local copies, waits for them, and re-layouts  3.2 us
  transfers between devices with their start and end apart: 28, of which 7 were waited for; matrix products, arithmetic and copies ran while one was open for 1% of the time, Pallas kernels for 57%

profile of v2, /device:TPU:0, one launch (start us, length us, event | category | flops | bytes accessed | tf_op | source)
XLA Modules:
  0.0 113.3 jit_solution(9560935680454761788)
XLA Ops:
  0.7 1.3 %constant_dynamic-slice_fusion.3 = (bf16[2,256,128]{2,1,0:T(8,128)(2,1)S(1)}, bf16[2,256,128]{2,1,0:T(8,128)(2,1)S(1)}, bf16[2,256,128]{2,1,0:T(8,128)(2,1)S(1)}, bf16[2,256,128]{2,1,0:T(8,128)(2,1)S(1)}) fusion(bf16[2,256,512]{2,1,0:T(8,128)(2,1)} %refs_4_.7, s32[]{:T(128)S(6)} %select_n.40, s32[]{:T(128)S(6)} %select_n.39, s32[]{:T(128)S(6)} %select_n.38, ...), kind=kLoop, calls=%fused_computation.21 | loop fusion | bytes 1048592 | tf_op jit(solution)/shard_map/dynamic_slice | solution.py:317
  2.0 3.1 %collective-permute-start = (bf16[2,256,128]{2,1,0:T(8,128)(2,1)S(1)}, bf16[2,256,128]{2,1,0:T(8,128)(2,1)S(1)}, u32[]{:S(2)}, u32[]{:S(2)}) collective-permute-start(bf16[2,256,128]{2,1,0:T(8,128)(2,1)S(1)} %get-tuple-element.75), channel_id=1, source_target_pairs={{0,1},{1,0},{2,3},{3,2},{4,5},{5,4},{6,7},{7,6},{8,9},{9,8},{10,11... | collective-permute-start | bytes 393224 | tf_op jit(solution)/shard_map/ppermute | solution.py:28
  5.0 1.5 %collective-permute-start.1 = (bf16[2,256,128]{2,1,0:T(8,128)(2,1)S(1)}, bf16[2,256,128]{2,1,0:T(8,128)(2,1)S(1)}, u32[]{:S(2)}, u32[]{:S(2)}) collective-permute-start(bf16[2,256,128]{2,1,0:T(8,128)(2,1)S(1)} %get-tuple-element.74), channel_id=1, source_target_pairs={{0,8},{4,12},{8,0},{12,4},{1,9},{5,13},{9,1},{13,5},{2,10},{6,14},... | collective-permute-start | bytes 393224 | tf_op jit(solution)/shard_map/ppermute | solution.py:28
  6.5 2.0 %collective-permute-done.refs_8_ = bf16[2,256,128]{2,1,0:T(8,128)(2,1)S(1)} collective-permute-done((bf16[2,256,128]{2,1,0:T(8,128)(2,1)S(1)}, bf16[2,256,128]{2,1,0:T(8,128)(2,1)S(1)}, u32[]{:S(2)}, u32[]{:S(2)}) %collective-permute-start) | collective-permute-done | bytes 131104 | tf_op jit(solution)/shard_map/ppermute | solution.py:28
  8.5 1.5 %collective-permute-done.1.refs_5_ = bf16[2,256,128]{2,1,0:T(8,128)(2,1)S(1)} collective-permute-done((bf16[2,256,128]{2,1,0:T(8,128)(2,1)S(1)}, bf16[2,256,128]{2,1,0:T(8,128)(2,1)S(1)}, u32[]{:S(2)}, u32[]{:S(2)}) %collective-permute-start.1) | collective-permute-done | bytes 131104 | tf_op jit(solution)/shard_map/ppermute | solution.py:28
  10.0 1.5 %collective-permute-start.2 = (bf16[2,256,128]{2,1,0:T(8,128)(2,1)S(1)}, bf16[2,256,128]{2,1,0:T(8,128)(2,1)S(1)}, u32[]{:S(2)}, u32[]{:S(2)}) collective-permute-start(bf16[2,256,128]{2,1,0:T(8,128)(2,1)S(1)} %collective-permute-done.refs_8_), channel_id=1, source_target_pairs={{0,8},{4,12},{8,0},{12,4},{1,9},{5,13},{9,1},{13,5},{2,10},{6,14},... | collective-permute-start | bytes 393224 | tf_op jit(solution)/shard_map/ppermute | solution.py:28
  13.4 1.6 %collective-permute-done.2.refs_9_ = bf16[2,256,128]{2,1,0:T(8,128)(2,1)S(1)} collective-permute-done((bf16[2,256,128]{2,1,0:T(8,128)(2,1)S(1)}, bf16[2,256,128]{2,1,0:T(8,128)(2,1)S(1)}, u32[]{:S(2)}, u32[]{:S(2)}) %collective-permute-start.2) | collective-permute-done | bytes 131104 | tf_op jit(solution)/shard_map/ppermute | solution.py:28
  15.0 1.5 %collective-permute-start.10 = (bf16[2,256,128]{2,1,0:T(8,128)(2,1)S(1)}, bf16[2,256,128]{2,1,0:T(8,128)(2,1)S(1)}, u32[]{:S(2)}, u32[]{:S(2)}) collective-permute-start(bf16[2,256,128]{2,1,0:T(8,128)(2,1)S(1)} %get-tuple-element.41), channel_id=1, source_target_pairs={{0,8},{4,12},{8,0},{12,4},{1,9},{5,13},{9,1},{13,5},{2,10},{6,14},... | collective-permute-start | bytes 393224 | tf_op jit(solution)/shard_map/ppermute | solution.py:28
  17.1 1.6 %collective-permute-done.4.refs_3_ = bf16[1,512,128]{2,1,0:T(8,128)(2,1)S(1)} collective-permute-done((bf16[1,512,128]{2,1,0:T(8,128)(2,1)S(1)}, bf16[1,512,128]{2,1,0:T(8,128)(2,1)S(1)}, u32[]{:S(2)}, u32[]{:S(2)}) %collective-permute-start.4) | collective-permute-done | bytes 131104 | tf_op jit(solution)/shard_map/ppermute | solution.py:28
  19.1 1.6 %collective-permute-start.17 = (bf16[1,512,128]{2,1,0:T(8,128)(2,1)S(1)}, bf16[1,512,128]{2,1,0:T(8,128)(2,1)S(1)}, u32[]{:S(2)}, u32[]{:S(2)}) collective-permute-start(bf16[1,512,128]{2,1,0:T(8,128)(2,1)S(1)} %get-tuple-element.44), channel_id=1, source_target_pairs={{0,1},{1,0},{2,3},{3,2},{4,5},{5,4},{6,7},{7,6},{8,9},{9,8},{10,11... | collective-permute-start | bytes 393224 | tf_op jit(solution)/shard_map/ppermute | solution.py:28
  20.7 1.6 %copy-done.2 = bf16[2,512,1024]{2,1,0:T(8,128)(2,1)S(1)} copy-done((bf16[2,512,1024]{2,1,0:T(8,128)(2,1)S(1)}, bf16[2,512,1024]{2,1,0:T(8,128)(2,1)}, u32[]{:S(2)}) %copy-start.2) | copy-done | bytes 2097176
  22.3 1.6 %copy-done.3 = bf16[2,512,1024]{2,1,0:T(8,128)(2,1)S(1)} copy-done((bf16[2,512,1024]{2,1,0:T(8,128)(2,1)S(1)}, bf16[2,512,1024]{2,1,0:T(8,128)(2,1)}, u32[]{:S(2)}) %copy-start.3) | copy-done | bytes 2097176
  23.9 16.0 %shard_map.84 = (bf16[2,512,1024]{2,1,0:T(8,128)(2,1)}, bf16[2,512,1024]{2,1,0:T(8,128)(2,1)}, bf16[2,512,512]{2,1,0:T(8,128)(2,1)}, bf16[1,512,128]{2,1,0:T(8,128)(2,1)S(1)}, f32[2,1,1024,128]{3,2,1,0:T(8,128)S(1)}) custom-call(s32[3]{0:T(128)S(1)} %pad_add_fusion.scalars, bf16[2,512,1024]{2,1,0:T(8,128)(2,1)S(1)} %copy-done.2, ...), custom_call_target="tpu_custom_call" | custom-call | flops 9663676416 | bytes 4194304 | tf_op jit(solution)/shard_map/pallas_call | solution.py:276
  42.8 16.1 %shard_map.85 = (bf16[2,512,1024]{2,1,0:T(8,128)(2,1)}, bf16[2,512,1024]{2,1,0:T(8,128)(2,1)}, bf16[2,512,512]{2,1,0:T(8,128)(2,1)}, bf16[1,512,128]{2,1,0:T(8,1...) custom-call(s32[3]{0:T(128)S(1)} %pad_add_fusion.scalars, ...), custom_call_target="tpu_custom_call", output_to_operand_aliasing={{0}: (14, {}), {1}: (15, {}), {2}: (16, {})} | custom-call | flops 9663676416 | bytes 4194304 | tf_op jit(solution)/shard_map/pallas_call | solution.py:276
  58.9 1.7 %collective-permute-start.19 = (bf16[1,512,128]{2,1,0:T(8,128)(2,1)S(1)}, bf16[1,512,128]{2,1,0:T(8,128)(2,1)S(1)}, u32[]{:S(2)}, u32[]{:S(2)}) collective-permute-start(bf16[1,512,128]{2,1,0:T(8,128)(2,1)S(1)} %get-tuple-element.39), channel_id=1, source_target_pairs={{0,1},{1,0},{2,3},{3,2},{4,5},{5,4},{6,7},{7,6},{8,9},{9,8},{10,11... | collective-permute-start | bytes 393224 | tf_op jit(solution)/shard_map/ppermute | solution.py:28
  61.0 1.6 %collective-permute-start.20 = (bf16[1,512,128]{2,1,0:T(8,128)(2,1)S(1)}, bf16[1,512,128]{2,1,0:T(8,128)(2,1)S(1)}, u32[]{:S(2)}, u32[]{:S(2)}) collective-permute-start(bf16[1,512,128]{2,1,0:T(8,128)(2,1)S(1)} %get-tuple-element.58), channel_id=1, source_target_pairs={{0,1},{1,0},{2,3},{3,2},{4,5},{5,4},{6,7},{7,6},{8,9},{9,8},{10,11... | collective-permute-start | bytes 393224 | tf_op jit(solution)/shard_map/ppermute | solution.py:28
  62.6 16.2 %shard_map.86 = (bf16[2,512,1024]{2,1,0:T(8,128)(2,1)}, bf16[2,512,1024]{2,1,0:T(8,128)(2,1)}, bf16[2,512,512]{2,1,0:T(8,128)(2,1)}, bf16[1,512,128]{2,1,0:T(8,128)(2,1)S(1)}, f32[2,1,1024,128]{3,2,1,0:T(8,128)S(1)}) custom-call(s32[3]{0:T(128)S(1)} %pad_add_fusion.scalars, ...), custom_call_target="tpu_custom_call", output_to_operand_aliasing={{0}: (13, {}), {1}: (14, {}), {2}: (15, {})} | custom-call | flops 9663676416 | bytes 4194304 | tf_op jit(solution)/shard_map/pallas_call | solution.py:276
  80.2 16.1 %shard_map.87 = (bf16[2,512,1024]{2,1,0:T(8,128)(2,1)}, bf16[2,512,1024]{2,1,0:T(8,128)(2,1)}, bf16[2,512,512]{2,1,0:T(8,128)(2,1)}, bf16[1,512,128]{2,1,0:T(8,1...) custom-call(s32[3]{0:T(128)S(1)} %pad_add_fusion.scalars, ...), custom_call_target="tpu_custom_call", output_to_operand_aliasing={{0}: (14, {}), {1}: (15, {}), {2}: (16, {})} | custom-call | flops 9663676416 | bytes 4194304 | tf_op jit(solution)/shard_map/pallas_call | solution.py:276
  96.4 1.9 %collective-permute-done.24 = bf16[2,2,256,256]{3,2,1,0:T(8,128)(2,1)S(1)} collective-permute-done((bf16[2,2,256,256]{3,2,1,0:T(8,128)(2,1)S(1)}, bf16[2,2,256,256]{3,2,1,0:T(8,128)(2,1)S(1)}, u32[]{:S(2)}, u32[]{:S(2)}) %collective-permute-start.24) | collective-permute-done | bytes 524320 | tf_op jit(solution)/shard_map/ppermute | solution.py:28
  98.5 1.3 %collective-permute-start.25 = (bf16[2,256,256]{2,1,0:T(8,128)(2,1)S(1)}, bf16[2,256,256]{2,1,0:T(8,128)(2,1)S(1)}, u32[]{:S(2)}, u32[]{:S(2)}) collective-permute-start(bf16[2,256,256]{2,1,0:T(8,128)(2,1)S(1)} %fusion.3), channel_id=1, source_target_pairs={{0,8},{4,12},{8,0},{12,4},{1,9},{5,13},{9,1},{13,5},{2,10},{6,14},... | collective-permute-start | bytes 786440 | tf_op jit(solution)/shard_map/ppermute | solution.py:28
  99.9 1.7 %collective-permute-start.26 = (bf16[2,256,128]{2,1,0:T(8,128)(2,1)S(1)}, bf16[2,256,128]{2,1,0:T(8,128)(2,1)S(1)}, u32[]{:S(2)}, u32[]{:S(2)}) collective-permute-start(bf16[2,256,128]{2,1,0:T(8,128)(2,1)S(1)} %slice.59), channel_id=1, source_target_pairs={{0,1},{1,0},{2,3},{3,2},{4,5},{5,4},{6,7},{7,6},{8,9},{9,8},{10,11... | collective-permute-start | bytes 393224 | tf_op jit(solution)/shard_map/ppermute | solution.py:28
  102.0 4.9 %collective-permute-done.25 = bf16[2,256,256]{2,1,0:T(8,128)(2,1)S(1)} collective-permute-done((bf16[2,256,256]{2,1,0:T(8,128)(2,1)S(1)}, bf16[2,256,256]{2,1,0:T(8,128)(2,1)S(1)}, u32[]{:S(2)}, u32[]{:S(2)}) %collective-permute-start.25) | collective-permute-done | bytes 262176 | tf_op jit(solution)/shard_map/ppermute | solution.py:28
  107.0 1.6 %collective-permute-start.27 = (bf16[2,256,128]{2,1,0:T(8,128)(2,1)S(1)}, bf16[2,256,128]{2,1,0:T(8,128)(2,1)S(1)}, u32[]{:S(2)}, u32[]{:S(2)}) collective-permute-start(bf16[2,256,128]{2,1,0:T(8,128)(2,1)S(1)} %slice.58), channel_id=1, source_target_pairs={{0,1},{1,0},{2,3},{3,2},{4,5},{5,4},{6,7},{7,6},{8,9},{9,8},{10,11... | collective-permute-start | bytes 393224 | tf_op jit(solution)/shard_map/ppermute | solution.py:28
  108.9 3.2 %collective-permute-done.27 = bf16[2,256,128]{2,1,0:T(8,128)(2,1)S(1)} collective-permute-done((bf16[2,256,128]{2,1,0:T(8,128)(2,1)S(1)}, bf16[2,256,128]{2,1,0:T(8,128)(2,1)S(1)}, u32[]{:S(2)}, u32[]{:S(2)}) %collective-permute-start.27) | collective-permute-done | bytes 131104 | tf_op jit(solution)/shard_map/ppermute | solution.py:28
  (66 shorter events, 9.9 us)
Async XLA Ops:
  2.0 6.6 %collective-permute-start = (bf16[2,256,128]{2,1,0:T(8,128)(2,1)S(1)}, bf16[2,256,128]{2,1,0:T(8,128)(2,1)S(1)}, u32[]{:S(2)}, u32[]{:S(2)}) collective-permute-start(bf16[2,256,128]{2,1,0:T(8,128)(2,1)S(1)} %get-tuple-element.75), channel_id=1, source_target_pairs={{0,1},{1,0},{2,3},{3,2},{4,5},{5,4},{6,7},{7,6},{8,9},{9,8},{10,11... | collective-permute-start | bytes 393224 | tf_op jit(solution)/shard_map/ppermute | solution.py:28
  5.0 5.0 %collective-permute-start.1 = (bf16[2,256,128]{2,1,0:T(8,128)(2,1)S(1)}, bf16[2,256,128]{2,1,0:T(8,128)(2,1)S(1)}, u32[]{:S(2)}, u32[]{:S(2)}) collective-permute-start(bf16[2,256,128]{2,1,0:T(8,128)(2,1)S(1)} %get-tuple-element.74), channel_id=1, source_target_pairs={{0,8},{4,12},{8,0},{12,4},{1,9},{5,13},{9,1},{13,5},{2,10},{6,14},... | collective-permute-start | bytes 393224 | tf_op jit(solution)/shard_map/ppermute | solution.py:28
  11.5 5.0 %collective-permute-start.5 = (bf16[2,256,128]{2,1,0:T(8,128)(2,1)S(1)}, bf16[2,256,128]{2,1,0:T(8,128)(2,1)S(1)}, u32[]{:S(2)}, u32[]{:S(2)}) collective-permute-start(bf16[2,256,128]{2,1,0:T(8,128)(2,1)S(1)} %get-tuple-element.74), channel_id=1, source_target_pairs={{0,4},{4,0},{8,12},{12,8},{1,5},{5,1},{9,13},{13,9},{2,6},{6,2},{1... | collective-permute-start | bytes 393224 | tf_op jit(solution)/shard_map/ppermute | solution.py:28
  12.7 6.0 %collective-permute-start.4 = (bf16[1,512,128]{2,1,0:T(8,128)(2,1)S(1)}, bf16[1,512,128]{2,1,0:T(8,128)(2,1)S(1)}, u32[]{:S(2)}, u32[]{:S(2)}) collective-permute-start(bf16[1,512,128]{2,1,0:T(8,128)(2,1)S(1)} %get-tuple-element.68), channel_id=1, source_target_pairs={{0,1},{1,0},{2,3},{3,2},{4,5},{5,4},{6,7},{7,6},{8,9},{9,8},{10,11... | collective-permute-start | bytes 393224 | tf_op jit(solution)/shard_map/ppermute | solution.py:28
  13.2 5.9 %collective-permute-start.7 = (bf16[2,256,128]{2,1,0:T(8,128)(2,1)S(1)}, bf16[2,256,128]{2,1,0:T(8,128)(2,1)S(1)}, u32[]{:S(2)}, u32[]{:S(2)}) collective-permute-start(bf16[2,256,128]{2,1,0:T(8,128)(2,1)S(1)} %collective-permute-done.refs_8_), channel_id=1, source_target_pairs={{0,4},{4,0},{8,12},{12,8},{1,5},{5,1},{9,13},{13,9},{2,6},{6,2},{1... | collective-permute-start | bytes 393224 | tf_op jit(solution)/shard_map/ppermute | solution.py:28
  15.0 5.7 %collective-permute-start.10 = (bf16[2,256,128]{2,1,0:T(8,128)(2,1)S(1)}, bf16[2,256,128]{2,1,0:T(8,128)(2,1)S(1)}, u32[]{:S(2)}, u32[]{:S(2)}) collective-permute-start(bf16[2,256,128]{2,1,0:T(8,128)(2,1)S(1)} %get-tuple-element.41), channel_id=1, source_target_pairs={{0,8},{4,12},{8,0},{12,4},{1,9},{5,13},{9,1},{13,5},{2,10},{6,14},... | collective-permute-start | bytes 393224 | tf_op jit(solution)/shard_map/ppermute | solution.py:28
  18.6 21.2 %collective-permute-start.3 = (bf16[2,256,128]{2,1,0:T(8,128)(2,1)S(1)}, bf16[2,256,128]{2,1,0:T(8,128)(2,1)S(1)}, u32[]{:S(2)}, u32[]{:S(2)}) collective-permute-start(bf16[2,256,128]{2,1,0:T(8,128)(2,1)S(1)} %get-tuple-element.38), channel_id=1, source_target_pairs={{0,1},{1,0},{2,3},{3,2},{4,5},{5,4},{6,7},{7,6},{8,9},{9,8},{10,11... | collective-permute-start | bytes 393224 | tf_op jit(solution)/shard_map/ppermute | solution.py:28
  19.1 23.0 %collective-permute-start.17 = (bf16[1,512,128]{2,1,0:T(8,128)(2,1)S(1)}, bf16[1,512,128]{2,1,0:T(8,128)(2,1)S(1)}, u32[]{:S(2)}, u32[]{:S(2)}) collective-permute-start(bf16[1,512,128]{2,1,0:T(8,128)(2,1)S(1)} %get-tuple-element.44), channel_id=1, source_target_pairs={{0,1},{1,0},{2,3},{3,2},{4,5},{5,4},{6,7},{7,6},{8,9},{9,8},{10,11... | collective-permute-start | bytes 393224 | tf_op jit(solution)/shard_map/ppermute | solution.py:28
  20.7 21.6 %collective-permute-start.12 = (bf16[2,256,128]{2,1,0:T(8,128)(2,1)S(1)}, bf16[2,256,128]{2,1,0:T(8,128)(2,1)S(1)}, u32[]{:S(2)}, u32[]{:S(2)}) collective-permute-start(bf16[2,256,128]{2,1,0:T(8,128)(2,1)S(1)} %collective-permute-done.10.refs_5_), channel_id=1, source_target_pairs={{0,4},{4,0},{8,12},{12,8},{1,5},{5,1},{9,13},{13,9},{2,6},{6,2},{1... | collective-permute-start | bytes 393224 | tf_op jit(solution)/shard_map/ppermute | solution.py:28
  39.9 21.1 %collective-permute-start.15 = (bf16[2,256,128]{2,1,0:T(8,128)(2,1)S(1)}, bf16[2,256,128]{2,1,0:T(8,128)(2,1)S(1)}, u32[]{:S(2)}, u32[]{:S(2)}) collective-permute-start(bf16[2,256,128]{2,1,0:T(8,128)(2,1)S(1)} %collective-permute-done.3.refs_8_), channel_id=1, source_target_pairs={{0,12},{4,8},{8,4},{12,0},{1,13},{5,9},{9,5},{13,1},{2,14},{6,10},... | collective-permute-start | bytes 393224 | tf_op jit(solution)/shard_map/ppermute | solution.py:28
  40.8 21.7 %collective-permute-start.14 = (bf16[2,256,128]{2,1,0:T(8,128)(2,1)S(1)}, bf16[2,256,128]{2,1,0:T(8,128)(2,1)S(1)}, u32[]{:S(2)}, u32[]{:S(2)}) collective-permute-start(bf16[2,256,128]{2,1,0:T(8,128)(2,1)S(1)} %collective-permute-done.3.refs_8_), channel_id=1, source_target_pairs={{0,4},{4,0},{8,12},{12,8},{1,5},{5,1},{9,13},{13,9},{2,6},{6,2},{1... | collective-permute-start | bytes 393224 | tf_op jit(solution)/shard_map/ppermute | solution.py:28
  40.8 21.7 %collective-permute-start.13 = (bf16[2,256,128]{2,1,0:T(8,128)(2,1)S(1)}, bf16[2,256,128]{2,1,0:T(8,128)(2,1)S(1)}, u32[]{:S(2)}, u32[]{:S(2)}) collective-permute-start(bf16[2,256,128]{2,1,0:T(8,128)(2,1)S(1)} %collective-permute-done.3.refs_8_), channel_id=1, source_target_pairs={{0,8},{4,12},{8,0},{12,4},{1,9},{5,13},{9,1},{13,5},{2,10},{6,14},... | collective-permute-start | bytes 393224 | tf_op jit(solution)/shard_map/ppermute | solution.py:28
  42.1 16.8 %collective-permute-start.11 = (bf16[2,256,128]{2,1,0:T(8,128)(2,1)S(1)}, bf16[2,256,128]{2,1,0:T(8,128)(2,1)S(1)}, u32[]{:S(2)}, u32[]{:S(2)}) collective-permute-start(bf16[2,256,128]{2,1,0:T(8,128)(2,1)S(1)} %get-tuple-element.41), channel_id=1, source_target_pairs={{0,4},{4,0},{8,12},{12,8},{1,5},{5,1},{9,13},{13,9},{2,6},{6,2},{1... | collective-permute-start | bytes 393224 | tf_op jit(solution)/shard_map/ppermute | solution.py:28
  42.3 18.2 %collective-permute-start.16 = (bf16[1,512,128]{2,1,0:T(8,128)(2,1)S(1)}, bf16[1,512,128]{2,1,0:T(8,128)(2,1)S(1)}, u32[]{:S(2)}, u32[]{:S(2)}) collective-permute-start(bf16[1,512,128]{2,1,0:T(8,128)(2,1)S(1)} %get-tuple-element.43), channel_id=1, source_target_pairs={{0,1},{1,0},{2,3},{3,2},{4,5},{5,4},{6,7},{7,6},{8,9},{9,8},{10,11... | collective-permute-start | bytes 393224 | tf_op jit(solution)/shard_map/ppermute | solution.py:28
  58.9 21.4 %collective-permute-start.19 = (bf16[1,512,128]{2,1,0:T(8,128)(2,1)S(1)}, bf16[1,512,128]{2,1,0:T(8,128)(2,1)S(1)}, u32[]{:S(2)}, u32[]{:S(2)}) collective-permute-start(bf16[1,512,128]{2,1,0:T(8,128)(2,1)S(1)} %get-tuple-element.39), channel_id=1, source_target_pairs={{0,1},{1,0},{2,3},{3,2},{4,5},{5,4},{6,7},{7,6},{8,9},{9,8},{10,11... | collective-permute-start | bytes 393224 | tf_op jit(solution)/shard_map/ppermute | solution.py:28
  60.5 19.7 %collective-permute-start.9 = (bf16[1,512,128]{2,1,0:T(8,128)(2,1)S(1)}, bf16[1,512,128]{2,1,0:T(8,128)(2,1)S(1)}, u32[]{:S(2)}, u32[]{:S(2)}) collective-permute-start(bf16[1,512,128]{2,1,0:T(8,128)(2,1)S(1)} %get-tuple-element.40), channel_id=1, source_target_pairs={{0,1},{1,0},{2,3},{3,2},{4,5},{5,4},{6,7},{7,6},{8,9},{9,8},{10,11... | collective-permute-start | bytes 393224 | tf_op jit(solution)/shard_map/ppermute | solution.py:28
  61.0 19.3 %collective-permute-start.20 = (bf16[1,512,128]{2,1,0:T(8,128)(2,1)S(1)}, bf16[1,512,128]{2,1,0:T(8,128)(2,1)S(1)}, u32[]{:S(2)}, u32[]{:S(2)}) collective-permute-start(bf16[1,512,128]{2,1,0:T(8,128)(2,1)S(1)} %get-tuple-element.58), channel_id=1, source_target_pairs={{0,1},{1,0},{2,3},{3,2},{4,5},{5,4},{6,7},{7,6},{8,9},{9,8},{10,11... | collective-permute-start | bytes 393224 | tf_op jit(solution)/shard_map/ppermute | solution.py:28
  62.6 16.6 %collective-permute-start.18 = (bf16[2,2,256,256]{3,2,1,0:T(8,128)(2,1)S(1)}, bf16[2,2,256,256]{3,2,1,0:T(8,128)(2,1)S(1)}, u32[]{:S(2)}, u32[]{:S(2)}) collective-permute-start(bf16[2,2,256,256]{3,2,1,0:T(8,128)(2,1)S(1)} %get-tuple-element.57), channel_id=1, source_target_pairs={{0,4},{4,0},{8,12},{12,8},{1,5},{5,1},{9,13},{13,9},{2,6},{6,2},{1... | collective-permute-start | bytes 1572872 | tf_op jit(solution)/shard_map/ppermute | solution.py:28
  78.7 17.6 %collective-permute-start.21 = (bf16[1,512,128]{2,1,0:T(8,128)(2,1)S(1)}, bf16[1,512,128]{2,1,0:T(8,128)(2,1)S(1)}, u32[]{:S(2)}, u32[]{:S(2)}) collective-permute-start(bf16[1,512,128]{2,1,0:T(8,128)(2,1)S(1)} %get-tuple-element.62), channel_id=1, source_target_pairs={{0,1},{1,0},{2,3},{3,2},{4,5},{5,4},{6,7},{7,6},{8,9},{9,8},{10,11... | collective-permute-start | bytes 393224 | tf_op jit(solution)/shard_map/ppermute | solution.py:28
  79.4 17.0 %collective-permute-start.22 = (bf16[2,256,256]{2,1,0:T(8,128)(2,1)S(1)}, bf16[2,256,256]{2,1,0:T(8,128)(2,1)S(1)}, u32[]{:S(2)}, u32[]{:S(2)}) collective-permute-start(bf16[2,256,256]{2,1,0:T(8,128)(2,1)S(1)} %fusion.2.refs_16_), channel_id=1, source_target_pairs={{0,8},{4,12},{8,0},{12,4},{1,9},{5,13},{9,1},{13,5},{2,10},{6,14},... | collective-permute-start | bytes 786440 | tf_op jit(solution)/shard_map/ppermute | solution.py:28
  98.5 8.4 %collective-permute-start.25 = (bf16[2,256,256]{2,1,0:T(8,128)(2,1)S(1)}, bf16[2,256,256]{2,1,0:T(8,128)(2,1)S(1)}, u32[]{:S(2)}, u32[]{:S(2)}) collective-permute-start(bf16[2,256,256]{2,1,0:T(8,128)(2,1)S(1)} %fusion.3), channel_id=1, source_target_pairs={{0,8},{4,12},{8,0},{12,4},{1,9},{5,13},{9,1},{13,5},{2,10},{6,14},... | collective-permute-start | bytes 786440 | tf_op jit(solution)/shard_map/ppermute | solution.py:28
  99.9 9.0 %collective-permute-start.26 = (bf16[2,256,128]{2,1,0:T(8,128)(2,1)S(1)}, bf16[2,256,128]{2,1,0:T(8,128)(2,1)S(1)}, u32[]{:S(2)}, u32[]{:S(2)}) collective-permute-start(bf16[2,256,128]{2,1,0:T(8,128)(2,1)S(1)} %slice.59), channel_id=1, source_target_pairs={{0,1},{1,0},{2,3},{3,2},{4,5},{5,4},{6,7},{7,6},{8,9},{9,8},{10,11... | collective-permute-start | bytes 393224 | tf_op jit(solution)/shard_map/ppermute | solution.py:28
  101.6 7.1 %collective-permute-start.23 = (bf16[1,512,128]{2,1,0:T(8,128)(2,1)S(1)}, bf16[1,512,128]{2,1,0:T(8,128)(2,1)S(1)}, u32[]{:S(2)}, u32[]{:S(2)}) collective-permute-start(bf16[1,512,128]{2,1,0:T(8,128)(2,1)S(1)} %get-tuple-element.65), channel_id=1, source_target_pairs={{0,1},{1,0},{2,3},{3,2},{4,5},{5,4},{6,7},{7,6},{8,9},{9,8},{10,11... | collective-permute-start | bytes 393224 | tf_op jit(solution)/shard_map/ppermute | solution.py:28
  107.0 5.0 %collective-permute-start.27 = (bf16[2,256,128]{2,1,0:T(8,128)(2,1)S(1)}, bf16[2,256,128]{2,1,0:T(8,128)(2,1)S(1)}, u32[]{:S(2)}, u32[]{:S(2)}) collective-permute-start(bf16[2,256,128]{2,1,0:T(8,128)(2,1)S(1)} %slice.58), channel_id=1, source_target_pairs={{0,1},{1,0},{2,3},{3,2},{4,5},{5,4},{6,7},{7,6},{8,9},{9,8},{10,11... | collective-permute-start | bytes 393224 | tf_op jit(solution)/shard_map/ppermute | solution.py:28
  (11 other events, 89.7 us)

commit v3 on v2

--- a/solution.py
+++ b/solution.py
@@ -40,28 +40,15 @@
     final = turn == n_resp - 1
     n_out = 4 + (1 if not final or pieces == n_keep else 2)
     grads = rest[4:n_out]
-    k_all, v_all, k_t, v_t, weights, probs, dscores, acc_k, acc_v, res_k, res_v = rest[n_out:]
+    k_all, v_all, k_t, v_t, weights, probs, dscores, q_scaled, do_scaled, acc_k, acc_v = rest[n_out:]
 
     head = pl.program_id(0)
-    prompt = scalars[turn]
     even = scalars[n_resp] == 0
     n_prompt = pieces * rows
     n_query = q_ref.shape[1]
-
-    @pl.when(head == 0)
-    def _():
-        if turn == 0:
-            acc_k[...] = jnp.zeros_like(acc_k)
-            acc_v[...] = jnp.zeros_like(acc_v)
-        elif turn == 1:
-            before = scalars[0]
-            acc_k[1 - before] = jnp.zeros(acc_k.shape[1:], jnp.float32)
-            acc_v[1 - before] = jnp.zeros(acc_v.shape[1:], jnp.float32)
-            acc_k[before] = prior_ref[0, 0]
-            acc_v[before] = prior_ref[1, 0]
-        else:
-            acc_k[...] = prior_ref[0]
-            acc_v[...] = prior_ref[1]
+    n_blocks = n_query // BLOCK
+    n_first = n_prompt // BLOCK
+    n_all = n_first + n_blocks
 
     def gather(dst, piece_refs, resp_ref):
         for i, ref in enumerate(piece_refs):
@@ -80,14 +67,9 @@
 
     @pl.when(head == 0)
     def _():
-        res_k[...] = jnp.zeros_like(res_k)
-        res_v[...] = jnp.zeros_like(res_v)
         k_t[...] = k_all[...].T
         v_t[...] = v_all[...].T
 
-    n_blocks = n_query // BLOCK
-    state = [dict() for _ in range(n_blocks)]
-
     def span(c):
         return slice(c * BLOCK, (c + 1) * BLOCK)
 
@@ -95,17 +77,15 @@
         return op(x.reshape(-1, 8, x.shape[-1]), axis=0)
 
     def stages(i):
-        st = state[i]
+        st = {}
         t = span(i)
-        n_chunks = n_prompt // BLOCK + i + 1
+        n_chunks = n_first + i + 1
         seen = n_chunks * BLOCK
         q = q_ref[0, t, :]
         do = do_ref[0, t, :]
 
         def score(c):
-            if c == 0:
-                st["s"] = dot(k_all[:seen, :], q, NT)
-            s = st["s"][span(c), :]
+            s = dot(k_all[span(c), :], q, NT)
             if c == n_chunks - 1:
                 row = lax.broadcasted_iota(jnp.int32, (BLOCK, BLOCK), 0)
                 col = lax.broadcasted_iota(jnp.int32, (BLOCK, BLOCK), 1)
@@ -119,93 +99,120 @@
         def weigh(c):
             w = jnp.exp(weights[span(c), t] * SCALE - st["top"])
             weights[span(c), t] = w
+            probs[span(c), t] = w.astype(jnp.bfloat16)
             total = fold(w, jnp.sum)
             st["sum"] = total if c == 0 else st["sum"] + total
-            if c == n_chunks - 1:
-                st["inv"] = 1.0 / jnp.sum(st["sum"], axis=0, keepdims=True)
-
-        def norm(c):
-            probs[span(c), t] = (weights[span(c), t] * st["inv"]).astype(jnp.bfloat16)
-            if c == n_chunks - 1:
-                o = dot(v_t[:, :seen], probs[:seen, t], NN)
-                out_ref[0, t, :] = o.T.astype(jnp.bfloat16)
-                do_t = do.astype(jnp.float32).T
-                st["delta"] = jnp.sum(o * do_t, axis=0, keepdims=True)
-                st["inv"] = st["inv"] * SCALE
+
+        def output(c):
+            if c > 0:
+                return
+            st["inv"] = 1.0 / jnp.sum(st["sum"], axis=0, keepdims=True)
+            o = dot(v_t[:, :seen], probs[:seen, t], NN) * st["inv"]
+            do_t = do.astype(jnp.float32).T
+            st["delta"] = jnp.sum(o * do_t, axis=0, keepdims=True)
+            out_ref[0, t, :] = o.T.astype(jnp.bfloat16)
+            inv_rows = jnp.broadcast_to(st["inv"], (HD, BLOCK)).T
+            do_scaled[t, :] = (do.astype(jnp.float32) * inv_rows).astype(jnp.bfloat16)
+            q_scaled[t, :] = (q.astype(jnp.float32) * (inv_rows * SCALE)).astype(jnp.bfloat16)
 
         def grad(c):
-            if c == 0:
-                st["dp"] = dot(v_all[:seen, :], do, NT)
-            dp = st["dp"][span(c), :]
-            ds = (weights[span(c), t] * st["inv"]) * (dp - st["delta"])
+            dp = dot(v_all[span(c), :], do, NT)
+            ds = weights[span(c), t] * (dp - st["delta"])
             dscores[span(c), t] = ds.astype(jnp.bfloat16)
-            if c == n_chunks - 1:
-                dq = dot(k_t[:, :seen], dscores[:seen, t], NN)
-                dq_ref[0, t, :] = dq.T.astype(jnp.bfloat16)
-
-        return [[functools.partial(f, c) for c in range(n_chunks)] for f in (score, weigh, norm, grad)]
+
+        def query(c):
+            if c > 0:
+                return
+            dq = dot(k_t[:, :seen], dscores[:seen, t], NN) * (st["inv"] * SCALE)
+            dq_ref[0, t, :] = dq.T.astype(jnp.bfloat16)
+
+        return [[functools.partial(f, c) for c in range(n_chunks)] for f in (score, weigh, output, grad, query)]
+
+    def add_values(c):
+        t0 = max(c - n_first, 0) * BLOCK
+        acc_v[span(c), :] += dot(probs[span(c), t0:], do_scaled[t0:, :], NN)
+
+    def add_keys(c):
+        t0 = max(c - n_first, 0) * BLOCK
+        acc_k[span(c), :] += dot(dscores[span(c), t0:], q_scaled[t0:, :], NN)
 
     plan = [stages(i) for i in range(n_blocks)]
-    for slot in range(4 + n_blocks - 1):
-        groups = [plan[i][slot - i] for i in reversed(range(n_blocks)) if 0 <= slot - i < 4]
+    former = [[functools.partial(add_values, c) for c in range(n_all)]]
+    former += [[functools.partial(add_keys, c) for c in range(n_all)]]
+    for slot in range(5 + n_blocks - 1):
+        groups = [former[slot]] if slot < 2 else []
+        groups += [plan[i][slot - i] for i in reversed(range(n_blocks)) if 0 <= slot - i < 5]
         for c in range(max(len(g) for g in groups)):
             for g in groups:
                 if c < len(g):
                     g[c]()
 
-    q_all = q_ref[0]
-    do_all = do_ref[0]
-    acc_v[prompt] += dot(probs[:n_prompt, :], do_all, NN)
-    acc_k[prompt] += dot(dscores[:n_prompt, :], q_all, NN)
-    for i in range(n_blocks):
-        u = span(n_prompt // BLOCK + i)
-        t0 = i * BLOCK
-        res_v[span(i), :] += dot(probs[u, t0:], do_all[t0:], NN)
-        res_k[span(i), :] += dot(dscores[u, t0:], q_all[t0:], NN)
+    @pl.when(head == 0)
+    def _():
+        acc_k[...] = jnp.zeros_like(acc_k)
+        acc_v[...] = jnp.zeros_like(acc_v)
 
     last = head == heads - 1
 
+    @pl.when(last)
+    def _():
+        for c in range(n_all):
+            add_values(c)
+            add_keys(c)
+
+    def respond(ref, acc):
+        ref[0] = acc[n_prompt:, :].astype(jnp.bfloat16)
+
     @pl.when(last & even)
     def _():
-        dra_ref[0] = res_k[...].astype(jnp.bfloat16)
-        drb_ref[0] = res_v[...].astype(jnp.bfloat16)
+        respond(dra_ref, acc_k)
+        respond(drb_ref, acc_v)
 
     @pl.when(last & jnp.logical_not(even))
     def _():
-        dra_ref[0] = res_v[...].astype(jnp.bfloat16)
-        drb_ref[0] = res_k[...].astype(jnp.bfloat16)
+        respond(dra_ref, acc_v)
+        respond(drb_ref, acc_k)
+
+    def total(which, acc, p_id, at):
+        val = jnp.where(scalars[turn] == p_id, acc[at, :], 0.0)
+        if turn == 1:
+            val += jnp.where(scalars[0] == p_id, prior_ref[which, 0, at, :], 0.0)
+        elif turn > 1:
+            val += prior_ref[which, p_id, at, :]
+        return val
 
     if not final:
 
         @pl.when(last)
         def _():
-            if turn == 0:
-                grads[0][0, 0] = acc_k[prompt]
-                grads[0][1, 0] = acc_v[prompt]
-            else:
-                grads[0][0] = acc_k[...]
-                grads[0][1] = acc_v[...]
+            for which, acc in enumerate((acc_k, acc_v)):
+                if turn == 0:
+                    grads[0][which, 0] = acc[:n_prompt, :]
+                else:
+                    for p_id in range(P_SIZE):
+                        grads[0][which, p_id] = total(which, acc, p_id, slice(0, n_prompt))
 
         return
 
-    def scatter(slot, acc):
+    def scatter(slot, which, acc):
+        lanes = slice(slot * HD, (slot + 1) * HD)
         for i in range(pieces):
             for p_id in range(P_SIZE):
-                val = acc[p_id, i * rows : (i + 1) * rows, :]
+                val = total(which, acc, p_id, slice(i * rows, (i + 1) * rows))
                 if i < n_keep:
-                    grads[0][i, p_id, :, slot * HD : (slot + 1) * HD] = val
+                    grads[0][i, p_id, :, lanes] = val
                 else:
-                    grads[1][i - n_keep, p_id, :, slot * HD : (slot + 1) * HD] = val.astype(jnp.bfloat16)
+                    grads[1][i - n_keep, p_id, :, lanes] = val.astype(jnp.bfloat16)
 
     @pl.when(last & even)
     def _():
-        scatter(0, acc_k)
-        scatter(1, acc_v)
+        scatter(0, 0, acc_k)
+        scatter(1, 1, acc_v)
 
     @pl.when(last & jnp.logical_not(even))
     def _():
-        scatter(0, acc_v)
-        scatter(1, acc_k)
+        scatter(0, 1, acc_v)
+        scatter(1, 0, acc_k)
 
 
 def attend(scalars, queries, d_out, resp_a, resp_b, prompt_a, prompt_b, n_keep, chunk, heads, turn, prior, shared, after=()):
@@ -267,10 +274,10 @@
         pltpu.VMEM((n_keys, n_query), jnp.float32),
         pltpu.VMEM((n_keys, n_query), jnp.bfloat16),
         pltpu.VMEM((n_keys, n_query), jnp.bfloat16),
-        pltpu.VMEM((P_SIZE, n_prompt, HD), jnp.float32),
-        pltpu.VMEM((P_SIZE, n_prompt, HD), jnp.float32),
-        pltpu.VMEM((n_query, HD), jnp.float32),
-        pltpu.VMEM((n_query, HD), jnp.float32),
+        pltpu.VMEM((n_query, HD), jnp.bfloat16),
+        pltpu.VMEM((n_query, HD), jnp.bfloat16),
+        pltpu.VMEM((n_keys, HD), jnp.float32),
+        pltpu.VMEM((n_keys, HD), jnp.float32),
     ]
     flops = 12 * heads * n_query * n_keys * HD
     return pl.pallas_call(

time: 113 us -> 115 us (1.018)
  Pallas kernels: 64.4 us -> 65.6 us
    pallas_call x4, Pallas kernels: 64.4 us -> 65.6 us  [attend(): pl.pallas_call(functools.partial(attend_kernel, (pieces, rows, n_keep, he...]
where the time goes in v3:
time: 115 us; the launch traced here: 114 us
  Pallas kernels  65.6 us (57%)
  starting transfers between devices  23.8 us (21%)
  waiting for transfers between devices  16.7 us (15%)
  local copies, waits for them, and re-layouts  5.74 us (5%)
  other arithmetic  1.76 us (2%)
    pallas_call x4, Pallas kernels, attend(): pl.pallas_call(functools.partial(attend_kernel, (pieces, rows, n_keep, he...  65.6 us
    ppermute x28, starting transfers between devices, swap(): lax.ppermute(block, axis, [(i, i ^ step) for i in range(lax.axis_size(axi...  23.8 us
    ppermute x28, waiting for transfers between devices, swap(): lax.ppermute(block, axis, [(i, i ^ step) for i in range(lax.axis_size(axi...  16.7 us
    unnamed x14, local copies, waits for them, and re-layouts  3.2 us
  transfers between devices with their start and end apart: 28, of which 7 were waited for; matrix products, arithmetic and copies ran while one was open for 1% of the time, Pallas kernels for 57%

profile of v3, /device:TPU:0, one launch (start us, length us, event | category | flops | bytes accessed | tf_op | source)
XLA Modules:
  0.0 114.5 jit_solution(5148245570201465345)
XLA Ops:
  0.7 1.3 %constant_dynamic-slice_fusion.3 = (bf16[2,256,128]{2,1,0:T(8,128)(2,1)S(1)}, bf16[2,256,128]{2,1,0:T(8,128)(2,1)S(1)}, bf16[2,256,128]{2,1,0:T(8,128)(2,1)S(1)}, bf16[2,256,128]{2,1,0:T(8,128)(2,1)S(1)}) fusion(bf16[2,256,512]{2,1,0:T(8,128)(2,1)} %refs_4_.7, s32[]{:T(128)S(6)} %select_n.40, s32[]{:T(128)S(6)} %select_n.39, s32[]{:T(128)S(6)} %select_n.38, ...), kind=kLoop, calls=%fused_computation.21 | loop fusion | bytes 1048592 | tf_op jit(solution)/shard_map/dynamic_slice | solution.py:324
  2.0 3.1 %collective-permute-start = (bf16[2,256,128]{2,1,0:T(8,128)(2,1)S(1)}, bf16[2,256,128]{2,1,0:T(8,128)(2,1)S(1)}, u32[]{:S(2)}, u32[]{:S(2)}) collective-permute-start(bf16[2,256,128]{2,1,0:T(8,128)(2,1)S(1)} %get-tuple-element.75), channel_id=1, source_target_pairs={{0,1},{1,0},{2,3},{3,2},{4,5},{5,4},{6,7},{7,6},{8,9},{9,8},{10,11... | collective-permute-start | bytes 393224 | tf_op jit(solution)/shard_map/ppermute | solution.py:28
  5.0 1.5 %collective-permute-start.1 = (bf16[2,256,128]{2,1,0:T(8,128)(2,1)S(1)}, bf16[2,256,128]{2,1,0:T(8,128)(2,1)S(1)}, u32[]{:S(2)}, u32[]{:S(2)}) collective-permute-start(bf16[2,256,128]{2,1,0:T(8,128)(2,1)S(1)} %get-tuple-element.74), channel_id=1, source_target_pairs={{0,8},{4,12},{8,0},{12,4},{1,9},{5,13},{9,1},{13,5},{2,10},{6,14},... | collective-permute-start | bytes 393224 | tf_op jit(solution)/shard_map/ppermute | solution.py:28
  6.5 2.0 %collective-permute-done.refs_8_ = bf16[2,256,128]{2,1,0:T(8,128)(2,1)S(1)} collective-permute-done((bf16[2,256,128]{2,1,0:T(8,128)(2,1)S(1)}, bf16[2,256,128]{2,1,0:T(8,128)(2,1)S(1)}, u32[]{:S(2)}, u32[]{:S(2)}) %collective-permute-start) | collective-permute-done | bytes 131104 | tf_op jit(solution)/shard_map/ppermute | solution.py:28
  8.5 1.5 %collective-permute-done.1.refs_5_ = bf16[2,256,128]{2,1,0:T(8,128)(2,1)S(1)} collective-permute-done((bf16[2,256,128]{2,1,0:T(8,128)(2,1)S(1)}, bf16[2,256,128]{2,1,0:T(8,128)(2,1)S(1)}, u32[]{:S(2)}, u32[]{:S(2)}) %collective-permute-start.1) | collective-permute-done | bytes 131104 | tf_op jit(solution)/shard_map/ppermute | solution.py:28
  10.0 1.5 %collective-permute-start.2 = (bf16[2,256,128]{2,1,0:T(8,128)(2,1)S(1)}, bf16[2,256,128]{2,1,0:T(8,128)(2,1)S(1)}, u32[]{:S(2)}, u32[]{:S(2)}) collective-permute-start(bf16[2,256,128]{2,1,0:T(8,128)(2,1)S(1)} %collective-permute-done.refs_8_), channel_id=1, source_target_pairs={{0,8},{4,12},{8,0},{12,4},{1,9},{5,13},{9,1},{13,5},{2,10},{6,14},... | collective-permute-start | bytes 393224 | tf_op jit(solution)/shard_map/ppermute | solution.py:28
  13.4 1.6 %collective-permute-done.2.refs_9_ = bf16[2,256,128]{2,1,0:T(8,128)(2,1)S(1)} collective-permute-done((bf16[2,256,128]{2,1,0:T(8,128)(2,1)S(1)}, bf16[2,256,128]{2,1,0:T(8,128)(2,1)S(1)}, u32[]{:S(2)}, u32[]{:S(2)}) %collective-permute-start.2) | collective-permute-done | bytes 131104 | tf_op jit(solution)/shard_map/ppermute | solution.py:28
  15.0 1.5 %collective-permute-start.10 = (bf16[2,256,128]{2,1,0:T(8,128)(2,1)S(1)}, bf16[2,256,128]{2,1,0:T(8,128)(2,1)S(1)}, u32[]{:S(2)}, u32[]{:S(2)}) collective-permute-start(bf16[2,256,128]{2,1,0:T(8,128)(2,1)S(1)} %get-tuple-element.41), channel_id=1, source_target_pairs={{0,8},{4,12},{8,0},{12,4},{1,9},{5,13},{9,1},{13,5},{2,10},{6,14},... | collective-permute-start | bytes 393224 | tf_op jit(solution)/shard_map/ppermute | solution.py:28
  17.1 1.6 %collective-permute-done.4.refs_3_ = bf16[1,512,128]{2,1,0:T(8,128)(2,1)S(1)} collective-permute-done((bf16[1,512,128]{2,1,0:T(8,128)(2,1)S(1)}, bf16[1,512,128]{2,1,0:T(8,128)(2,1)S(1)}, u32[]{:S(2)}, u32[]{:S(2)}) %collective-permute-start.4) | collective-permute-done | bytes 131104 | tf_op jit(solution)/shard_map/ppermute | solution.py:28
  19.1 1.6 %collective-permute-start.17 = (bf16[1,512,128]{2,1,0:T(8,128)(2,1)S(1)}, bf16[1,512,128]{2,1,0:T(8,128)(2,1)S(1)}, u32[]{:S(2)}, u32[]{:S(2)}) collective-permute-start(bf16[1,512,128]{2,1,0:T(8,128)(2,1)S(1)} %get-tuple-element.44), channel_id=1, source_target_pairs={{0,1},{1,0},{2,3},{3,2},{4,5},{5,4},{6,7},{7,6},{8,9},{9,8},{10,11... | collective-permute-start | bytes 393224 | tf_op jit(solution)/shard_map/ppermute | solution.py:28
  20.7 1.6 %copy-done.2 = bf16[2,512,1024]{2,1,0:T(8,128)(2,1)S(1)} copy-done((bf16[2,512,1024]{2,1,0:T(8,128)(2,1)S(1)}, bf16[2,512,1024]{2,1,0:T(8,128)(2,1)}, u32[]{:S(2)}) %copy-start.2) | copy-done | bytes 2097176
  22.3 1.6 %copy-done.3 = bf16[2,512,1024]{2,1,0:T(8,128)(2,1)S(1)} copy-done((bf16[2,512,1024]{2,1,0:T(8,128)(2,1)S(1)}, bf16[2,512,1024]{2,1,0:T(8,128)(2,1)}, u32[]{:S(2)}) %copy-start.3) | copy-done | bytes 2097176
  23.9 16.2 %shard_map.84 = (bf16[2,512,1024]{2,1,0:T(8,128)(2,1)}, bf16[2,512,1024]{2,1,0:T(8,128)(2,1)}, bf16[2,512,512]{2,1,0:T(8,128)(2,1)}, bf16[1,512,128]{2,1,0:T(8,128)(2,1)S(1)}, f32[2,1,1024,128]{3,2,1,0:T(8,128)S(1)}) custom-call(s32[3]{0:T(128)S(1)} %pad_add_fusion.scalars, bf16[2,512,1024]{2,1,0:T(8,128)(2,1)S(1)} %copy-done.2, ...), custom_call_target="tpu_custom_call" | custom-call | flops 9663676416 | bytes 4194304 | tf_op jit(solution)/shard_map/pallas_call | solution.py:283
  43.0 16.5 %shard_map.85 = (bf16[2,512,1024]{2,1,0:T(8,128)(2,1)}, bf16[2,512,1024]{2,1,0:T(8,128)(2,1)}, bf16[2,512,512]{2,1,0:T(8,128)(2,1)}, bf16[1,512,128]{2,1,0:T(8,1...) custom-call(s32[3]{0:T(128)S(1)} %pad_add_fusion.scalars, ...), custom_call_target="tpu_custom_call", output_to_operand_aliasing={{0}: (14, {}), {1}: (15, {}), {2}: (16, {})} | custom-call | flops 9663676416 | bytes 4194304 | tf_op jit(solution)/shard_map/pallas_call | solution.py:283
  59.5 1.6 %collective-permute-start.19 = (bf16[1,512,128]{2,1,0:T(8,128)(2,1)S(1)}, bf16[1,512,128]{2,1,0:T(8,128)(2,1)S(1)}, u32[]{:S(2)}, u32[]{:S(2)}) collective-permute-start(bf16[1,512,128]{2,1,0:T(8,128)(2,1)S(1)} %get-tuple-element.39), channel_id=1, source_target_pairs={{0,1},{1,0},{2,3},{3,2},{4,5},{5,4},{6,7},{7,6},{8,9},{9,8},{10,11... | collective-permute-start | bytes 393224 | tf_op jit(solution)/shard_map/ppermute | solution.py:28
  61.6 1.6 %collective-permute-start.20 = (bf16[1,512,128]{2,1,0:T(8,128)(2,1)S(1)}, bf16[1,512,128]{2,1,0:T(8,128)(2,1)S(1)}, u32[]{:S(2)}, u32[]{:S(2)}) collective-permute-start(bf16[1,512,128]{2,1,0:T(8,128)(2,1)S(1)} %get-tuple-element.58), channel_id=1, source_target_pairs={{0,1},{1,0},{2,3},{3,2},{4,5},{5,4},{6,7},{7,6},{8,9},{9,8},{10,11... | collective-permute-start | bytes 393224 | tf_op jit(solution)/shard_map/ppermute | solution.py:28
  63.2 16.4 %shard_map.86 = (bf16[2,512,1024]{2,1,0:T(8,128)(2,1)}, bf16[2,512,1024]{2,1,0:T(8,128)(2,1)}, bf16[2,512,512]{2,1,0:T(8,128)(2,1)}, bf16[1,512,128]{2,1,0:T(8,128)(2,1)S(1)}, f32[2,1,1024,128]{3,2,1,0:T(8,128)S(1)}) custom-call(s32[3]{0:T(128)S(1)} %pad_add_fusion.scalars, ...), custom_call_target="tpu_custom_call", output_to_operand_aliasing={{0}: (13, {}), {1}: (14, {}), {2}: (15, {})} | custom-call | flops 9663676416 | bytes 4194304 | tf_op jit(solution)/shard_map/pallas_call | solution.py:283
  81.1 16.5 %shard_map.87 = (bf16[2,512,1024]{2,1,0:T(8,128)(2,1)}, bf16[2,512,1024]{2,1,0:T(8,128)(2,1)}, bf16[2,512,512]{2,1,0:T(8,128)(2,1)}, bf16[1,512,128]{2,1,0:T(8,1...) custom-call(s32[3]{0:T(128)S(1)} %pad_add_fusion.scalars, ...), custom_call_target="tpu_custom_call", output_to_operand_aliasing={{0}: (14, {}), {1}: (15, {}), {2}: (16, {})} | custom-call | flops 9663676416 | bytes 4194304 | tf_op jit(solution)/shard_map/pallas_call | solution.py:283
  97.7 1.9 %collective-permute-done.24 = bf16[2,2,256,256]{3,2,1,0:T(8,128)(2,1)S(1)} collective-permute-done((bf16[2,2,256,256]{3,2,1,0:T(8,128)(2,1)S(1)}, bf16[2,2,256,256]{3,2,1,0:T(8,128)(2,1)S(1)}, u32[]{:S(2)}, u32[]{:S(2)}) %collective-permute-start.24) | collective-permute-done | bytes 524320 | tf_op jit(solution)/shard_map/ppermute | solution.py:28
  99.7 1.3 %collective-permute-start.25 = (bf16[2,256,256]{2,1,0:T(8,128)(2,1)S(1)}, bf16[2,256,256]{2,1,0:T(8,128)(2,1)S(1)}, u32[]{:S(2)}, u32[]{:S(2)}) collective-permute-start(bf16[2,256,256]{2,1,0:T(8,128)(2,1)S(1)} %fusion.3), channel_id=1, source_target_pairs={{0,8},{4,12},{8,0},{12,4},{1,9},{5,13},{9,1},{13,5},{2,10},{6,14},... | collective-permute-start | bytes 786440 | tf_op jit(solution)/shard_map/ppermute | solution.py:28
  101.1 1.6 %collective-permute-start.26 = (bf16[2,256,128]{2,1,0:T(8,128)(2,1)S(1)}, bf16[2,256,128]{2,1,0:T(8,128)(2,1)S(1)}, u32[]{:S(2)}, u32[]{:S(2)}) collective-permute-start(bf16[2,256,128]{2,1,0:T(8,128)(2,1)S(1)} %slice.59), channel_id=1, source_target_pairs={{0,1},{1,0},{2,3},{3,2},{4,5},{5,4},{6,7},{7,6},{8,9},{9,8},{10,11... | collective-permute-start | bytes 393224 | tf_op jit(solution)/shard_map/ppermute | solution.py:28
  103.2 4.9 %collective-permute-done.25 = bf16[2,256,256]{2,1,0:T(8,128)(2,1)S(1)} collective-permute-done((bf16[2,256,256]{2,1,0:T(8,128)(2,1)S(1)}, bf16[2,256,256]{2,1,0:T(8,128)(2,1)S(1)}, u32[]{:S(2)}, u32[]{:S(2)}) %collective-permute-start.25) | collective-permute-done | bytes 262176 | tf_op jit(solution)/shard_map/ppermute | solution.py:28
  108.2 1.6 %collective-permute-start.27 = (bf16[2,256,128]{2,1,0:T(8,128)(2,1)S(1)}, bf16[2,256,128]{2,1,0:T(8,128)(2,1)S(1)}, u32[]{:S(2)}, u32[]{:S(2)}) collective-permute-start(bf16[2,256,128]{2,1,0:T(8,128)(2,1)S(1)} %slice.58), channel_id=1, source_target_pairs={{0,1},{1,0},{2,3},{3,2},{4,5},{5,4},{6,7},{7,6},{8,9},{9,8},{10,11... | collective-permute-start | bytes 393224 | tf_op jit(solution)/shard_map/ppermute | solution.py:28
  110.1 3.2 %collective-permute-done.27 = bf16[2,256,128]{2,1,0:T(8,128)(2,1)S(1)} collective-permute-done((bf16[2,256,128]{2,1,0:T(8,128)(2,1)S(1)}, bf16[2,256,128]{2,1,0:T(8,128)(2,1)S(1)}, u32[]{:S(2)}, u32[]{:S(2)}) %collective-permute-start.27) | collective-permute-done | bytes 131104 | tf_op jit(solution)/shard_map/ppermute | solution.py:28
  (66 shorter events, 10.0 us)
Async XLA Ops:
  2.0 6.6 %collective-permute-start = (bf16[2,256,128]{2,1,0:T(8,128)(2,1)S(1)}, bf16[2,256,128]{2,1,0:T(8,128)(2,1)S(1)}, u32[]{:S(2)}, u32[]{:S(2)}) collective-permute-start(bf16[2,256,128]{2,1,0:T(8,128)(2,1)S(1)} %get-tuple-element.75), channel_id=1, source_target_pairs={{0,1},{1,0},{2,3},{3,2},{4,5},{5,4},{6,7},{7,6},{8,9},{9,8},{10,11... | collective-permute-start | bytes 393224 | tf_op jit(solution)/shard_map/ppermute | solution.py:28
  5.0 5.0 %collective-permute-start.1 = (bf16[2,256,128]{2,1,0:T(8,128)(2,1)S(1)}, bf16[2,256,128]{2,1,0:T(8,128)(2,1)S(1)}, u32[]{:S(2)}, u32[]{:S(2)}) collective-permute-start(bf16[2,256,128]{2,1,0:T(8,128)(2,1)S(1)} %get-tuple-element.74), channel_id=1, source_target_pairs={{0,8},{4,12},{8,0},{12,4},{1,9},{5,13},{9,1},{13,5},{2,10},{6,14},... | collective-permute-start | bytes 393224 | tf_op jit(solution)/shard_map/ppermute | solution.py:28
  11.5 5.0 %collective-permute-start.5 = (bf16[2,256,128]{2,1,0:T(8,128)(2,1)S(1)}, bf16[2,256,128]{2,1,0:T(8,128)(2,1)S(1)}, u32[]{:S(2)}, u32[]{:S(2)}) collective-permute-start(bf16[2,256,128]{2,1,0:T(8,128)(2,1)S(1)} %get-tuple-element.74), channel_id=1, source_target_pairs={{0,4},{4,0},{8,12},{12,8},{1,5},{5,1},{9,13},{13,9},{2,6},{6,2},{1... | collective-permute-start | bytes 393224 | tf_op jit(solution)/shard_map/ppermute | solution.py:28
  12.7 6.0 %collective-permute-start.4 = (bf16[1,512,128]{2,1,0:T(8,128)(2,1)S(1)}, bf16[1,512,128]{2,1,0:T(8,128)(2,1)S(1)}, u32[]{:S(2)}, u32[]{:S(2)}) collective-permute-start(bf16[1,512,128]{2,1,0:T(8,128)(2,1)S(1)} %get-tuple-element.68), channel_id=1, source_target_pairs={{0,1},{1,0},{2,3},{3,2},{4,5},{5,4},{6,7},{7,6},{8,9},{9,8},{10,11... | collective-permute-start | bytes 393224 | tf_op jit(solution)/shard_map/ppermute | solution.py:28
  13.2 5.9 %collective-permute-start.7 = (bf16[2,256,128]{2,1,0:T(8,128)(2,1)S(1)}, bf16[2,256,128]{2,1,0:T(8,128)(2,1)S(1)}, u32[]{:S(2)}, u32[]{:S(2)}) collective-permute-start(bf16[2,256,128]{2,1,0:T(8,128)(2,1)S(1)} %collective-permute-done.refs_8_), channel_id=1, source_target_pairs={{0,4},{4,0},{8,12},{12,8},{1,5},{5,1},{9,13},{13,9},{2,6},{6,2},{1... | collective-permute-start | bytes 393224 | tf_op jit(solution)/shard_map/ppermute | solution.py:28
  15.0 5.7 %collective-permute-start.10 = (bf16[2,256,128]{2,1,0:T(8,128)(2,1)S(1)}, bf16[2,256,128]{2,1,0:T(8,128)(2,1)S(1)}, u32[]{:S(2)}, u32[]{:S(2)}) collective-permute-start(bf16[2,256,128]{2,1,0:T(8,128)(2,1)S(1)} %get-tuple-element.41), channel_id=1, source_target_pairs={{0,8},{4,12},{8,0},{12,4},{1,9},{5,13},{9,1},{13,5},{2,10},{6,14},... | collective-permute-start | bytes 393224 | tf_op jit(solution)/shard_map/ppermute | solution.py:28
  18.6 21.5 %collective-permute-start.3 = (bf16[2,256,128]{2,1,0:T(8,128)(2,1)S(1)}, bf16[2,256,128]{2,1,0:T(8,128)(2,1)S(1)}, u32[]{:S(2)}, u32[]{:S(2)}) collective-permute-start(bf16[2,256,128]{2,1,0:T(8,128)(2,1)S(1)} %get-tuple-element.38), channel_id=1, source_target_pairs={{0,1},{1,0},{2,3},{3,2},{4,5},{5,4},{6,7},{7,6},{8,9},{9,8},{10,11... | collective-permute-start | bytes 393224 | tf_op jit(solution)/shard_map/ppermute | solution.py:28
  19.1 23.3 %collective-permute-start.17 = (bf16[1,512,128]{2,1,0:T(8,128)(2,1)S(1)}, bf16[1,512,128]{2,1,0:T(8,128)(2,1)S(1)}, u32[]{:S(2)}, u32[]{:S(2)}) collective-permute-start(bf16[1,512,128]{2,1,0:T(8,128)(2,1)S(1)} %get-tuple-element.44), channel_id=1, source_target_pairs={{0,1},{1,0},{2,3},{3,2},{4,5},{5,4},{6,7},{7,6},{8,9},{9,8},{10,11... | collective-permute-start | bytes 393224 | tf_op jit(solution)/shard_map/ppermute | solution.py:28
  20.7 21.9 %collective-permute-start.12 = (bf16[2,256,128]{2,1,0:T(8,128)(2,1)S(1)}, bf16[2,256,128]{2,1,0:T(8,128)(2,1)S(1)}, u32[]{:S(2)}, u32[]{:S(2)}) collective-permute-start(bf16[2,256,128]{2,1,0:T(8,128)(2,1)S(1)} %collective-permute-done.10.refs_5_), channel_id=1, source_target_pairs={{0,4},{4,0},{8,12},{12,8},{1,5},{5,1},{9,13},{13,9},{2,6},{6,2},{1... | collective-permute-start | bytes 393224 | tf_op jit(solution)/shard_map/ppermute | solution.py:28
  40.1 21.5 %collective-permute-start.15 = (bf16[2,256,128]{2,1,0:T(8,128)(2,1)S(1)}, bf16[2,256,128]{2,1,0:T(8,128)(2,1)S(1)}, u32[]{:S(2)}, u32[]{:S(2)}) collective-permute-start(bf16[2,256,128]{2,1,0:T(8,128)(2,1)S(1)} %collective-permute-done.3.refs_8_), channel_id=1, source_target_pairs={{0,12},{4,8},{8,4},{12,0},{1,13},{5,9},{9,5},{13,1},{2,14},{6,10},... | collective-permute-start | bytes 393224 | tf_op jit(solution)/shard_map/ppermute | solution.py:28
  41.1 22.1 %collective-permute-start.14 = (bf16[2,256,128]{2,1,0:T(8,128)(2,1)S(1)}, bf16[2,256,128]{2,1,0:T(8,128)(2,1)S(1)}, u32[]{:S(2)}, u32[]{:S(2)}) collective-permute-start(bf16[2,256,128]{2,1,0:T(8,128)(2,1)S(1)} %collective-permute-done.3.refs_8_), channel_id=1, source_target_pairs={{0,4},{4,0},{8,12},{12,8},{1,5},{5,1},{9,13},{13,9},{2,6},{6,2},{1... | collective-permute-start | bytes 393224 | tf_op jit(solution)/shard_map/ppermute | solution.py:28
  41.1 22.1 %collective-permute-start.13 = (bf16[2,256,128]{2,1,0:T(8,128)(2,1)S(1)}, bf16[2,256,128]{2,1,0:T(8,128)(2,1)S(1)}, u32[]{:S(2)}, u32[]{:S(2)}) collective-permute-start(bf16[2,256,128]{2,1,0:T(8,128)(2,1)S(1)} %collective-permute-done.3.refs_8_), channel_id=1, source_target_pairs={{0,8},{4,12},{8,0},{12,4},{1,9},{5,13},{9,1},{13,5},{2,10},{6,14},... | collective-permute-start | bytes 393224 | tf_op jit(solution)/shard_map/ppermute | solution.py:28
  42.3 17.1 %collective-permute-start.11 = (bf16[2,256,128]{2,1,0:T(8,128)(2,1)S(1)}, bf16[2,256,128]{2,1,0:T(8,128)(2,1)S(1)}, u32[]{:S(2)}, u32[]{:S(2)}) collective-permute-start(bf16[2,256,128]{2,1,0:T(8,128)(2,1)S(1)} %get-tuple-element.41), channel_id=1, source_target_pairs={{0,4},{4,0},{8,12},{12,8},{1,5},{5,1},{9,13},{13,9},{2,6},{6,2},{1... | collective-permute-start | bytes 393224 | tf_op jit(solution)/shard_map/ppermute | solution.py:28
  42.6 18.6 %collective-permute-start.16 = (bf16[1,512,128]{2,1,0:T(8,128)(2,1)S(1)}, bf16[1,512,128]{2,1,0:T(8,128)(2,1)S(1)}, u32[]{:S(2)}, u32[]{:S(2)}) collective-permute-start(bf16[1,512,128]{2,1,0:T(8,128)(2,1)S(1)} %get-tuple-element.43), channel_id=1, source_target_pairs={{0,1},{1,0},{2,3},{3,2},{4,5},{5,4},{6,7},{7,6},{8,9},{9,8},{10,11... | collective-permute-start | bytes 393224 | tf_op jit(solution)/shard_map/ppermute | solution.py:28
  59.5 21.6 %collective-permute-start.19 = (bf16[1,512,128]{2,1,0:T(8,128)(2,1)S(1)}, bf16[1,512,128]{2,1,0:T(8,128)(2,1)S(1)}, u32[]{:S(2)}, u32[]{:S(2)}) collective-permute-start(bf16[1,512,128]{2,1,0:T(8,128)(2,1)S(1)} %get-tuple-element.39), channel_id=1, source_target_pairs={{0,1},{1,0},{2,3},{3,2},{4,5},{5,4},{6,7},{7,6},{8,9},{9,8},{10,11... | collective-permute-start | bytes 393224 | tf_op jit(solution)/shard_map/ppermute | solution.py:28
  61.1 19.9 %collective-permute-start.9 = (bf16[1,512,128]{2,1,0:T(8,128)(2,1)S(1)}, bf16[1,512,128]{2,1,0:T(8,128)(2,1)S(1)}, u32[]{:S(2)}, u32[]{:S(2)}) collective-permute-start(bf16[1,512,128]{2,1,0:T(8,128)(2,1)S(1)} %get-tuple-element.40), channel_id=1, source_target_pairs={{0,1},{1,0},{2,3},{3,2},{4,5},{5,4},{6,7},{7,6},{8,9},{9,8},{10,11... | collective-permute-start | bytes 393224 | tf_op jit(solution)/shard_map/ppermute | solution.py:28
  61.6 19.5 %collective-permute-start.20 = (bf16[1,512,128]{2,1,0:T(8,128)(2,1)S(1)}, bf16[1,512,128]{2,1,0:T(8,128)(2,1)S(1)}, u32[]{:S(2)}, u32[]{:S(2)}) collective-permute-start(bf16[1,512,128]{2,1,0:T(8,128)(2,1)S(1)} %get-tuple-element.58), channel_id=1, source_target_pairs={{0,1},{1,0},{2,3},{3,2},{4,5},{5,4},{6,7},{7,6},{8,9},{9,8},{10,11... | collective-permute-start | bytes 393224 | tf_op jit(solution)/shard_map/ppermute | solution.py:28
  63.2 16.9 %collective-permute-start.18 = (bf16[2,2,256,256]{3,2,1,0:T(8,128)(2,1)S(1)}, bf16[2,2,256,256]{3,2,1,0:T(8,128)(2,1)S(1)}, u32[]{:S(2)}, u32[]{:S(2)}) collective-permute-start(bf16[2,2,256,256]{3,2,1,0:T(8,128)(2,1)S(1)} %get-tuple-element.57), channel_id=1, source_target_pairs={{0,4},{4,0},{8,12},{12,8},{1,5},{5,1},{9,13},{13,9},{2,6},{6,2},{1... | collective-permute-start | bytes 1572872 | tf_op jit(solution)/shard_map/ppermute | solution.py:28
  79.6 18.0 %collective-permute-start.21 = (bf16[1,512,128]{2,1,0:T(8,128)(2,1)S(1)}, bf16[1,512,128]{2,1,0:T(8,128)(2,1)S(1)}, u32[]{:S(2)}, u32[]{:S(2)}) collective-permute-start(bf16[1,512,128]{2,1,0:T(8,128)(2,1)S(1)} %get-tuple-element.62), channel_id=1, source_target_pairs={{0,1},{1,0},{2,3},{3,2},{4,5},{5,4},{6,7},{7,6},{8,9},{9,8},{10,11... | collective-permute-start | bytes 393224 | tf_op jit(solution)/shard_map/ppermute | solution.py:28
  80.2 17.4 %collective-permute-start.22 = (bf16[2,256,256]{2,1,0:T(8,128)(2,1)S(1)}, bf16[2,256,256]{2,1,0:T(8,128)(2,1)S(1)}, u32[]{:S(2)}, u32[]{:S(2)}) collective-permute-start(bf16[2,256,256]{2,1,0:T(8,128)(2,1)S(1)} %fusion.2.refs_16_), channel_id=1, source_target_pairs={{0,8},{4,12},{8,0},{12,4},{1,9},{5,13},{9,1},{13,5},{2,10},{6,14},... | collective-permute-start | bytes 786440 | tf_op jit(solution)/shard_map/ppermute | solution.py:28
  99.7 8.4 %collective-permute-start.25 = (bf16[2,256,256]{2,1,0:T(8,128)(2,1)S(1)}, bf16[2,256,256]{2,1,0:T(8,128)(2,1)S(1)}, u32[]{:S(2)}, u32[]{:S(2)}) collective-permute-start(bf16[2,256,256]{2,1,0:T(8,128)(2,1)S(1)} %fusion.3), channel_id=1, source_target_pairs={{0,8},{4,12},{8,0},{12,4},{1,9},{5,13},{9,1},{13,5},{2,10},{6,14},... | collective-permute-start | bytes 786440 | tf_op jit(solution)/shard_map/ppermute | solution.py:28
  101.1 9.0 %collective-permute-start.26 = (bf16[2,256,128]{2,1,0:T(8,128)(2,1)S(1)}, bf16[2,256,128]{2,1,0:T(8,128)(2,1)S(1)}, u32[]{:S(2)}, u32[]{:S(2)}) collective-permute-start(bf16[2,256,128]{2,1,0:T(8,128)(2,1)S(1)} %slice.59), channel_id=1, source_target_pairs={{0,1},{1,0},{2,3},{3,2},{4,5},{5,4},{6,7},{7,6},{8,9},{9,8},{10,11... | collective-permute-start | bytes 393224 | tf_op jit(solution)/shard_map/ppermute | solution.py:28
  102.8 7.1 %collective-permute-start.23 = (bf16[1,512,128]{2,1,0:T(8,128)(2,1)S(1)}, bf16[1,512,128]{2,1,0:T(8,128)(2,1)S(1)}, u32[]{:S(2)}, u32[]{:S(2)}) collective-permute-start(bf16[1,512,128]{2,1,0:T(8,128)(2,1)S(1)} %get-tuple-element.65), channel_id=1, source_target_pairs={{0,1},{1,0},{2,3},{3,2},{4,5},{5,4},{6,7},{7,6},{8,9},{9,8},{10,11... | collective-permute-start | bytes 393224 | tf_op jit(solution)/shard_map/ppermute | solution.py:28
  108.2 5.0 %collective-permute-start.27 = (bf16[2,256,128]{2,1,0:T(8,128)(2,1)S(1)}, bf16[2,256,128]{2,1,0:T(8,128)(2,1)S(1)}, u32[]{:S(2)}, u32[]{:S(2)}) collective-permute-start(bf16[2,256,128]{2,1,0:T(8,128)(2,1)S(1)} %slice.58), channel_id=1, source_target_pairs={{0,1},{1,0},{2,3},{3,2},{4,5},{5,4},{6,7},{7,6},{8,9},{9,8},{10,11... | collective-permute-start | bytes 393224 | tf_op jit(solution)/shard_map/ppermute | solution.py:28
  (11 other events, 89.7 us)

commit v4 on v3

--- a/solution.py
+++ b/solution.py
@@ -13,6 +13,7 @@
 P_SIZE = 2
 GROUP = H // KVH
 BLOCK = 256
+CHUNK = 512
 MASKED = -1e30
 SCALE = HD ** (-0.5)
 
@@ -40,7 +41,7 @@
     final = turn == n_resp - 1
     n_out = 4 + (1 if not final or pieces == n_keep else 2)
     grads = rest[4:n_out]
-    k_all, v_all, k_t, v_t, weights, probs, dscores, q_scaled, do_scaled, acc_k, acc_v = rest[n_out:]
+    k_all, v_all, k_t, v_t, weights, probs, dscores, acc_k, acc_v = rest[n_out:]
 
     head = pl.program_id(0)
     even = scalars[n_resp] == 0
@@ -48,7 +49,6 @@
     n_query = q_ref.shape[1]
     n_blocks = n_query // BLOCK
     n_first = n_prompt // BLOCK
-    n_all = n_first + n_blocks
 
     def gather(dst, piece_refs, resp_ref):
         for i, ref in enumerate(piece_refs):
@@ -79,69 +79,55 @@
     def stages(i):
         st = {}
         t = span(i)
-        n_chunks = n_first + i + 1
-        seen = n_chunks * BLOCK
+        seen = n_prompt + (i + 1) * BLOCK
+        parts = [slice(u, min(u + CHUNK, seen)) for u in range(0, seen, CHUNK)]
+        n_parts = len(parts)
         q = q_ref[0, t, :]
         do = do_ref[0, t, :]
 
         def score(c):
-            s = dot(k_all[span(c), :], q, NT)
-            if c == n_chunks - 1:
+            s = dot(k_all[parts[c], :], q, NT)
+            if c == n_parts - 1:
                 row = lax.broadcasted_iota(jnp.int32, (BLOCK, BLOCK), 0)
                 col = lax.broadcasted_iota(jnp.int32, (BLOCK, BLOCK), 1)
-                s = jnp.where(row <= col, s, MASKED)
-            weights[span(c), t] = s
+                diag = jnp.where(row <= col, s[-BLOCK:], MASKED)
+                s = diag if s.shape[0] == BLOCK else jnp.concatenate([s[:-BLOCK], diag], axis=0)
+            weights[parts[c], t] = s
             top = fold(s, jnp.max)
             st["top"] = top if c == 0 else jnp.maximum(st["top"], top)
-            if c == n_chunks - 1:
+            if c == n_parts - 1:
                 st["top"] = jnp.max(st["top"], axis=0, keepdims=True) * SCALE
 
         def weigh(c):
-            w = jnp.exp(weights[span(c), t] * SCALE - st["top"])
-            weights[span(c), t] = w
-            probs[span(c), t] = w.astype(jnp.bfloat16)
+            w = jnp.exp(weights[parts[c], t] * SCALE - st["top"])
+            weights[parts[c], t] = w
             total = fold(w, jnp.sum)
             st["sum"] = total if c == 0 else st["sum"] + total
-
-        def output(c):
-            if c > 0:
-                return
-            st["inv"] = 1.0 / jnp.sum(st["sum"], axis=0, keepdims=True)
-            o = dot(v_t[:, :seen], probs[:seen, t], NN) * st["inv"]
-            do_t = do.astype(jnp.float32).T
-            st["delta"] = jnp.sum(o * do_t, axis=0, keepdims=True)
-            out_ref[0, t, :] = o.T.astype(jnp.bfloat16)
-            inv_rows = jnp.broadcast_to(st["inv"], (HD, BLOCK)).T
-            do_scaled[t, :] = (do.astype(jnp.float32) * inv_rows).astype(jnp.bfloat16)
-            q_scaled[t, :] = (q.astype(jnp.float32) * (inv_rows * SCALE)).astype(jnp.bfloat16)
+            if c == n_parts - 1:
+                st["inv"] = 1.0 / jnp.sum(st["sum"], axis=0, keepdims=True)
+
+        def norm(c):
+            probs[parts[c], t] = (weights[parts[c], t] * st["inv"]).astype(jnp.bfloat16)
+            if c == n_parts - 1:
+                o = dot(v_t[:, :seen], probs[:seen, t], NN)
+                out_ref[0, t, :] = o.T.astype(jnp.bfloat16)
+                do_t = do.astype(jnp.float32).T
+                st["delta"] = jnp.sum(o * do_t, axis=0, keepdims=True)
+                st["inv"] = st["inv"] * SCALE
 
         def grad(c):
-            dp = dot(v_all[span(c), :], do, NT)
-            ds = weights[span(c), t] * (dp - st["delta"])
-            dscores[span(c), t] = ds.astype(jnp.bfloat16)
-
-        def query(c):
-            if c > 0:
-                return
-            dq = dot(k_t[:, :seen], dscores[:seen, t], NN) * (st["inv"] * SCALE)
-            dq_ref[0, t, :] = dq.T.astype(jnp.bfloat16)
-
-        return [[functools.partial(f, c) for c in range(n_chunks)] for f in (score, weigh, output, grad, query)]
-
-    def add_values(c):
-        t0 = max(c - n_first, 0) * BLOCK
-        acc_v[span(c), :] += dot(probs[span(c), t0:], do_scaled[t0:, :], NN)
-
-    def add_keys(c):
-        t0 = max(c - n_first, 0) * BLOCK
-        acc_k[span(c), :] += dot(dscores[span(c), t0:], q_scaled[t0:, :], NN)
+            dp = dot(v_all[parts[c], :], do, NT)
+            ds = (weights[parts[c], t] * st["inv"]) * (dp - st["delta"])
+            dscores[parts[c], t] = ds.astype(jnp.bfloat16)
+            if c == n_parts - 1:
+                dq = dot(k_t[:, :seen], dscores[:seen, t], NN)
+                dq_ref[0, t, :] = dq.T.astype(jnp.bfloat16)
+
+        return [[functools.partial(f, c) for c in range(n_parts)] for f in (score, weigh, norm, grad)]
 
     plan = [stages(i) for i in range(n_blocks)]
-    former = [[functools.partial(add_values, c) for c in range(n_all)]]
-    former += [[functools.partial(add_keys, c) for c in range(n_all)]]
-    for slot in range(5 + n_blocks - 1):
-        groups = [former[slot]] if slot < 2 else []
-        groups += [plan[i][slot - i] for i in reversed(range(n_blocks)) if 0 <= slot - i < 5]
+    for slot in range(4 + n_blocks - 1):
+        groups = [plan[i][slot - i] for i in reversed(range(n_blocks)) if 0 <= slot - i < 4]
         for c in range(max(len(g) for g in groups)):
             for g in groups:
                 if c < len(g):
@@ -152,13 +138,15 @@
         acc_k[...] = jnp.zeros_like(acc_k)
         acc_v[...] = jnp.zeros_like(acc_v)
 
+    q_all = q_ref[0]
+    do_all = do_ref[0]
+    bounds = [(slice(u, min(u + CHUNK, n_prompt)), 0) for u in range(0, n_prompt, CHUNK)]
+    bounds += [(span(n_first + i), i * BLOCK) for i in range(n_blocks)]
+    for u, t0 in bounds:
+        acc_v[u, :] += dot(probs[u, t0:], do_all[t0:], NN)
+        acc_k[u, :] += dot(dscores[u, t0:], q_all[t0:], NN)
+
     last = head == heads - 1
-
-    @pl.when(last)
-    def _():
-        for c in range(n_all):
-            add_values(c)
-            add_keys(c)
 
     def respond(ref, acc):
         ref[0] = acc[n_prompt:, :].astype(jnp.bfloat16)
@@ -274,8 +262,6 @@
         pltpu.VMEM((n_keys, n_query), jnp.float32),
         pltpu.VMEM((n_keys, n_query), jnp.bfloat16),
         pltpu.VMEM((n_keys, n_query), jnp.bfloat16),
-        pltpu.VMEM((n_query, HD), jnp.bfloat16),
-        pltpu.VMEM((n_query, HD), jnp.bfloat16),
         pltpu.VMEM((n_keys, HD), jnp.float32),
         pltpu.VMEM((n_keys, HD), jnp.float32),
     ]
@@ -291,7 +277,7 @@
         ),
         out_shape=out_shape,
         input_output_aliases=aliases,
-        compiler_params=pltpu.CompilerParams(vmem_limit_bytes=40 * 2**20),
+        compiler_params=pltpu.CompilerParams(vmem_limit_bytes=60 * 2**20),
         cost_estimate=pl.CostEstimate(flops=2 * flops, bytes_accessed=4 * 2**20, transcendentals=0),
     )(scalars, *args)
 

time: 115 us -> 122 us (1.061)
  Pallas kernels: 65.6 us -> 71.4 us
  other arithmetic: 1.76 us -> 3.59 us
    pallas_call x4, Pallas kernels: 65.6 us -> 71.4 us  [attend(): pl.pallas_call(functools.partial(attend_kernel, (pieces, rows, n_keep, he...]
    add x2, other arithmetic: 0.24 us -> 1.49 us  [whole_heads(): sums = keep + core(send).astype(jnp.float32)]
    unnamed x14 -> x58, local copies, waits for them, and re-layouts: 3.2 us -> 2.69 us
  transfers between devices with their start and end apart: 28 -> 28, of which waited for: 7 -> 7; matrix products, arithmetic and copies ran while one was open for 1% -> 2% of each run, Pallas kernels for 57% -> 59%
where the time goes in v4:
time: 122 us; the launch traced here: 121 us
  Pallas kernels  71.4 us (59%)
  starting transfers between devices  23.9 us (20%)
  waiting for transfers between devices  16.3 us (13%)
  local copies, waits for them, and re-layouts  5.12 us (4%)
  other arithmetic  3.59 us (3%)
    pallas_call x4, Pallas kernels, attend(): pl.pallas_call(functools.partial(attend_kernel, (pieces, rows, n_keep, he...  71.4 us
    ppermute x28, starting transfers between devices, swap(): lax.ppermute(block, axis, [(i, i ^ step) for i in range(lax.axis_size(axi...  23.9 us
    ppermute x28, waiting for transfers between devices, swap(): lax.ppermute(block, axis, [(i, i ^ step) for i in range(lax.axis_size(axi...  16.3 us
    unnamed x58, local copies, waits for them, and re-layouts  2.69 us
  transfers between devices with their start and end apart: 28, of which 7 were waited for; matrix products, arithmetic and copies ran while one was open for 2% of the time, Pallas kernels for 59%

profile of v4, /device:TPU:0, one launch (start us, length us, event | category | flops | bytes accessed | tf_op | source)
XLA Modules:
  0.0 121.4 jit_solution(10454142827508236770)
XLA Ops:
  0.7 1.2 constant_dynamic-slice_fusion.3
  1.8 3.1 %collective-permute-start = (bf16[2,256,128]{2,1,0:T(8,128)(2,1)S(1)}, bf16[2,256,128]{2,1,0:T(8,128)(2,1)S(1)}, u32[]{:S(2)}, u32[]{:S(2)}) collective-permute-start(bf16[2,256,128]{2,1,0:T(8,128)(2,1)S(1)} %get-tuple-element.75), channel_id=1, source_target_pairs={{0,1},{1,0},{2,3},{3,2},{4,5},{5,4},{6,7},{7,6},{8,9},{9,8},{10,11... | collective-permute-start | bytes 393224 | tf_op jit(solution)/shard_map/ppermute | solution.py:29
  4.9 1.5 %collective-permute-start.1 = (bf16[2,256,128]{2,1,0:T(8,128)(2,1)S(1)}, bf16[2,256,128]{2,1,0:T(8,128)(2,1)S(1)}, u32[]{:S(2)}, u32[]{:S(2)}) collective-permute-start(bf16[2,256,128]{2,1,0:T(8,128)(2,1)S(1)} %get-tuple-element.74), channel_id=1, source_target_pairs={{0,8},{4,12},{8,0},{12,4},{1,9},{5,13},{9,1},{13,5},{2,10},{6,14},... | collective-permute-start | bytes 393224 | tf_op jit(solution)/shard_map/ppermute | solution.py:29
  6.4 2.0 %collective-permute-done.refs_8_ = bf16[2,256,128]{2,1,0:T(8,128)(2,1)S(1)} collective-permute-done((bf16[2,256,128]{2,1,0:T(8,128)(2,1)S(1)}, bf16[2,256,128]{2,1,0:T(8,128)(2,1)S(1)}, u32[]{:S(2)}, u32[]{:S(2)}) %collective-permute-start) | collective-permute-done | bytes 131104 | tf_op jit(solution)/shard_map/ppermute | solution.py:29
  8.4 1.5 %collective-permute-done.1.refs_5_ = bf16[2,256,128]{2,1,0:T(8,128)(2,1)S(1)} collective-permute-done((bf16[2,256,128]{2,1,0:T(8,128)(2,1)S(1)}, bf16[2,256,128]{2,1,0:T(8,128)(2,1)S(1)}, u32[]{:S(2)}, u32[]{:S(2)}) %collective-permute-start.1) | collective-permute-done | bytes 131104 | tf_op jit(solution)/shard_map/ppermute | solution.py:29
  9.9 1.5 %collective-permute-start.2 = (bf16[2,256,128]{2,1,0:T(8,128)(2,1)S(1)}, bf16[2,256,128]{2,1,0:T(8,128)(2,1)S(1)}, u32[]{:S(2)}, u32[]{:S(2)}) collective-permute-start(bf16[2,256,128]{2,1,0:T(8,128)(2,1)S(1)} %collective-permute-done.refs_8_), channel_id=1, source_target_pairs={{0,8},{4,12},{8,0},{12,4},{1,9},{5,13},{9,1},{13,5},{2,10},{6,14},... | collective-permute-start | bytes 393224 | tf_op jit(solution)/shard_map/ppermute | solution.py:29
  11.4 1.1 constant_dynamic-slice_fusion
  13.3 1.6 %collective-permute-done.2.refs_9_ = bf16[2,256,128]{2,1,0:T(8,128)(2,1)S(1)} collective-permute-done((bf16[2,256,128]{2,1,0:T(8,128)(2,1)S(1)}, bf16[2,256,128]{2,1,0:T(8,128)(2,1)S(1)}, u32[]{:S(2)}, u32[]{:S(2)}) %collective-permute-start.2) | collective-permute-done | bytes 131104 | tf_op jit(solution)/shard_map/ppermute | solution.py:29
  14.9 1.5 %collective-permute-start.10 = (bf16[2,256,128]{2,1,0:T(8,128)(2,1)S(1)}, bf16[2,256,128]{2,1,0:T(8,128)(2,1)S(1)}, u32[]{:S(2)}, u32[]{:S(2)}) collective-permute-start(bf16[2,256,128]{2,1,0:T(8,128)(2,1)S(1)} %get-tuple-element.41), channel_id=1, source_target_pairs={{0,8},{4,12},{8,0},{12,4},{1,9},{5,13},{9,1},{13,5},{2,10},{6,14},... | collective-permute-start | bytes 393224 | tf_op jit(solution)/shard_map/ppermute | solution.py:29
  19.0 1.6 %collective-permute-start.17 = (bf16[1,512,128]{2,1,0:T(8,128)(2,1)S(1)}, bf16[1,512,128]{2,1,0:T(8,128)(2,1)S(1)}, u32[]{:S(2)}, u32[]{:S(2)}) collective-permute-start(bf16[1,512,128]{2,1,0:T(8,128)(2,1)S(1)} %get-tuple-element.44), channel_id=1, source_target_pairs={{0,1},{1,0},{2,3},{3,2},{4,5},{5,4},{6,7},{7,6},{8,9},{9,8},{10,11... | collective-permute-start | bytes 393224 | tf_op jit(solution)/shard_map/ppermute | solution.py:29
  21.9 17.3 %shard_map.84 = (bf16[2,512,1024]{2,1,0:T(8,128)(2,1)}, bf16[2,512,1024]{2,1,0:T(8,128)(2,1)}, bf16[2,512,512]{2,1,0:T(8,128)(2,1)}, bf16[1,512,128]{2,1,0:T(8,128)(2,1)}, f32[2,1,1024,128]{3,2,1,0:T(8,128)}) custom-call(s32[3]{0:T(128)} %pad_add_fusion.scalars, bf16[2,512,1024]{2,1,0:T(8,128)(2,1)} %refs_0_.7, bf16[2,512,1024]{2,1,0:T(8,128)(2,1)} %refs_1_.7, ...), custom_call_target="tpu_custom_call" | custom-call | flops 9663676416 | bytes 4194304 | tf_op jit(solution)/shard_map/pallas_call | solution.py:269
  40.2 1.2 %collective-permute-start.13 = (bf16[2,256,128]{2,1,0:T(8,128)(2,1)S(1)}, bf16[2,256,128]{2,1,0:T(8,128)(2,1)S(1)}, u32[]{:S(2)}, u32[]{:S(2)}) collective-permute-start(bf16[2,256,128]{2,1,0:T(8,128)(2,1)S(1)} %collective-permute-done.3.refs_8_), channel_id=1, source_target_pairs={{0,8},{4,12},{8,0},{12,4},{1,9},{5,13},{9,1},{13,5},{2,10},{6,14},... | collective-permute-start | bytes 393224 | tf_op jit(solution)/shard_map/ppermute | solution.py:29
  42.1 18.3 %shard_map.85 = (bf16[2,512,1024]{2,1,0:T(8,128)(2,1)}, bf16[2,512,1024]{2,1,0:T(8,128)(2,1)}, bf16[2,512,512]{2,1,0:T(8,128)(2,1)}, bf16[1,512,128]{2,1,0:T(8,1...) custom-call(s32[3]{0:T(128)} %pad_add_fusion.scalars, ...), custom_call_target="tpu_custom_call", output_to_operand_aliasing={{0}: (14, {}), {1}: (15, {}), {2}: (16, {})} | custom-call | flops 9663676416 | bytes 4194304 | tf_op jit(solution)/shard_map/pallas_call | solution.py:269
  60.5 1.6 %collective-permute-start.19 = (bf16[1,512,128]{2,1,0:T(8,128)(2,1)S(1)}, bf16[1,512,128]{2,1,0:T(8,128)(2,1)S(1)}, u32[]{:S(2)}, u32[]{:S(2)}) collective-permute-start(bf16[1,512,128]{2,1,0:T(8,128)(2,1)S(1)} %copy-done.15), channel_id=1, source_target_pairs={{0,1},{1,0},{2,3},{3,2},{4,5},{5,4},{6,7},{7,6},{8,9},{9,8},{10,11... | collective-permute-start | bytes 393224 | tf_op jit(solution)/shard_map/ppermute | solution.py:29
  62.6 1.6 %collective-permute-start.20 = (bf16[1,512,128]{2,1,0:T(8,128)(2,1)}, bf16[1,512,128]{2,1,0:T(8,128)(2,1)S(1)}, u32[]{:S(2)}, u32[]{:S(2)}) collective-permute-start(bf16[1,512,128]{2,1,0:T(8,128)(2,1)} %get-tuple-element.58), channel_id=1, source_target_pairs={{0,1},{1,0},{2,3},{3,2},{4,5},{5,4},{6,7},{7,6},{8,9},{9,8},{10,11... | collective-permute-start | bytes 393224 | tf_op jit(solution)/shard_map/ppermute | solution.py:29
  64.8 17.6 %shard_map.86 = (bf16[2,512,1024]{2,1,0:T(8,128)(2,1)}, bf16[2,512,1024]{2,1,0:T(8,128)(2,1)}, bf16[2,512,512]{2,1,0:T(8,128)(2,1)}, bf16[1,512,128]{2,1,0:T(8,128)(2,1)}, f32[2,1,1024,128]{3,2,1,0:T(8,128)}) custom-call(s32[3]{0:T(128)} %pad_add_fusion.scalars, ...), custom_call_target="tpu_custom_call", output_to_operand_aliasing={{0}: (13, {}), {1}: (14, {}), {2}: (15, {})} | custom-call | flops 9663676416 | bytes 4194304 | tf_op jit(solution)/shard_map/pallas_call | solution.py:269
  84.8 18.2 %shard_map.87 = (bf16[2,512,1024]{2,1,0:T(8,128)(2,1)}, bf16[2,512,1024]{2,1,0:T(8,128)(2,1)}, bf16[2,512,512]{2,1,0:T(8,128)(2,1)}, bf16[1,512,128]{2,1,0:T(8,1...) custom-call(s32[3]{0:T(128)} %pad_add_fusion.scalars, ...), custom_call_target="tpu_custom_call", output_to_operand_aliasing={{0}: (14, {}), {1}: (15, {}), {2}: (16, {})} | custom-call | flops 9663676416 | bytes 4194304 | tf_op jit(solution)/shard_map/pallas_call | solution.py:269
  103.1 2.1 %collective-permute-done.24 = bf16[2,2,256,256]{3,2,1,0:T(8,128)(2,1)S(1)} collective-permute-done((bf16[2,2,256,256]{3,2,1,0:T(8,128)(2,1)}, bf16[2,2,256,256]{3,2,1,0:T(8,128)(2,1)S(1)}, u32[]{:S(2)}, u32[]{:S(2)}) %collective-permute-start.24) | collective-permute-done | bytes 524320 | tf_op jit(solution)/shard_map/ppermute | solution.py:29
  105.2 1.4 %convert_add_fusion = f32[2,2,256,256]{3,2,1,0:T(8,128)S(1)} fusion(f32[2,2,256,256]{3,2,1,0:T(8,128)} %get-tuple-element.66, bf16[2,2,256,256]{3,2,1,0:T(8,128)(2,1)S(1)} %collective-permute-done.24), kind=kLoop, calls=%fused_computation.1 | loop fusion | flops 524288 | bytes 2621440 | tf_op jit(solution)/shard_map/add | solution.py:371
  106.6 1.3 %collective-permute-start.25 = (bf16[2,256,256]{2,1,0:T(8,128)(2,1)S(1)}, bf16[2,256,256]{2,1,0:T(8,128)(2,1)S(1)}, u32[]{:S(2)}, u32[]{:S(2)}) collective-permute-start(bf16[2,256,256]{2,1,0:T(8,128)(2,1)S(1)} %fusion.3), channel_id=1, source_target_pairs={{0,8},{4,12},{8,0},{12,4},{1,9},{5,13},{9,1},{13,5},{2,10},{6,14},... | collective-permute-start | bytes 786440 | tf_op jit(solution)/shard_map/ppermute | solution.py:29
  108.0 1.6 %collective-permute-start.26 = (bf16[2,256,128]{2,1,0:T(8,128)(2,1)S(1)}, bf16[2,256,128]{2,1,0:T(8,128)(2,1)S(1)}, u32[]{:S(2)}, u32[]{:S(2)}) collective-permute-start(bf16[2,256,128]{2,1,0:T(8,128)(2,1)S(1)} %slice.59), channel_id=1, source_target_pairs={{0,1},{1,0},{2,3},{3,2},{4,5},{5,4},{6,7},{7,6},{8,9},{9,8},{10,11... | collective-permute-start | bytes 393224 | tf_op jit(solution)/shard_map/ppermute | solution.py:29
  110.1 4.9 %collective-permute-done.25 = bf16[2,256,256]{2,1,0:T(8,128)(2,1)S(1)} collective-permute-done((bf16[2,256,256]{2,1,0:T(8,128)(2,1)S(1)}, bf16[2,256,256]{2,1,0:T(8,128)(2,1)S(1)}, u32[]{:S(2)}, u32[]{:S(2)}) %collective-permute-start.25) | collective-permute-done | bytes 262176 | tf_op jit(solution)/shard_map/ppermute | solution.py:29
  115.1 1.6 %collective-permute-start.27 = (bf16[2,256,128]{2,1,0:T(8,128)(2,1)S(1)}, bf16[2,256,128]{2,1,0:T(8,128)(2,1)S(1)}, u32[]{:S(2)}, u32[]{:S(2)}) collective-permute-start(bf16[2,256,128]{2,1,0:T(8,128)(2,1)S(1)} %slice.58), channel_id=1, source_target_pairs={{0,1},{1,0},{2,3},{3,2},{4,5},{5,4},{6,7},{7,6},{8,9},{9,8},{10,11... | collective-permute-start | bytes 393224 | tf_op jit(solution)/shard_map/ppermute | solution.py:29
  117.0 3.2 %collective-permute-done.27 = bf16[2,256,128]{2,1,0:T(8,128)(2,1)S(1)} collective-permute-done((bf16[2,256,128]{2,1,0:T(8,128)(2,1)S(1)}, bf16[2,256,128]{2,1,0:T(8,128)(2,1)S(1)}, u32[]{:S(2)}, u32[]{:S(2)}) %collective-permute-start.27) | collective-permute-done | bytes 131104 | tf_op jit(solution)/shard_map/ppermute | solution.py:29
  (110 shorter events, 11.8 us)
Async XLA Ops:
  1.8 6.6 %collective-permute-start = (bf16[2,256,128]{2,1,0:T(8,128)(2,1)S(1)}, bf16[2,256,128]{2,1,0:T(8,128)(2,1)S(1)}, u32[]{:S(2)}, u32[]{:S(2)}) collective-permute-start(bf16[2,256,128]{2,1,0:T(8,128)(2,1)S(1)} %get-tuple-element.75), channel_id=1, source_target_pairs={{0,1},{1,0},{2,3},{3,2},{4,5},{5,4},{6,7},{7,6},{8,9},{9,8},{10,11... | collective-permute-start | bytes 393224 | tf_op jit(solution)/shard_map/ppermute | solution.py:29
  9.9 5.0 %collective-permute-start.2 = (bf16[2,256,128]{2,1,0:T(8,128)(2,1)S(1)}, bf16[2,256,128]{2,1,0:T(8,128)(2,1)S(1)}, u32[]{:S(2)}, u32[]{:S(2)}) collective-permute-start(bf16[2,256,128]{2,1,0:T(8,128)(2,1)S(1)} %collective-permute-done.refs_8_), channel_id=1, source_target_pairs={{0,8},{4,12},{8,0},{12,4},{1,9},{5,13},{9,1},{13,5},{2,10},{6,14},... | collective-permute-start | bytes 393224 | tf_op jit(solution)/shard_map/ppermute | solution.py:29
  11.4 5.0 %collective-permute-start.5 = (bf16[2,256,128]{2,1,0:T(8,128)(2,1)S(1)}, bf16[2,256,128]{2,1,0:T(8,128)(2,1)S(1)}, u32[]{:S(2)}, u32[]{:S(2)}) collective-permute-start(bf16[2,256,128]{2,1,0:T(8,128)(2,1)S(1)} %get-tuple-element.74), channel_id=1, source_target_pairs={{0,4},{4,0},{8,12},{12,8},{1,5},{5,1},{9,13},{13,9},{2,6},{6,2},{1... | collective-permute-start | bytes 393224 | tf_op jit(solution)/shard_map/ppermute | solution.py:29
  12.5 6.0 %collective-permute-start.4 = (bf16[1,512,128]{2,1,0:T(8,128)(2,1)S(1)}, bf16[1,512,128]{2,1,0:T(8,128)(2,1)S(1)}, u32[]{:S(2)}, u32[]{:S(2)}) collective-permute-start(bf16[1,512,128]{2,1,0:T(8,128)(2,1)S(1)} %get-tuple-element.68), channel_id=1, source_target_pairs={{0,1},{1,0},{2,3},{3,2},{4,5},{5,4},{6,7},{7,6},{8,9},{9,8},{10,11... | collective-permute-start | bytes 393224 | tf_op jit(solution)/shard_map/ppermute | solution.py:29
  13.0 5.9 %collective-permute-start.7 = (bf16[2,256,128]{2,1,0:T(8,128)(2,1)S(1)}, bf16[2,256,128]{2,1,0:T(8,128)(2,1)S(1)}, u32[]{:S(2)}, u32[]{:S(2)}) collective-permute-start(bf16[2,256,128]{2,1,0:T(8,128)(2,1)S(1)} %collective-permute-done.refs_8_), channel_id=1, source_target_pairs={{0,4},{4,0},{8,12},{12,8},{1,5},{5,1},{9,13},{13,9},{2,6},{6,2},{1... | collective-permute-start | bytes 393224 | tf_op jit(solution)/shard_map/ppermute | solution.py:29
  14.9 5.7 %collective-permute-start.10 = (bf16[2,256,128]{2,1,0:T(8,128)(2,1)S(1)}, bf16[2,256,128]{2,1,0:T(8,128)(2,1)S(1)}, u32[]{:S(2)}, u32[]{:S(2)}) collective-permute-start(bf16[2,256,128]{2,1,0:T(8,128)(2,1)S(1)} %get-tuple-element.41), channel_id=1, source_target_pairs={{0,8},{4,12},{8,0},{12,4},{1,9},{5,13},{9,1},{13,5},{2,10},{6,14},... | collective-permute-start | bytes 393224 | tf_op jit(solution)/shard_map/ppermute | solution.py:29
  18.5 20.7 %collective-permute-start.3 = (bf16[2,256,128]{2,1,0:T(8,128)(2,1)S(1)}, bf16[2,256,128]{2,1,0:T(8,128)(2,1)S(1)}, u32[]{:S(2)}, u32[]{:S(2)}) collective-permute-start(bf16[2,256,128]{2,1,0:T(8,128)(2,1)S(1)} %get-tuple-element.38), channel_id=1, source_target_pairs={{0,1},{1,0},{2,3},{3,2},{4,5},{5,4},{6,7},{7,6},{8,9},{9,8},{10,11... | collective-permute-start | bytes 393224 | tf_op jit(solution)/shard_map/ppermute | solution.py:29
  19.0 22.5 %collective-permute-start.17 = (bf16[1,512,128]{2,1,0:T(8,128)(2,1)S(1)}, bf16[1,512,128]{2,1,0:T(8,128)(2,1)S(1)}, u32[]{:S(2)}, u32[]{:S(2)}) collective-permute-start(bf16[1,512,128]{2,1,0:T(8,128)(2,1)S(1)} %get-tuple-element.44), channel_id=1, source_target_pairs={{0,1},{1,0},{2,3},{3,2},{4,5},{5,4},{6,7},{7,6},{8,9},{9,8},{10,11... | collective-permute-start | bytes 393224 | tf_op jit(solution)/shard_map/ppermute | solution.py:29
  20.5 21.1 %collective-permute-start.12 = (bf16[2,256,128]{2,1,0:T(8,128)(2,1)S(1)}, bf16[2,256,128]{2,1,0:T(8,128)(2,1)S(1)}, u32[]{:S(2)}, u32[]{:S(2)}) collective-permute-start(bf16[2,256,128]{2,1,0:T(8,128)(2,1)S(1)} %collective-permute-done.10.refs_5_), channel_id=1, source_target_pairs={{0,4},{4,0},{8,12},{12,8},{1,5},{5,1},{9,13},{13,9},{2,6},{6,2},{1... | collective-permute-start | bytes 393224 | tf_op jit(solution)/shard_map/ppermute | solution.py:29
  39.2 23.3 %collective-permute-start.15 = (bf16[2,256,128]{2,1,0:T(8,128)(2,1)S(1)}, bf16[2,256,128]{2,1,0:T(8,128)(2,1)S(1)}, u32[]{:S(2)}, u32[]{:S(2)}) collective-permute-start(bf16[2,256,128]{2,1,0:T(8,128)(2,1)S(1)} %collective-permute-done.3.refs_8_), channel_id=1, source_target_pairs={{0,12},{4,8},{8,4},{12,0},{1,13},{5,9},{9,5},{13,1},{2,14},{6,10},... | collective-permute-start | bytes 393224 | tf_op jit(solution)/shard_map/ppermute | solution.py:29
  40.2 24.0 %collective-permute-start.14 = (bf16[2,256,128]{2,1,0:T(8,128)(2,1)S(1)}, bf16[2,256,128]{2,1,0:T(8,128)(2,1)S(1)}, u32[]{:S(2)}, u32[]{:S(2)}) collective-permute-start(bf16[2,256,128]{2,1,0:T(8,128)(2,1)S(1)} %collective-permute-done.3.refs_8_), channel_id=1, source_target_pairs={{0,4},{4,0},{8,12},{12,8},{1,5},{5,1},{9,13},{13,9},{2,6},{6,2},{1... | collective-permute-start | bytes 393224 | tf_op jit(solution)/shard_map/ppermute | solution.py:29
  40.2 23.9 %collective-permute-start.13 = (bf16[2,256,128]{2,1,0:T(8,128)(2,1)S(1)}, bf16[2,256,128]{2,1,0:T(8,128)(2,1)S(1)}, u32[]{:S(2)}, u32[]{:S(2)}) collective-permute-start(bf16[2,256,128]{2,1,0:T(8,128)(2,1)S(1)} %collective-permute-done.3.refs_8_), channel_id=1, source_target_pairs={{0,8},{4,12},{8,0},{12,4},{1,9},{5,13},{9,1},{13,5},{2,10},{6,14},... | collective-permute-start | bytes 393224 | tf_op jit(solution)/shard_map/ppermute | solution.py:29
  41.5 19.0 %collective-permute-start.11 = (bf16[2,256,128]{2,1,0:T(8,128)(2,1)S(1)}, bf16[2,256,128]{2,1,0:T(8,128)(2,1)S(1)}, u32[]{:S(2)}, u32[]{:S(2)}) collective-permute-start(bf16[2,256,128]{2,1,0:T(8,128)(2,1)S(1)} %get-tuple-element.41), channel_id=1, source_target_pairs={{0,4},{4,0},{8,12},{12,8},{1,5},{5,1},{9,13},{13,9},{2,6},{6,2},{1... | collective-permute-start | bytes 393224 | tf_op jit(solution)/shard_map/ppermute | solution.py:29
  41.6 20.4 %collective-permute-start.16 = (bf16[1,512,128]{2,1,0:T(8,128)(2,1)S(1)}, bf16[1,512,128]{2,1,0:T(8,128)(2,1)S(1)}, u32[]{:S(2)}, u32[]{:S(2)}) collective-permute-start(bf16[1,512,128]{2,1,0:T(8,128)(2,1)S(1)} %get-tuple-element.43), channel_id=1, source_target_pairs={{0,1},{1,0},{2,3},{3,2},{4,5},{5,4},{6,7},{7,6},{8,9},{9,8},{10,11... | collective-permute-start | bytes 393224 | tf_op jit(solution)/shard_map/ppermute | solution.py:29
  60.5 23.6 %collective-permute-start.19 = (bf16[1,512,128]{2,1,0:T(8,128)(2,1)S(1)}, bf16[1,512,128]{2,1,0:T(8,128)(2,1)S(1)}, u32[]{:S(2)}, u32[]{:S(2)}) collective-permute-start(bf16[1,512,128]{2,1,0:T(8,128)(2,1)S(1)} %copy-done.15), channel_id=1, source_target_pairs={{0,1},{1,0},{2,3},{3,2},{4,5},{5,4},{6,7},{7,6},{8,9},{9,8},{10,11... | collective-permute-start | bytes 393224 | tf_op jit(solution)/shard_map/ppermute | solution.py:29
  62.1 21.9 %collective-permute-start.9 = (bf16[1,512,128]{2,1,0:T(8,128)(2,1)S(1)}, bf16[1,512,128]{2,1,0:T(8,128)(2,1)S(1)}, u32[]{:S(2)}, u32[]{:S(2)}) collective-permute-start(bf16[1,512,128]{2,1,0:T(8,128)(2,1)S(1)} %get-tuple-element.40), channel_id=1, source_target_pairs={{0,1},{1,0},{2,3},{3,2},{4,5},{5,4},{6,7},{7,6},{8,9},{9,8},{10,11... | collective-permute-start | bytes 393224 | tf_op jit(solution)/shard_map/ppermute | solution.py:29
  62.6 21.5 %collective-permute-start.20 = (bf16[1,512,128]{2,1,0:T(8,128)(2,1)}, bf16[1,512,128]{2,1,0:T(8,128)(2,1)S(1)}, u32[]{:S(2)}, u32[]{:S(2)}) collective-permute-start(bf16[1,512,128]{2,1,0:T(8,128)(2,1)} %get-tuple-element.58), channel_id=1, source_target_pairs={{0,1},{1,0},{2,3},{3,2},{4,5},{5,4},{6,7},{7,6},{8,9},{9,8},{10,11... | collective-permute-start | bytes 393224 | tf_op jit(solution)/shard_map/ppermute | solution.py:29
  64.1 18.9 %collective-permute-start.18 = (bf16[2,2,256,256]{3,2,1,0:T(8,128)(2,1)}, bf16[2,2,256,256]{3,2,1,0:T(8,128)(2,1)S(1)}, u32[]{:S(2)}, u32[]{:S(2)}) collective-permute-start(bf16[2,2,256,256]{3,2,1,0:T(8,128)(2,1)} %get-tuple-element.57), channel_id=1, source_target_pairs={{0,4},{4,0},{8,12},{12,8},{1,5},{5,1},{9,13},{13,9},{2,6},{6,2},{1... | collective-permute-start | bytes 1572872 | tf_op jit(solution)/shard_map/ppermute | solution.py:29
  82.5 20.5 %collective-permute-start.21 = (bf16[1,512,128]{2,1,0:T(8,128)(2,1)}, bf16[1,512,128]{2,1,0:T(8,128)(2,1)S(1)}, u32[]{:S(2)}, u32[]{:S(2)}) collective-permute-start(bf16[1,512,128]{2,1,0:T(8,128)(2,1)} %get-tuple-element.62), channel_id=1, source_target_pairs={{0,1},{1,0},{2,3},{3,2},{4,5},{5,4},{6,7},{7,6},{8,9},{9,8},{10,11... | collective-permute-start | bytes 393224 | tf_op jit(solution)/shard_map/ppermute | solution.py:29
  83.2 19.8 %collective-permute-start.22 = (bf16[2,256,256]{2,1,0:T(8,128)(2,1)S(1)}, bf16[2,256,256]{2,1,0:T(8,128)(2,1)S(1)}, u32[]{:S(2)}, u32[]{:S(2)}) collective-permute-start(bf16[2,256,256]{2,1,0:T(8,128)(2,1)S(1)} %fusion.2.refs_16_), channel_id=1, source_target_pairs={{0,8},{4,12},{8,0},{12,4},{1,9},{5,13},{9,1},{13,5},{2,10},{6,14},... | collective-permute-start | bytes 786440 | tf_op jit(solution)/shard_map/ppermute | solution.py:29
  106.6 8.4 %collective-permute-start.25 = (bf16[2,256,256]{2,1,0:T(8,128)(2,1)S(1)}, bf16[2,256,256]{2,1,0:T(8,128)(2,1)S(1)}, u32[]{:S(2)}, u32[]{:S(2)}) collective-permute-start(bf16[2,256,256]{2,1,0:T(8,128)(2,1)S(1)} %fusion.3), channel_id=1, source_target_pairs={{0,8},{4,12},{8,0},{12,4},{1,9},{5,13},{9,1},{13,5},{2,10},{6,14},... | collective-permute-start | bytes 786440 | tf_op jit(solution)/shard_map/ppermute | solution.py:29
  108.0 9.0 %collective-permute-start.26 = (bf16[2,256,128]{2,1,0:T(8,128)(2,1)S(1)}, bf16[2,256,128]{2,1,0:T(8,128)(2,1)S(1)}, u32[]{:S(2)}, u32[]{:S(2)}) collective-permute-start(bf16[2,256,128]{2,1,0:T(8,128)(2,1)S(1)} %slice.59), channel_id=1, source_target_pairs={{0,1},{1,0},{2,3},{3,2},{4,5},{5,4},{6,7},{7,6},{8,9},{9,8},{10,11... | collective-permute-start | bytes 393224 | tf_op jit(solution)/shard_map/ppermute | solution.py:29
  109.7 7.1 %collective-permute-start.23 = (bf16[1,512,128]{2,1,0:T(8,128)(2,1)S(1)}, bf16[1,512,128]{2,1,0:T(8,128)(2,1)S(1)}, u32[]{:S(2)}, u32[]{:S(2)}) collective-permute-start(bf16[1,512,128]{2,1,0:T(8,128)(2,1)S(1)} %copy-done.24), channel_id=1, source_target_pairs={{0,1},{1,0},{2,3},{3,2},{4,5},{5,4},{6,7},{7,6},{8,9},{9,8},{10,11... | collective-permute-start | bytes 393224 | tf_op jit(solution)/shard_map/ppermute | solution.py:29
  115.1 5.0 %collective-permute-start.27 = (bf16[2,256,128]{2,1,0:T(8,128)(2,1)S(1)}, bf16[2,256,128]{2,1,0:T(8,128)(2,1)S(1)}, u32[]{:S(2)}, u32[]{:S(2)}) collective-permute-start(bf16[2,256,128]{2,1,0:T(8,128)(2,1)S(1)} %slice.58), channel_id=1, source_target_pairs={{0,1},{1,0},{2,3},{3,2},{4,5},{5,4},{6,7},{7,6},{8,9},{9,8},{10,11... | collective-permute-start | bytes 393224 | tf_op jit(solution)/shard_map/ppermute | solution.py:29
  (33 other events, 217.0 us)

commit v5 on v1

v5 whole, which is shorter than its diff:
```python
import functools

import jax
import jax.numpy as jnp
from jax import lax
from jax.experimental import pallas as pl
from jax.experimental.pallas import tpu as pltpu
from jax.sharding import PartitionSpec as P

H = 32
KVH = 8
HD = 128
P_SIZE = 2
GROUP = H // KVH
BLOCK = 256
CHUNK = 128
MASKED = -1e30
SCALE = HD ** (-0.5)

NT = (((1,), (1,)), ((), ()))
NN = (((1,), (0,)), ((), ()))


def dot(a, b, dims):
    return lax.dot_general(a, b, dims, preferred_element_type=jnp.float32)


def swap(block, axis, step):
    return lax.ppermute(block, axis, [(i, i ^ step) for i in range(lax.axis_size(axis))])


def attend_kernel(sizes, scalars, *refs):
    pieces, rows, keep, sends, n_pass = sizes
    refs = list(refs)
    q_ref, do_ref, ra_ref, rb_ref = refs[:4]
    pa_refs = refs[4 : 4 + pieces]
    pb_refs = refs[4 + pieces : 4 + 2 * pieces]
    rest = refs[4 + 2 * pieces + n_pass :]
    out_ref, dq_ref, dra_ref, drb_ref, keep_ref = rest[:5]
    send_refs = rest[5 : 5 + len(sends)]
    k_all, v_all, k_t, v_t, weights, probs, dscores, acc_k, acc_v, sum_k, sum_v = rest[5 + len(sends) :]

    r = pl.program_id(0)
    head = pl.program_id(1)
    n_resp = pl.num_programs(0)
    last = head == pl.num_programs(1) - 1
    prompt = scalars[r]
    even = scalars[n_resp] == 0
    n_prompt = pieces * rows
    n_query = q_ref.shape[1]
    n_blocks = n_query // BLOCK

    def gather(dst, piece_refs, resp_ref):
        for i, ref in enumerate(piece_refs):
            dst[i * rows : (i + 1) * rows, :] = ref[0]
        dst[n_prompt:, :] = resp_ref[0]

    @pl.when((head == 0) & even)
    def _():
        gather(k_all, pa_refs, ra_ref)
        gather(v_all, pb_refs, rb_ref)

    @pl.when((head == 0) & jnp.logical_not(even))
    def _():
        gather(k_all, pb_refs, rb_ref)
        gather(v_all, pa_refs, ra_ref)

    @pl.when(head == 0)
    def _():
        k_t[...] = k_all[...].T
        v_t[...] = v_all[...].T
        acc_k[...] = jnp.zeros_like(acc_k)
        acc_v[...] = jnp.zeros_like(acc_v)

    def fold(x, op):
        return op(x.reshape(-1, 8, x.shape[-1]), axis=0)

    def stages(i):
        st = {}
        t = slice(i * BLOCK, (i + 1) * BLOCK)
        seen = n_prompt + (i + 1) * BLOCK
        parts = [slice(u, u + CHUNK) for u in range(0, seen, CHUNK)]
        n_parts = len(parts)
        q = q_ref[0, t, :]
        do = do_ref[0, t, :]

        def score(c):
            s = dot(k_all[parts[c], :], q, NT)
            below = parts[c].start - (seen - BLOCK)
            if below >= 0:
                row = lax.broadcasted_iota(jnp.int32, (CHUNK, BLOCK), 0) + below
                col = lax.broadcasted_iota(jnp.int32, (CHUNK, BLOCK), 1)
                s = jnp.where(row <= col, s, MASKED)
            weights[parts[c], t] = s
            top = fold(s, jnp.max)
            st["top"] = top if c == 0 else jnp.maximum(st["top"], top)
            if c == n_parts - 1:
                st["top"] = jnp.max(st["top"], axis=0, keepdims=True) * SCALE

        def weigh(c):
            w = jnp.exp(weights[parts[c], t] * SCALE - st["top"])
            weights[parts[c], t] = w
            total = fold(w, jnp.sum)
            st["sum"] = total if c == 0 else st["sum"] + total
            if c == n_parts - 1:
                st["inv"] = 1.0 / jnp.sum(st["sum"], axis=0, keepdims=True)

        def norm(c):
            probs[parts[c], t] = (weights[parts[c], t] * st["inv"]).astype(jnp.bfloat16)
            if c == n_parts - 1:
                o = dot(v_t[:, :seen], probs[:seen, t], NN)
                out_ref[0, t, :] = o.T.astype(jnp.bfloat16)
                do_t = do.astype(jnp.float32).T
                st["delta"] = jnp.sum(o * do_t, axis=0, keepdims=True)
                st["inv"] = st["inv"] * SCALE

        def grad(c):
            dp = dot(v_all[parts[c], :], do, NT)
            ds = (weights[parts[c], t] * st["inv"]) * (dp - st["delta"])
            dscores[parts[c], t] = ds.astype(jnp.bfloat16)
            if c == n_parts - 1:
                dq = dot(k_t[:, :seen], dscores[:seen, t], NN)
                dq_ref[0, t, :] = dq.T.astype(jnp.bfloat16)

        return [[functools.partial(f, c) for c in range(n_parts)] for f in (score, weigh, norm, grad)]

    plan = [stages(i) for i in range(n_blocks)]
    for slot in range(4 + n_blocks - 1):
        groups = [plan[i][slot - i] for i in reversed(range(n_blocks)) if 0 <= slot - i < 4]
        for c in range(max(len(g) for g in groups)):
            for g in groups:
                if c < len(g):
                    g[c]()

    q_all = q_ref[0]
    do_all = do_ref[0]
    for u in range(0, n_prompt + n_query, BLOCK):
        t0 = max(u - n_prompt, 0)
        acc_v[u : u + BLOCK, :] += dot(probs[u : u + BLOCK, t0:], do_all[t0:], NN)
        acc_k[u : u + BLOCK, :] += dot(dscores[u : u + BLOCK, t0:], q_all[t0:], NN)

    def respond(ref, acc):
        ref[0] = acc[n_prompt:, :].astype(jnp.bfloat16)

    @pl.when(last & even)
    def _():
        respond(dra_ref, acc_k)
        respond(drb_ref, acc_v)

    @pl.when(last & jnp.logical_not(even))
    def _():
        respond(dra_ref, acc_v)
        respond(drb_ref, acc_k)

    @pl.when(last & (r == 0))
    def _():
        for whole, acc in ((sum_k, acc_k), (sum_v, acc_v)):
            whole[prompt] = acc[:n_prompt, :]
            whole[1 - prompt] = jnp.zeros((n_prompt, HD), jnp.float32)

    @pl.when(last & (r > 0))
    def _():
        for whole, acc in ((sum_k, acc_k), (sum_v, acc_v)):
            whole[prompt] += acc[:n_prompt, :]

    done = last & (r == n_resp - 1)

    def scatter(slot, whole):
        lanes = slice(slot * HD, (slot + 1) * HD)
        for ref, group in ((keep_ref, keep), *zip(send_refs, sends)):
            for at, i in enumerate(group):
                ref[at, :, :, lanes] = whole[:, i * rows : (i + 1) * rows, :].astype(ref.dtype)

    @pl.when(done & even)
    def _():
        scatter(0, sum_k)
        scatter(1, sum_v)

    @pl.when(done & jnp.logical_not(even))
    def _():
        scatter(0, sum_v)
        scatter(1, sum_k)


def attend(scalars, queries, d_out, resp_a, resp_b, prompt_a, prompt_b, keep, sends, chunk, heads, shared):
    n_resp, n_query, _ = queries.shape
    pieces = len(prompt_a)
    rows = prompt_a[0][0].shape[1]
    n_prompt = pieces * rows
    n_keys = n_prompt + n_query
    shape = jax.ShapeDtypeStruct

    def resp_map(column):
        return lambda r, j, sc: (r, 0, column(sc[n_resp]))

    def prompt_map(column):
        return lambda r, j, sc: (sc[r], 0, column(sc[n_resp]))

    q_spec = pl.BlockSpec((1, n_query, HD), lambda r, j, sc: (r, 0, chunk * heads + j))
    in_specs = [q_spec, q_spec]
    in_specs += [pl.BlockSpec((1, n_query, HD), resp_map(c)) for _, c in (resp_a, resp_b)]
    in_specs += [pl.BlockSpec((1, rows, HD), prompt_map(c)) for _, c in (*prompt_a, *prompt_b)]
    args = [queries, d_out, resp_a[0], resp_b[0], *[a for a, _ in (*prompt_a, *prompt_b)]]
    aliases = {}
    if shared is not None:
        aliases = {1 + len(args) + i: i for i in range(3)}
        args += list(shared)
    n_pass = len(args) - len(in_specs)
    in_specs += [pl.BlockSpec(memory_space=pl.ANY)] * n_pass
    grads = [shape((len(keep), P_SIZE, rows, 2 * HD), jnp.float32)]
    grads += [shape((len(g), P_SIZE, rows, 2 * HD), jnp.bfloat16) for g in sends]
    out_specs = [
        q_spec,
        q_spec,
        pl.BlockSpec((1, n_query, HD), resp_map(resp_a[1])),
        pl.BlockSpec((1, n_query, HD), lambda r, j, sc: (r, 0, 0)),
    ]
    out_specs += [pl.BlockSpec(g.shape, lambda r, j, sc: (0, 0, 0, 0)) for g in grads]
    out_shape = [
        shape(queries.shape, jnp.bfloat16),
        shape(queries.shape, jnp.bfloat16),
        shape(resp_a[0].shape, jnp.bfloat16),
        shape((n_resp, n_query, HD), jnp.bfloat16),
    ] + grads
    scratch = [
        pltpu.VMEM((n_keys, HD), jnp.bfloat16),
        pltpu.VMEM((n_keys, HD), jnp.bfloat16),
        pltpu.VMEM((HD, n_keys), jnp.bfloat16),
        pltpu.VMEM((HD, n_keys), jnp.bfloat16),
        pltpu.VMEM((n_keys, n_query), jnp.float32),
        pltpu.VMEM((n_keys, n_query), jnp.bfloat16),
        pltpu.VMEM((n_keys, n_query), jnp.bfloat16),
        pltpu.VMEM((n_keys, HD), jnp.float32),
        pltpu.VMEM((n_keys, HD), jnp.float32),
        pltpu.VMEM((P_SIZE, n_prompt, HD), jnp.float32),
        pltpu.VMEM((P_SIZE, n_prompt, HD), jnp.float32),
    ]
    flops = 12 * n_resp * heads * n_query * n_keys * HD
    return pl.pallas_call(
        functools.partial(attend_kernel, (pieces, rows, keep, sends, n_pass)),
        grid_spec=pltpu.PrefetchScalarGridSpec(
            num_scalar_prefetch=1,
            grid=(n_resp, heads),
            in_specs=in_specs,
            out_specs=out_specs,
            scratch_shapes=scratch,
        ),
        out_shape=out_shape,
        input_output_aliases=aliases,
        compiler_params=pltpu.CompilerParams(vmem_limit_bytes=48 * 2**20),
        cost_estimate=pl.CostEstimate(flops=2 * flops, bytes_accessed=4 * 2**20, transcendentals=0),
    )(scalars, *args)


def per_device(queries, resp_kv, prompt_kv, prompt_of, d_out):
    pair_heads = prompt_kv.shape[2] // HD
    parity = lax.axis_index("prefix") % 2
    scalars = jnp.concatenate([prompt_of, parity[None].astype(jnp.int32)])
    if lax.axis_size("dp") == 4 and pair_heads % 2 == 0:
        return whole_heads(queries, resp_kv, prompt_kv, scalars, parity, d_out)
    return shared_head(queries, resp_kv, prompt_kv, scalars, parity, d_out)


def whole_heads(queries, resp_kv, prompt_kv, scalars, parity, d_out):
    n_own = prompt_kv.shape[2] // HD // 2
    width = n_own * HD
    z = functools.partial(swap, axis="prefix", step=1)
    core, x, both = [functools.partial(swap, axis="dp", step=k) for k in (1, 2, 3)]
    own, theirs = parity * n_own, (1 - parity) * n_own

    def columns(array, which, count):
        return lax.dynamic_slice_in_dim(array, which * HD, count * HD, axis=2)

    def order(values, done):
        return lax.optimization_barrier((tuple(values), tuple(done)))[0]

    b0 = z(columns(prompt_kv, theirs, n_own))
    a0 = columns(prompt_kv, own, n_own)
    a2 = x(a0)
    resp_b = [z(columns(resp_kv, theirs, 1))]
    a0, b0 = order([a0, b0], [a2])
    b2 = x(b0)
    pa = [a0, core(a0), a2, core(a2)]
    pb = [b0, core(b0), b2, core(b2)]
    for h in range(1, n_own):
        (later,) = order([resp_kv], [resp_b[h - 1], b2])
        resp_b.append(z(columns(later, theirs + h, 1)))

    shared = None
    d_resp, d_prompt = [], []
    for h in range(n_own):
        final = h == n_own - 1
        here = lambda par, h=h: par * n_own + h
        at = lambda par, h=h: h
        att, dq, dra, drb, keep, *sends = attend(
            scalars,
            queries,
            d_out,
            (resp_kv, here),
            (resp_b[h], lambda par: 0),
            [(prompt_kv, here)] + [(a, at) for a in pa[1:]],
            [(b, at) for b in pb],
            (0, 2) if final else (0,),
            ((1, 3),) if final else ((1,), (2,), (3,)),
            h,
            GROUP,
            shared,
        )
        shared = (att, dq, dra)
        if final:
            (send, drb) = order([sends[0], drb], arrived)
            sums = keep + core(send).astype(jnp.float32)
            total = sums[0] + x(sums[1].astype(jnp.bfloat16)).astype(jnp.float32)
            d_resp.append(z(drb))
        else:
            parts = [move(part[0]) for move, part in zip((core, x, both), sends)]
            d_resp.append(z(drb))
            arrived = [*parts, d_resp[-1]]
            total = keep[0] + sum(p.astype(jnp.float32) for p in parts)
        other = z(total[:, :, HD:].astype(jnp.bfloat16))
        d_prompt.append((total[:, :, :HD], other.astype(jnp.float32)))

    even = parity == 0
    mine = jnp.concatenate([a for a, _ in d_prompt], axis=-1)
    other = jnp.concatenate([b for _, b in d_prompt], axis=-1)
    d_prompt = jnp.concatenate([jnp.where(even, mine, other), jnp.where(even, other, mine)], axis=-1)
    att, dq, d_resp_kv = shared
    received = jnp.concatenate(d_resp, axis=-1)
    d_resp_kv = lax.dynamic_update_slice_in_dim(d_resp_kv, received, theirs * HD, axis=2)
    return att, dq, d_resp_kv, d_prompt


def shared_head(queries, resp_kv, prompt_kv, scalars, parity, d_out):
    first = lambda par: 0
    prompt_a = lax.all_gather(prompt_kv, "dp", axis=1, tiled=True)
    prompt_b = swap(prompt_a, "prefix", 1)
    resp_b = swap(resp_kv, "prefix", 1)
    att, dq, dra, drb, keep = attend(
        scalars,
        queries,
        d_out,
        (resp_kv, first),
        (resp_b, first),
        [(prompt_a, first)],
        [(prompt_b, first)],
        (0,),
        (),
        0,
        queries.shape[2] // HD,
        None,
    )
    d_resp = (dra.astype(jnp.float32) + swap(drb, "prefix", 1).astype(jnp.float32)).astype(jnp.bfloat16)
    other = swap(keep[0, :, :, HD:].astype(jnp.bfloat16), "prefix", 1)
    paired = keep[0, :, :, :HD] + other.astype(jnp.float32)
    d_prompt = lax.psum_scatter(paired, "dp", scatter_dimension=1, tiled=True)
    return att, dq, d_resp, d_prompt


def solution(mesh):
    in_specs = (
        P(("groups", "dp"), None, "prefix"),
        P(("groups", "dp"), None, "prefix"),
        P("groups", "dp", "prefix"),
        P(("groups", "dp")),
        P(("groups", "dp"), None, "prefix"),
    )
    out_specs = (
        P(("groups", "dp"), None, "prefix"),
        P(("groups", "dp"), None, "prefix"),
        P(("groups", "dp"), None, "prefix"),
        P("groups", "dp", "prefix"),
    )
    return jax.shard_map(
        per_device, mesh=mesh, in_specs=in_specs, out_specs=out_specs, check_vma=False
    )
```

time: 106 us -> 104 us (0.981)
  Pallas kernels: 53.5 us -> 57.1 us
  starting transfers between devices: 17.6 us -> 14.2 us
  waiting for transfers between devices: 27.5 us -> 24.5 us
  local copies, waits for them, and re-layouts: 3.4 us -> 4.65 us
    pallas_call x2, Pallas kernels: 53.5 us -> 57.1 us  [attend(): pl.pallas_call(functools.partial(attend_kernel, (pieces, rows, keep, send...]
    ppermute x24 -> x18, starting transfers between devices: 17.6 us -> 14.2 us  [swap(): lax.ppermute(block, axis, [(i, i ^ step) for i in range(lax.axis_size(axi...]
    ppermute x24 -> x18, waiting for transfers between devices: 27.5 us -> 24.5 us  [swap(): lax.ppermute(block, axis, [(i, i ^ step) for i in range(lax.axis_size(axi...]
    dynamic_slice x2 -> x3, local copies, waits for them, and re-layouts: 3.03 us -> 4.52 us  [columns(): return lax.dynamic_slice_in_dim(array, which * HD, count * HD, axis=2)]
    concatenate x2 -> x1, other arithmetic: 2.18 us -> 1.13 us  [whole_heads(): jnp.concatenate([jnp.where(even, mine, other), jnp.where(even, other, min...]
  transfers between devices with their start and end apart: 24 -> 18, of which waited for: 8 -> 8; matrix products, arithmetic and copies ran while one was open for 3% -> 4% of each run, Pallas kernels for 51% -> 55%
where the time goes in v5:
time: 104 us
  Pallas kernels  57.1 us (55%)
  waiting for transfers between devices  24.5 us (24%)
  starting transfers between devices  14.2 us (14%)
  local copies, waits for them, and re-layouts  4.65 us (4%)
  other arithmetic  2.35 us (2%)
    pallas_call x2, Pallas kernels, attend(): pl.pallas_call(functools.partial(attend_kernel, (pieces, rows, keep, send...  57.1 us
    ppermute x18, waiting for transfers between devices, swap(): lax.ppermute(block, axis, [(i, i ^ step) for i in range(lax.axis_size(axi...  24.5 us
    ppermute x18, starting transfers between devices, swap(): lax.ppermute(block, axis, [(i, i ^ step) for i in range(lax.axis_size(axi...  14.2 us
    dynamic_slice x3, local copies, waits for them, and re-layouts, columns(): return lax.dynamic_slice_in_dim(array, which * HD, count * HD, axis=2)  4.52 us
  transfers between devices with their start and end apart: 18, of which 8 were waited for; matrix products, arithmetic and copies ran while one was open for 4% of the time, Pallas kernels for 55%

profile of v5, /device:TPU:0, one launch (start us, length us, event | category | flops | bytes accessed | tf_op | source)
XLA Modules:
  0.0 103.6 jit_solution(6409974025255147057)
XLA Ops:
  0.7 1.9 %constant_dynamic-slice_fusion.1 = (bf16[2,256,256]{2,1,0:T(8,128)(2,1)S(1)}, bf16[2,256,256]{2,1,0:T(8,128)(2,1)}) fusion(bf16[2,256,512]{2,1,0:T(8,128)(2,1)} %refs_4_.3, s32[]{:T(128)S(6)} %select_n.31, s32[]{:T(128)S(6)} %select_n.32), kind=kLoop, calls=%fused_computation.15 | loop fusion | bytes 1048584 | tf_op jit(solution)/shard_map/dynamic_slice | solution.py:272
  2.6 3.0 %collective-permute-start.1 = (bf16[2,256,256]{2,1,0:T(8,128)(2,1)S(1)}, bf16[2,256,256]{2,1,0:T(8,128)(2,1)S(1)}, u32[]{:S(2)}, u32[]{:S(2)}) collective-permute-start(bf16[2,256,256]{2,1,0:T(8,128)(2,1)S(1)} %get-tuple-element.44), channel_id=1, source_target_pairs={{0,1},{1,0},{2,3},{3,2},{4,5},{5,4},{6,7},{7,6},{8,9},{9,8},{10,11... | collective-permute-start | bytes 786440 | tf_op jit(solution)/shard_map/ppermute | solution.py:29
  5.6 1.5 %collective-permute-start.2 = (bf16[2,256,256]{2,1,0:T(8,128)(2,1)}, bf16[2,256,256]{2,1,0:T(8,128)(2,1)S(1)}, u32[]{:S(2)}, u32[]{:S(2)}) collective-permute-start(bf16[2,256,256]{2,1,0:T(8,128)(2,1)} %get-tuple-element.25), channel_id=1, source_target_pairs={{0,8},{4,12},{8,0},{12,4},{1,9},{5,13},{9,1},{13,5},{2,10},{6,14},... | collective-permute-start | bytes 786440 | tf_op jit(solution)/shard_map/ppermute | solution.py:29
  7.1 4.8 %collective-permute-done.1.refs_8_ = bf16[2,256,256]{2,1,0:T(8,128)(2,1)S(1)} collective-permute-done((bf16[2,256,256]{2,1,0:T(8,128)(2,1)S(1)}, bf16[2,256,256]{2,1,0:T(8,128)(2,1)S(1)}, u32[]{:S(2)}, u32[]{:S(2)}) %collective-permute-start.1) | collective-permute-done | bytes 262176 | tf_op jit(solution)/shard_map/ppermute | solution.py:29
  11.9 1.7 %collective-permute-done.2.refs_6_ = bf16[2,256,256]{2,1,0:T(8,128)(2,1)S(1)} collective-permute-done((bf16[2,256,256]{2,1,0:T(8,128)(2,1)}, bf16[2,256,256]{2,1,0:T(8,128)(2,1)S(1)}, u32[]{:S(2)}, u32[]{:S(2)}) %collective-permute-start.2) | collective-permute-done | bytes 262176 | tf_op jit(solution)/shard_map/ppermute | solution.py:29
  13.6 1.5 %collective-permute-start.3 = (bf16[2,256,256]{2,1,0:T(8,128)(2,1)S(1)}, bf16[2,256,256]{2,1,0:T(8,128)(2,1)S(1)}, u32[]{:S(2)}, u32[]{:S(2)}) collective-permute-start(bf16[2,256,256]{2,1,0:T(8,128)(2,1)S(1)} %collective-permute-done.1.refs_8_), channel_id=1, source_target_pairs={{0,8},{4,12},{8,0},{12,4},{1,9},{5,13},{9,1},{13,5},{2,10},{6,14},... | collective-permute-start | bytes 786440 | tf_op jit(solution)/shard_map/ppermute | solution.py:29
  15.0 1.7 %constant_dynamic-slice_fusion.3 = bf16[2,512,128]{2,1,0:T(8,128)(2,1)} fusion(bf16[2,512,512]{2,1,0:T(8,128)(2,1)} %refs_2_.3, s32[]{:T(128)S(6)} %select_n.31), kind=kLoop, calls=%fused_computation.17 | loop fusion | bytes 524292 | tf_op jit(solution)/shard_map/dynamic_slice | solution.py:272
  17.7 2.7 %collective-permute-done.3.refs_10_ = bf16[2,256,256]{2,1,0:T(8,128)(2,1)S(1)} collective-permute-done((bf16[2,256,256]{2,1,0:T(8,128)(2,1)S(1)}, bf16[2,256,256]{2,1,0:T(8,128)(2,1)S(1)}, u32[]{:S(2)}, u32[]{:S(2)}) %collective-permute-start.3) | collective-permute-done | bytes 262176 | tf_op jit(solution)/shard_map/ppermute | solution.py:29
  20.4 0.7 pad_add_fusion.scalars
  21.1 2.5 %collective-permute-done.refs_3_ = bf16[2,512,128]{2,1,0:T(8,128)(2,1)} collective-permute-done((bf16[2,512,128]{2,1,0:T(8,128)(2,1)}, bf16[2,512,128]{2,1,0:T(8,128)(2,1)}, u32[]{:S(2)}, u32[]{:S(2)}) %collective-permute-start) | collective-permute-done | bytes 262176 | tf_op jit(solution)/shard_map/ppermute | solution.py:29
  23.6 1.0 constant_dynamic-slice_fusion
  25.1 28.5 %shard_map.84 = (bf16[2,512,1024]{2,1,0:T(8,128)(2,1)}, bf16[2,512,1024]{2,1,0:T(8,128)(2,1)}, bf16[2,512,512]{2,1,0:T(8,128)(2,1)}, bf16[2,512,128]{2,1,0:T(8,1...) custom-call(s32[3]{0:T(128)S(1)} %pad_add_fusion.scalars, ...), custom_call_target="tpu_custom_call" | custom-call | flops 19327352832 | bytes 4194304 | tf_op jit(solution)/shard_map/pallas_call | solution.py:239
  53.7 0.7 collective-permute-start.11
  54.4 1.1 %collective-permute-start.12 = (bf16[2,256,256]{2,1,0:T(8,128)(2,1)S(1)}, bf16[2,256,256]{2,1,0:T(8,128)(2,1)S(1)}, u32[]{:S(2)}, u32[]{:S(2)}) collective-permute-start(bf16[2,256,256]{2,1,0:T(8,128)(2,1)S(1)} %bitcast.12), channel_id=1, source_target_pairs={{0,12},{4,8},{8,4},{12,0},{1,13},{5,9},{9,5},{13,1},{2,14},{6,10},... | collective-permute-start | bytes 786440 | tf_op jit(solution)/shard_map/ppermute | solution.py:29
  55.5 1.6 %collective-permute-start.9 = (bf16[2,512,128]{2,1,0:T(8,128)(2,1)S(1)}, bf16[2,512,128]{2,1,0:T(8,128)(2,1)S(1)}, u32[]{:S(2)}, u32[]{:S(2)}) collective-permute-start(bf16[2,512,128]{2,1,0:T(8,128)(2,1)S(1)} %get-tuple-element.32), channel_id=1, source_target_pairs={{0,1},{1,0},{2,3},{3,2},{4,5},{5,4},{6,7},{7,6},{8,9},{9,8},{10,11... | collective-permute-start | bytes 786440 | tf_op jit(solution)/shard_map/ppermute | solution.py:29
  57.1 28.6 %shard_map.85 = (bf16[2,512,1024]{2,1,0:T(8,128)(2,1)}, bf16[2,512,1024]{2,1,0:T(8,128)(2,1)}, bf16[2,512,512]{2,1,0:T(8,128)(2,1)}, bf16[2,512,128]{2,1,0:T(8,1...) custom-call(s32[3]{0:T(128)S(1)} %pad_add_fusion.scalars, ...), custom_call_target="tpu_custom_call", output_to_operand_aliasing={{0}: (13, {}), {1}: (14, {}), {2}: (15, {})} | custom-call | flops 19327352832 | bytes 4194304 | tf_op jit(solution)/shard_map/pallas_call | solution.py:239
  85.8 1.9 %collective-permute-done.14 = bf16[2,2,256,256]{3,2,1,0:T(8,128)(2,1)S(1)} collective-permute-done((bf16[2,2,256,256]{3,2,1,0:T(8,128)(2,1)S(1)}, bf16[2,2,256,256]{3,2,1,0:T(8,128)(2,1)S(1)}, u32[]{:S(2)}, u32[]{:S(2)}) %collective-permute-start.14) | collective-permute-done | bytes 524320 | tf_op jit(solution)/shard_map/ppermute | solution.py:29
  87.9 0.6 collective-permute-start.15
  88.7 0.7 collective-permute-start.16
  89.3 1.4 %collective-permute-start.13 = (bf16[2,512,128]{2,1,0:T(8,128)(2,1)}, bf16[2,512,128]{2,1,0:T(8,128)(2,1)S(1)}, u32[]{:S(2)}, u32[]{:S(2)}) collective-permute-start(bf16[2,512,128]{2,1,0:T(8,128)(2,1)} %get-tuple-element.38), channel_id=1, source_target_pairs={{0,1},{1,0},{2,3},{3,2},{4,5},{5,4},{6,7},{7,6},{8,9},{9,8},{10,11... | collective-permute-start | bytes 786440 | tf_op jit(solution)/shard_map/ppermute | solution.py:29
  90.8 5.5 %collective-permute-done.15 = bf16[2,256,256]{2,1,0:T(8,128)(2,1)S(1)} collective-permute-done((bf16[2,256,256]{2,1,0:T(8,128)(2,1)S(1)}, bf16[2,256,256]{2,1,0:T(8,128)(2,1)S(1)}, u32[]{:S(2)}, u32[]{:S(2)}) %collective-permute-start.15) | collective-permute-done | bytes 262176 | tf_op jit(solution)/shard_map/ppermute | solution.py:29
  96.9 3.8 %collective-permute-done.13 = bf16[2,512,128]{2,1,0:T(8,128)(2,1)S(1)} collective-permute-done((bf16[2,512,128]{2,1,0:T(8,128)(2,1)}, bf16[2,512,128]{2,1,0:T(8,128)(2,1)S(1)}, u32[]{:S(2)}, u32[]{:S(2)}) %collective-permute-start.13) | collective-permute-done | bytes 262176 | tf_op jit(solution)/shard_map/ppermute | solution.py:29
  100.9 1.5 %collective-permute-done.17 = bf16[2,256,128]{2,1,0:T(8,128)(2,1)S(1)} collective-permute-done((bf16[2,256,128]{2,1,0:T(8,128)(2,1)S(1)}, bf16[2,256,128]{2,1,0:T(8,128)(2,1)S(1)}, u32[]{:S(2)}, u32[]{:S(2)}) %collective-permute-start.17) | collective-permute-done | bytes 131104 | tf_op jit(solution)/shard_map/ppermute | solution.py:29
  102.5 1.1 %pad_maximum_fusion = f32[2,256,512]{2,1,0:T(8,128)} fusion(f32[2,256,256]{2,1,0:T(8,128)S(1)} %get-tuple-element.43, f32[2,256,256]{2,1,0:T(8,128)S(1)} %get-tuple-element.42), kind=kLoop, calls=%fused_computation | loop fusion | flops 262144 | bytes 2097152 | tf_op jit(solution)/shard_map/concatenate | solution.py:326
  (41 shorter events, 2.7 us)
Async XLA Ops:
  0.6 24.5 %copy-start = (bf16[2,256,512]{2,1,0:T(8,128)(2,1)S(1)}, bf16[2,256,512]{2,1,0:T(8,128)(2,1)}, u32[]{:S(2)}) copy-start(bf16[2,256,512]{2,1,0:T(8,128)(2,1)} %refs_4_.3) | copy-start | bytes 1572868
  0.6 24.5 %copy-start.1 = (bf16[2,512,512]{2,1,0:T(8,128)(2,1)S(1)}, bf16[2,512,512]{2,1,0:T(8,128)(2,1)}, u32[]{:S(2)}) copy-start(bf16[2,512,512]{2,1,0:T(8,128)(2,1)} %refs_2_.3) | copy-start | bytes 3145732
  2.6 9.3 %collective-permute-start.1 = (bf16[2,256,256]{2,1,0:T(8,128)(2,1)S(1)}, bf16[2,256,256]{2,1,0:T(8,128)(2,1)S(1)}, u32[]{:S(2)}, u32[]{:S(2)}) collective-permute-start(bf16[2,256,256]{2,1,0:T(8,128)(2,1)S(1)} %get-tuple-element.44), channel_id=1, source_target_pairs={{0,1},{1,0},{2,3},{3,2},{4,5},{5,4},{6,7},{7,6},{8,9},{9,8},{10,11... | collective-permute-start | bytes 786440 | tf_op jit(solution)/shard_map/ppermute | solution.py:29
  5.6 8.0 %collective-permute-start.2 = (bf16[2,256,256]{2,1,0:T(8,128)(2,1)}, bf16[2,256,256]{2,1,0:T(8,128)(2,1)S(1)}, u32[]{:S(2)}, u32[]{:S(2)}) collective-permute-start(bf16[2,256,256]{2,1,0:T(8,128)(2,1)} %get-tuple-element.25), channel_id=1, source_target_pairs={{0,8},{4,12},{8,0},{12,4},{1,9},{5,13},{9,1},{13,5},{2,10},{6,14},... | collective-permute-start | bytes 786440 | tf_op jit(solution)/shard_map/ppermute | solution.py:29
  13.6 6.9 %collective-permute-start.3 = (bf16[2,256,256]{2,1,0:T(8,128)(2,1)S(1)}, bf16[2,256,256]{2,1,0:T(8,128)(2,1)S(1)}, u32[]{:S(2)}, u32[]{:S(2)}) collective-permute-start(bf16[2,256,256]{2,1,0:T(8,128)(2,1)S(1)} %collective-permute-done.1.refs_8_), channel_id=1, source_target_pairs={{0,8},{4,12},{8,0},{12,4},{1,9},{5,13},{9,1},{13,5},{2,10},{6,14},... | collective-permute-start | bytes 786440 | tf_op jit(solution)/shard_map/ppermute | solution.py:29
  16.7 6.9 %collective-permute-start = (bf16[2,512,128]{2,1,0:T(8,128)(2,1)}, bf16[2,512,128]{2,1,0:T(8,128)(2,1)}, u32[]{:S(2)}, u32[]{:S(2)}) collective-permute-start(bf16[2,512,128]{2,1,0:T(8,128)(2,1)} %constant_dynamic-slice_fusion.3), channel_id=1, source_target_pairs={{0,1},{1,0},{2,3},{3,2},{4,5},{5,4},{6,7},{7,6},{8,9},{9,8},{10,11... | collective-permute-start | bytes 786440 | tf_op jit(solution)/shard_map/ppermute | solution.py:29
  17.2 7.9 %collective-permute-start.7 = (bf16[2,256,256]{2,1,0:T(8,128)(2,1)S(1)}, bf16[2,256,256]{2,1,0:T(8,128)(2,1)S(1)}, u32[]{:S(2)}, u32[]{:S(2)}) collective-permute-start(bf16[2,256,256]{2,1,0:T(8,128)(2,1)S(1)} %collective-permute-done.1.refs_8_), channel_id=1, source_target_pairs={{0,4},{4,0},{8,12},{12,8},{1,5},{5,1},{9,13},{13,9},{2,6},{6,2},{1... | collective-permute-start | bytes 786440 | tf_op jit(solution)/shard_map/ppermute | solution.py:29
  17.2 7.9 %collective-permute-start.5 = (bf16[2,256,256]{2,1,0:T(8,128)(2,1)}, bf16[2,256,256]{2,1,0:T(8,128)(2,1)S(1)}, u32[]{:S(2)}, u32[]{:S(2)}) collective-permute-start(bf16[2,256,256]{2,1,0:T(8,128)(2,1)} %get-tuple-element.25), channel_id=1, source_target_pairs={{0,4},{4,0},{8,12},{12,8},{1,5},{5,1},{9,13},{13,9},{2,6},{6,2},{1... | collective-permute-start | bytes 786440 | tf_op jit(solution)/shard_map/ppermute | solution.py:29
  17.7 7.4 %collective-permute-start.6 = (bf16[2,256,256]{2,1,0:T(8,128)(2,1)S(1)}, bf16[2,256,256]{2,1,0:T(8,128)(2,1)S(1)}, u32[]{:S(2)}, u32[]{:S(2)}) collective-permute-start(bf16[2,256,256]{2,1,0:T(8,128)(2,1)S(1)} %collective-permute-done.2.refs_6_), channel_id=1, source_target_pairs={{0,4},{4,0},{8,12},{12,8},{1,5},{5,1},{9,13},{13,9},{2,6},{6,2},{1... | collective-permute-start | bytes 786440 | tf_op jit(solution)/shard_map/ppermute | solution.py:29
  20.4 4.7 %collective-permute-start.8 = (bf16[2,256,256]{2,1,0:T(8,128)(2,1)S(1)}, bf16[2,256,256]{2,1,0:T(8,128)(2,1)S(1)}, u32[]{:S(2)}, u32[]{:S(2)}) collective-permute-start(bf16[2,256,256]{2,1,0:T(8,128)(2,1)S(1)} %collective-permute-done.3.refs_10_), channel_id=1, source_target_pairs={{0,4},{4,0},{8,12},{12,8},{1,5},{5,1},{9,13},{13,9},{2,6},{6,2},{1... | collective-permute-start | bytes 786440 | tf_op jit(solution)/shard_map/ppermute | solution.py:29
  24.6 32.6 %collective-permute-start.4 = (bf16[2,512,128]{2,1,0:T(8,128)(2,1)S(1)}, bf16[2,512,128]{2,1,0:T(8,128)(2,1)S(1)}, u32[]{:S(2)}, u32[]{:S(2)}) collective-permute-start(bf16[2,512,128]{2,1,0:T(8,128)(2,1)S(1)} %constant_dynamic-slice_fusion), channel_id=1, source_target_pairs={{0,1},{1,0},{2,3},{3,2},{4,5},{5,4},{6,7},{7,6},{8,9},{9,8},{10,11... | collective-permute-start | bytes 786440 | tf_op jit(solution)/shard_map/ppermute | solution.py:29
  53.7 32.0 %collective-permute-start.10 = (bf16[2,256,256]{2,1,0:T(8,128)(2,1)S(1)}, bf16[2,256,256]{2,1,0:T(8,128)(2,1)S(1)}, u32[]{:S(2)}, u32[]{:S(2)}) collective-permute-start(bf16[2,256,256]{2,1,0:T(8,128)(2,1)S(1)} %bitcast.14), channel_id=1, source_target_pairs={{0,4},{4,0},{8,12},{12,8},{1,5},{5,1},{9,13},{13,9},{2,6},{6,2},{1... | collective-permute-start | bytes 786440 | tf_op jit(solution)/shard_map/ppermute | solution.py:29
  53.7 32.0 %collective-permute-start.11 = (bf16[2,256,256]{2,1,0:T(8,128)(2,1)S(1)}, bf16[2,256,256]{2,1,0:T(8,128)(2,1)S(1)}, u32[]{:S(2)}, u32[]{:S(2)}) collective-permute-start(bf16[2,256,256]{2,1,0:T(8,128)(2,1)S(1)} %bitcast.13), channel_id=1, source_target_pairs={{0,8},{4,12},{8,0},{12,4},{1,9},{5,13},{9,1},{13,5},{2,10},{6,14},... | collective-permute-start | bytes 786440 | tf_op jit(solution)/shard_map/ppermute | solution.py:29
  54.4 31.3 %collective-permute-start.12 = (bf16[2,256,256]{2,1,0:T(8,128)(2,1)S(1)}, bf16[2,256,256]{2,1,0:T(8,128)(2,1)S(1)}, u32[]{:S(2)}, u32[]{:S(2)}) collective-permute-start(bf16[2,256,256]{2,1,0:T(8,128)(2,1)S(1)} %bitcast.12), channel_id=1, source_target_pairs={{0,12},{4,8},{8,4},{12,0},{1,13},{5,9},{9,5},{13,1},{2,14},{6,10},... | collective-permute-start | bytes 786440 | tf_op jit(solution)/shard_map/ppermute | solution.py:29
  55.5 30.2 %collective-permute-start.9 = (bf16[2,512,128]{2,1,0:T(8,128)(2,1)S(1)}, bf16[2,512,128]{2,1,0:T(8,128)(2,1)S(1)}, u32[]{:S(2)}, u32[]{:S(2)}) collective-permute-start(bf16[2,512,128]{2,1,0:T(8,128)(2,1)S(1)} %get-tuple-element.32), channel_id=1, source_target_pairs={{0,1},{1,0},{2,3},{3,2},{4,5},{5,4},{6,7},{7,6},{8,9},{9,8},{10,11... | collective-permute-start | bytes 786440 | tf_op jit(solution)/shard_map/ppermute | solution.py:29
  85.7 2.9 %copy-start.2 = (bf16[2,512,128]{2,1,0:T(8,128)(2,1)}, bf16[2,512,128]{2,1,0:T(8,128)(2,1)S(1)}, u32[]{:S(2)}) copy-start(bf16[2,512,128]{2,1,0:T(8,128)(2,1)S(1)} %collective-permute-done.9) | copy-start | bytes 786436
  85.7 2.0 %collective-permute-start.14 = (bf16[2,2,256,256]{3,2,1,0:T(8,128)(2,1)S(1)}, bf16[2,2,256,256]{3,2,1,0:T(8,128)(2,1)S(1)}, u32[]{:S(2)}, u32[]{:S(2)}) collective-permute-start(bf16[2,2,256,256]{3,2,1,0:T(8,128)(2,1)S(1)} %get-tuple-element.41), channel_id=1, source_target_pairs={{0,4},{4,0},{8,12},{12,8},{1,5},{5,1},{9,13},{13,9},{2,6},{6,2},{1... | collective-permute-start | bytes 1572872 | tf_op jit(solution)/shard_map/ppermute | solution.py:29
  87.9 8.4 %collective-permute-start.15 = (bf16[2,256,256]{2,1,0:T(8,128)(2,1)S(1)}, bf16[2,256,256]{2,1,0:T(8,128)(2,1)S(1)}, u32[]{:S(2)}, u32[]{:S(2)}) collective-permute-start(bf16[2,256,256]{2,1,0:T(8,128)(2,1)S(1)} %fusion.1), channel_id=1, source_target_pairs={{0,8},{4,12},{8,0},{12,4},{1,9},{5,13},{9,1},{13,5},{2,10},{6,14},... | collective-permute-start | bytes 786440 | tf_op jit(solution)/shard_map/ppermute | solution.py:29
  88.5 12.2 %copy-start.4 = (bf16[2,512,512]{2,1,0:T(8,128)(2,1)S(1)}, bf16[2,512,512]{2,1,0:T(8,128)(2,1)}, u32[]{:S(2)}) copy-start(bf16[2,512,512]{2,1,0:T(8,128)(2,1)} %get-tuple-element.31) | copy-start | bytes 3145732
  88.6 12.1 %copy-start.3 = (bf16[2,512,128]{2,1,0:T(8,128)(2,1)S(1)}, bf16[2,512,128]{2,1,0:T(8,128)(2,1)}, u32[]{:S(2)}) copy-start(bf16[2,512,128]{2,1,0:T(8,128)(2,1)} %copy-done.2) | copy-start | bytes 786436
  88.7 12.2 %collective-permute-start.16 = (bf16[2,256,128]{2,1,0:T(8,128)(2,1)S(1)}, bf16[2,256,128]{2,1,0:T(8,128)(2,1)S(1)}, u32[]{:S(2)}, u32[]{:S(2)}) collective-permute-start(bf16[2,256,128]{2,1,0:T(8,128)(2,1)S(1)} %slice.42), channel_id=1, source_target_pairs={{0,1},{1,0},{2,3},{3,2},{4,5},{5,4},{6,7},{7,6},{8,9},{9,8},{10,11... | collective-permute-start | bytes 393224 | tf_op jit(solution)/shard_map/ppermute | solution.py:29
  89.3 11.4 %collective-permute-start.13 = (bf16[2,512,128]{2,1,0:T(8,128)(2,1)}, bf16[2,512,128]{2,1,0:T(8,128)(2,1)S(1)}, u32[]{:S(2)}, u32[]{:S(2)}) collective-permute-start(bf16[2,512,128]{2,1,0:T(8,128)(2,1)} %get-tuple-element.38), channel_id=1, source_target_pairs={{0,1},{1,0},{2,3},{3,2},{4,5},{5,4},{6,7},{7,6},{8,9},{9,8},{10,11... | collective-permute-start | bytes 786440 | tf_op jit(solution)/shard_map/ppermute | solution.py:29
  96.4 6.0 %collective-permute-start.17 = (bf16[2,256,128]{2,1,0:T(8,128)(2,1)S(1)}, bf16[2,256,128]{2,1,0:T(8,128)(2,1)S(1)}, u32[]{:S(2)}, u32[]{:S(2)}) collective-permute-start(bf16[2,256,128]{2,1,0:T(8,128)(2,1)S(1)} %slice.41), channel_id=1, source_target_pairs={{0,1},{1,0},{2,3},{3,2},{4,5},{5,4},{6,7},{7,6},{8,9},{9,8},{10,11... | collective-permute-start | bytes 393224 | tf_op jit(solution)/shard_map/ppermute | solution.py:29
  100.8 2.8 %copy-start.5 = (bf16[2,512,512]{2,1,0:T(8,128)(2,1)}, bf16[2,512,512]{2,1,0:T(8,128)(2,1)S(1)}, u32[]{:S(2)}) copy-start(bf16[2,512,512]{2,1,0:T(8,128)(2,1)S(1)} %maximum_dynamic-update-slice_fusion) | copy-start | bytes 3145732

commit v6 on v5

--- a/solution.py
+++ b/solution.py
@@ -13,12 +13,13 @@
 P_SIZE = 2
 GROUP = H // KVH
 BLOCK = 256
-CHUNK = 128
+STRIP = 16
 MASKED = -1e30
 SCALE = HD ** (-0.5)
 
 NT = (((1,), (1,)), ((), ()))
 NN = (((1,), (0,)), ((), ()))
+TN = (((0,), (0,)), ((), ()))
 
 
 def dot(a, b, dims):
@@ -38,7 +39,7 @@
     rest = refs[4 + 2 * pieces + n_pass :]
     out_ref, dq_ref, dra_ref, drb_ref, keep_ref = rest[:5]
     send_refs = rest[5 : 5 + len(sends)]
-    k_all, v_all, k_t, v_t, weights, probs, dscores, acc_k, acc_v, sum_k, sum_v = rest[5 + len(sends) :]
+    k_all, v_all, scores, grad_probs, probs, dscores, acc_k, acc_v, sum_k, sum_v = rest[5 + len(sends) :]
 
     r = pl.program_id(0)
     head = pl.program_id(1)
@@ -67,77 +68,79 @@
 
     @pl.when(head == 0)
     def _():
-        k_t[...] = k_all[...].T
-        v_t[...] = v_all[...].T
         acc_k[...] = jnp.zeros_like(acc_k)
         acc_v[...] = jnp.zeros_like(acc_v)
 
-    def fold(x, op):
-        return op(x.reshape(-1, 8, x.shape[-1]), axis=0)
-
     def stages(i):
         st = {}
-        t = slice(i * BLOCK, (i + 1) * BLOCK)
-        seen = n_prompt + (i + 1) * BLOCK
-        parts = [slice(u, u + CHUNK) for u in range(0, seen, CHUNK)]
-        n_parts = len(parts)
+        t0 = i * BLOCK
+        t = slice(t0, t0 + BLOCK)
+        seen = n_prompt + t0 + BLOCK
+        edge = seen - BLOCK
         q = q_ref[0, t, :]
         do = do_ref[0, t, :]
 
-        def score(c):
-            s = dot(k_all[parts[c], :], q, NT)
-            below = parts[c].start - (seen - BLOCK)
-            if below >= 0:
-                row = lax.broadcasted_iota(jnp.int32, (CHUNK, BLOCK), 0) + below
-                col = lax.broadcasted_iota(jnp.int32, (CHUNK, BLOCK), 1)
-                s = jnp.where(row <= col, s, MASKED)
-            weights[parts[c], t] = s
-            top = fold(s, jnp.max)
-            st["top"] = top if c == 0 else jnp.maximum(st["top"], top)
-            if c == n_parts - 1:
-                st["top"] = jnp.max(st["top"], axis=0, keepdims=True) * SCALE
-
-        def weigh(c):
-            w = jnp.exp(weights[parts[c], t] * SCALE - st["top"])
-            weights[parts[c], t] = w
-            total = fold(w, jnp.sum)
-            st["sum"] = total if c == 0 else st["sum"] + total
-            if c == n_parts - 1:
-                st["inv"] = 1.0 / jnp.sum(st["sum"], axis=0, keepdims=True)
-
-        def norm(c):
-            probs[parts[c], t] = (weights[parts[c], t] * st["inv"]).astype(jnp.bfloat16)
-            if c == n_parts - 1:
-                o = dot(v_t[:, :seen], probs[:seen, t], NN)
-                out_ref[0, t, :] = o.T.astype(jnp.bfloat16)
-                do_t = do.astype(jnp.float32).T
-                st["delta"] = jnp.sum(o * do_t, axis=0, keepdims=True)
-                st["inv"] = st["inv"] * SCALE
-
-        def grad(c):
-            dp = dot(v_all[parts[c], :], do, NT)
-            ds = (weights[parts[c], t] * st["inv"]) * (dp - st["delta"])
-            dscores[parts[c], t] = ds.astype(jnp.bfloat16)
-            if c == n_parts - 1:
-                dq = dot(k_t[:, :seen], dscores[:seen, t], NN)
-                dq_ref[0, t, :] = dq.T.astype(jnp.bfloat16)
-
-        return [[functools.partial(f, c) for c in range(n_parts)] for f in (score, weigh, norm, grad)]
+        def score(u):
+            scores[t, u : u + BLOCK] = dot(q, k_all[u : u + BLOCK, :], NT)
+
+        def softmax(row):
+            at = slice(t0 + row, t0 + row + STRIP)
+            left = scores[at, :edge]
+            rows_at = lax.broadcasted_iota(jnp.int32, (STRIP, BLOCK), 0) + row
+            columns = lax.broadcasted_iota(jnp.int32, (STRIP, BLOCK), 1)
+            right = jnp.where(columns <= rows_at, scores[at, edge:seen], MASKED)
+            top = jnp.maximum(jnp.max(left, axis=1, keepdims=True), jnp.max(right, axis=1, keepdims=True)) * SCALE
+            left = jnp.exp(left * SCALE - top)
+            right = jnp.exp(right * SCALE - top)
+            inv = 1.0 / (jnp.sum(left, axis=1, keepdims=True) + jnp.sum(right, axis=1, keepdims=True))
+            for part, u in ((left * inv, slice(0, edge)), (right * inv, slice(edge, seen))):
+                scores[at, u] = part
+                probs[at, u] = part.astype(jnp.bfloat16)
+
+        def grad_prob(u):
+            grad_probs[t, u : u + BLOCK] = dot(do, v_all[u : u + BLOCK, :], NT)
+
+        def output():
+            o = dot(probs[t, :seen], v_all[:seen, :], NN)
+            out_ref[0, t, :] = o.astype(jnp.bfloat16)
+            st["delta"] = jnp.sum(o * do.astype(jnp.float32), axis=1, keepdims=True)
+
+        def grad_score(row):
+            at = slice(t0 + row, t0 + row + STRIP)
+            delta = st["delta"][row : row + STRIP]
+            ds = (scores[at, :seen] * SCALE) * (grad_probs[at, :seen] - delta)
+            dscores[at, :seen] = ds.astype(jnp.bfloat16)
+
+        def query():
+            dq_ref[0, t, :] = dot(dscores[t, :seen], k_all[:seen, :], NN).astype(jnp.bfloat16)
+
+        blocks = range(0, seen, BLOCK)
+        strips = range(0, BLOCK, STRIP)
+        each = lambda f, xs: [functools.partial(f, x) for x in xs]
+        return [
+            each(score, blocks),
+            each(softmax, strips),
+            each(grad_prob, blocks) + [output],
+            each(grad_score, strips),
+            [query],
+        ]
+
+    def mix(lists):
+        steps = [((at + 0.5) / len(x), k, f) for k, x in enumerate(lists) for at, f in enumerate(x)]
+        return [f for _, _, f in sorted(steps, key=lambda e: e[:2])]
 
     plan = [stages(i) for i in range(n_blocks)]
-    for slot in range(4 + n_blocks - 1):
-        groups = [plan[i][slot - i] for i in reversed(range(n_blocks)) if 0 <= slot - i < 4]
-        for c in range(max(len(g) for g in groups)):
-            for g in groups:
-                if c < len(g):
-                    g[c]()
+    depth = len(plan[0])
+    for slot in range(depth + n_blocks - 1):
+        for step in mix([plan[i][slot - i] for i in range(n_blocks) if 0 <= slot - i < depth]):
+            step()
 
     q_all = q_ref[0]
     do_all = do_ref[0]
     for u in range(0, n_prompt + n_query, BLOCK):
         t0 = max(u - n_prompt, 0)
-        acc_v[u : u + BLOCK, :] += dot(probs[u : u + BLOCK, t0:], do_all[t0:], NN)
-        acc_k[u : u + BLOCK, :] += dot(dscores[u : u + BLOCK, t0:], q_all[t0:], NN)
+        acc_v[u : u + BLOCK, :] += dot(probs[t0:, u : u + BLOCK], do_all[t0:], TN)
+        acc_k[u : u + BLOCK, :] += dot(dscores[t0:, u : u + BLOCK], q_all[t0:], TN)
 
     def respond(ref, acc):
         ref[0] = acc[n_prompt:, :].astype(jnp.bfloat16)
@@ -225,11 +228,10 @@
     scratch = [
         pltpu.VMEM((n_keys, HD), jnp.bfloat16),
         pltpu.VMEM((n_keys, HD), jnp.bfloat16),
-        pltpu.VMEM((HD, n_keys), jnp.bfloat16),
-        pltpu.VMEM((HD, n_keys), jnp.bfloat16),
-        pltpu.VMEM((n_keys, n_query), jnp.float32),
-        pltpu.VMEM((n_keys, n_query), jnp.bfloat16),
-        pltpu.VMEM((n_keys, n_query), jnp.bfloat16),
+        pltpu.VMEM((n_query, n_keys), jnp.float32),
+        pltpu.VMEM((n_query, n_keys), jnp.float32),
+        pltpu.VMEM((n_query, n_keys), jnp.bfloat16),
+        pltpu.VMEM((n_query, n_keys), jnp.bfloat16),
         pltpu.VMEM((n_keys, HD), jnp.float32),
         pltpu.VMEM((n_keys, HD), jnp.float32),
         pltpu.VMEM((P_SIZE, n_prompt, HD), jnp.float32),

time: 104 us -> 105 us (level)
  Pallas kernels: 57.1 us -> 58.7 us
    pallas_call x2, Pallas kernels: 57.1 us -> 58.7 us  [attend(): pl.pallas_call(functools.partial(attend_kernel, (pieces, rows, keep, send...]
  transfers between devices with their start and end apart: 18 -> 18, of which waited for: 8 -> 8; matrix products, arithmetic and copies ran while one was open for 4% -> 4% of each run, Pallas kernels for 55% -> 56%
where the time goes in v6:
time: 105 us
  Pallas kernels  58.7 us (56%)
  waiting for transfers between devices  24.4 us (23%)
  starting transfers between devices  14.3 us (14%)
  local copies, waits for them, and re-layouts  4.65 us (4%)
  other arithmetic  2.35 us (2%)
    pallas_call x2, Pallas kernels, attend(): pl.pallas_call(functools.partial(attend_kernel, (pieces, rows, keep, send...  58.7 us
    ppermute x18, waiting for transfers between devices, swap(): lax.ppermute(block, axis, [(i, i ^ step) for i in range(lax.axis_size(axi...  24.4 us
    ppermute x18, starting transfers between devices, swap(): lax.ppermute(block, axis, [(i, i ^ step) for i in range(lax.axis_size(axi...  14.3 us
    dynamic_slice x3, local copies, waits for them, and re-layouts, columns(): return lax.dynamic_slice_in_dim(array, which * HD, count * HD, axis=2)  4.52 us
  transfers between devices with their start and end apart: 18, of which 8 were waited for; matrix products, arithmetic and copies ran while one was open for 4% of the time, Pallas kernels for 56%

profile of v6, /device:TPU:0, one launch (start us, length us, event | category | flops | bytes accessed | tf_op | source)
XLA Modules:
  0.0 105.2 jit_solution(3615091913099920107)
XLA Ops:
  0.7 1.9 %constant_dynamic-slice_fusion.1 = (bf16[2,256,256]{2,1,0:T(8,128)(2,1)S(1)}, bf16[2,256,256]{2,1,0:T(8,128)(2,1)}) fusion(bf16[2,256,512]{2,1,0:T(8,128)(2,1)} %refs_4_.3, s32[]{:T(128)S(6)} %select_n.31, s32[]{:T(128)S(6)} %select_n.32), kind=kLoop, calls=%fused_computation.15 | loop fusion | bytes 1048584 | tf_op jit(solution)/shard_map/dynamic_slice | solution.py:274
  2.6 3.0 %collective-permute-start.1 = (bf16[2,256,256]{2,1,0:T(8,128)(2,1)S(1)}, bf16[2,256,256]{2,1,0:T(8,128)(2,1)S(1)}, u32[]{:S(2)}, u32[]{:S(2)}) collective-permute-start(bf16[2,256,256]{2,1,0:T(8,128)(2,1)S(1)} %get-tuple-element.44), channel_id=1, source_target_pairs={{0,1},{1,0},{2,3},{3,2},{4,5},{5,4},{6,7},{7,6},{8,9},{9,8},{10,11... | collective-permute-start | bytes 786440 | tf_op jit(solution)/shard_map/ppermute | solution.py:30
  5.6 1.5 %collective-permute-start.2 = (bf16[2,256,256]{2,1,0:T(8,128)(2,1)}, bf16[2,256,256]{2,1,0:T(8,128)(2,1)S(1)}, u32[]{:S(2)}, u32[]{:S(2)}) collective-permute-start(bf16[2,256,256]{2,1,0:T(8,128)(2,1)} %get-tuple-element.25), channel_id=1, source_target_pairs={{0,8},{4,12},{8,0},{12,4},{1,9},{5,13},{9,1},{13,5},{2,10},{6,14},... | collective-permute-start | bytes 786440 | tf_op jit(solution)/shard_map/ppermute | solution.py:30
  7.1 4.8 %collective-permute-done.1.refs_8_ = bf16[2,256,256]{2,1,0:T(8,128)(2,1)S(1)} collective-permute-done((bf16[2,256,256]{2,1,0:T(8,128)(2,1)S(1)}, bf16[2,256,256]{2,1,0:T(8,128)(2,1)S(1)}, u32[]{:S(2)}, u32[]{:S(2)}) %collective-permute-start.1) | collective-permute-done | bytes 262176 | tf_op jit(solution)/shard_map/ppermute | solution.py:30
  11.9 1.7 %collective-permute-done.2.refs_6_ = bf16[2,256,256]{2,1,0:T(8,128)(2,1)S(1)} collective-permute-done((bf16[2,256,256]{2,1,0:T(8,128)(2,1)}, bf16[2,256,256]{2,1,0:T(8,128)(2,1)S(1)}, u32[]{:S(2)}, u32[]{:S(2)}) %collective-permute-start.2) | collective-permute-done | bytes 262176 | tf_op jit(solution)/shard_map/ppermute | solution.py:30
  13.6 1.5 %collective-permute-start.3 = (bf16[2,256,256]{2,1,0:T(8,128)(2,1)S(1)}, bf16[2,256,256]{2,1,0:T(8,128)(2,1)S(1)}, u32[]{:S(2)}, u32[]{:S(2)}) collective-permute-start(bf16[2,256,256]{2,1,0:T(8,128)(2,1)S(1)} %collective-permute-done.1.refs_8_), channel_id=1, source_target_pairs={{0,8},{4,12},{8,0},{12,4},{1,9},{5,13},{9,1},{13,5},{2,10},{6,14},... | collective-permute-start | bytes 786440 | tf_op jit(solution)/shard_map/ppermute | solution.py:30
  15.0 1.7 %constant_dynamic-slice_fusion.3 = bf16[2,512,128]{2,1,0:T(8,128)(2,1)} fusion(bf16[2,512,512]{2,1,0:T(8,128)(2,1)} %refs_2_.3, s32[]{:T(128)S(6)} %select_n.31), kind=kLoop, calls=%fused_computation.17 | loop fusion | bytes 524292 | tf_op jit(solution)/shard_map/dynamic_slice | solution.py:274
  17.7 2.7 %collective-permute-done.3.refs_10_ = bf16[2,256,256]{2,1,0:T(8,128)(2,1)S(1)} collective-permute-done((bf16[2,256,256]{2,1,0:T(8,128)(2,1)S(1)}, bf16[2,256,256]{2,1,0:T(8,128)(2,1)S(1)}, u32[]{:S(2)}, u32[]{:S(2)}) %collective-permute-start.3) | collective-permute-done | bytes 262176 | tf_op jit(solution)/shard_map/ppermute | solution.py:30
  20.4 0.7 pad_add_fusion.scalars
  21.1 2.5 %collective-permute-done.refs_3_ = bf16[2,512,128]{2,1,0:T(8,128)(2,1)} collective-permute-done((bf16[2,512,128]{2,1,0:T(8,128)(2,1)}, bf16[2,512,128]{2,1,0:T(8,128)(2,1)}, u32[]{:S(2)}, u32[]{:S(2)}) %collective-permute-start) | collective-permute-done | bytes 262176 | tf_op jit(solution)/shard_map/ppermute | solution.py:30
  23.6 1.0 constant_dynamic-slice_fusion
  25.1 29.3 %shard_map.84 = (bf16[2,512,1024]{2,1,0:T(8,128)(2,1)}, bf16[2,512,1024]{2,1,0:T(8,128)(2,1)}, bf16[2,512,512]{2,1,0:T(8,128)(2,1)}, bf16[2,512,128]{2,1,0:T(8,1...) custom-call(s32[3]{0:T(128)S(1)} %pad_add_fusion.scalars, ...), custom_call_target="tpu_custom_call" | custom-call | flops 19327352832 | bytes 4194304 | tf_op jit(solution)/shard_map/pallas_call | solution.py:241
  54.5 0.7 collective-permute-start.11
  55.2 1.1 %collective-permute-start.12 = (bf16[2,256,256]{2,1,0:T(8,128)(2,1)S(1)}, bf16[2,256,256]{2,1,0:T(8,128)(2,1)S(1)}, u32[]{:S(2)}, u32[]{:S(2)}) collective-permute-start(bf16[2,256,256]{2,1,0:T(8,128)(2,1)S(1)} %bitcast.12), channel_id=1, source_target_pairs={{0,12},{4,8},{8,4},{12,0},{1,13},{5,9},{9,5},{13,1},{2,14},{6,10},... | collective-permute-start | bytes 786440 | tf_op jit(solution)/shard_map/ppermute | solution.py:30
  56.4 1.6 %collective-permute-start.9 = (bf16[2,512,128]{2,1,0:T(8,128)(2,1)S(1)}, bf16[2,512,128]{2,1,0:T(8,128)(2,1)S(1)}, u32[]{:S(2)}, u32[]{:S(2)}) collective-permute-start(bf16[2,512,128]{2,1,0:T(8,128)(2,1)S(1)} %get-tuple-element.32), channel_id=1, source_target_pairs={{0,1},{1,0},{2,3},{3,2},{4,5},{5,4},{6,7},{7,6},{8,9},{9,8},{10,11... | collective-permute-start | bytes 786440 | tf_op jit(solution)/shard_map/ppermute | solution.py:30
  57.9 29.4 %shard_map.85 = (bf16[2,512,1024]{2,1,0:T(8,128)(2,1)}, bf16[2,512,1024]{2,1,0:T(8,128)(2,1)}, bf16[2,512,512]{2,1,0:T(8,128)(2,1)}, bf16[2,512,128]{2,1,0:T(8,1...) custom-call(s32[3]{0:T(128)S(1)} %pad_add_fusion.scalars, ...), custom_call_target="tpu_custom_call", output_to_operand_aliasing={{0}: (13, {}), {1}: (14, {}), {2}: (15, {})} | custom-call | flops 19327352832 | bytes 4194304 | tf_op jit(solution)/shard_map/pallas_call | solution.py:241
  87.5 1.9 %collective-permute-done.14 = bf16[2,2,256,256]{3,2,1,0:T(8,128)(2,1)S(1)} collective-permute-done((bf16[2,2,256,256]{3,2,1,0:T(8,128)(2,1)S(1)}, bf16[2,2,256,256]{3,2,1,0:T(8,128)(2,1)S(1)}, u32[]{:S(2)}, u32[]{:S(2)}) %collective-permute-start.14) | collective-permute-done | bytes 524320 | tf_op jit(solution)/shard_map/ppermute | solution.py:30
  89.5 0.6 collective-permute-start.15
  90.2 0.7 collective-permute-start.16
  90.9 1.4 %collective-permute-start.13 = (bf16[2,512,128]{2,1,0:T(8,128)(2,1)}, bf16[2,512,128]{2,1,0:T(8,128)(2,1)S(1)}, u32[]{:S(2)}, u32[]{:S(2)}) collective-permute-start(bf16[2,512,128]{2,1,0:T(8,128)(2,1)} %get-tuple-element.38), channel_id=1, source_target_pairs={{0,1},{1,0},{2,3},{3,2},{4,5},{5,4},{6,7},{7,6},{8,9},{9,8},{10,11... | collective-permute-start | bytes 786440 | tf_op jit(solution)/shard_map/ppermute | solution.py:30
  92.3 5.5 %collective-permute-done.15 = bf16[2,256,256]{2,1,0:T(8,128)(2,1)S(1)} collective-permute-done((bf16[2,256,256]{2,1,0:T(8,128)(2,1)S(1)}, bf16[2,256,256]{2,1,0:T(8,128)(2,1)S(1)}, u32[]{:S(2)}, u32[]{:S(2)}) %collective-permute-start.15) | collective-permute-done | bytes 262176 | tf_op jit(solution)/shard_map/ppermute | solution.py:30
  98.5 3.8 %collective-permute-done.13 = bf16[2,512,128]{2,1,0:T(8,128)(2,1)S(1)} collective-permute-done((bf16[2,512,128]{2,1,0:T(8,128)(2,1)}, bf16[2,512,128]{2,1,0:T(8,128)(2,1)S(1)}, u32[]{:S(2)}, u32[]{:S(2)}) %collective-permute-start.13) | collective-permute-done | bytes 262176 | tf_op jit(solution)/shard_map/ppermute | solution.py:30
  102.5 1.5 %collective-permute-done.17 = bf16[2,256,128]{2,1,0:T(8,128)(2,1)S(1)} collective-permute-done((bf16[2,256,128]{2,1,0:T(8,128)(2,1)S(1)}, bf16[2,256,128]{2,1,0:T(8,128)(2,1)S(1)}, u32[]{:S(2)}, u32[]{:S(2)}) %collective-permute-start.17) | collective-permute-done | bytes 131104 | tf_op jit(solution)/shard_map/ppermute | solution.py:30
  104.1 1.1 %pad_maximum_fusion = f32[2,256,512]{2,1,0:T(8,128)} fusion(f32[2,256,256]{2,1,0:T(8,128)S(1)} %get-tuple-element.43, f32[2,256,256]{2,1,0:T(8,128)S(1)} %get-tuple-element.42), kind=kLoop, calls=%fused_computation | loop fusion | flops 262144 | bytes 2097152 | tf_op jit(solution)/shard_map/concatenate | solution.py:328
  (41 shorter events, 2.8 us)
Async XLA Ops:
  0.6 24.5 %copy-start = (bf16[2,256,512]{2,1,0:T(8,128)(2,1)S(1)}, bf16[2,256,512]{2,1,0:T(8,128)(2,1)}, u32[]{:S(2)}) copy-start(bf16[2,256,512]{2,1,0:T(8,128)(2,1)} %refs_4_.3) | copy-start | bytes 1572868
  0.6 24.5 %copy-start.1 = (bf16[2,512,512]{2,1,0:T(8,128)(2,1)S(1)}, bf16[2,512,512]{2,1,0:T(8,128)(2,1)}, u32[]{:S(2)}) copy-start(bf16[2,512,512]{2,1,0:T(8,128)(2,1)} %refs_2_.3) | copy-start | bytes 3145732
  2.6 9.3 %collective-permute-start.1 = (bf16[2,256,256]{2,1,0:T(8,128)(2,1)S(1)}, bf16[2,256,256]{2,1,0:T(8,128)(2,1)S(1)}, u32[]{:S(2)}, u32[]{:S(2)}) collective-permute-start(bf16[2,256,256]{2,1,0:T(8,128)(2,1)S(1)} %get-tuple-element.44), channel_id=1, source_target_pairs={{0,1},{1,0},{2,3},{3,2},{4,5},{5,4},{6,7},{7,6},{8,9},{9,8},{10,11... | collective-permute-start | bytes 786440 | tf_op jit(solution)/shard_map/ppermute | solution.py:30
  5.6 8.0 %collective-permute-start.2 = (bf16[2,256,256]{2,1,0:T(8,128)(2,1)}, bf16[2,256,256]{2,1,0:T(8,128)(2,1)S(1)}, u32[]{:S(2)}, u32[]{:S(2)}) collective-permute-start(bf16[2,256,256]{2,1,0:T(8,128)(2,1)} %get-tuple-element.25), channel_id=1, source_target_pairs={{0,8},{4,12},{8,0},{12,4},{1,9},{5,13},{9,1},{13,5},{2,10},{6,14},... | collective-permute-start | bytes 786440 | tf_op jit(solution)/shard_map/ppermute | solution.py:30
  13.6 6.9 %collective-permute-start.3 = (bf16[2,256,256]{2,1,0:T(8,128)(2,1)S(1)}, bf16[2,256,256]{2,1,0:T(8,128)(2,1)S(1)}, u32[]{:S(2)}, u32[]{:S(2)}) collective-permute-start(bf16[2,256,256]{2,1,0:T(8,128)(2,1)S(1)} %collective-permute-done.1.refs_8_), channel_id=1, source_target_pairs={{0,8},{4,12},{8,0},{12,4},{1,9},{5,13},{9,1},{13,5},{2,10},{6,14},... | collective-permute-start | bytes 786440 | tf_op jit(solution)/shard_map/ppermute | solution.py:30
  16.7 6.9 %collective-permute-start = (bf16[2,512,128]{2,1,0:T(8,128)(2,1)}, bf16[2,512,128]{2,1,0:T(8,128)(2,1)}, u32[]{:S(2)}, u32[]{:S(2)}) collective-permute-start(bf16[2,512,128]{2,1,0:T(8,128)(2,1)} %constant_dynamic-slice_fusion.3), channel_id=1, source_target_pairs={{0,1},{1,0},{2,3},{3,2},{4,5},{5,4},{6,7},{7,6},{8,9},{9,8},{10,11... | collective-permute-start | bytes 786440 | tf_op jit(solution)/shard_map/ppermute | solution.py:30
  17.2 7.9 %collective-permute-start.7 = (bf16[2,256,256]{2,1,0:T(8,128)(2,1)S(1)}, bf16[2,256,256]{2,1,0:T(8,128)(2,1)S(1)}, u32[]{:S(2)}, u32[]{:S(2)}) collective-permute-start(bf16[2,256,256]{2,1,0:T(8,128)(2,1)S(1)} %collective-permute-done.1.refs_8_), channel_id=1, source_target_pairs={{0,4},{4,0},{8,12},{12,8},{1,5},{5,1},{9,13},{13,9},{2,6},{6,2},{1... | collective-permute-start | bytes 786440 | tf_op jit(solution)/shard_map/ppermute | solution.py:30
  17.2 7.9 %collective-permute-start.5 = (bf16[2,256,256]{2,1,0:T(8,128)(2,1)}, bf16[2,256,256]{2,1,0:T(8,128)(2,1)S(1)}, u32[]{:S(2)}, u32[]{:S(2)}) collective-permute-start(bf16[2,256,256]{2,1,0:T(8,128)(2,1)} %get-tuple-element.25), channel_id=1, source_target_pairs={{0,4},{4,0},{8,12},{12,8},{1,5},{5,1},{9,13},{13,9},{2,6},{6,2},{1... | collective-permute-start | bytes 786440 | tf_op jit(solution)/shard_map/ppermute | solution.py:30
  17.7 7.4 %collective-permute-start.6 = (bf16[2,256,256]{2,1,0:T(8,128)(2,1)S(1)}, bf16[2,256,256]{2,1,0:T(8,128)(2,1)S(1)}, u32[]{:S(2)}, u32[]{:S(2)}) collective-permute-start(bf16[2,256,256]{2,1,0:T(8,128)(2,1)S(1)} %collective-permute-done.2.refs_6_), channel_id=1, source_target_pairs={{0,4},{4,0},{8,12},{12,8},{1,5},{5,1},{9,13},{13,9},{2,6},{6,2},{1... | collective-permute-start | bytes 786440 | tf_op jit(solution)/shard_map/ppermute | solution.py:30
  20.4 4.7 %collective-permute-start.8 = (bf16[2,256,256]{2,1,0:T(8,128)(2,1)S(1)}, bf16[2,256,256]{2,1,0:T(8,128)(2,1)S(1)}, u32[]{:S(2)}, u32[]{:S(2)}) collective-permute-start(bf16[2,256,256]{2,1,0:T(8,128)(2,1)S(1)} %collective-permute-done.3.refs_10_), channel_id=1, source_target_pairs={{0,4},{4,0},{8,12},{12,8},{1,5},{5,1},{9,13},{13,9},{2,6},{6,2},{1... | collective-permute-start | bytes 786440 | tf_op jit(solution)/shard_map/ppermute | solution.py:30
  24.6 33.4 %collective-permute-start.4 = (bf16[2,512,128]{2,1,0:T(8,128)(2,1)S(1)}, bf16[2,512,128]{2,1,0:T(8,128)(2,1)S(1)}, u32[]{:S(2)}, u32[]{:S(2)}) collective-permute-start(bf16[2,512,128]{2,1,0:T(8,128)(2,1)S(1)} %constant_dynamic-slice_fusion), channel_id=1, source_target_pairs={{0,1},{1,0},{2,3},{3,2},{4,5},{5,4},{6,7},{7,6},{8,9},{9,8},{10,11... | collective-permute-start | bytes 786440 | tf_op jit(solution)/shard_map/ppermute | solution.py:30
  54.5 32.8 %collective-permute-start.10 = (bf16[2,256,256]{2,1,0:T(8,128)(2,1)S(1)}, bf16[2,256,256]{2,1,0:T(8,128)(2,1)S(1)}, u32[]{:S(2)}, u32[]{:S(2)}) collective-permute-start(bf16[2,256,256]{2,1,0:T(8,128)(2,1)S(1)} %bitcast.14), channel_id=1, source_target_pairs={{0,4},{4,0},{8,12},{12,8},{1,5},{5,1},{9,13},{13,9},{2,6},{6,2},{1... | collective-permute-start | bytes 786440 | tf_op jit(solution)/shard_map/ppermute | solution.py:30
  54.5 32.8 %collective-permute-start.11 = (bf16[2,256,256]{2,1,0:T(8,128)(2,1)S(1)}, bf16[2,256,256]{2,1,0:T(8,128)(2,1)S(1)}, u32[]{:S(2)}, u32[]{:S(2)}) collective-permute-start(bf16[2,256,256]{2,1,0:T(8,128)(2,1)S(1)} %bitcast.13), channel_id=1, source_target_pairs={{0,8},{4,12},{8,0},{12,4},{1,9},{5,13},{9,1},{13,5},{2,10},{6,14},... | collective-permute-start | bytes 786440 | tf_op jit(solution)/shard_map/ppermute | solution.py:30
  55.2 32.1 %collective-permute-start.12 = (bf16[2,256,256]{2,1,0:T(8,128)(2,1)S(1)}, bf16[2,256,256]{2,1,0:T(8,128)(2,1)S(1)}, u32[]{:S(2)}, u32[]{:S(2)}) collective-permute-start(bf16[2,256,256]{2,1,0:T(8,128)(2,1)S(1)} %bitcast.12), channel_id=1, source_target_pairs={{0,12},{4,8},{8,4},{12,0},{1,13},{5,9},{9,5},{13,1},{2,14},{6,10},... | collective-permute-start | bytes 786440 | tf_op jit(solution)/shard_map/ppermute | solution.py:30
  56.4 31.0 %collective-permute-start.9 = (bf16[2,512,128]{2,1,0:T(8,128)(2,1)S(1)}, bf16[2,512,128]{2,1,0:T(8,128)(2,1)S(1)}, u32[]{:S(2)}, u32[]{:S(2)}) collective-permute-start(bf16[2,512,128]{2,1,0:T(8,128)(2,1)S(1)} %get-tuple-element.32), channel_id=1, source_target_pairs={{0,1},{1,0},{2,3},{3,2},{4,5},{5,4},{6,7},{7,6},{8,9},{9,8},{10,11... | collective-permute-start | bytes 786440 | tf_op jit(solution)/shard_map/ppermute | solution.py:30
  87.3 2.9 %copy-start.2 = (bf16[2,512,128]{2,1,0:T(8,128)(2,1)}, bf16[2,512,128]{2,1,0:T(8,128)(2,1)S(1)}, u32[]{:S(2)}) copy-start(bf16[2,512,128]{2,1,0:T(8,128)(2,1)S(1)} %collective-permute-done.9) | copy-start | bytes 786436
  87.3 2.0 %collective-permute-start.14 = (bf16[2,2,256,256]{3,2,1,0:T(8,128)(2,1)S(1)}, bf16[2,2,256,256]{3,2,1,0:T(8,128)(2,1)S(1)}, u32[]{:S(2)}, u32[]{:S(2)}) collective-permute-start(bf16[2,2,256,256]{3,2,1,0:T(8,128)(2,1)S(1)} %get-tuple-element.41), channel_id=1, source_target_pairs={{0,4},{4,0},{8,12},{12,8},{1,5},{5,1},{9,13},{13,9},{2,6},{6,2},{1... | collective-permute-start | bytes 1572872 | tf_op jit(solution)/shard_map/ppermute | solution.py:30
  89.5 8.4 %collective-permute-start.15 = (bf16[2,256,256]{2,1,0:T(8,128)(2,1)S(1)}, bf16[2,256,256]{2,1,0:T(8,128)(2,1)S(1)}, u32[]{:S(2)}, u32[]{:S(2)}) collective-permute-start(bf16[2,256,256]{2,1,0:T(8,128)(2,1)S(1)} %fusion.1), channel_id=1, source_target_pairs={{0,8},{4,12},{8,0},{12,4},{1,9},{5,13},{9,1},{13,5},{2,10},{6,14},... | collective-permute-start | bytes 786440 | tf_op jit(solution)/shard_map/ppermute | solution.py:30
  90.1 12.2 %copy-start.4 = (bf16[2,512,512]{2,1,0:T(8,128)(2,1)S(1)}, bf16[2,512,512]{2,1,0:T(8,128)(2,1)}, u32[]{:S(2)}) copy-start(bf16[2,512,512]{2,1,0:T(8,128)(2,1)} %get-tuple-element.31) | copy-start | bytes 3145732
  90.2 12.1 %copy-start.3 = (bf16[2,512,128]{2,1,0:T(8,128)(2,1)S(1)}, bf16[2,512,128]{2,1,0:T(8,128)(2,1)}, u32[]{:S(2)}) copy-start(bf16[2,512,128]{2,1,0:T(8,128)(2,1)} %copy-done.2) | copy-start | bytes 786436
  90.2 12.2 %collective-permute-start.16 = (bf16[2,256,128]{2,1,0:T(8,128)(2,1)S(1)}, bf16[2,256,128]{2,1,0:T(8,128)(2,1)S(1)}, u32[]{:S(2)}, u32[]{:S(2)}) collective-permute-start(bf16[2,256,128]{2,1,0:T(8,128)(2,1)S(1)} %slice.42), channel_id=1, source_target_pairs={{0,1},{1,0},{2,3},{3,2},{4,5},{5,4},{6,7},{7,6},{8,9},{9,8},{10,11... | collective-permute-start | bytes 393224 | tf_op jit(solution)/shard_map/ppermute | solution.py:30
  90.9 11.4 %collective-permute-start.13 = (bf16[2,512,128]{2,1,0:T(8,128)(2,1)}, bf16[2,512,128]{2,1,0:T(8,128)(2,1)S(1)}, u32[]{:S(2)}, u32[]{:S(2)}) collective-permute-start(bf16[2,512,128]{2,1,0:T(8,128)(2,1)} %get-tuple-element.38), channel_id=1, source_target_pairs={{0,1},{1,0},{2,3},{3,2},{4,5},{5,4},{6,7},{7,6},{8,9},{9,8},{10,11... | collective-permute-start | bytes 786440 | tf_op jit(solution)/shard_map/ppermute | solution.py:30
  98.0 6.0 %collective-permute-start.17 = (bf16[2,256,128]{2,1,0:T(8,128)(2,1)S(1)}, bf16[2,256,128]{2,1,0:T(8,128)(2,1)S(1)}, u32[]{:S(2)}, u32[]{:S(2)}) collective-permute-start(bf16[2,256,128]{2,1,0:T(8,128)(2,1)S(1)} %slice.41), channel_id=1, source_target_pairs={{0,1},{1,0},{2,3},{3,2},{4,5},{5,4},{6,7},{7,6},{8,9},{9,8},{10,11... | collective-permute-start | bytes 393224 | tf_op jit(solution)/shard_map/ppermute | solution.py:30
  102.4 2.8 %copy-start.5 = (bf16[2,512,512]{2,1,0:T(8,128)(2,1)}, bf16[2,512,512]{2,1,0:T(8,128)(2,1)S(1)}, u32[]{:S(2)}) copy-start(bf16[2,512,512]{2,1,0:T(8,128)(2,1)S(1)} %maximum_dynamic-update-slice_fusion) | copy-start | bytes 3145732

commit v7 on v6

--- a/solution.py
+++ b/solution.py
@@ -19,7 +19,6 @@
 
 NT = (((1,), (1,)), ((), ()))
 NN = (((1,), (0,)), ((), ()))
-TN = (((0,), (0,)), ((), ()))
 
 
 def dot(a, b, dims):
@@ -39,7 +38,7 @@
     rest = refs[4 + 2 * pieces + n_pass :]
     out_ref, dq_ref, dra_ref, drb_ref, keep_ref = rest[:5]
     send_refs = rest[5 : 5 + len(sends)]
-    k_all, v_all, scores, grad_probs, probs, dscores, acc_k, acc_v, sum_k, sum_v = rest[5 + len(sends) :]
+    k_all, v_all, q_t, do_t, scores, grad_probs, probs, dscores, acc_k, acc_v, sum_k, sum_v = rest[5 + len(sends) :]
 
     r = pl.program_id(0)
     head = pl.program_id(1)
@@ -71,17 +70,32 @@
         acc_k[...] = jnp.zeros_like(acc_k)
         acc_v[...] = jnp.zeros_like(acc_v)
 
+    def score(u):
+        t = slice(max(u - n_prompt, 0), n_query)
+        scores[t, u : u + BLOCK] = dot(q_ref[0, t, :], k_all[u : u + BLOCK, :], NT)
+
+    def grad_prob(u):
+        t = slice(max(u - n_prompt, 0), n_query)
+        grad_probs[t, u : u + BLOCK] = dot(do_ref[0, t, :], v_all[u : u + BLOCK, :], NT)
+
+    def grad_value(u):
+        t = slice(max(u - n_prompt, 0), n_query)
+        acc_v[:, u : u + BLOCK] += dot(do_t[:, t], probs[t, u : u + BLOCK], NN)
+
+    def grad_key(u):
+        t = slice(max(u - n_prompt, 0), n_query)
+        acc_k[:, u : u + BLOCK] += dot(q_t[:, t], dscores[t, u : u + BLOCK], NN)
+
+    def turn():
+        q_t[...] = q_ref[0].T
+        do_t[...] = do_ref[0].T
+
     def stages(i):
         st = {}
         t0 = i * BLOCK
         t = slice(t0, t0 + BLOCK)
-        seen = n_prompt + t0 + BLOCK
-        edge = seen - BLOCK
-        q = q_ref[0, t, :]
-        do = do_ref[0, t, :]
-
-        def score(u):
-            scores[t, u : u + BLOCK] = dot(q, k_all[u : u + BLOCK, :], NT)
+        edge = n_prompt + t0
+        seen = edge + BLOCK
 
         def softmax(row):
             at = slice(t0 + row, t0 + row + STRIP)
@@ -97,13 +111,10 @@
                 scores[at, u] = part
                 probs[at, u] = part.astype(jnp.bfloat16)
 
-        def grad_prob(u):
-            grad_probs[t, u : u + BLOCK] = dot(do, v_all[u : u + BLOCK, :], NT)
-
         def output():
             o = dot(probs[t, :seen], v_all[:seen, :], NN)
             out_ref[0, t, :] = o.astype(jnp.bfloat16)
-            st["delta"] = jnp.sum(o * do.astype(jnp.float32), axis=1, keepdims=True)
+            st["delta"] = jnp.sum(o * do_ref[0, t, :].astype(jnp.float32), axis=1, keepdims=True)
 
         def grad_score(row):
             at = slice(t0 + row, t0 + row + STRIP)
@@ -114,36 +125,29 @@
         def query():
             dq_ref[0, t, :] = dot(dscores[t, :seen], k_all[:seen, :], NN).astype(jnp.bfloat16)
 
-        blocks = range(0, seen, BLOCK)
         strips = range(0, BLOCK, STRIP)
-        each = lambda f, xs: [functools.partial(f, x) for x in xs]
-        return [
-            each(score, blocks),
-            each(softmax, strips),
-            each(grad_prob, blocks) + [output],
-            each(grad_score, strips),
-            [query],
-        ]
-
-    def mix(lists):
-        steps = [((at + 0.5) / len(x), k, f) for k, x in enumerate(lists) for at, f in enumerate(x)]
-        return [f for _, _, f in sorted(steps, key=lambda e: e[:2])]
+        each = lambda f: [functools.partial(f, x) for x in strips]
+        return {"softmax": each(softmax), "output": [output], "grad": each(grad_score), "query": [query]}
+
+    def mix(*lists):
+        order = [((at + 0.5) / len(x), k, f) for k, x in enumerate(lists) for at, f in enumerate(x)]
+        for _, _, f in sorted(order, key=lambda e: e[:2]):
+            f()
 
     plan = [stages(i) for i in range(n_blocks)]
-    depth = len(plan[0])
-    for slot in range(depth + n_blocks - 1):
-        for step in mix([plan[i][slot - i] for i in range(n_blocks) if 0 <= slot - i < depth]):
-            step()
-
-    q_all = q_ref[0]
-    do_all = do_ref[0]
-    for u in range(0, n_prompt + n_query, BLOCK):
-        t0 = max(u - n_prompt, 0)
-        acc_v[u : u + BLOCK, :] += dot(probs[t0:, u : u + BLOCK], do_all[t0:], TN)
-        acc_k[u : u + BLOCK, :] += dot(dscores[t0:, u : u + BLOCK], q_all[t0:], TN)
+    over = lambda f: [functools.partial(f, u) for u in range(0, n_prompt + n_query, BLOCK)]
+    mix(over(score), [turn])
+    mix(plan[0]["softmax"], over(grad_prob))
+    for i in range(1, n_blocks):
+        mix(plan[i]["softmax"], plan[i - 1]["output"])
+        mix(plan[i - 1]["grad"], plan[i]["output"] if i == n_blocks - 1 else [])
+    if n_blocks == 1:
+        mix(plan[0]["output"])
+    mix(plan[-1]["grad"], *[p["query"] for p in plan[:-1]], over(grad_value))
+    mix(plan[-1]["query"], over(grad_key))
 
     def respond(ref, acc):
-        ref[0] = acc[n_prompt:, :].astype(jnp.bfloat16)
+        ref[0] = acc[:, n_prompt:].T.astype(jnp.bfloat16)
 
     @pl.when(last & even)
     def _():
@@ -158,13 +162,13 @@
     @pl.when(last & (r == 0))
     def _():
         for whole, acc in ((sum_k, acc_k), (sum_v, acc_v)):
-            whole[prompt] = acc[:n_prompt, :]
+            whole[prompt] = acc[:, :n_prompt].T
             whole[1 - prompt] = jnp.zeros((n_prompt, HD), jnp.float32)
 
     @pl.when(last & (r > 0))
     def _():
         for whole, acc in ((sum_k, acc_k), (sum_v, acc_v)):
-            whole[prompt] += acc[:n_prompt, :]
+            whole[prompt] += acc[:, :n_prompt].T
 
     done = last & (r == n_resp - 1)
 
@@ -228,12 +232,14 @@
     scratch = [
         pltpu.VMEM((n_keys, HD), jnp.bfloat16),
         pltpu.VMEM((n_keys, HD), jnp.bfloat16),
+        pltpu.VMEM((HD, n_query), jnp.bfloat16),
+        pltpu.VMEM((HD, n_query), jnp.bfloat16),
         pltpu.VMEM((n_query, n_keys), jnp.float32),
         pltpu.VMEM((n_query, n_keys), jnp.float32),
         pltpu.VMEM((n_query, n_keys), jnp.bfloat16),
         pltpu.VMEM((n_query, n_keys), jnp.bfloat16),
-        pltpu.VMEM((n_keys, HD), jnp.float32),
-        pltpu.VMEM((n_keys, HD), jnp.float32),
+        pltpu.VMEM((HD, n_keys), jnp.float32),
+        pltpu.VMEM((HD, n_keys), jnp.float32),
         pltpu.VMEM((P_SIZE, n_prompt, HD), jnp.float32),
         pltpu.VMEM((P_SIZE, n_prompt, HD), jnp.float32),
     ]
@@ -254,6 +260,39 @@
     )(scalars, *args)
 
 
+def pack_kernel(n_own, n_resp, scalars, prompt_ref, resp_ref, *rest):
+    outs, sems = rest[:-1], rest[-1]
+    own = scalars[n_resp] * n_own
+    theirs = (1 - scalars[n_resp]) * n_own
+    copies = []
+    for h in range(n_own):
+        for ref, at in ((prompt_ref, own + h), (prompt_ref, theirs + h), (resp_ref, theirs + h)):
+            lanes = pl.ds(pl.multiple_of(at * HD, HD), HD)
+            k = len(copies)
+            copies.append(pltpu.make_async_copy(ref.at[:, :, lanes], outs[k], sems.at[k]))
+    for copy in copies:
+        copy.start()
+    for copy in copies:
+        copy.wait()
+
+
+def pack(scalars, prompt_kv, resp_kv, n_own):
+    shape = lambda x: jax.ShapeDtypeStruct(x.shape[:2] + (HD,), x.dtype)
+    anywhere = pl.BlockSpec(memory_space=pltpu.HBM)
+    return pl.pallas_call(
+        functools.partial(pack_kernel, n_own, resp_kv.shape[0]),
+        grid_spec=pltpu.PrefetchScalarGridSpec(
+            num_scalar_prefetch=1,
+            grid=(1,),
+            in_specs=[anywhere, anywhere],
+            out_specs=[anywhere] * (3 * n_own),
+            scratch_shapes=[pltpu.SemaphoreType.DMA((3 * n_own,))],
+        ),
+        out_shape=[shape(prompt_kv), shape(prompt_kv), shape(resp_kv)] * n_own,
+        compiler_params=pltpu.CompilerParams(vmem_limit_bytes=60 * 2**20),
+    )(scalars, prompt_kv, resp_kv)
+
+
 def per_device(queries, resp_kv, prompt_kv, prompt_of, d_out):
     pair_heads = prompt_kv.shape[2] // HD
     parity = lax.axis_index("prefix") % 2
@@ -265,43 +304,43 @@
 
 def whole_heads(queries, resp_kv, prompt_kv, scalars, parity, d_out):
     n_own = prompt_kv.shape[2] // HD // 2
-    width = n_own * HD
     z = functools.partial(swap, axis="prefix", step=1)
     core, x, both = [functools.partial(swap, axis="dp", step=k) for k in (1, 2, 3)]
-    own, theirs = parity * n_own, (1 - parity) * n_own
-
-    def columns(array, which, count):
-        return lax.dynamic_slice_in_dim(array, which * HD, count * HD, axis=2)
+    theirs = (1 - parity) * n_own
 
     def order(values, done):
         return lax.optimization_barrier((tuple(values), tuple(done)))[0]
 
-    b0 = z(columns(prompt_kv, theirs, n_own))
-    a0 = columns(prompt_kv, own, n_own)
-    a2 = x(a0)
-    resp_b = [z(columns(resp_kv, theirs, 1))]
-    a0, b0 = order([a0, b0], [a2])
-    b2 = x(b0)
-    pa = [a0, core(a0), a2, core(a2)]
-    pb = [b0, core(b0), b2, core(b2)]
-    for h in range(1, n_own):
-        (later,) = order([resp_kv], [resp_b[h - 1], b2])
-        resp_b.append(z(columns(later, theirs + h, 1)))
+    packed = pack(scalars, prompt_kv, resp_kv, n_own)
+    pa, pb, resp_b = [], [], []
+    for h in range(n_own):
+        a0, b0, rb = packed[3 * h : 3 * h + 3]
+        if h > 0:
+            (b0,) = order([b0], [pb[h - 1][0]])
+            (a0,) = order([a0], [pb[h - 1][2]])
+            (rb,) = order([rb], [resp_b[h - 1]])
+        b0 = z(b0)
+        a2 = x(a0)
+        resp_b.append(z(rb))
+        (ready,) = order([b0], [a2])
+        b2 = x(ready)
+        pa.append([a0, core(a0), a2, core(a2)])
+        pb.append([b0, core(b0), b2, core(b2) if h == 0 else None])
 
     shared = None
     d_resp, d_prompt = [], []
     for h in range(n_own):
         final = h == n_own - 1
         here = lambda par, h=h: par * n_own + h
-        at = lambda par, h=h: h
+        at = lambda par: 0
         att, dq, dra, drb, keep, *sends = attend(
             scalars,
             queries,
             d_out,
             (resp_kv, here),
-            (resp_b[h], lambda par: 0),
-            [(prompt_kv, here)] + [(a, at) for a in pa[1:]],
-            [(b, at) for b in pb],
+            (resp_b[h], at),
+            [(prompt_kv, here)] + [(a, at) for a in pa[h][1:]],
+            [(b, at) for b in pb[h]],
             (0, 2) if final else (0,),
             ((1, 3),) if final else ((1,), (2,), (3,)),
             h,
@@ -309,22 +348,24 @@
             shared,
         )
         shared = (att, dq, dra)
+        d_resp.append(z(drb))
+        if not final:
+            pb[h + 1][3] = core(order([pb[h + 1][2]], [drb])[0])
         if final:
-            (send, drb) = order([sends[0], drb], arrived)
+            (send,) = order([sends[0]], arrived)
             sums = keep + core(send).astype(jnp.float32)
-            total = sums[0] + x(sums[1].astype(jnp.bfloat16)).astype(jnp.float32)
-            d_resp.append(z(drb))
+            (across,) = order([x(sums[1].astype(jnp.bfloat16))], [d_resp[-1], *[b for _, b in d_prompt]])
+            total = sums[0] + across.astype(jnp.float32)
         else:
             parts = [move(part[0]) for move, part in zip((core, x, both), sends)]
-            d_resp.append(z(drb))
             arrived = [*parts, d_resp[-1]]
             total = keep[0] + sum(p.astype(jnp.float32) for p in parts)
         other = z(total[:, :, HD:].astype(jnp.bfloat16))
-        d_prompt.append((total[:, :, :HD], other.astype(jnp.float32)))
+        d_prompt.append((total[:, :, :HD], other))
 
     even = parity == 0
     mine = jnp.concatenate([a for a, _ in d_prompt], axis=-1)
-    other = jnp.concatenate([b for _, b in d_prompt], axis=-1)
+    other = jnp.concatenate([b.astype(jnp.float32) for _, b in d_prompt], axis=-1)
     d_prompt = jnp.concatenate([jnp.where(even, mine, other), jnp.where(even, other, mine)], axis=-1)
     att, dq, d_resp_kv = shared
     received = jnp.concatenate(d_resp, axis=-1)

time: 105 us -> 132 us (1.26)
  Pallas kernels: 58.7 us -> 84.2 us
  starting transfers between devices: 14.3 us -> 22.5 us
  waiting for transfers between devices: 24.4 us -> 18.3 us
  local copies, waits for them, and re-layouts: 4.65 us -> 3.05 us
    pallas_call x0 -> x1, Pallas kernels: none -> 33.6 us  [pack(): pl.pallas_call(functools.partial(pack_kernel, n_own, resp_kv.shape[0]), g...]
    ppermute x18 -> x25, starting transfers between devices: 14.3 us -> 22.5 us  [swap(): lax.ppermute(block, axis, [(i, i ^ step) for i in range(lax.axis_size(axi...]
    pallas_call x2, Pallas kernels: 58.7 us -> 50.6 us  [attend(): pl.pallas_call(functools.partial(attend_kernel, (pieces, rows, keep, send...]
    ppermute x18 -> x25, waiting for transfers between devices: 24.4 us -> 18.3 us  [swap(): lax.ppermute(block, axis, [(i, i ^ step) for i in range(lax.axis_size(axi...]
    dynamic_slice x3 -> x0, local copies, waits for them, and re-layouts: 4.52 us -> none  [columns(): return lax.dynamic_slice_in_dim(array, which * HD, count * HD, axis=2)]
    unnamed x12 -> x10, local copies, waits for them, and re-layouts: 0.03 us -> 2.94 us
  transfers between devices with their start and end apart: 18 -> 25, of which waited for: 8 -> 6; matrix products, arithmetic and copies ran while one was open for 4% -> 0% of each run, Pallas kernels for 56% -> 38%
where the time goes in v7:
time: 132 us
  Pallas kernels  84.2 us (64%)
  starting transfers between devices  22.5 us (17%)
  waiting for transfers between devices  18.3 us (14%)
  local copies, waits for them, and re-layouts  3.05 us (2%)
  other arithmetic  2.91 us (2%)
    pallas_call x2, Pallas kernels, attend(): pl.pallas_call(functools.partial(attend_kernel, (pieces, rows, keep, send...  50.6 us
    pallas_call x1, Pallas kernels, pack(): pl.pallas_call(functools.partial(pack_kernel, n_own, resp_kv.shape[0]), g...  33.6 us
    ppermute x25, starting transfers between devices, swap(): lax.ppermute(block, axis, [(i, i ^ step) for i in range(lax.axis_size(axi...  22.5 us
    ppermute x25, waiting for transfers between devices, swap(): lax.ppermute(block, axis, [(i, i ^ step) for i in range(lax.axis_size(axi...  18.3 us
    unnamed x10, local copies, waits for them, and re-layouts  2.94 us
  transfers between devices with their start and end apart: 25, of which 6 were waited for; matrix products, arithmetic and copies ran while one was open for 0% of the time, Pallas kernels for 38%

profile of v7, /device:TPU:0, one launch (start us, length us, event | category | flops | bytes accessed | tf_op | source)
XLA Modules:
  0.0 131.7 jit_solution(7583671041493211964)
XLA Ops:
  0.6 1.3 pad_add_fusion.scalars
  1.9 33.6 %shard_map.84 = (bf16[2,256,128]{2,1,0:T(8,128)(2,1)}, bf16[2,256,128]{2,1,0:T(8,128)(2,1)}, bf16[2,512,128]{2,1,0:T(8,128)(2,1)}, bf16[2,256,128]{2,1,0:T(8,128...) custom-call(s32[3]{0:T(128)} %pad_add_fusion.scalars, bf16[2,256,512]{2,1,0:T(8,128)(2,1)} %refs_4_.3, ...), custom_call_target="tpu_custom_call" | custom-call | tf_op jit(solution)/shard_map/pallas_call | solution.py:282
  35.5 3.1 %collective-permute-start.2 = (bf16[2,256,128]{2,1,0:T(8,128)(2,1)}, bf16[2,256,128]{2,1,0:T(8,128)(2,1)S(1)}, u32[]{:S(2)}, u32[]{:S(2)}) collective-permute-start(bf16[2,256,128]{2,1,0:T(8,128)(2,1)} %get-tuple-element.36), channel_id=1, source_target_pairs={{0,1},{1,0},{2,3},{3,2},{4,5},{5,4},{6,7},{7,6},{8,9},{9,8},{10,11... | collective-permute-start | bytes 393224 | tf_op jit(solution)/shard_map/ppermute | solution.py:29
  38.6 1.5 %collective-permute-start.3 = (bf16[2,256,128]{2,1,0:T(8,128)(2,1)}, bf16[2,256,128]{2,1,0:T(8,128)(2,1)S(1)}, u32[]{:S(2)}, u32[]{:S(2)}) collective-permute-start(bf16[2,256,128]{2,1,0:T(8,128)(2,1)} %get-tuple-element.37), channel_id=1, source_target_pairs={{0,8},{4,12},{8,0},{12,4},{1,9},{5,13},{9,1},{13,5},{2,10},{6,14},... | collective-permute-start | bytes 393224 | tf_op jit(solution)/shard_map/ppermute | solution.py:29
  40.6 2.3 %collective-permute-done.2.refs_8_ = bf16[2,256,128]{2,1,0:T(8,128)(2,1)S(1)} collective-permute-done((bf16[2,256,128]{2,1,0:T(8,128)(2,1)}, bf16[2,256,128]{2,1,0:T(8,128)(2,1)S(1)}, u32[]{:S(2)}, u32[]{:S(2)}) %collective-permute-start.2) | collective-permute-done | bytes 131104 | tf_op jit(solution)/shard_map/ppermute | solution.py:29
  42.8 1.0 collective-permute-done.3.refs_6_
  43.8 1.5 %collective-permute-start.4 = (bf16[2,256,128]{2,1,0:T(8,128)(2,1)S(1)}, bf16[2,256,128]{2,1,0:T(8,128)(2,1)S(1)}, u32[]{:S(2)}, u32[]{:S(2)}) collective-permute-start(bf16[2,256,128]{2,1,0:T(8,128)(2,1)S(1)} %collective-permute-done.2.refs_8_), channel_id=1, source_target_pairs={{0,8},{4,12},{8,0},{12,4},{1,9},{5,13},{9,1},{13,5},{2,10},{6,14},... | collective-permute-start | bytes 393224 | tf_op jit(solution)/shard_map/ppermute | solution.py:29
  45.3 1.4 %collective-permute-start.8 = (bf16[2,256,128]{2,1,0:T(8,128)(2,1)}, bf16[2,256,128]{2,1,0:T(8,128)(2,1)S(1)}, u32[]{:S(2)}, u32[]{:S(2)}) collective-permute-start(bf16[2,256,128]{2,1,0:T(8,128)(2,1)} %get-tuple-element.41), channel_id=1, source_target_pairs={{0,1},{1,0},{2,3},{3,2},{4,5},{5,4},{6,7},{7,6},{8,9},{9,8},{10,11... | collective-permute-start | bytes 393224 | tf_op jit(solution)/shard_map/ppermute | solution.py:29
  46.7 2.1 %collective-permute-done.4.refs_10_ = bf16[2,256,128]{2,1,0:T(8,128)(2,1)S(1)} collective-permute-done((bf16[2,256,128]{2,1,0:T(8,128)(2,1)S(1)}, bf16[2,256,128]{2,1,0:T(8,128)(2,1)S(1)}, u32[]{:S(2)}, u32[]{:S(2)}) %collective-permute-start.4) | collective-permute-done | bytes 131104 | tf_op jit(solution)/shard_map/ppermute | solution.py:29
  48.8 1.5 %collective-permute-start.6 = (bf16[2,256,128]{2,1,0:T(8,128)(2,1)}, bf16[2,256,128]{2,1,0:T(8,128)(2,1)S(1)}, u32[]{:S(2)}, u32[]{:S(2)}) collective-permute-start(bf16[2,256,128]{2,1,0:T(8,128)(2,1)} %get-tuple-element.39), channel_id=1, source_target_pairs={{0,8},{4,12},{8,0},{12,4},{1,9},{5,13},{9,1},{13,5},{2,10},{6,14},... | collective-permute-start | bytes 393224 | tf_op jit(solution)/shard_map/ppermute | solution.py:29
  51.3 2.7 %collective-permute-done.6.refs_6_ = bf16[2,256,128]{2,1,0:T(8,128)(2,1)S(1)} collective-permute-done((bf16[2,256,128]{2,1,0:T(8,128)(2,1)}, bf16[2,256,128]{2,1,0:T(8,128)(2,1)S(1)}, u32[]{:S(2)}, u32[]{:S(2)}) %collective-permute-start.6) | collective-permute-done | bytes 131104 | tf_op jit(solution)/shard_map/ppermute | solution.py:29
  54.0 1.5 %collective-permute-start.1 = (bf16[2,512,128]{2,1,0:T(8,128)(2,1)}, bf16[2,512,128]{2,1,0:T(8,128)(2,1)S(1)}, u32[]{:S(2)}, u32[]{:S(2)}) collective-permute-start(bf16[2,512,128]{2,1,0:T(8,128)(2,1)} %get-tuple-element.34), channel_id=1, source_target_pairs={{0,1},{1,0},{2,3},{3,2},{4,5},{5,4},{6,7},{7,6},{8,9},{9,8},{10,11... | collective-permute-start | bytes 786440 | tf_op jit(solution)/shard_map/ppermute | solution.py:29
  55.7 1.6 %collective-permute-start.10 = (bf16[2,256,128]{2,1,0:T(8,128)(2,1)S(1)}, bf16[2,256,128]{2,1,0:T(8,128)(2,1)S(1)}, u32[]{:S(2)}, u32[]{:S(2)}) collective-permute-start(bf16[2,256,128]{2,1,0:T(8,128)(2,1)S(1)} %collective-permute-done.8.refs_8_), channel_id=1, source_target_pairs={{0,8},{4,12},{8,0},{12,4},{1,9},{5,13},{9,1},{13,5},{2,10},{6,14},... | collective-permute-start | bytes 393224 | tf_op jit(solution)/shard_map/ppermute | solution.py:29
  57.3 1.2 copy-done
  58.5 1.0 copy-done.1
  60.3 25.3 %shard_map.85 = (bf16[2,512,1024]{2,1,0:T(8,128)(2,1)}, bf16[2,512,1024]{2,1,0:T(8,128)(2,1)}, bf16[2,512,512]{2,1,0:T(8,128)(2,1)}, bf16[2,512,128]{2,1,0:T(8,1...) custom-call(s32[3]{0:T(128)S(1)} %copy-done.2, ...), custom_call_target="tpu_custom_call" | custom-call | flops 19327352832 | bytes 4194304 | tf_op jit(solution)/shard_map/pallas_call | solution.py:247
  87.1 1.2 collective-permute-start.20
  88.4 25.3 %shard_map.86 = (bf16[2,512,1024]{2,1,0:T(8,128)(2,1)}, bf16[2,512,1024]{2,1,0:T(8,128)(2,1)}, bf16[2,512,512]{2,1,0:T(8,128)(2,1)}, bf16[2,512,128]{2,1,0:T(8,1...) custom-call(s32[3]{0:T(128)S(1)} %copy-done.2, ...), custom_call_target="tpu_custom_call", output_to_operand_aliasing={{0}: (13, {}), {1}: (14, {}), {2}: (15, {})} | custom-call | flops 19327352832 | bytes 4194304 | tf_op jit(solution)/shard_map/pallas_call | solution.py:247
  114.1 1.6 %collective-permute-start.17 = (bf16[2,512,128]{2,1,0:T(8,128)(2,1)S(1)}, bf16[2,512,128]{2,1,0:T(8,128)(2,1)S(1)}, u32[]{:S(2)}, u32[]{:S(2)}) collective-permute-start(bf16[2,512,128]{2,1,0:T(8,128)(2,1)S(1)} %get-tuple-element.51), channel_id=1, source_target_pairs={{0,1},{1,0},{2,3},{3,2},{4,5},{5,4},{6,7},{7,6},{8,9},{9,8},{10,11... | collective-permute-start | bytes 786440 | tf_op jit(solution)/shard_map/ppermute | solution.py:29
  116.6 1.6 %collective-permute-start.23 = (bf16[2,256,128]{2,1,0:T(8,128)(2,1)S(1)}, bf16[2,256,128]{2,1,0:T(8,128)(2,1)S(1)}, u32[]{:S(2)}, u32[]{:S(2)}) collective-permute-start(bf16[2,256,128]{2,1,0:T(8,128)(2,1)S(1)} %slice.42), channel_id=1, source_target_pairs={{0,1},{1,0},{2,3},{3,2},{4,5},{5,4},{6,7},{7,6},{8,9},{9,8},{10,11... | collective-permute-start | bytes 393224 | tf_op jit(solution)/shard_map/ppermute | solution.py:29
  118.2 7.1 %collective-permute-done.23 = bf16[2,256,128]{2,1,0:T(8,128)(2,1)S(1)} collective-permute-done((bf16[2,256,128]{2,1,0:T(8,128)(2,1)S(1)}, bf16[2,256,128]{2,1,0:T(8,128)(2,1)S(1)}, u32[]{:S(2)}, u32[]{:S(2)}) %collective-permute-start.23) | collective-permute-done | bytes 131104 | tf_op jit(solution)/shard_map/ppermute | solution.py:29
  125.4 1.7 %collective-permute-start.24 = (bf16[2,256,128]{2,1,0:T(8,128)(2,1)S(1)}, bf16[2,256,128]{2,1,0:T(8,128)(2,1)S(1)}, u32[]{:S(2)}, u32[]{:S(2)}) collective-permute-start(bf16[2,256,128]{2,1,0:T(8,128)(2,1)S(1)} %slice.41), channel_id=1, source_target_pairs={{0,1},{1,0},{2,3},{3,2},{4,5},{5,4},{6,7},{7,6},{8,9},{9,8},{10,11... | collective-permute-start | bytes 393224 | tf_op jit(solution)/shard_map/ppermute | solution.py:29
  127.3 3.2 %collective-permute-done.24 = bf16[2,256,128]{2,1,0:T(8,128)(2,1)S(1)} collective-permute-done((bf16[2,256,128]{2,1,0:T(8,128)(2,1)S(1)}, bf16[2,256,128]{2,1,0:T(8,128)(2,1)S(1)}, u32[]{:S(2)}, u32[]{:S(2)}) %collective-permute-start.24) | collective-permute-done | bytes 131104 | tf_op jit(solution)/shard_map/ppermute | solution.py:29
  130.5 1.1 pad_maximum_fusion
  (51 shorter events, 5.5 us)
Async XLA Ops:
  35.5 7.3 %collective-permute-start.2 = (bf16[2,256,128]{2,1,0:T(8,128)(2,1)}, bf16[2,256,128]{2,1,0:T(8,128)(2,1)S(1)}, u32[]{:S(2)}, u32[]{:S(2)}) collective-permute-start(bf16[2,256,128]{2,1,0:T(8,128)(2,1)} %get-tuple-element.36), channel_id=1, source_target_pairs={{0,1},{1,0},{2,3},{3,2},{4,5},{5,4},{6,7},{7,6},{8,9},{9,8},{10,11... | collective-permute-start | bytes 393224 | tf_op jit(solution)/shard_map/ppermute | solution.py:29
  38.6 5.2 %collective-permute-start.3 = (bf16[2,256,128]{2,1,0:T(8,128)(2,1)}, bf16[2,256,128]{2,1,0:T(8,128)(2,1)S(1)}, u32[]{:S(2)}, u32[]{:S(2)}) collective-permute-start(bf16[2,256,128]{2,1,0:T(8,128)(2,1)} %get-tuple-element.37), channel_id=1, source_target_pairs={{0,8},{4,12},{8,0},{12,4},{1,9},{5,13},{9,1},{13,5},{2,10},{6,14},... | collective-permute-start | bytes 393224 | tf_op jit(solution)/shard_map/ppermute | solution.py:29
  40.1 10.7 %collective-permute-start = (bf16[2,512,128]{2,1,0:T(8,128)(2,1)}, bf16[2,512,128]{2,1,0:T(8,128)(2,1)S(1)}, u32[]{:S(2)}, u32[]{:S(2)}) collective-permute-start(bf16[2,512,128]{2,1,0:T(8,128)(2,1)} %get-tuple-element.33), channel_id=1, source_target_pairs={{0,1},{1,0},{2,3},{3,2},{4,5},{5,4},{6,7},{7,6},{8,9},{9,8},{10,11... | collective-permute-start | bytes 786440 | tf_op jit(solution)/shard_map/ppermute | solution.py:29
  43.8 5.0 %collective-permute-start.4 = (bf16[2,256,128]{2,1,0:T(8,128)(2,1)S(1)}, bf16[2,256,128]{2,1,0:T(8,128)(2,1)S(1)}, u32[]{:S(2)}, u32[]{:S(2)}) collective-permute-start(bf16[2,256,128]{2,1,0:T(8,128)(2,1)S(1)} %collective-permute-done.2.refs_8_), channel_id=1, source_target_pairs={{0,8},{4,12},{8,0},{12,4},{1,9},{5,13},{9,1},{13,5},{2,10},{6,14},... | collective-permute-start | bytes 393224 | tf_op jit(solution)/shard_map/ppermute | solution.py:29
  45.3 5.5 %collective-permute-start.8 = (bf16[2,256,128]{2,1,0:T(8,128)(2,1)}, bf16[2,256,128]{2,1,0:T(8,128)(2,1)S(1)}, u32[]{:S(2)}, u32[]{:S(2)}) collective-permute-start(bf16[2,256,128]{2,1,0:T(8,128)(2,1)} %get-tuple-element.41), channel_id=1, source_target_pairs={{0,1},{1,0},{2,3},{3,2},{4,5},{5,4},{6,7},{7,6},{8,9},{9,8},{10,11... | collective-permute-start | bytes 393224 | tf_op jit(solution)/shard_map/ppermute | solution.py:29
  48.8 5.2 %collective-permute-start.6 = (bf16[2,256,128]{2,1,0:T(8,128)(2,1)}, bf16[2,256,128]{2,1,0:T(8,128)(2,1)S(1)}, u32[]{:S(2)}, u32[]{:S(2)}) collective-permute-start(bf16[2,256,128]{2,1,0:T(8,128)(2,1)} %get-tuple-element.39), channel_id=1, source_target_pairs={{0,8},{4,12},{8,0},{12,4},{1,9},{5,13},{9,1},{13,5},{2,10},{6,14},... | collective-permute-start | bytes 393224 | tf_op jit(solution)/shard_map/ppermute | solution.py:29
  50.3 3.7 %collective-permute-start.11 = (bf16[2,256,128]{2,1,0:T(8,128)(2,1)}, bf16[2,256,128]{2,1,0:T(8,128)(2,1)S(1)}, u32[]{:S(2)}, u32[]{:S(2)}) collective-permute-start(bf16[2,256,128]{2,1,0:T(8,128)(2,1)} %get-tuple-element.37), channel_id=1, source_target_pairs={{0,4},{4,0},{8,12},{12,8},{1,5},{5,1},{9,13},{13,9},{2,6},{6,2},{1... | collective-permute-start | bytes 393224 | tf_op jit(solution)/shard_map/ppermute | solution.py:29
  50.3 5.2 %collective-permute-start.13 = (bf16[2,256,128]{2,1,0:T(8,128)(2,1)S(1)}, bf16[2,256,128]{2,1,0:T(8,128)(2,1)S(1)}, u32[]{:S(2)}, u32[]{:S(2)}) collective-permute-start(bf16[2,256,128]{2,1,0:T(8,128)(2,1)S(1)} %collective-permute-done.2.refs_8_), channel_id=1, source_target_pairs={{0,4},{4,0},{8,12},{12,8},{1,5},{5,1},{9,13},{13,9},{2,6},{6,2},{1... | collective-permute-start | bytes 393224 | tf_op jit(solution)/shard_map/ppermute | solution.py:29
  50.8 5.0 %collective-permute-start.12 = (bf16[2,256,128]{2,1,0:T(8,128)(2,1)S(1)}, bf16[2,256,128]{2,1,0:T(8,128)(2,1)S(1)}, u32[]{:S(2)}, u32[]{:S(2)}) collective-permute-start(bf16[2,256,128]{2,1,0:T(8,128)(2,1)S(1)} %collective-permute-done.3.refs_6_), channel_id=1, source_target_pairs={{0,4},{4,0},{8,12},{12,8},{1,5},{5,1},{9,13},{13,9},{2,6},{6,2},{1... | collective-permute-start | bytes 393224 | tf_op jit(solution)/shard_map/ppermute | solution.py:29
  50.8 6.5 %collective-permute-start.14 = (bf16[2,256,128]{2,1,0:T(8,128)(2,1)S(1)}, bf16[2,256,128]{2,1,0:T(8,128)(2,1)S(1)}, u32[]{:S(2)}, u32[]{:S(2)}) collective-permute-start(bf16[2,256,128]{2,1,0:T(8,128)(2,1)S(1)} %collective-permute-done.4.refs_10_), channel_id=1, source_target_pairs={{0,4},{4,0},{8,12},{12,8},{1,5},{5,1},{9,13},{13,9},{2,6},{6,2},{1... | collective-permute-start | bytes 393224 | tf_op jit(solution)/shard_map/ppermute | solution.py:29
  54.0 32.5 %collective-permute-start.5 = (bf16[2,256,128]{2,1,0:T(8,128)(2,1)}, bf16[2,256,128]{2,1,0:T(8,128)(2,1)S(1)}, u32[]{:S(2)}, u32[]{:S(2)}) collective-permute-start(bf16[2,256,128]{2,1,0:T(8,128)(2,1)} %get-tuple-element.39), channel_id=1, source_target_pairs={{0,4},{4,0},{8,12},{12,8},{1,5},{5,1},{9,13},{13,9},{2,6},{6,2},{1... | collective-permute-start | bytes 393224 | tf_op jit(solution)/shard_map/ppermute | solution.py:29
  54.0 33.2 %collective-permute-start.1 = (bf16[2,512,128]{2,1,0:T(8,128)(2,1)}, bf16[2,512,128]{2,1,0:T(8,128)(2,1)S(1)}, u32[]{:S(2)}, u32[]{:S(2)}) collective-permute-start(bf16[2,512,128]{2,1,0:T(8,128)(2,1)} %get-tuple-element.34), channel_id=1, source_target_pairs={{0,1},{1,0},{2,3},{3,2},{4,5},{5,4},{6,7},{7,6},{8,9},{9,8},{10,11... | collective-permute-start | bytes 786440 | tf_op jit(solution)/shard_map/ppermute | solution.py:29
  55.5 30.6 %collective-permute-start.9 = (bf16[2,256,128]{2,1,0:T(8,128)(2,1)S(1)}, bf16[2,256,128]{2,1,0:T(8,128)(2,1)S(1)}, u32[]{:S(2)}, u32[]{:S(2)}) collective-permute-start(bf16[2,256,128]{2,1,0:T(8,128)(2,1)S(1)} %collective-permute-done.8.refs_8_), channel_id=1, source_target_pairs={{0,4},{4,0},{8,12},{12,8},{1,5},{5,1},{9,13},{13,9},{2,6},{6,2},{1... | collective-permute-start | bytes 393224 | tf_op jit(solution)/shard_map/ppermute | solution.py:29
  55.7 29.8 %collective-permute-start.10 = (bf16[2,256,128]{2,1,0:T(8,128)(2,1)S(1)}, bf16[2,256,128]{2,1,0:T(8,128)(2,1)S(1)}, u32[]{:S(2)}, u32[]{:S(2)}) collective-permute-start(bf16[2,256,128]{2,1,0:T(8,128)(2,1)S(1)} %collective-permute-done.8.refs_8_), channel_id=1, source_target_pairs={{0,8},{4,12},{8,0},{12,4},{1,9},{5,13},{9,1},{13,5},{2,10},{6,14},... | collective-permute-start | bytes 393224 | tf_op jit(solution)/shard_map/ppermute | solution.py:29
  57.3 29.2 %collective-permute-start.7 = (bf16[2,256,128]{2,1,0:T(8,128)(2,1)S(1)}, bf16[2,256,128]{2,1,0:T(8,128)(2,1)S(1)}, u32[]{:S(2)}, u32[]{:S(2)}) collective-permute-start(bf16[2,256,128]{2,1,0:T(8,128)(2,1)S(1)} %collective-permute-done.6.refs_6_), channel_id=1, source_target_pairs={{0,4},{4,0},{8,12},{12,8},{1,5},{5,1},{9,13},{13,9},{2,6},{6,2},{1... | collective-permute-start | bytes 393224 | tf_op jit(solution)/shard_map/ppermute | solution.py:29
  85.5 2.8 %collective-permute-start.15 = (bf16[2,256,128]{2,1,0:T(8,128)(2,1)S(1)}, bf16[2,256,128]{2,1,0:T(8,128)(2,1)S(1)}, u32[]{:S(2)}, u32[]{:S(2)}) collective-permute-start(bf16[2,256,128]{2,1,0:T(8,128)(2,1)S(1)} %collective-permute-done.10.refs_10_), channel_id=1, source_target_pairs={{0,4},{4,0},{8,12},{12,8},{1,5},{5,1},{9,13},{13,9},{2,6},{6,2},{1... | collective-permute-start | bytes 393224 | tf_op jit(solution)/shard_map/ppermute | solution.py:29
  86.1 27.6 %collective-permute-start.16 = (bf16[2,512,128]{2,1,0:T(8,128)(2,1)S(1)}, bf16[2,512,128]{2,1,0:T(8,128)(2,1)S(1)}, u32[]{:S(2)}, u32[]{:S(2)}) collective-permute-start(bf16[2,512,128]{2,1,0:T(8,128)(2,1)S(1)} %get-tuple-element.43), channel_id=1, source_target_pairs={{0,1},{1,0},{2,3},{3,2},{4,5},{5,4},{6,7},{7,6},{8,9},{9,8},{10,11... | collective-permute-start | bytes 786440 | tf_op jit(solution)/shard_map/ppermute | solution.py:29
  86.5 27.2 %collective-permute-start.18 = (bf16[2,256,256]{2,1,0:T(8,128)(2,1)S(1)}, bf16[2,256,256]{2,1,0:T(8,128)(2,1)S(1)}, u32[]{:S(2)}, u32[]{:S(2)}) collective-permute-start(bf16[2,256,256]{2,1,0:T(8,128)(2,1)S(1)} %bitcast.14), channel_id=1, source_target_pairs={{0,4},{4,0},{8,12},{12,8},{1,5},{5,1},{9,13},{13,9},{2,6},{6,2},{1... | collective-permute-start | bytes 786440 | tf_op jit(solution)/shard_map/ppermute | solution.py:29
  86.5 27.2 %collective-permute-start.19 = (bf16[2,256,256]{2,1,0:T(8,128)(2,1)S(1)}, bf16[2,256,256]{2,1,0:T(8,128)(2,1)S(1)}, u32[]{:S(2)}, u32[]{:S(2)}) collective-permute-start(bf16[2,256,256]{2,1,0:T(8,128)(2,1)S(1)} %bitcast.13), channel_id=1, source_target_pairs={{0,8},{4,12},{8,0},{12,4},{1,9},{5,13},{9,1},{13,5},{2,10},{6,14},... | collective-permute-start | bytes 786440 | tf_op jit(solution)/shard_map/ppermute | solution.py:29
  87.1 26.6 %collective-permute-start.20 = (bf16[2,256,256]{2,1,0:T(8,128)(2,1)S(1)}, bf16[2,256,256]{2,1,0:T(8,128)(2,1)S(1)}, u32[]{:S(2)}, u32[]{:S(2)}) collective-permute-start(bf16[2,256,256]{2,1,0:T(8,128)(2,1)S(1)} %bitcast.12), channel_id=1, source_target_pairs={{0,12},{4,8},{8,4},{12,0},{1,13},{5,9},{9,5},{13,1},{2,14},{6,10},... | collective-permute-start | bytes 786440 | tf_op jit(solution)/shard_map/ppermute | solution.py:29
  114.1 11.2 %collective-permute-start.17 = (bf16[2,512,128]{2,1,0:T(8,128)(2,1)S(1)}, bf16[2,512,128]{2,1,0:T(8,128)(2,1)S(1)}, u32[]{:S(2)}, u32[]{:S(2)}) collective-permute-start(bf16[2,512,128]{2,1,0:T(8,128)(2,1)S(1)} %get-tuple-element.51), channel_id=1, source_target_pairs={{0,1},{1,0},{2,3},{3,2},{4,5},{5,4},{6,7},{7,6},{8,9},{9,8},{10,11... | collective-permute-start | bytes 786440 | tf_op jit(solution)/shard_map/ppermute | solution.py:29
  115.9 9.4 %collective-permute-start.22 = (bf16[2,256,256]{2,1,0:T(8,128)(2,1)S(1)}, bf16[2,256,256]{2,1,0:T(8,128)(2,1)S(1)}, u32[]{:S(2)}, u32[]{:S(2)}) collective-permute-start(bf16[2,256,256]{2,1,0:T(8,128)(2,1)S(1)} %fusion.1), channel_id=1, source_target_pairs={{0,8},{4,12},{8,0},{12,4},{1,9},{5,13},{9,1},{13,5},{2,10},{6,14},... | collective-permute-start | bytes 786440 | tf_op jit(solution)/shard_map/ppermute | solution.py:29
  116.6 8.7 %collective-permute-start.23 = (bf16[2,256,128]{2,1,0:T(8,128)(2,1)S(1)}, bf16[2,256,128]{2,1,0:T(8,128)(2,1)S(1)}, u32[]{:S(2)}, u32[]{:S(2)}) collective-permute-start(bf16[2,256,128]{2,1,0:T(8,128)(2,1)S(1)} %slice.42), channel_id=1, source_target_pairs={{0,1},{1,0},{2,3},{3,2},{4,5},{5,4},{6,7},{7,6},{8,9},{9,8},{10,11... | collective-permute-start | bytes 393224 | tf_op jit(solution)/shard_map/ppermute | solution.py:29
  125.4 5.0 %collective-permute-start.24 = (bf16[2,256,128]{2,1,0:T(8,128)(2,1)S(1)}, bf16[2,256,128]{2,1,0:T(8,128)(2,1)S(1)}, u32[]{:S(2)}, u32[]{:S(2)}) collective-permute-start(bf16[2,256,128]{2,1,0:T(8,128)(2,1)S(1)} %slice.41), channel_id=1, source_target_pairs={{0,1},{1,0},{2,3},{3,2},{4,5},{5,4},{6,7},{7,6},{8,9},{9,8},{10,11... | collective-permute-start | bytes 393224 | tf_op jit(solution)/shard_map/ppermute | solution.py:29
  (6 other events, 20.0 us)

commit v8 on v7

--- a/solution.py
+++ b/solution.py
@@ -189,7 +189,7 @@
         scatter(1, sum_k)
 
 
-def attend(scalars, queries, d_out, resp_a, resp_b, prompt_a, prompt_b, keep, sends, chunk, heads, shared):
+def attend(scalars, queries, d_out, resp_a, resp_b, prompt_a, prompt_b, keep, sends, chunk, heads, shared, own):
     n_resp, n_query, _ = queries.shape
     pieces = len(prompt_a)
     rows = prompt_a[0][0].shape[1]
@@ -219,14 +219,14 @@
     out_specs = [
         q_spec,
         q_spec,
-        pl.BlockSpec((1, n_query, HD), resp_map(resp_a[1])),
+        pl.BlockSpec((1, n_query, HD), resp_map(own[1])),
         pl.BlockSpec((1, n_query, HD), lambda r, j, sc: (r, 0, 0)),
     ]
     out_specs += [pl.BlockSpec(g.shape, lambda r, j, sc: (0, 0, 0, 0)) for g in grads]
     out_shape = [
         shape(queries.shape, jnp.bfloat16),
         shape(queries.shape, jnp.bfloat16),
-        shape(resp_a[0].shape, jnp.bfloat16),
+        shape(own[0].shape, jnp.bfloat16),
         shape((n_resp, n_query, HD), jnp.bfloat16),
     ] + grads
     scratch = [
@@ -260,36 +260,40 @@
     )(scalars, *args)
 
 
-def pack_kernel(n_own, n_resp, scalars, prompt_ref, resp_ref, *rest):
-    outs, sems = rest[:-1], rest[-1]
-    own = scalars[n_resp] * n_own
-    theirs = (1 - scalars[n_resp]) * n_own
-    copies = []
-    for h in range(n_own):
-        for ref, at in ((prompt_ref, own + h), (prompt_ref, theirs + h), (resp_ref, theirs + h)):
-            lanes = pl.ds(pl.multiple_of(at * HD, HD), HD)
-            k = len(copies)
-            copies.append(pltpu.make_async_copy(ref.at[:, :, lanes], outs[k], sems.at[k]))
-    for copy in copies:
-        copy.start()
-    for copy in copies:
-        copy.wait()
+def pack_kernel(n_own, n_resp, scalars, prompt_ref, resp_ref, *outs):
+    width = n_own * HD
+
+    def split(own):
+        for h in range(n_own):
+            mine = slice(own + h * HD, own + (h + 1) * HD)
+            theirs = slice(width - own + h * HD, width - own + (h + 1) * HD)
+            for k, (ref, lanes) in enumerate(
+                ((prompt_ref, mine), (prompt_ref, theirs), (resp_ref, mine), (resp_ref, theirs))
+            ):
+                outs[4 * h + k][...] = ref[:, :, lanes]
+
+    @pl.when(scalars[n_resp] == 0)
+    def _():
+        split(0)
+
+    @pl.when(scalars[n_resp] != 0)
+    def _():
+        split(width)
 
 
 def pack(scalars, prompt_kv, resp_kv, n_own):
-    shape = lambda x: jax.ShapeDtypeStruct(x.shape[:2] + (HD,), x.dtype)
-    anywhere = pl.BlockSpec(memory_space=pltpu.HBM)
+    block = lambda shape: pl.BlockSpec(shape, lambda i, sc: (0, 0, 0))
+    shapes = [x.shape[:2] + (HD,) for x in (prompt_kv, prompt_kv, resp_kv, resp_kv)] * n_own
     return pl.pallas_call(
         functools.partial(pack_kernel, n_own, resp_kv.shape[0]),
         grid_spec=pltpu.PrefetchScalarGridSpec(
             num_scalar_prefetch=1,
             grid=(1,),
-            in_specs=[anywhere, anywhere],
-            out_specs=[anywhere] * (3 * n_own),
-            scratch_shapes=[pltpu.SemaphoreType.DMA((3 * n_own,))],
+            in_specs=[block(prompt_kv.shape), block(resp_kv.shape)],
+            out_specs=[block(s) for s in shapes],
         ),
-        out_shape=[shape(prompt_kv), shape(prompt_kv), shape(resp_kv)] * n_own,
-        compiler_params=pltpu.CompilerParams(vmem_limit_bytes=60 * 2**20),
+        out_shape=[jax.ShapeDtypeStruct(s, prompt_kv.dtype) for s in shapes],
+        compiler_params=pltpu.CompilerParams(vmem_limit_bytes=48 * 2**20),
     )(scalars, prompt_kv, resp_kv)
 
 
@@ -312,19 +316,21 @@
         return lax.optimization_barrier((tuple(values), tuple(done)))[0]
 
     packed = pack(scalars, prompt_kv, resp_kv, n_own)
-    pa, pb, resp_b = [], [], []
+    pa, pb, resp_a, resp_b = [], [], [], []
     for h in range(n_own):
-        a0, b0, rb = packed[3 * h : 3 * h + 3]
+        a0, b0, ra, rb = packed[4 * h : 4 * h + 4]
         if h > 0:
-            (b0,) = order([b0], [pb[h - 1][0]])
-            (a0,) = order([a0], [pb[h - 1][2]])
             (rb,) = order([rb], [resp_b[h - 1]])
         b0 = z(b0)
         a2 = x(a0)
+        resp_a.append(ra)
         resp_b.append(z(rb))
-        (ready,) = order([b0], [a2])
+        if h == 0:
+            (ready,) = order([b0], [a2])
+        else:
+            (ready,) = order([b0], [pb[0][2]])
         b2 = x(ready)
-        pa.append([a0, core(a0), a2, core(a2)])
+        pa.append([a0, core(a0), a2, core(a2) if h == 0 else None])
         pb.append([b0, core(b0), b2, core(b2) if h == 0 else None])
 
     shared = None
@@ -337,20 +343,21 @@
             scalars,
             queries,
             d_out,
-            (resp_kv, here),
+            (resp_a[h], at),
             (resp_b[h], at),
-            [(prompt_kv, here)] + [(a, at) for a in pa[h][1:]],
+            [(a, at) for a in pa[h]],
             [(b, at) for b in pb[h]],
             (0, 2) if final else (0,),
             ((1, 3),) if final else ((1,), (2,), (3,)),
             h,
             GROUP,
             shared,
+            (resp_kv, here),
         )
         shared = (att, dq, dra)
         d_resp.append(z(drb))
         if not final:
-            pb[h + 1][3] = core(order([pb[h + 1][2]], [drb])[0])
+            pa[h + 1][3], pb[h + 1][3] = [core(v) for v in order([pa[h + 1][2], pb[h + 1][2]], [drb])]
         if final:
             (send,) = order([sends[0]], arrived)
             sums = keep + core(send).astype(jnp.float32)
@@ -391,6 +398,7 @@
         0,
         queries.shape[2] // HD,
         None,
+        (resp_kv, first),
     )
     d_resp = (dra.astype(jnp.float32) + swap(drb, "prefix", 1).astype(jnp.float32)).astype(jnp.bfloat16)
     other = swap(keep[0, :, :, HD:].astype(jnp.bfloat16), "prefix", 1)

time: 132 us -> 96.7 us (0.73)
  Pallas kernels: 84.2 us -> 51.4 us
  waiting for transfers between devices: 18.3 us -> 15 us
    pallas_call x1, Pallas kernels: 33.6 us -> 0.82 us  [pack(): pl.pallas_call(functools.partial(pack_kernel, n_own, resp_kv.shape[0]), g...]
    ppermute x25, waiting for transfers between devices: 18.3 us -> 15 us  [swap(): lax.ppermute(block, axis, [(i, i ^ step) for i in range(lax.axis_size(axi...]
  transfers between devices with their start and end apart: 25 -> 25, of which waited for: 6 -> 7; matrix products, arithmetic and copies ran while one was open for 0% -> 0% of each run, Pallas kernels for 38% -> 52%
where the time goes in v8:
time: 96.7 us; the launch traced here: 96.4 us
  Pallas kernels  51.4 us (53%)
  starting transfers between devices  22.8 us (24%)
  waiting for transfers between devices  15 us (16%)
  local copies, waits for them, and re-layouts  3.97 us (4%)
  other arithmetic  2.36 us (2%)
    pallas_call x2, Pallas kernels, attend(): pl.pallas_call(functools.partial(attend_kernel, (pieces, rows, keep, send...  50.6 us
    ppermute x25, starting transfers between devices, swap(): lax.ppermute(block, axis, [(i, i ^ step) for i in range(lax.axis_size(axi...  22.8 us
    ppermute x25, waiting for transfers between devices, swap(): lax.ppermute(block, axis, [(i, i ^ step) for i in range(lax.axis_size(axi...  15 us
    unnamed x10, local copies, waits for them, and re-layouts  3.87 us
  transfers between devices with their start and end apart: 25, of which 7 were waited for; matrix products, arithmetic and copies ran while one was open for 0% of the time, Pallas kernels for 52%

profile of v8, /device:TPU:0, one launch (start us, length us, event | category | flops | bytes accessed | tf_op | source)
XLA Modules:
  0.0 96.4 jit_solution(6280789357311150174)
XLA Ops:
  1.4 1.2 %copy-done = bf16[2,512,512]{2,1,0:T(8,128)(2,1)S(1)} copy-done((bf16[2,512,512]{2,1,0:T(8,128)(2,1)S(1)}, bf16[2,512,512]{2,1,0:T(8,128)(2,1)}, u32[]{:S(2)}) %copy-start) | copy-done | bytes 1048600
  2.6 1.0 %copy-done.1 = bf16[2,256,512]{2,1,0:T(8,128)(2,1)S(1)} copy-done((bf16[2,256,512]{2,1,0:T(8,128)(2,1)S(1)}, bf16[2,256,512]{2,1,0:T(8,128)(2,1)}, u32[]{:S(2)}) %copy-start.1) | copy-done | bytes 524312
  4.5 3.1 %collective-permute-start.5 = (bf16[2,256,128]{2,1,0:T(8,128)(2,1)S(1)}, bf16[2,256,128]{2,1,0:T(8,128)(2,1)S(1)}, u32[]{:S(2)}, u32[]{:S(2)}) collective-permute-start(bf16[2,256,128]{2,1,0:T(8,128)(2,1)S(1)} %get-tuple-element.39), channel_id=1, source_target_pairs={{0,1},{1,0},{2,3},{3,2},{4,5},{5,4},{6,7},{7,6},{8,9},{9,8},{10,11... | collective-permute-start | bytes 393224 | tf_op jit(solution)/shard_map/ppermute | solution.py:29
  7.6 1.5 %collective-permute-start.6 = (bf16[2,256,128]{2,1,0:T(8,128)(2,1)S(1)}, bf16[2,256,128]{2,1,0:T(8,128)(2,1)S(1)}, u32[]{:S(2)}, u32[]{:S(2)}) collective-permute-start(bf16[2,256,128]{2,1,0:T(8,128)(2,1)S(1)} %get-tuple-element.40.refs_4_), channel_id=1, source_target_pairs={{0,8},{4,12},{8,0},{12,4},{1,9},{5,13},{9,1},{13,5},{2,10},{6,14},... | collective-permute-start | bytes 393224 | tf_op jit(solution)/shard_map/ppermute | solution.py:29
  9.5 2.0 %collective-permute-done.5.refs_8_ = bf16[2,256,128]{2,1,0:T(8,128)(2,1)S(1)} collective-permute-done((bf16[2,256,128]{2,1,0:T(8,128)(2,1)S(1)}, bf16[2,256,128]{2,1,0:T(8,128)(2,1)S(1)}, u32[]{:S(2)}, u32[]{:S(2)}) %collective-permute-start.5) | collective-permute-done | bytes 131104 | tf_op jit(solution)/shard_map/ppermute | solution.py:29
  11.5 1.1 %collective-permute-done.6.refs_6_ = bf16[2,256,128]{2,1,0:T(8,128)(2,1)S(1)} collective-permute-done((bf16[2,256,128]{2,1,0:T(8,128)(2,1)S(1)}, bf16[2,256,128]{2,1,0:T(8,128)(2,1)S(1)}, u32[]{:S(2)}, u32[]{:S(2)}) %collective-permute-start.6) | collective-permute-done | bytes 131104 | tf_op jit(solution)/shard_map/ppermute | solution.py:29
  12.5 1.5 %collective-permute-start.7 = (bf16[2,256,128]{2,1,0:T(8,128)(2,1)S(1)}, bf16[2,256,128]{2,1,0:T(8,128)(2,1)S(1)}, u32[]{:S(2)}, u32[]{:S(2)}) collective-permute-start(bf16[2,256,128]{2,1,0:T(8,128)(2,1)S(1)} %collective-permute-done.5.refs_8_), channel_id=1, source_target_pairs={{0,8},{4,12},{8,0},{12,4},{1,9},{5,13},{9,1},{13,5},{2,10},{6,14},... | collective-permute-start | bytes 393224 | tf_op jit(solution)/shard_map/ppermute | solution.py:29
  14.0 1.4 %collective-permute-start.4 = (bf16[2,256,128]{2,1,0:T(8,128)(2,1)S(1)}, bf16[2,256,128]{2,1,0:T(8,128)(2,1)S(1)}, u32[]{:S(2)}, u32[]{:S(2)}) collective-permute-start(bf16[2,256,128]{2,1,0:T(8,128)(2,1)S(1)} %get-tuple-element.38), channel_id=1, source_target_pairs={{0,1},{1,0},{2,3},{3,2},{4,5},{5,4},{6,7},{7,6},{8,9},{9,8},{10,11... | collective-permute-start | bytes 393224 | tf_op jit(solution)/shard_map/ppermute | solution.py:29
  15.9 2.1 %collective-permute-done.refs_3_ = bf16[2,512,128]{2,1,0:T(8,128)(2,1)S(1)} collective-permute-done((bf16[2,512,128]{2,1,0:T(8,128)(2,1)S(1)}, bf16[2,512,128]{2,1,0:T(8,128)(2,1)S(1)}, u32[]{:S(2)}, u32[]{:S(2)}) %collective-permute-start) | collective-permute-done | bytes 262176 | tf_op jit(solution)/shard_map/ppermute | solution.py:29
  18.6 0.9 collective-permute-done.4.refs_8_
  19.5 1.7 %collective-permute-start.3 = (bf16[2,256,128]{2,1,0:T(8,128)(2,1)S(1)}, bf16[2,256,128]{2,1,0:T(8,128)(2,1)S(1)}, u32[]{:S(2)}, u32[]{:S(2)}) collective-permute-start(bf16[2,256,128]{2,1,0:T(8,128)(2,1)S(1)} %get-tuple-element.37.refs_4_), channel_id=1, source_target_pairs={{0,8},{4,12},{8,0},{12,4},{1,9},{5,13},{9,1},{13,5},{2,10},{6,14},... | collective-permute-start | bytes 393224 | tf_op jit(solution)/shard_map/ppermute | solution.py:29
  21.4 1.6 %collective-permute-start.1 = (bf16[2,512,128]{2,1,0:T(8,128)(2,1)S(1)}, bf16[2,512,128]{2,1,0:T(8,128)(2,1)S(1)}, u32[]{:S(2)}, u32[]{:S(2)}) collective-permute-start(bf16[2,512,128]{2,1,0:T(8,128)(2,1)S(1)} %get-tuple-element.36), channel_id=1, source_target_pairs={{0,1},{1,0},{2,3},{3,2},{4,5},{5,4},{6,7},{7,6},{8,9},{9,8},{10,11... | collective-permute-start | bytes 786440 | tf_op jit(solution)/shard_map/ppermute | solution.py:29
  23.5 1.6 %copy-done.2 = bf16[2,512,1024]{2,1,0:T(8,128)(2,1)S(1)} copy-done((bf16[2,512,1024]{2,1,0:T(8,128)(2,1)S(1)}, bf16[2,512,1024]{2,1,0:T(8,128)(2,1)}, u32[]{:S(2)}) %copy-start.2) | copy-done | bytes 2097176
  25.1 25.3 %shard_map.85 = (bf16[2,512,1024]{2,1,0:T(8,128)(2,1)}, bf16[2,512,1024]{2,1,0:T(8,128)(2,1)}, bf16[2,512,512]{2,1,0:T(8,128)(2,1)}, bf16[2,512,128]{2,1,0:T(8,1...) custom-call(s32[3]{0:T(128)S(1)} %pad_add_fusion.scalars, ...), custom_call_target="tpu_custom_call" | custom-call | flops 19327352832 | bytes 4194304 | tf_op jit(solution)/shard_map/pallas_call | solution.py:247
  51.2 1.7 %collective-permute-start.19 = (bf16[2,256,256]{2,1,0:T(8,128)(2,1)S(1)}, bf16[2,256,256]{2,1,0:T(8,128)(2,1)S(1)}, u32[]{:S(2)}, u32[]{:S(2)}) collective-permute-start(bf16[2,256,256]{2,1,0:T(8,128)(2,1)S(1)} %bitcast.13), channel_id=1, source_target_pairs={{0,8},{4,12},{8,0},{12,4},{1,9},{5,13},{9,1},{13,5},{2,10},{6,14},... | collective-permute-start | bytes 786440 | tf_op jit(solution)/shard_map/ppermute | solution.py:29
  53.1 25.3 %shard_map.86 = (bf16[2,512,1024]{2,1,0:T(8,128)(2,1)}, bf16[2,512,1024]{2,1,0:T(8,128)(2,1)}, bf16[2,512,512]{2,1,0:T(8,128)(2,1)}, bf16[2,512,128]{2,1,0:T(8,1...) custom-call(s32[3]{0:T(128)S(1)} %pad_add_fusion.scalars, ...), custom_call_target="tpu_custom_call", output_to_operand_aliasing={{0}: (13, {}), {1}: (14, {}), {2}: (15, {})} | custom-call | flops 19327352832 | bytes 4194304 | tf_op jit(solution)/shard_map/pallas_call | solution.py:247
  78.9 1.7 %collective-permute-start.17 = (bf16[2,512,128]{2,1,0:T(8,128)(2,1)S(1)}, bf16[2,512,128]{2,1,0:T(8,128)(2,1)S(1)}, u32[]{:S(2)}, u32[]{:S(2)}) collective-permute-start(bf16[2,512,128]{2,1,0:T(8,128)(2,1)S(1)} %get-tuple-element.53), channel_id=1, source_target_pairs={{0,1},{1,0},{2,3},{3,2},{4,5},{5,4},{6,7},{7,6},{8,9},{9,8},{10,11... | collective-permute-start | bytes 786440 | tf_op jit(solution)/shard_map/ppermute | solution.py:29
  80.8 1.6 %collective-permute-start.22 = (bf16[2,256,256]{2,1,0:T(8,128)(2,1)S(1)}, bf16[2,256,256]{2,1,0:T(8,128)(2,1)S(1)}, u32[]{:S(2)}, u32[]{:S(2)}) collective-permute-start(bf16[2,256,256]{2,1,0:T(8,128)(2,1)S(1)} %fusion.1), channel_id=1, source_target_pairs={{0,8},{4,12},{8,0},{12,4},{1,9},{5,13},{9,1},{13,5},{2,10},{6,14},... | collective-permute-start | bytes 786440 | tf_op jit(solution)/shard_map/ppermute | solution.py:29
  82.5 1.6 %collective-permute-start.23 = (bf16[2,256,128]{2,1,0:T(8,128)(2,1)S(1)}, bf16[2,256,128]{2,1,0:T(8,128)(2,1)S(1)}, u32[]{:S(2)}, u32[]{:S(2)}) collective-permute-start(bf16[2,256,128]{2,1,0:T(8,128)(2,1)S(1)} %slice.42), channel_id=1, source_target_pairs={{0,1},{1,0},{2,3},{3,2},{4,5},{5,4},{6,7},{7,6},{8,9},{9,8},{10,11... | collective-permute-start | bytes 393224 | tf_op jit(solution)/shard_map/ppermute | solution.py:29
  84.1 3.9 %collective-permute-done.17 = bf16[2,512,128]{2,1,0:T(8,128)(2,1)S(1)} collective-permute-done((bf16[2,512,128]{2,1,0:T(8,128)(2,1)S(1)}, bf16[2,512,128]{2,1,0:T(8,128)(2,1)S(1)}, u32[]{:S(2)}, u32[]{:S(2)}) %collective-permute-start.17) | collective-permute-done | bytes 262176 | tf_op jit(solution)/shard_map/ppermute | solution.py:29
  88.0 2.0 %collective-permute-done.23 = bf16[2,256,128]{2,1,0:T(8,128)(2,1)S(1)} collective-permute-done((bf16[2,256,128]{2,1,0:T(8,128)(2,1)S(1)}, bf16[2,256,128]{2,1,0:T(8,128)(2,1)S(1)}, u32[]{:S(2)}, u32[]{:S(2)}) %collective-permute-start.23) | collective-permute-done | bytes 131104 | tf_op jit(solution)/shard_map/ppermute | solution.py:29
  90.1 1.8 %collective-permute-start.24 = (bf16[2,256,128]{2,1,0:T(8,128)(2,1)S(1)}, bf16[2,256,128]{2,1,0:T(8,128)(2,1)S(1)}, u32[]{:S(2)}, u32[]{:S(2)}) collective-permute-start(bf16[2,256,128]{2,1,0:T(8,128)(2,1)S(1)} %slice.41), channel_id=1, source_target_pairs={{0,1},{1,0},{2,3},{3,2},{4,5},{5,4},{6,7},{7,6},{8,9},{9,8},{10,11... | collective-permute-start | bytes 393224 | tf_op jit(solution)/shard_map/ppermute | solution.py:29
  92.1 3.0 %collective-permute-done.24 = bf16[2,256,128]{2,1,0:T(8,128)(2,1)S(1)} collective-permute-done((bf16[2,256,128]{2,1,0:T(8,128)(2,1)S(1)}, bf16[2,256,128]{2,1,0:T(8,128)(2,1)S(1)}, u32[]{:S(2)}, u32[]{:S(2)}) %collective-permute-start.24) | collective-permute-done | bytes 131104 | tf_op jit(solution)/shard_map/ppermute | solution.py:29
  95.3 1.1 %pad_maximum_fusion = f32[2,256,512]{2,1,0:T(8,128)} fusion(f32[2,256,256]{2,1,0:T(8,128)S(1)} %get-tuple-element.63, f32[2,256,256]{2,1,0:T(8,128)S(1)} %get-tuple-element.62), kind=kLoop, calls=%fused_computation | loop fusion | flops 262144 | bytes 2097152 | tf_op jit(solution)/shard_map/concatenate | solution.py:376
  (51 shorter events, 5.9 us)
Async XLA Ops:
  4.5 7.0 %collective-permute-start.5 = (bf16[2,256,128]{2,1,0:T(8,128)(2,1)S(1)}, bf16[2,256,128]{2,1,0:T(8,128)(2,1)S(1)}, u32[]{:S(2)}, u32[]{:S(2)}) collective-permute-start(bf16[2,256,128]{2,1,0:T(8,128)(2,1)S(1)} %get-tuple-element.39), channel_id=1, source_target_pairs={{0,1},{1,0},{2,3},{3,2},{4,5},{5,4},{6,7},{7,6},{8,9},{9,8},{10,11... | collective-permute-start | bytes 393224 | tf_op jit(solution)/shard_map/ppermute | solution.py:29
  7.6 5.0 %collective-permute-start.6 = (bf16[2,256,128]{2,1,0:T(8,128)(2,1)S(1)}, bf16[2,256,128]{2,1,0:T(8,128)(2,1)S(1)}, u32[]{:S(2)}, u32[]{:S(2)}) collective-permute-start(bf16[2,256,128]{2,1,0:T(8,128)(2,1)S(1)} %get-tuple-element.40.refs_4_), channel_id=1, source_target_pairs={{0,8},{4,12},{8,0},{12,4},{1,9},{5,13},{9,1},{13,5},{2,10},{6,14},... | collective-permute-start | bytes 393224 | tf_op jit(solution)/shard_map/ppermute | solution.py:29
  9.0 9.0 %collective-permute-start = (bf16[2,512,128]{2,1,0:T(8,128)(2,1)S(1)}, bf16[2,512,128]{2,1,0:T(8,128)(2,1)S(1)}, u32[]{:S(2)}, u32[]{:S(2)}) collective-permute-start(bf16[2,512,128]{2,1,0:T(8,128)(2,1)S(1)} %get-tuple-element.35), channel_id=1, source_target_pairs={{0,1},{1,0},{2,3},{3,2},{4,5},{5,4},{6,7},{7,6},{8,9},{9,8},{10,11... | collective-permute-start | bytes 786440 | tf_op jit(solution)/shard_map/ppermute | solution.py:29
  12.5 5.6 %collective-permute-start.7 = (bf16[2,256,128]{2,1,0:T(8,128)(2,1)S(1)}, bf16[2,256,128]{2,1,0:T(8,128)(2,1)S(1)}, u32[]{:S(2)}, u32[]{:S(2)}) collective-permute-start(bf16[2,256,128]{2,1,0:T(8,128)(2,1)S(1)} %collective-permute-done.5.refs_8_), channel_id=1, source_target_pairs={{0,8},{4,12},{8,0},{12,4},{1,9},{5,13},{9,1},{13,5},{2,10},{6,14},... | collective-permute-start | bytes 393224 | tf_op jit(solution)/shard_map/ppermute | solution.py:29
  14.0 5.5 %collective-permute-start.4 = (bf16[2,256,128]{2,1,0:T(8,128)(2,1)S(1)}, bf16[2,256,128]{2,1,0:T(8,128)(2,1)S(1)}, u32[]{:S(2)}, u32[]{:S(2)}) collective-permute-start(bf16[2,256,128]{2,1,0:T(8,128)(2,1)S(1)} %get-tuple-element.38), channel_id=1, source_target_pairs={{0,1},{1,0},{2,3},{3,2},{4,5},{5,4},{6,7},{7,6},{8,9},{9,8},{10,11... | collective-permute-start | bytes 393224 | tf_op jit(solution)/shard_map/ppermute | solution.py:29
  15.4 4.0 %collective-permute-start.9 = (bf16[2,256,128]{2,1,0:T(8,128)(2,1)S(1)}, bf16[2,256,128]{2,1,0:T(8,128)(2,1)S(1)}, u32[]{:S(2)}, u32[]{:S(2)}) collective-permute-start(bf16[2,256,128]{2,1,0:T(8,128)(2,1)S(1)} %get-tuple-element.40.refs_4_), channel_id=1, source_target_pairs={{0,4},{4,0},{8,12},{12,8},{1,5},{5,1},{9,13},{13,9},{2,6},{6,2},{1... | collective-permute-start | bytes 393224 | tf_op jit(solution)/shard_map/ppermute | solution.py:29
  15.4 5.7 %collective-permute-start.10 = (bf16[2,256,128]{2,1,0:T(8,128)(2,1)S(1)}, bf16[2,256,128]{2,1,0:T(8,128)(2,1)S(1)}, u32[]{:S(2)}, u32[]{:S(2)}) collective-permute-start(bf16[2,256,128]{2,1,0:T(8,128)(2,1)S(1)} %collective-permute-done.6.refs_6_), channel_id=1, source_target_pairs={{0,4},{4,0},{8,12},{12,8},{1,5},{5,1},{9,13},{13,9},{2,6},{6,2},{1... | collective-permute-start | bytes 393224 | tf_op jit(solution)/shard_map/ppermute | solution.py:29
  18.1 3.3 %collective-permute-start.11 = (bf16[2,256,128]{2,1,0:T(8,128)(2,1)S(1)}, bf16[2,256,128]{2,1,0:T(8,128)(2,1)S(1)}, u32[]{:S(2)}, u32[]{:S(2)}) collective-permute-start(bf16[2,256,128]{2,1,0:T(8,128)(2,1)S(1)} %collective-permute-done.5.refs_8_), channel_id=1, source_target_pairs={{0,4},{4,0},{8,12},{12,8},{1,5},{5,1},{9,13},{13,9},{2,6},{6,2},{1... | collective-permute-start | bytes 393224 | tf_op jit(solution)/shard_map/ppermute | solution.py:29
  18.1 4.9 %collective-permute-start.12 = (bf16[2,256,128]{2,1,0:T(8,128)(2,1)S(1)}, bf16[2,256,128]{2,1,0:T(8,128)(2,1)S(1)}, u32[]{:S(2)}, u32[]{:S(2)}) collective-permute-start(bf16[2,256,128]{2,1,0:T(8,128)(2,1)S(1)} %collective-permute-done.7.refs_10_), channel_id=1, source_target_pairs={{0,4},{4,0},{8,12},{12,8},{1,5},{5,1},{9,13},{13,9},{2,6},{6,2},{1... | collective-permute-start | bytes 393224 | tf_op jit(solution)/shard_map/ppermute | solution.py:29
  19.5 31.5 %collective-permute-start.2 = (bf16[2,256,128]{2,1,0:T(8,128)(2,1)S(1)}, bf16[2,256,128]{2,1,0:T(8,128)(2,1)S(1)}, u32[]{:S(2)}, u32[]{:S(2)}) collective-permute-start(bf16[2,256,128]{2,1,0:T(8,128)(2,1)S(1)} %get-tuple-element.37.refs_4_), channel_id=1, source_target_pairs={{0,4},{4,0},{8,12},{12,8},{1,5},{5,1},{9,13},{13,9},{2,6},{6,2},{1... | collective-permute-start | bytes 393224 | tf_op jit(solution)/shard_map/ppermute | solution.py:29
  19.5 30.9 %collective-permute-start.3 = (bf16[2,256,128]{2,1,0:T(8,128)(2,1)S(1)}, bf16[2,256,128]{2,1,0:T(8,128)(2,1)S(1)}, u32[]{:S(2)}, u32[]{:S(2)}) collective-permute-start(bf16[2,256,128]{2,1,0:T(8,128)(2,1)S(1)} %get-tuple-element.37.refs_4_), channel_id=1, source_target_pairs={{0,8},{4,12},{8,0},{12,4},{1,9},{5,13},{9,1},{13,5},{2,10},{6,14},... | collective-permute-start | bytes 393224 | tf_op jit(solution)/shard_map/ppermute | solution.py:29
  21.1 30.1 %collective-permute-start.14 = (bf16[2,256,128]{2,1,0:T(8,128)(2,1)S(1)}, bf16[2,256,128]{2,1,0:T(8,128)(2,1)S(1)}, u32[]{:S(2)}, u32[]{:S(2)}) collective-permute-start(bf16[2,256,128]{2,1,0:T(8,128)(2,1)S(1)} %collective-permute-done.4.refs_8_), channel_id=1, source_target_pairs={{0,4},{4,0},{8,12},{12,8},{1,5},{5,1},{9,13},{13,9},{2,6},{6,2},{1... | collective-permute-start | bytes 393224 | tf_op jit(solution)/shard_map/ppermute | solution.py:29
  21.4 29.9 %collective-permute-start.1 = (bf16[2,512,128]{2,1,0:T(8,128)(2,1)S(1)}, bf16[2,512,128]{2,1,0:T(8,128)(2,1)S(1)}, u32[]{:S(2)}, u32[]{:S(2)}) collective-permute-start(bf16[2,512,128]{2,1,0:T(8,128)(2,1)S(1)} %get-tuple-element.36), channel_id=1, source_target_pairs={{0,1},{1,0},{2,3},{3,2},{4,5},{5,4},{6,7},{7,6},{8,9},{9,8},{10,11... | collective-permute-start | bytes 786440 | tf_op jit(solution)/shard_map/ppermute | solution.py:29
  23.0 27.4 %collective-permute-start.8 = (bf16[2,256,128]{2,1,0:T(8,128)(2,1)S(1)}, bf16[2,256,128]{2,1,0:T(8,128)(2,1)S(1)}, u32[]{:S(2)}, u32[]{:S(2)}) collective-permute-start(bf16[2,256,128]{2,1,0:T(8,128)(2,1)S(1)} %collective-permute-done.4.refs_8_), channel_id=1, source_target_pairs={{0,8},{4,12},{8,0},{12,4},{1,9},{5,13},{9,1},{13,5},{2,10},{6,14},... | collective-permute-start | bytes 393224 | tf_op jit(solution)/shard_map/ppermute | solution.py:29
  50.4 2.6 %collective-permute-start.13 = (bf16[2,256,128]{2,1,0:T(8,128)(2,1)S(1)}, bf16[2,256,128]{2,1,0:T(8,128)(2,1)S(1)}, u32[]{:S(2)}, u32[]{:S(2)}) collective-permute-start(bf16[2,256,128]{2,1,0:T(8,128)(2,1)S(1)} %collective-permute-done.3.refs_6_), channel_id=1, source_target_pairs={{0,4},{4,0},{8,12},{12,8},{1,5},{5,1},{9,13},{13,9},{2,6},{6,2},{1... | collective-permute-start | bytes 393224 | tf_op jit(solution)/shard_map/ppermute | solution.py:29
  50.5 2.7 %collective-permute-start.15 = (bf16[2,256,128]{2,1,0:T(8,128)(2,1)S(1)}, bf16[2,256,128]{2,1,0:T(8,128)(2,1)S(1)}, u32[]{:S(2)}, u32[]{:S(2)}) collective-permute-start(bf16[2,256,128]{2,1,0:T(8,128)(2,1)S(1)} %collective-permute-done.8.refs_10_), channel_id=1, source_target_pairs={{0,4},{4,0},{8,12},{12,8},{1,5},{5,1},{9,13},{13,9},{2,6},{6,2},{1... | collective-permute-start | bytes 393224 | tf_op jit(solution)/shard_map/ppermute | solution.py:29
  51.0 27.5 %collective-permute-start.16 = (bf16[2,512,128]{2,1,0:T(8,128)(2,1)S(1)}, bf16[2,512,128]{2,1,0:T(8,128)(2,1)S(1)}, u32[]{:S(2)}, u32[]{:S(2)}) collective-permute-start(bf16[2,512,128]{2,1,0:T(8,128)(2,1)S(1)} %get-tuple-element.44), channel_id=1, source_target_pairs={{0,1},{1,0},{2,3},{3,2},{4,5},{5,4},{6,7},{7,6},{8,9},{9,8},{10,11... | collective-permute-start | bytes 786440 | tf_op jit(solution)/shard_map/ppermute | solution.py:29
  51.2 27.2 %collective-permute-start.18 = (bf16[2,256,256]{2,1,0:T(8,128)(2,1)S(1)}, bf16[2,256,256]{2,1,0:T(8,128)(2,1)S(1)}, u32[]{:S(2)}, u32[]{:S(2)}) collective-permute-start(bf16[2,256,256]{2,1,0:T(8,128)(2,1)S(1)} %bitcast.14), channel_id=1, source_target_pairs={{0,4},{4,0},{8,12},{12,8},{1,5},{5,1},{9,13},{13,9},{2,6},{6,2},{1... | collective-permute-start | bytes 786440 | tf_op jit(solution)/shard_map/ppermute | solution.py:29
  51.2 27.2 %collective-permute-start.19 = (bf16[2,256,256]{2,1,0:T(8,128)(2,1)S(1)}, bf16[2,256,256]{2,1,0:T(8,128)(2,1)S(1)}, u32[]{:S(2)}, u32[]{:S(2)}) collective-permute-start(bf16[2,256,256]{2,1,0:T(8,128)(2,1)S(1)} %bitcast.13), channel_id=1, source_target_pairs={{0,8},{4,12},{8,0},{12,4},{1,9},{5,13},{9,1},{13,5},{2,10},{6,14},... | collective-permute-start | bytes 786440 | tf_op jit(solution)/shard_map/ppermute | solution.py:29
  53.0 25.5 %collective-permute-start.20 = (bf16[2,256,256]{2,1,0:T(8,128)(2,1)S(1)}, bf16[2,256,256]{2,1,0:T(8,128)(2,1)S(1)}, u32[]{:S(2)}, u32[]{:S(2)}) collective-permute-start(bf16[2,256,256]{2,1,0:T(8,128)(2,1)S(1)} %bitcast.12), channel_id=1, source_target_pairs={{0,12},{4,8},{8,4},{12,0},{1,13},{5,9},{9,5},{13,1},{2,14},{6,10},... | collective-permute-start | bytes 786440 | tf_op jit(solution)/shard_map/ppermute | solution.py:29
  78.9 9.2 %collective-permute-start.17 = (bf16[2,512,128]{2,1,0:T(8,128)(2,1)S(1)}, bf16[2,512,128]{2,1,0:T(8,128)(2,1)S(1)}, u32[]{:S(2)}, u32[]{:S(2)}) collective-permute-start(bf16[2,512,128]{2,1,0:T(8,128)(2,1)S(1)} %get-tuple-element.53), channel_id=1, source_target_pairs={{0,1},{1,0},{2,3},{3,2},{4,5},{5,4},{6,7},{7,6},{8,9},{9,8},{10,11... | collective-permute-start | bytes 786440 | tf_op jit(solution)/shard_map/ppermute | solution.py:29
  80.8 9.3 %collective-permute-start.22 = (bf16[2,256,256]{2,1,0:T(8,128)(2,1)S(1)}, bf16[2,256,256]{2,1,0:T(8,128)(2,1)S(1)}, u32[]{:S(2)}, u32[]{:S(2)}) collective-permute-start(bf16[2,256,256]{2,1,0:T(8,128)(2,1)S(1)} %fusion.1), channel_id=1, source_target_pairs={{0,8},{4,12},{8,0},{12,4},{1,9},{5,13},{9,1},{13,5},{2,10},{6,14},... | collective-permute-start | bytes 786440 | tf_op jit(solution)/shard_map/ppermute | solution.py:29
  82.5 7.5 %collective-permute-start.23 = (bf16[2,256,128]{2,1,0:T(8,128)(2,1)S(1)}, bf16[2,256,128]{2,1,0:T(8,128)(2,1)S(1)}, u32[]{:S(2)}, u32[]{:S(2)}) collective-permute-start(bf16[2,256,128]{2,1,0:T(8,128)(2,1)S(1)} %slice.42), channel_id=1, source_target_pairs={{0,1},{1,0},{2,3},{3,2},{4,5},{5,4},{6,7},{7,6},{8,9},{9,8},{10,11... | collective-permute-start | bytes 393224 | tf_op jit(solution)/shard_map/ppermute | solution.py:29
  90.1 5.0 %collective-permute-start.24 = (bf16[2,256,128]{2,1,0:T(8,128)(2,1)S(1)}, bf16[2,256,128]{2,1,0:T(8,128)(2,1)S(1)}, u32[]{:S(2)}, u32[]{:S(2)}) collective-permute-start(bf16[2,256,128]{2,1,0:T(8,128)(2,1)S(1)} %slice.41), channel_id=1, source_target_pairs={{0,1},{1,0},{2,3},{3,2},{4,5},{5,4},{6,7},{7,6},{8,9},{9,8},{10,11... | collective-permute-start | bytes 393224 | tf_op jit(solution)/shard_map/ppermute | solution.py:29
  (6 other events, 19.9 us)

commit v9 on v8

--- a/solution.py
+++ b/solution.py
@@ -15,6 +15,8 @@
 BLOCK = 256
 STRIP = 16
 MASKED = -1e30
+ATTEND_VMEM = 50 * 2**20
+PACK_VMEM = 60 * 2**20
 SCALE = HD ** (-0.5)
 
 NT = (((1,), (1,)), ((), ()))
@@ -255,46 +257,42 @@
         ),
         out_shape=out_shape,
         input_output_aliases=aliases,
-        compiler_params=pltpu.CompilerParams(vmem_limit_bytes=48 * 2**20),
+        compiler_params=pltpu.CompilerParams(vmem_limit_bytes=ATTEND_VMEM),
         cost_estimate=pl.CostEstimate(flops=2 * flops, bytes_accessed=4 * 2**20, transcendentals=0),
     )(scalars, *args)
 
 
-def pack_kernel(n_own, n_resp, scalars, prompt_ref, resp_ref, *outs):
-    width = n_own * HD
-
-    def split(own):
-        for h in range(n_own):
-            mine = slice(own + h * HD, own + (h + 1) * HD)
-            theirs = slice(width - own + h * HD, width - own + (h + 1) * HD)
-            for k, (ref, lanes) in enumerate(
-                ((prompt_ref, mine), (prompt_ref, theirs), (resp_ref, mine), (resp_ref, theirs))
-            ):
-                outs[4 * h + k][...] = ref[:, :, lanes]
-
-    @pl.when(scalars[n_resp] == 0)
+def pack_kernel(src, own, *others):
+    half = src.shape[2] // 2
+
+    def split(start):
+        own[...] = src[:, :, start : start + half]
+        for k, out in enumerate(others):
+            n = out.shape[2]
+            at = half - start + k * n
+            out[...] = src[:, :, at : at + n]
+
+    @pl.when(lax.axis_index("prefix") % 2 == 0)
     def _():
         split(0)
 
-    @pl.when(scalars[n_resp] != 0)
-    def _():
-        split(width)
-
-
-def pack(scalars, prompt_kv, resp_kv, n_own):
-    block = lambda shape: pl.BlockSpec(shape, lambda i, sc: (0, 0, 0))
-    shapes = [x.shape[:2] + (HD,) for x in (prompt_kv, prompt_kv, resp_kv, resp_kv)] * n_own
+    @pl.when(lax.axis_index("prefix") % 2 != 0)
+    def _():
+        split(half)
+
+
+def pack(array, sections):
+    block = lambda shape: pl.BlockSpec(shape, lambda i: (0, 0, 0))
+    half = array.shape[2] // 2
+    shapes = [array.shape[:2] + (n,) for n in (half, *[half // sections] * sections)]
     return pl.pallas_call(
-        functools.partial(pack_kernel, n_own, resp_kv.shape[0]),
-        grid_spec=pltpu.PrefetchScalarGridSpec(
-            num_scalar_prefetch=1,
-            grid=(1,),
-            in_specs=[block(prompt_kv.shape), block(resp_kv.shape)],
-            out_specs=[block(s) for s in shapes],
-        ),
-        out_shape=[jax.ShapeDtypeStruct(s, prompt_kv.dtype) for s in shapes],
-        compiler_params=pltpu.CompilerParams(vmem_limit_bytes=48 * 2**20),
-    )(scalars, prompt_kv, resp_kv)
+        pack_kernel,
+        grid=(1,),
+        in_specs=[block(array.shape)],
+        out_specs=[block(s) for s in shapes],
+        out_shape=[jax.ShapeDtypeStruct(s, array.dtype) for s in shapes],
+        compiler_params=pltpu.CompilerParams(vmem_limit_bytes=PACK_VMEM),
+    )(array)
 
 
 def per_device(queries, resp_kv, prompt_kv, prompt_of, d_out):
@@ -315,38 +313,33 @@
     def order(values, done):
         return lax.optimization_barrier((tuple(values), tuple(done)))[0]
 
-    packed = pack(scalars, prompt_kv, resp_kv, n_own)
-    pa, pb, resp_a, resp_b = [], [], [], []
-    for h in range(n_own):
-        a0, b0, ra, rb = packed[4 * h : 4 * h + 4]
-        if h > 0:
-            (rb,) = order([rb], [resp_b[h - 1]])
-        b0 = z(b0)
-        a2 = x(a0)
-        resp_a.append(ra)
-        resp_b.append(z(rb))
-        if h == 0:
-            (ready,) = order([b0], [a2])
-        else:
-            (ready,) = order([b0], [pb[0][2]])
-        b2 = x(ready)
-        pa.append([a0, core(a0), a2, core(a2) if h == 0 else None])
-        pb.append([b0, core(b0), b2, core(b2) if h == 0 else None])
+    a0, b0 = pack(prompt_kv, 1)
+    b0 = z(b0)
+    a2 = x(a0)
+    resp_a, *resp_b = pack(resp_kv, n_own)
+    resp_b[0] = z(resp_b[0])
+    (ready,) = order([b0], [resp_a])
+    b2 = x(ready)
+    for h in range(1, n_own):
+        resp_b[h] = z(order([resp_b[h]], [b0])[0])
+    pa = [a0, core(a0), a2, core(a2)]
+    pb = [b0, core(b0), b2, core(b2)]
 
     shared = None
     d_resp, d_prompt = [], []
     for h in range(n_own):
         final = h == n_own - 1
         here = lambda par, h=h: par * n_own + h
+        own = lambda par, h=h: h
         at = lambda par: 0
         att, dq, dra, drb, keep, *sends = attend(
             scalars,
             queries,
             d_out,
-            (resp_a[h], at),
+            (resp_a, own),
             (resp_b[h], at),
-            [(a, at) for a in pa[h]],
-            [(b, at) for b in pb[h]],
+            [(a, own) for a in pa],
+            [(b, own) for b in pb],
             (0, 2) if final else (0,),
             ((1, 3),) if final else ((1,), (2,), (3,)),
             h,
@@ -356,12 +349,10 @@
         )
         shared = (att, dq, dra)
         d_resp.append(z(drb))
-        if not final:
-            pa[h + 1][3], pb[h + 1][3] = [core(v) for v in order([pa[h + 1][2], pb[h + 1][2]], [drb])]
         if final:
             (send,) = order([sends[0]], arrived)
             sums = keep + core(send).astype(jnp.float32)
-            (across,) = order([x(sums[1].astype(jnp.bfloat16))], [d_resp[-1], *[b for _, b in d_prompt]])
+            (across,) = order([x(sums[1].astype(jnp.bfloat16))], [d_resp[-1]])
             total = sums[0] + across.astype(jnp.float32)
         else:
             parts = [move(part[0]) for move, part in zip((core, x, both), sends)]
@@ -372,8 +363,11 @@
 
     even = parity == 0
     mine = jnp.concatenate([a for a, _ in d_prompt], axis=-1)
-    other = jnp.concatenate([b.astype(jnp.float32) for _, b in d_prompt], axis=-1)
+    *others, final = [b.astype(jnp.float32) for _, b in d_prompt]
+    other = jnp.concatenate([*others, jnp.zeros_like(final)], axis=-1)
     d_prompt = jnp.concatenate([jnp.where(even, mine, other), jnp.where(even, other, mine)], axis=-1)
+    (d_prompt,) = order([d_prompt], [])
+    d_prompt = lax.dynamic_update_slice_in_dim(d_prompt, final, (theirs + n_own - 1) * HD, axis=2)
     att, dq, d_resp_kv = shared
     received = jnp.concatenate(d_resp, axis=-1)
     d_resp_kv = lax.dynamic_update_slice_in_dim(d_resp_kv, received, theirs * HD, axis=2)

time: 96.7 us -> 99.1 us (1.025)
  starting transfers between devices: 22.8 us -> 15.5 us
  Pallas kernels: 51.4 us -> 56.6 us
  waiting for transfers between devices: 15 us -> 19.9 us
    ppermute x25 -> x18, starting transfers between devices: 22.8 us -> 15.5 us  [swap(): lax.ppermute(block, axis, [(i, i ^ step) for i in range(lax.axis_size(axi...]
    ppermute x25 -> x18, waiting for transfers between devices: 15 us -> 19.9 us  [swap(): lax.ppermute(block, axis, [(i, i ^ step) for i in range(lax.axis_size(axi...]
    pallas_call x1 -> x2, Pallas kernels: 0.82 us -> 4.16 us  [pack(): pl.pallas_call(pack_kernel, grid=(1,), in_specs=[block(array.shape)], out...]
    pallas_call x2, Pallas kernels: 50.6 us -> 52.4 us  [attend(): pl.pallas_call(functools.partial(attend_kernel, (pieces, rows, keep, send...]
    add x1, other arithmetic: 0.13 us -> 1.34 us  [whole_heads(): sums = keep + core(send).astype(jnp.float32)]
    unnamed x10 -> x22, local copies, waits for them, and re-layouts: 3.87 us -> 3.31 us
  transfers between devices with their start and end apart: 25 -> 18, of which waited for: 7 -> 7; matrix products, arithmetic and copies ran while one was open for 0% -> 3% of each run, Pallas kernels for 52% -> 55%
where the time goes in v9:
time: 99.1 us; the launch traced here: 98.8 us
  Pallas kernels  56.6 us (57%)
  waiting for transfers between devices  19.9 us (20%)
  starting transfers between devices  15.5 us (16%)
  local copies, waits for them, and re-layouts  3.42 us (3%)
  other arithmetic  2.58 us (3%)
    pallas_call x2, Pallas kernels, attend(): pl.pallas_call(functools.partial(attend_kernel, (pieces, rows, keep, send...  52.4 us
    ppermute x18, waiting for transfers between devices, swap(): lax.ppermute(block, axis, [(i, i ^ step) for i in range(lax.axis_size(axi...  19.9 us
    ppermute x18, starting transfers between devices, swap(): lax.ppermute(block, axis, [(i, i ^ step) for i in range(lax.axis_size(axi...  15.5 us
    pallas_call x2, Pallas kernels, pack(): pl.pallas_call(pack_kernel, grid=(1,), in_specs=[block(array.shape)], out...  4.16 us
    unnamed x22, local copies, waits for them, and re-layouts  3.31 us
  transfers between devices with their start and end apart: 18, of which 7 were waited for; matrix products, arithmetic and copies ran while one was open for 3% of the time, Pallas kernels for 55%

profile of v9, /device:TPU:0, one launch (start us, length us, event | category | flops | bytes accessed | tf_op | source)
XLA Modules:
  0.0 98.8 jit_solution(7011066101195033291)
XLA Ops:
  0.6 1.9 %shard_map.85 = (bf16[2,256,256]{2,1,0:T(8,128)(2,1)}, bf16[2,256,256]{2,1,0:T(8,128)(2,1)}) custom-call(bf16[2,256,512]{2,1,0:T(8,128)(2,1)} %src.3), custom_call_target="tpu_custom_call" | custom-call | tf_op jit(solution)/shard_map/pallas_call | solution.py:288
  2.5 3.0 %collective-permute-start = (bf16[2,256,256]{2,1,0:T(8,128)(2,1)}, bf16[2,256,256]{2,1,0:T(8,128)(2,1)S(1)}, u32[]{:S(2)}, u32[]{:S(2)}) collective-permute-start(bf16[2,256,256]{2,1,0:T(8,128)(2,1)} %get-tuple-element.29), channel_id=1, source_target_pairs={{0,1},{1,0},{2,3},{3,2},{4,5},{5,4},{6,7},{7,6},{8,9},{9,8},{10,11... | collective-permute-start | bytes 786440 | tf_op jit(solution)/shard_map/ppermute | solution.py:31
  5.5 1.5 %collective-permute-start.3 = (bf16[2,256,256]{2,1,0:T(8,128)(2,1)}, bf16[2,256,256]{2,1,0:T(8,128)(2,1)S(1)}, u32[]{:S(2)}, u32[]{:S(2)}) collective-permute-start(bf16[2,256,256]{2,1,0:T(8,128)(2,1)} %get-tuple-element.31.refs_4_), channel_id=1, source_target_pairs={{0,8},{4,12},{8,0},{12,4},{1,9},{5,13},{9,1},{13,5},{2,10},{6,14},... | collective-permute-start | bytes 786440 | tf_op jit(solution)/shard_map/ppermute | solution.py:31
  7.0 2.3 %shard_map.84 = (bf16[2,512,256]{2,1,0:T(8,128)(2,1)}, bf16[2,512,128]{2,1,0:T(8,128)(2,1)}, bf16[2,512,128]{2,1,0:T(8,128)(2,1)}) custom-call(bf16[2,512,512]{2,1,0:T(8,128)(2,1)} %src.2), custom_call_target="tpu_custom_call" | custom-call | tf_op jit(solution)/shard_map/pallas_call | solution.py:288
  9.3 2.7 %collective-permute-done.refs_8_ = bf16[2,256,256]{2,1,0:T(8,128)(2,1)S(1)} collective-permute-done((bf16[2,256,256]{2,1,0:T(8,128)(2,1)}, bf16[2,256,256]{2,1,0:T(8,128)(2,1)S(1)}, u32[]{:S(2)}, u32[]{:S(2)}) %collective-permute-start) | collective-permute-done | bytes 262176 | tf_op jit(solution)/shard_map/ppermute | solution.py:31
  12.0 1.7 %collective-permute-start.6 = (bf16[2,256,256]{2,1,0:T(8,128)(2,1)S(1)}, bf16[2,256,256]{2,1,0:T(8,128)(2,1)S(1)}, u32[]{:S(2)}, u32[]{:S(2)}) collective-permute-start(bf16[2,256,256]{2,1,0:T(8,128)(2,1)S(1)} %collective-permute-done.refs_8_), channel_id=1, source_target_pairs={{0,8},{4,12},{8,0},{12,4},{1,9},{5,13},{9,1},{13,5},{2,10},{6,14},... | collective-permute-start | bytes 786440 | tf_op jit(solution)/shard_map/ppermute | solution.py:31
  13.7 1.6 %collective-permute-start.8 = (bf16[2,512,128]{2,1,0:T(8,128)(2,1)}, bf16[2,512,128]{2,1,0:T(8,128)(2,1)S(1)}, u32[]{:S(2)}, u32[]{:S(2)}) collective-permute-start(bf16[2,512,128]{2,1,0:T(8,128)(2,1)} %get-tuple-element.33), channel_id=1, source_target_pairs={{0,1},{1,0},{2,3},{3,2},{4,5},{5,4},{6,7},{7,6},{8,9},{9,8},{10,11... | collective-permute-start | bytes 786440 | tf_op jit(solution)/shard_map/ppermute | solution.py:31
  15.8 3.7 %collective-permute-done.6.refs_10_ = bf16[2,256,256]{2,1,0:T(8,128)(2,1)S(1)} collective-permute-done((bf16[2,256,256]{2,1,0:T(8,128)(2,1)S(1)}, bf16[2,256,256]{2,1,0:T(8,128)(2,1)S(1)}, u32[]{:S(2)}, u32[]{:S(2)}) %collective-permute-start.6) | collective-permute-done | bytes 262176 | tf_op jit(solution)/shard_map/ppermute | solution.py:31
  19.5 0.7 pad_add_fusion.scalars
  20.3 1.4 %collective-permute-start.1 = (bf16[2,512,128]{2,1,0:T(8,128)(2,1)}, bf16[2,512,128]{2,1,0:T(8,128)(2,1)S(1)}, u32[]{:S(2)}, u32[]{:S(2)}) collective-permute-start(bf16[2,512,128]{2,1,0:T(8,128)(2,1)} %get-tuple-element.30), channel_id=1, source_target_pairs={{0,1},{1,0},{2,3},{3,2},{4,5},{5,4},{6,7},{7,6},{8,9},{9,8},{10,11... | collective-permute-start | bytes 786440 | tf_op jit(solution)/shard_map/ppermute | solution.py:31
  21.7 0.9 collective-permute-done.8.refs_3_
  22.7 0.9 copy-done.1
  23.6 26.1 %shard_map.86 = (bf16[2,512,1024]{2,1,0:T(8,128)(2,1)}, bf16[2,512,1024]{2,1,0:T(8,128)(2,1)}, bf16[2,512,512]{2,1,0:T(8,128)(2,1)}, bf16[2,512,128]{2,1,0:T(8,1...) custom-call(s32[3]{0:T(128)S(1)} %pad_add_fusion.scalars, ...), custom_call_target="tpu_custom_call" | custom-call | flops 19327352832 | bytes 4194304 | tf_op jit(solution)/shard_map/pallas_call | solution.py:249
  49.7 0.9 collective-permute-start.12
  50.6 1.0 collective-permute-start.13
  51.5 1.6 %collective-permute-start.9 = (bf16[2,512,128]{2,1,0:T(8,128)(2,1)S(1)}, bf16[2,512,128]{2,1,0:T(8,128)(2,1)S(1)}, u32[]{:S(2)}, u32[]{:S(2)}) collective-permute-start(bf16[2,512,128]{2,1,0:T(8,128)(2,1)S(1)} %get-tuple-element.40), channel_id=1, source_target_pairs={{0,1},{1,0},{2,3},{3,2},{4,5},{5,4},{6,7},{7,6},{8,9},{9,8},{10,11... | collective-permute-start | bytes 786440 | tf_op jit(solution)/shard_map/ppermute | solution.py:31
  53.1 26.3 %shard_map.87 = (bf16[2,512,1024]{2,1,0:T(8,128)(2,1)}, bf16[2,512,1024]{2,1,0:T(8,128)(2,1)}, bf16[2,512,512]{2,1,0:T(8,128)(2,1)}, bf16[2,512,128]{2,1,0:T(8,1...) custom-call(s32[3]{0:T(128)S(1)} %pad_add_fusion.scalars, ...), custom_call_target="tpu_custom_call", output_to_operand_aliasing={{0}: (13, {}), {1}: (14, {}), {2}: (15, {})} | custom-call | flops 19327352832 | bytes 4194304 | tf_op jit(solution)/shard_map/pallas_call | solution.py:249
  81.4 1.4 %collective-permute-done.14 = bf16[2,2,256,256]{3,2,1,0:T(8,128)(2,1)S(1)} collective-permute-done((bf16[2,2,256,256]{3,2,1,0:T(8,128)(2,1)S(1)}, bf16[2,2,256,256]{3,2,1,0:T(8,128)(2,1)S(1)}, u32[]{:S(2)}, u32[]{:S(2)}) %collective-permute-start.14) | collective-permute-done | bytes 524320 | tf_op jit(solution)/shard_map/ppermute | solution.py:31
  82.8 1.3 %convert_add_fusion = f32[2,2,256,256]{3,2,1,0:T(8,128)S(1)} fusion(f32[2,2,256,256]{3,2,1,0:T(8,128)} %get-tuple-element.46, bf16[2,2,256,256]{3,2,1,0:T(8,128)(2,1)S(1)} %collective-permute-done.14), kind=kLoop, calls=%fused_computation.1 | loop fusion | flops 524288 | bytes 2621440 | tf_op jit(solution)/shard_map/add | solution.py:354
  84.2 0.8 collective-permute-start.15
  85.7 4.3 %collective-permute-done.10 = bf16[2,512,128]{2,1,0:T(8,128)(2,1)S(1)} collective-permute-done((bf16[2,512,128]{2,1,0:T(8,128)(2,1)S(1)}, bf16[2,512,128]{2,1,0:T(8,128)(2,1)S(1)}, u32[]{:S(2)}, u32[]{:S(2)}) %collective-permute-start.10) | collective-permute-done | bytes 262176 | tf_op jit(solution)/shard_map/ppermute | solution.py:31
  90.2 2.4 %collective-permute-done.15 = bf16[2,256,256]{2,1,0:T(8,128)(2,1)S(1)} collective-permute-done((bf16[2,256,256]{2,1,0:T(8,128)(2,1)S(1)}, bf16[2,256,256]{2,1,0:T(8,128)(2,1)S(1)}, u32[]{:S(2)}, u32[]{:S(2)}) %collective-permute-start.15) | collective-permute-done | bytes 262176 | tf_op jit(solution)/shard_map/ppermute | solution.py:31
  93.5 4.3 %collective-permute-done.17 = bf16[2,256,128]{2,1,0:T(8,128)(2,1)S(1)} collective-permute-done((bf16[2,256,128]{2,1,0:T(8,128)(2,1)S(1)}, bf16[2,256,128]{2,1,0:T(8,128)(2,1)S(1)}, u32[]{:S(2)}, u32[]{:S(2)}) %collective-permute-start.17) | collective-permute-done | bytes 131104 | tf_op jit(solution)/shard_map/ppermute | solution.py:31
  97.8 1.0 copy-done.2
  (51 shorter events, 4.1 us)
Async XLA Ops:
  2.5 9.5 %collective-permute-start = (bf16[2,256,256]{2,1,0:T(8,128)(2,1)}, bf16[2,256,256]{2,1,0:T(8,128)(2,1)S(1)}, u32[]{:S(2)}, u32[]{:S(2)}) collective-permute-start(bf16[2,256,256]{2,1,0:T(8,128)(2,1)} %get-tuple-element.29), channel_id=1, source_target_pairs={{0,1},{1,0},{2,3},{3,2},{4,5},{5,4},{6,7},{7,6},{8,9},{9,8},{10,11... | collective-permute-start | bytes 786440 | tf_op jit(solution)/shard_map/ppermute | solution.py:31
  5.5 10.0 %collective-permute-start.3 = (bf16[2,256,256]{2,1,0:T(8,128)(2,1)}, bf16[2,256,256]{2,1,0:T(8,128)(2,1)S(1)}, u32[]{:S(2)}, u32[]{:S(2)}) collective-permute-start(bf16[2,256,256]{2,1,0:T(8,128)(2,1)} %get-tuple-element.31.refs_4_), channel_id=1, source_target_pairs={{0,8},{4,12},{8,0},{12,4},{1,9},{5,13},{9,1},{13,5},{2,10},{6,14},... | collective-permute-start | bytes 786440 | tf_op jit(solution)/shard_map/ppermute | solution.py:31
  12.0 7.5 %collective-permute-start.6 = (bf16[2,256,256]{2,1,0:T(8,128)(2,1)S(1)}, bf16[2,256,256]{2,1,0:T(8,128)(2,1)S(1)}, u32[]{:S(2)}, u32[]{:S(2)}) collective-permute-start(bf16[2,256,256]{2,1,0:T(8,128)(2,1)S(1)} %collective-permute-done.refs_8_), channel_id=1, source_target_pairs={{0,8},{4,12},{8,0},{12,4},{1,9},{5,13},{9,1},{13,5},{2,10},{6,14},... | collective-permute-start | bytes 786440 | tf_op jit(solution)/shard_map/ppermute | solution.py:31
  13.7 6.6 %collective-permute-start.2 = (bf16[2,256,256]{2,1,0:T(8,128)(2,1)}, bf16[2,256,256]{2,1,0:T(8,128)(2,1)S(1)}, u32[]{:S(2)}, u32[]{:S(2)}) collective-permute-start(bf16[2,256,256]{2,1,0:T(8,128)(2,1)} %get-tuple-element.31.refs_4_), channel_id=1, source_target_pairs={{0,4},{4,0},{8,12},{12,8},{1,5},{5,1},{9,13},{13,9},{2,6},{6,2},{1... | collective-permute-start | bytes 786440 | tf_op jit(solution)/shard_map/ppermute | solution.py:31
  13.7 8.9 %collective-permute-start.8 = (bf16[2,512,128]{2,1,0:T(8,128)(2,1)}, bf16[2,512,128]{2,1,0:T(8,128)(2,1)S(1)}, u32[]{:S(2)}, u32[]{:S(2)}) collective-permute-start(bf16[2,512,128]{2,1,0:T(8,128)(2,1)} %get-tuple-element.33), channel_id=1, source_target_pairs={{0,1},{1,0},{2,3},{3,2},{4,5},{5,4},{6,7},{7,6},{8,9},{9,8},{10,11... | collective-permute-start | bytes 786440 | tf_op jit(solution)/shard_map/ppermute | solution.py:31
  15.3 7.4 %collective-permute-start.5 = (bf16[2,256,256]{2,1,0:T(8,128)(2,1)S(1)}, bf16[2,256,256]{2,1,0:T(8,128)(2,1)S(1)}, u32[]{:S(2)}, u32[]{:S(2)}) collective-permute-start(bf16[2,256,256]{2,1,0:T(8,128)(2,1)S(1)} %collective-permute-done.refs_8_), channel_id=1, source_target_pairs={{0,4},{4,0},{8,12},{12,8},{1,5},{5,1},{9,13},{13,9},{2,6},{6,2},{1... | collective-permute-start | bytes 786440 | tf_op jit(solution)/shard_map/ppermute | solution.py:31
  15.5 7.1 %collective-permute-start.4 = (bf16[2,256,256]{2,1,0:T(8,128)(2,1)S(1)}, bf16[2,256,256]{2,1,0:T(8,128)(2,1)S(1)}, u32[]{:S(2)}, u32[]{:S(2)}) collective-permute-start(bf16[2,256,256]{2,1,0:T(8,128)(2,1)S(1)} %collective-permute-done.3.refs_6_), channel_id=1, source_target_pairs={{0,4},{4,0},{8,12},{12,8},{1,5},{5,1},{9,13},{13,9},{2,6},{6,2},{1... | collective-permute-start | bytes 786440 | tf_op jit(solution)/shard_map/ppermute | solution.py:31
  19.5 3.1 %collective-permute-start.7 = (bf16[2,256,256]{2,1,0:T(8,128)(2,1)S(1)}, bf16[2,256,256]{2,1,0:T(8,128)(2,1)S(1)}, u32[]{:S(2)}, u32[]{:S(2)}) collective-permute-start(bf16[2,256,256]{2,1,0:T(8,128)(2,1)S(1)} %collective-permute-done.6.refs_10_), channel_id=1, source_target_pairs={{0,4},{4,0},{8,12},{12,8},{1,5},{5,1},{9,13},{13,9},{2,6},{6,2},{1... | collective-permute-start | bytes 786440 | tf_op jit(solution)/shard_map/ppermute | solution.py:31
  20.3 32.8 %copy-start = (bf16[2,512,256]{2,1,0:T(8,128)(2,1)S(1)}, bf16[2,512,256]{2,1,0:T(8,128)(2,1)}, u32[]{:S(2)}) copy-start(bf16[2,512,256]{2,1,0:T(8,128)(2,1)} %get-tuple-element.27.refs_2_) | copy-start | bytes 1572868
  20.3 32.8 %collective-permute-start.1 = (bf16[2,512,128]{2,1,0:T(8,128)(2,1)}, bf16[2,512,128]{2,1,0:T(8,128)(2,1)S(1)}, u32[]{:S(2)}, u32[]{:S(2)}) collective-permute-start(bf16[2,512,128]{2,1,0:T(8,128)(2,1)} %get-tuple-element.30), channel_id=1, source_target_pairs={{0,1},{1,0},{2,3},{3,2},{4,5},{5,4},{6,7},{7,6},{8,9},{9,8},{10,11... | collective-permute-start | bytes 786440 | tf_op jit(solution)/shard_map/ppermute | solution.py:31
  49.7 29.8 %collective-permute-start.11 = (bf16[2,256,256]{2,1,0:T(8,128)(2,1)S(1)}, bf16[2,256,256]{2,1,0:T(8,128)(2,1)S(1)}, u32[]{:S(2)}, u32[]{:S(2)}) collective-permute-start(bf16[2,256,256]{2,1,0:T(8,128)(2,1)S(1)} %bitcast.14), channel_id=1, source_target_pairs={{0,4},{4,0},{8,12},{12,8},{1,5},{5,1},{9,13},{13,9},{2,6},{6,2},{1... | collective-permute-start | bytes 786440 | tf_op jit(solution)/shard_map/ppermute | solution.py:31
  49.7 29.8 %collective-permute-start.12 = (bf16[2,256,256]{2,1,0:T(8,128)(2,1)S(1)}, bf16[2,256,256]{2,1,0:T(8,128)(2,1)S(1)}, u32[]{:S(2)}, u32[]{:S(2)}) collective-permute-start(bf16[2,256,256]{2,1,0:T(8,128)(2,1)S(1)} %bitcast.13), channel_id=1, source_target_pairs={{0,8},{4,12},{8,0},{12,4},{1,9},{5,13},{9,1},{13,5},{2,10},{6,14},... | collective-permute-start | bytes 786440 | tf_op jit(solution)/shard_map/ppermute | solution.py:31
  50.6 28.9 %collective-permute-start.13 = (bf16[2,256,256]{2,1,0:T(8,128)(2,1)S(1)}, bf16[2,256,256]{2,1,0:T(8,128)(2,1)S(1)}, u32[]{:S(2)}, u32[]{:S(2)}) collective-permute-start(bf16[2,256,256]{2,1,0:T(8,128)(2,1)S(1)} %bitcast.12), channel_id=1, source_target_pairs={{0,12},{4,8},{8,4},{12,0},{1,13},{5,9},{9,5},{13,1},{2,14},{6,10},... | collective-permute-start | bytes 786440 | tf_op jit(solution)/shard_map/ppermute | solution.py:31
  51.5 28.0 %collective-permute-start.9 = (bf16[2,512,128]{2,1,0:T(8,128)(2,1)S(1)}, bf16[2,512,128]{2,1,0:T(8,128)(2,1)S(1)}, u32[]{:S(2)}, u32[]{:S(2)}) collective-permute-start(bf16[2,512,128]{2,1,0:T(8,128)(2,1)S(1)} %get-tuple-element.40), channel_id=1, source_target_pairs={{0,1},{1,0},{2,3},{3,2},{4,5},{5,4},{6,7},{7,6},{8,9},{9,8},{10,11... | collective-permute-start | bytes 786440 | tf_op jit(solution)/shard_map/ppermute | solution.py:31
  80.9 4.1 %copy-start.4 = (bf16[2,256,256]{2,1,0:T(8,128)(2,1)S(1)}, bf16[2,256,256]{2,1,0:T(8,128)(2,1)}, u32[]{:S(2)}) copy-start(bf16[2,256,256]{2,1,0:T(8,128)(2,1)} %copy-done.3) | copy-start | bytes 786436
  80.9 1.9 %collective-permute-start.14 = (bf16[2,2,256,256]{3,2,1,0:T(8,128)(2,1)S(1)}, bf16[2,2,256,256]{3,2,1,0:T(8,128)(2,1)S(1)}, u32[]{:S(2)}, u32[]{:S(2)}) collective-permute-start(bf16[2,2,256,256]{3,2,1,0:T(8,128)(2,1)S(1)} %get-tuple-element.48), channel_id=1, source_target_pairs={{0,4},{4,0},{8,12},{12,8},{1,5},{5,1},{9,13},{13,9},{2,6},{6,2},{1... | collective-permute-start | bytes 1572872 | tf_op jit(solution)/shard_map/ppermute | solution.py:31
  80.9 4.1 %copy-start.6 = (bf16[2,256,256]{2,1,0:T(8,128)(2,1)S(1)}, bf16[2,256,256]{2,1,0:T(8,128)(2,1)}, u32[]{:S(2)}) copy-start(bf16[2,256,256]{2,1,0:T(8,128)(2,1)} %copy-done.5) | copy-start | bytes 786436
  80.9 9.1 %collective-permute-start.10 = (bf16[2,512,128]{2,1,0:T(8,128)(2,1)S(1)}, bf16[2,512,128]{2,1,0:T(8,128)(2,1)S(1)}, u32[]{:S(2)}, u32[]{:S(2)}) collective-permute-start(bf16[2,512,128]{2,1,0:T(8,128)(2,1)S(1)} %get-tuple-element.41), channel_id=1, source_target_pairs={{0,1},{1,0},{2,3},{3,2},{4,5},{5,4},{6,7},{7,6},{8,9},{9,8},{10,11... | collective-permute-start | bytes 786440 | tf_op jit(solution)/shard_map/ppermute | solution.py:31
  84.1 5.9 %copy-start.8 = (bf16[2,512,128]{2,1,0:T(8,128)(2,1)S(1)}, bf16[2,512,128]{2,1,0:T(8,128)(2,1)}, u32[]{:S(2)}) copy-start(bf16[2,512,128]{2,1,0:T(8,128)(2,1)} %copy-done.7) | copy-start | bytes 786436
  84.1 5.9 %copy-start.9 = (bf16[2,512,512]{2,1,0:T(8,128)(2,1)S(1)}, bf16[2,512,512]{2,1,0:T(8,128)(2,1)}, u32[]{:S(2)}) copy-start(bf16[2,512,512]{2,1,0:T(8,128)(2,1)} %get-tuple-element.39) | copy-start | bytes 3145732
  84.2 8.4 %collective-permute-start.15 = (bf16[2,256,256]{2,1,0:T(8,128)(2,1)S(1)}, bf16[2,256,256]{2,1,0:T(8,128)(2,1)S(1)}, u32[]{:S(2)}, u32[]{:S(2)}) collective-permute-start(bf16[2,256,256]{2,1,0:T(8,128)(2,1)S(1)} %fusion.1), channel_id=1, source_target_pairs={{0,8},{4,12},{8,0},{12,4},{1,9},{5,13},{9,1},{13,5},{2,10},{6,14},... | collective-permute-start | bytes 786440 | tf_op jit(solution)/shard_map/ppermute | solution.py:31
  85.2 8.1 %collective-permute-start.16 = (bf16[2,256,128]{2,1,0:T(8,128)(2,1)S(1)}, bf16[2,256,128]{2,1,0:T(8,128)(2,1)S(1)}, u32[]{:S(2)}, u32[]{:S(2)}) collective-permute-start(bf16[2,256,128]{2,1,0:T(8,128)(2,1)S(1)} %slice.42), channel_id=1, source_target_pairs={{0,1},{1,0},{2,3},{3,2},{4,5},{5,4},{6,7},{7,6},{8,9},{9,8},{10,11... | collective-permute-start | bytes 393224 | tf_op jit(solution)/shard_map/ppermute | solution.py:31
  90.1 3.3 %copy-start.10 = (bf16[2,512,512]{2,1,0:T(8,128)(2,1)}, bf16[2,512,512]{2,1,0:T(8,128)(2,1)S(1)}, u32[]{:S(2)}) copy-start(bf16[2,512,512]{2,1,0:T(8,128)(2,1)S(1)} %maximum_dynamic-update-slice_fusion) | copy-start | bytes 3145732
  92.7 5.0 %collective-permute-start.17 = (bf16[2,256,128]{2,1,0:T(8,128)(2,1)S(1)}, bf16[2,256,128]{2,1,0:T(8,128)(2,1)S(1)}, u32[]{:S(2)}, u32[]{:S(2)}) collective-permute-start(bf16[2,256,128]{2,1,0:T(8,128)(2,1)S(1)} %slice.41), channel_id=1, source_target_pairs={{0,1},{1,0},{2,3},{3,2},{4,5},{5,4},{6,7},{7,6},{8,9},{9,8},{10,11... | collective-permute-start | bytes 393224 | tf_op jit(solution)/shard_map/ppermute | solution.py:31
  (5 other events, 4.1 us)

commit v10 on v9

--- a/solution.py
+++ b/solution.py
@@ -14,9 +14,10 @@
 GROUP = H // KVH
 BLOCK = 256
 STRIP = 16
+PAIR = 2
 MASKED = -1e30
-ATTEND_VMEM = 50 * 2**20
-PACK_VMEM = 60 * 2**20
+ATTEND_VMEM = 48 * 2**20
+PACK_VMEM = 48 * 2**20
 SCALE = HD ** (-0.5)
 
 NT = (((1,), (1,)), ((), ()))
@@ -40,7 +41,7 @@
     rest = refs[4 + 2 * pieces + n_pass :]
     out_ref, dq_ref, dra_ref, drb_ref, keep_ref = rest[:5]
     send_refs = rest[5 : 5 + len(sends)]
-    k_all, v_all, q_t, do_t, scores, grad_probs, probs, dscores, acc_k, acc_v, sum_k, sum_v = rest[5 + len(sends) :]
+    k_all, v_all, q_all, do_all, q_t, do_t, scores, grad_probs, probs, dscores, acc_k, acc_v, sum_k, sum_v = rest[5 + len(sends) :]
 
     r = pl.program_id(0)
     head = pl.program_id(1)
@@ -72,37 +73,54 @@
         acc_k[...] = jnp.zeros_like(acc_k)
         acc_v[...] = jnp.zeros_like(acc_v)
 
+    size = PAIR * BLOCK
+
+    for i in range(n_blocks):
+        for j in range(PAIR):
+            at = slice(i * size + j * BLOCK, i * size + (j + 1) * BLOCK)
+            from_t, lanes = slice(i * BLOCK, (i + 1) * BLOCK), slice(j * HD, (j + 1) * HD)
+            q_all[at, :] = q_ref[0, from_t, lanes]
+            do_all[at, :] = do_ref[0, from_t, lanes]
+
+    def seeing(u):
+        return slice(max(u - n_prompt, 0) // BLOCK * size, n_blocks * size)
+
     def score(u):
-        t = slice(max(u - n_prompt, 0), n_query)
-        scores[t, u : u + BLOCK] = dot(q_ref[0, t, :], k_all[u : u + BLOCK, :], NT)
+        t = seeing(u)
+        scores[t, u : u + BLOCK] = dot(q_all[t, :], k_all[u : u + BLOCK, :], NT)
 
     def grad_prob(u):
-        t = slice(max(u - n_prompt, 0), n_query)
-        grad_probs[t, u : u + BLOCK] = dot(do_ref[0, t, :], v_all[u : u + BLOCK, :], NT)
+        t = seeing(u)
+        grad_probs[t, u : u + BLOCK] = dot(do_all[t, :], v_all[u : u + BLOCK, :], NT)
 
     def grad_value(u):
-        t = slice(max(u - n_prompt, 0), n_query)
+        t = seeing(u)
         acc_v[:, u : u + BLOCK] += dot(do_t[:, t], probs[t, u : u + BLOCK], NN)
 
     def grad_key(u):
-        t = slice(max(u - n_prompt, 0), n_query)
+        t = seeing(u)
         acc_k[:, u : u + BLOCK] += dot(q_t[:, t], dscores[t, u : u + BLOCK], NN)
 
     def turn():
-        q_t[...] = q_ref[0].T
-        do_t[...] = do_ref[0].T
+        q_t[...] = q_all[...].T
+        do_t[...] = do_all[...].T
 
     def stages(i):
         st = {}
-        t0 = i * BLOCK
-        t = slice(t0, t0 + BLOCK)
-        edge = n_prompt + t0
+        t0 = i * size
+        t = slice(t0, t0 + size)
+        edge = n_prompt + i * BLOCK
         seen = edge + BLOCK
+
+        def put(ref, rows_out):
+            for j in range(PAIR):
+                part = rows_out[j * BLOCK : (j + 1) * BLOCK].astype(jnp.bfloat16)
+                ref[0, i * BLOCK : (i + 1) * BLOCK, j * HD : (j + 1) * HD] = part
 
         def softmax(row):
             at = slice(t0 + row, t0 + row + STRIP)
             left = scores[at, :edge]
-            rows_at = lax.broadcasted_iota(jnp.int32, (STRIP, BLOCK), 0) + row
+            rows_at = lax.broadcasted_iota(jnp.int32, (STRIP, BLOCK), 0) + row % BLOCK
             columns = lax.broadcasted_iota(jnp.int32, (STRIP, BLOCK), 1)
             right = jnp.where(columns <= rows_at, scores[at, edge:seen], MASKED)
             top = jnp.maximum(jnp.max(left, axis=1, keepdims=True), jnp.max(right, axis=1, keepdims=True)) * SCALE
@@ -115,8 +133,8 @@
 
         def output():
             o = dot(probs[t, :seen], v_all[:seen, :], NN)
-            out_ref[0, t, :] = o.astype(jnp.bfloat16)
-            st["delta"] = jnp.sum(o * do_ref[0, t, :].astype(jnp.float32), axis=1, keepdims=True)
+            put(out_ref, o)
+            st["delta"] = jnp.sum(o * do_all[t, :].astype(jnp.float32), axis=1, keepdims=True)
 
         def grad_score(row):
             at = slice(t0 + row, t0 + row + STRIP)
@@ -125,9 +143,9 @@
             dscores[at, :seen] = ds.astype(jnp.bfloat16)
 
         def query():
-            dq_ref[0, t, :] = dot(dscores[t, :seen], k_all[:seen, :], NN).astype(jnp.bfloat16)
-
-        strips = range(0, BLOCK, STRIP)
+            put(dq_ref, dot(dscores[t, :seen], k_all[:seen, :], NN))
+
+        strips = range(0, size, STRIP)
         each = lambda f: [functools.partial(f, x) for x in strips]
         return {"softmax": each(softmax), "output": [output], "grad": each(grad_score), "query": [query]}
 
@@ -205,7 +223,9 @@
     def prompt_map(column):
         return lambda r, j, sc: (sc[r], 0, column(sc[n_resp]))
 
-    q_spec = pl.BlockSpec((1, n_query, HD), lambda r, j, sc: (r, 0, chunk * heads + j))
+    steps = heads // PAIR
+    n_rows = PAIR * n_query
+    q_spec = pl.BlockSpec((1, n_query, PAIR * HD), lambda r, j, sc: (r, 0, chunk * steps + j))
     in_specs = [q_spec, q_spec]
     in_specs += [pl.BlockSpec((1, n_query, HD), resp_map(c)) for _, c in (resp_a, resp_b)]
     in_specs += [pl.BlockSpec((1, rows, HD), prompt_map(c)) for _, c in (*prompt_a, *prompt_b)]
@@ -234,12 +254,14 @@
     scratch = [
         pltpu.VMEM((n_keys, HD), jnp.bfloat16),
         pltpu.VMEM((n_keys, HD), jnp.bfloat16),
-        pltpu.VMEM((HD, n_query), jnp.bfloat16),
-        pltpu.VMEM((HD, n_query), jnp.bfloat16),
-        pltpu.VMEM((n_query, n_keys), jnp.float32),
-        pltpu.VMEM((n_query, n_keys), jnp.float32),
-        pltpu.VMEM((n_query, n_keys), jnp.bfloat16),
-        pltpu.VMEM((n_query, n_keys), jnp.bfloat16),
+        pltpu.VMEM((n_rows, HD), jnp.bfloat16),
+        pltpu.VMEM((n_rows, HD), jnp.bfloat16),
+        pltpu.VMEM((HD, n_rows), jnp.bfloat16),
+        pltpu.VMEM((HD, n_rows), jnp.bfloat16),
+        pltpu.VMEM((n_rows, n_keys), jnp.float32),
+        pltpu.VMEM((n_rows, n_keys), jnp.float32),
+        pltpu.VMEM((n_rows, n_keys), jnp.bfloat16),
+        pltpu.VMEM((n_rows, n_keys), jnp.bfloat16),
         pltpu.VMEM((HD, n_keys), jnp.float32),
         pltpu.VMEM((HD, n_keys), jnp.float32),
         pltpu.VMEM((P_SIZE, n_prompt, HD), jnp.float32),
@@ -250,7 +272,7 @@
         functools.partial(attend_kernel, (pieces, rows, keep, sends, n_pass)),
         grid_spec=pltpu.PrefetchScalarGridSpec(
             num_scalar_prefetch=1,
-            grid=(n_resp, heads),
+            grid=(n_resp, steps),
             in_specs=in_specs,
             out_specs=out_specs,
             scratch_shapes=scratch,

time: 99.1 us -> 98.3 us (level)
  Pallas kernels: 56.6 us -> 47.6 us
  local copies, waits for them, and re-layouts: 3.42 us -> 12 us
  other arithmetic: 2.58 us -> 1.37 us
    unnamed x22 -> x52, local copies, waits for them, and re-layouts: 3.31 us -> 11.9 us
    pallas_call x2, Pallas kernels: 52.4 us -> 47.5 us  [attend(): pl.pallas_call(functools.partial(attend_kernel, (pieces, rows, keep, send...]
    pallas_call x2, Pallas kernels: 4.16 us -> 0.16 us  [pack(): pl.pallas_call(pack_kernel, grid=(1,), in_specs=[block(array.shape)], out...]
    add x1, other arithmetic: 1.34 us -> 0.11 us  [whole_heads(): sums = keep + core(send).astype(jnp.float32)]
  transfers between devices with their start and end apart: 18 -> 18, of which waited for: 7 -> 8; matrix products, arithmetic and copies ran while one was open for 3% -> 1% of each run, Pallas kernels for 55% -> 49%
where the time goes in v10:
time: 98.3 us; the launch traced here: 97.9 us
  Pallas kernels  47.6 us (48%)
  waiting for transfers between devices  20.3 us (21%)
  starting transfers between devices  15.7 us (16%)
  local copies, waits for them, and re-layouts  12 us (12%)
  other arithmetic  1.37 us (1%)
    pallas_call x2, Pallas kernels, attend(): pl.pallas_call(functools.partial(attend_kernel, (pieces, rows, keep, send...  47.5 us
    ppermute x18, waiting for transfers between devices, swap(): lax.ppermute(block, axis, [(i, i ^ step) for i in range(lax.axis_size(axi...  20.3 us
    ppermute x18, starting transfers between devices, swap(): lax.ppermute(block, axis, [(i, i ^ step) for i in range(lax.axis_size(axi...  15.7 us
    unnamed x52, local copies, waits for them, and re-layouts  11.9 us
  transfers between devices with their start and end apart: 18, of which 8 were waited for; matrix products, arithmetic and copies ran while one was open for 1% of the time, Pallas kernels for 49%

profile of v10, /device:TPU:0, one launch (start us, length us, event | category | flops | bytes accessed | tf_op | source)
XLA Modules:
  0.0 97.9 jit_solution(15498625692083899959)
XLA Ops:
  0.6 1.0 %copy-done.1 = bf16[2,256,512]{2,1,0:T(8,128)(2,1)S(1)} copy-done((bf16[2,256,512]{2,1,0:T(8,128)(2,1)S(1)}, bf16[2,256,512]{2,1,0:T(8,128)(2,1)}, u32[]{:S(2)}) %copy-start.1) | copy-done | bytes 524312
  1.7 3.1 %collective-permute-start = (bf16[2,256,256]{2,1,0:T(8,128)(2,1)S(1)}, bf16[2,256,256]{2,1,0:T(8,128)(2,1)S(1)}, u32[]{:S(2)}, u32[]{:S(2)}) collective-permute-start(bf16[2,256,256]{2,1,0:T(8,128)(2,1)S(1)} %get-tuple-element.29), channel_id=1, source_target_pairs={{0,1},{1,0},{2,3},{3,2},{4,5},{5,4},{6,7},{7,6},{8,9},{9,8},{10,11... | collective-permute-start | bytes 786440 | tf_op jit(solution)/shard_map/ppermute | solution.py:32
  4.8 1.5 %collective-permute-start.3 = (bf16[2,256,256]{2,1,0:T(8,128)(2,1)S(1)}, bf16[2,256,256]{2,1,0:T(8,128)(2,1)S(1)}, u32[]{:S(2)}, u32[]{:S(2)}) collective-permute-start(bf16[2,256,256]{2,1,0:T(8,128)(2,1)S(1)} %get-tuple-element.31.refs_4_), channel_id=1, source_target_pairs={{0,8},{4,12},{8,0},{12,4},{1,9},{5,13},{9,1},{13,5},{2,10},{6,14},... | collective-permute-start | bytes 786440 | tf_op jit(solution)/shard_map/ppermute | solution.py:32
  6.3 1.2 %copy-done = bf16[2,512,512]{2,1,0:T(8,128)(2,1)S(1)} copy-done((bf16[2,512,512]{2,1,0:T(8,128)(2,1)S(1)}, bf16[2,512,512]{2,1,0:T(8,128)(2,1)}, u32[]{:S(2)}) %copy-start) | copy-done | bytes 1048600
  7.7 3.5 %collective-permute-done.refs_8_ = bf16[2,256,256]{2,1,0:T(8,128)(2,1)S(1)} collective-permute-done((bf16[2,256,256]{2,1,0:T(8,128)(2,1)S(1)}, bf16[2,256,256]{2,1,0:T(8,128)(2,1)S(1)}, u32[]{:S(2)}, u32[]{:S(2)}) %collective-permute-start) | collective-permute-done | bytes 262176 | tf_op jit(solution)/shard_map/ppermute | solution.py:32
  11.1 1.7 %collective-permute-start.6 = (bf16[2,256,256]{2,1,0:T(8,128)(2,1)S(1)}, bf16[2,256,256]{2,1,0:T(8,128)(2,1)S(1)}, u32[]{:S(2)}, u32[]{:S(2)}) collective-permute-start(bf16[2,256,256]{2,1,0:T(8,128)(2,1)S(1)} %collective-permute-done.refs_8_), channel_id=1, source_target_pairs={{0,8},{4,12},{8,0},{12,4},{1,9},{5,13},{9,1},{13,5},{2,10},{6,14},... | collective-permute-start | bytes 786440 | tf_op jit(solution)/shard_map/ppermute | solution.py:32
  12.8 1.6 %collective-permute-start.8 = (bf16[2,512,128]{2,1,0:T(8,128)(2,1)S(1)}, bf16[2,512,128]{2,1,0:T(8,128)(2,1)S(1)}, u32[]{:S(2)}, u32[]{:S(2)}) collective-permute-start(bf16[2,512,128]{2,1,0:T(8,128)(2,1)S(1)} %get-tuple-element.33), channel_id=1, source_target_pairs={{0,1},{1,0},{2,3},{3,2},{4,5},{5,4},{6,7},{7,6},{8,9},{9,8},{10,11... | collective-permute-start | bytes 786440 | tf_op jit(solution)/shard_map/ppermute | solution.py:32
  14.9 3.7 %collective-permute-done.6.refs_10_ = bf16[2,256,256]{2,1,0:T(8,128)(2,1)S(1)} collective-permute-done((bf16[2,256,256]{2,1,0:T(8,128)(2,1)S(1)}, bf16[2,256,256]{2,1,0:T(8,128)(2,1)S(1)}, u32[]{:S(2)}, u32[]{:S(2)}) %collective-permute-start.6) | collective-permute-done | bytes 262176 | tf_op jit(solution)/shard_map/ppermute | solution.py:32
  19.4 1.4 %collective-permute-start.1 = (bf16[2,512,128]{2,1,0:T(8,128)(2,1)S(1)}, bf16[2,512,128]{2,1,0:T(8,128)(2,1)S(1)}, u32[]{:S(2)}, u32[]{:S(2)}) collective-permute-start(bf16[2,512,128]{2,1,0:T(8,128)(2,1)S(1)} %get-tuple-element.30), channel_id=1, source_target_pairs={{0,1},{1,0},{2,3},{3,2},{4,5},{5,4},{6,7},{7,6},{8,9},{9,8},{10,11... | collective-permute-start | bytes 786440 | tf_op jit(solution)/shard_map/ppermute | solution.py:32
  22.2 1.1 %copy-done.14 = bf16[2,512,128]{2,1,0:T(8,128)(2,1)S(1)} copy-done((bf16[2,512,128]{2,1,0:T(8,128)(2,1)S(1)}, bf16[2,512,128]{2,1,0:T(8,128)(2,1)}, u32[]{:S(2)}) %copy-start.14) | copy-done | bytes 262168
  23.4 23.6 %shard_map.86 = (bf16[2,512,1024]{2,1,0:T(8,128)(2,1)}, bf16[2,512,1024]{2,1,0:T(8,128)(2,1)}, bf16[2,512,512]{2,1,0:T(8,128)(2,1)}, bf16[2,512,128]{2,1,0:T(8,1...) custom-call(s32[3]{0:T(128)S(1)} %pad_add_fusion.scalars, ...), custom_call_target="tpu_custom_call" | custom-call | flops 19327352832 | bytes 4194304 | tf_op jit(solution)/shard_map/pallas_call | solution.py:271
  47.1 1.0 %collective-permute-start.12 = (bf16[2,256,256]{2,1,0:T(8,128)(2,1)S(1)}, bf16[2,256,256]{2,1,0:T(8,128)(2,1)S(1)}, u32[]{:S(2)}, u32[]{:S(2)}) collective-permute-start(bf16[2,256,256]{2,1,0:T(8,128)(2,1)S(1)} %bitcast.13), channel_id=1, source_target_pairs={{0,8},{4,12},{8,0},{12,4},{1,9},{5,13},{9,1},{13,5},{2,10},{6,14},... | collective-permute-start | bytes 786440 | tf_op jit(solution)/shard_map/ppermute | solution.py:32
  49.0 1.6 %collective-permute-start.9 = (bf16[2,512,128]{2,1,0:T(8,128)(2,1)S(1)}, bf16[2,512,128]{2,1,0:T(8,128)(2,1)S(1)}, u32[]{:S(2)}, u32[]{:S(2)}) collective-permute-start(bf16[2,512,128]{2,1,0:T(8,128)(2,1)S(1)} %get-tuple-element.40), channel_id=1, source_target_pairs={{0,1},{1,0},{2,3},{3,2},{4,5},{5,4},{6,7},{7,6},{8,9},{9,8},{10,11... | collective-permute-start | bytes 786440 | tf_op jit(solution)/shard_map/ppermute | solution.py:32
  50.6 0.9 copy-done.3
  51.5 0.9 copy-done.5
  52.5 0.9 copy-done.7
  53.4 0.9 copy-done.9
  54.4 0.9 copy-done.11
  55.3 23.8 %shard_map.87 = (bf16[2,512,1024]{2,1,0:T(8,128)(2,1)}, bf16[2,512,1024]{2,1,0:T(8,128)(2,1)}, bf16[2,512,512]{2,1,0:T(8,128)(2,1)}, bf16[2,512,128]{2,1,0:T(8,1...) custom-call(s32[3]{0:T(128)S(1)} %pad_add_fusion.scalars, ...), custom_call_target="tpu_custom_call", output_to_operand_aliasing={{0}: (13, {}), {1}: (14, {}), {2}: (15, {})} | custom-call | flops 19327352832 | bytes 4194304 | tf_op jit(solution)/shard_map/pallas_call | solution.py:271
  81.8 1.4 %collective-permute-done.14 = bf16[2,2,256,256]{3,2,1,0:T(8,128)(2,1)S(1)} collective-permute-done((bf16[2,2,256,256]{3,2,1,0:T(8,128)(2,1)S(1)}, bf16[2,2,256,256]{3,2,1,0:T(8,128)(2,1)S(1)}, u32[]{:S(2)}, u32[]{:S(2)}) %collective-permute-start.14) | collective-permute-done | bytes 524320 | tf_op jit(solution)/shard_map/ppermute | solution.py:32
  84.9 5.8 %collective-permute-done.10 = bf16[2,512,128]{2,1,0:T(8,128)(2,1)S(1)} collective-permute-done((bf16[2,512,128]{2,1,0:T(8,128)(2,1)}, bf16[2,512,128]{2,1,0:T(8,128)(2,1)S(1)}, u32[]{:S(2)}, u32[]{:S(2)}) %collective-permute-start.10) | collective-permute-done | bytes 262176 | tf_op jit(solution)/shard_map/ppermute | solution.py:32
  90.8 1.0 collective-permute-done.15
  93.3 3.6 %collective-permute-done.17 = bf16[2,256,128]{2,1,0:T(8,128)(2,1)S(1)} collective-permute-done((bf16[2,256,128]{2,1,0:T(8,128)(2,1)S(1)}, bf16[2,256,128]{2,1,0:T(8,128)(2,1)S(1)}, u32[]{:S(2)}, u32[]{:S(2)}) %collective-permute-start.17) | collective-permute-done | bytes 131104 | tf_op jit(solution)/shard_map/ppermute | solution.py:32
  97.0 1.0 copy-done.15
  (81 shorter events, 9.7 us)
Async XLA Ops:
  1.7 9.4 %collective-permute-start = (bf16[2,256,256]{2,1,0:T(8,128)(2,1)S(1)}, bf16[2,256,256]{2,1,0:T(8,128)(2,1)S(1)}, u32[]{:S(2)}, u32[]{:S(2)}) collective-permute-start(bf16[2,256,256]{2,1,0:T(8,128)(2,1)S(1)} %get-tuple-element.29), channel_id=1, source_target_pairs={{0,1},{1,0},{2,3},{3,2},{4,5},{5,4},{6,7},{7,6},{8,9},{9,8},{10,11... | collective-permute-start | bytes 786440 | tf_op jit(solution)/shard_map/ppermute | solution.py:32
  4.8 9.8 %collective-permute-start.3 = (bf16[2,256,256]{2,1,0:T(8,128)(2,1)S(1)}, bf16[2,256,256]{2,1,0:T(8,128)(2,1)S(1)}, u32[]{:S(2)}, u32[]{:S(2)}) collective-permute-start(bf16[2,256,256]{2,1,0:T(8,128)(2,1)S(1)} %get-tuple-element.31.refs_4_), channel_id=1, source_target_pairs={{0,8},{4,12},{8,0},{12,4},{1,9},{5,13},{9,1},{13,5},{2,10},{6,14},... | collective-permute-start | bytes 786440 | tf_op jit(solution)/shard_map/ppermute | solution.py:32
  11.1 7.5 %collective-permute-start.6 = (bf16[2,256,256]{2,1,0:T(8,128)(2,1)S(1)}, bf16[2,256,256]{2,1,0:T(8,128)(2,1)S(1)}, u32[]{:S(2)}, u32[]{:S(2)}) collective-permute-start(bf16[2,256,256]{2,1,0:T(8,128)(2,1)S(1)} %collective-permute-done.refs_8_), channel_id=1, source_target_pairs={{0,8},{4,12},{8,0},{12,4},{1,9},{5,13},{9,1},{13,5},{2,10},{6,14},... | collective-permute-start | bytes 786440 | tf_op jit(solution)/shard_map/ppermute | solution.py:32
  12.8 6.6 %collective-permute-start.2 = (bf16[2,256,256]{2,1,0:T(8,128)(2,1)S(1)}, bf16[2,256,256]{2,1,0:T(8,128)(2,1)S(1)}, u32[]{:S(2)}, u32[]{:S(2)}) collective-permute-start(bf16[2,256,256]{2,1,0:T(8,128)(2,1)S(1)} %get-tuple-element.31.refs_4_), channel_id=1, source_target_pairs={{0,4},{4,0},{8,12},{12,8},{1,5},{5,1},{9,13},{13,9},{2,6},{6,2},{1... | collective-permute-start | bytes 786440 | tf_op jit(solution)/shard_map/ppermute | solution.py:32
  12.8 8.7 %collective-permute-start.8 = (bf16[2,512,128]{2,1,0:T(8,128)(2,1)S(1)}, bf16[2,512,128]{2,1,0:T(8,128)(2,1)S(1)}, u32[]{:S(2)}, u32[]{:S(2)}) collective-permute-start(bf16[2,512,128]{2,1,0:T(8,128)(2,1)S(1)} %get-tuple-element.33), channel_id=1, source_target_pairs={{0,1},{1,0},{2,3},{3,2},{4,5},{5,4},{6,7},{7,6},{8,9},{9,8},{10,11... | collective-permute-start | bytes 786440 | tf_op jit(solution)/shard_map/ppermute | solution.py:32
  14.3 7.9 %collective-permute-start.5 = (bf16[2,256,256]{2,1,0:T(8,128)(2,1)S(1)}, bf16[2,256,256]{2,1,0:T(8,128)(2,1)S(1)}, u32[]{:S(2)}, u32[]{:S(2)}) collective-permute-start(bf16[2,256,256]{2,1,0:T(8,128)(2,1)S(1)} %collective-permute-done.refs_8_), channel_id=1, source_target_pairs={{0,4},{4,0},{8,12},{12,8},{1,5},{5,1},{9,13},{13,9},{2,6},{6,2},{1... | collective-permute-start | bytes 786440 | tf_op jit(solution)/shard_map/ppermute | solution.py:32
  14.6 7.6 %collective-permute-start.4 = (bf16[2,256,256]{2,1,0:T(8,128)(2,1)S(1)}, bf16[2,256,256]{2,1,0:T(8,128)(2,1)S(1)}, u32[]{:S(2)}, u32[]{:S(2)}) collective-permute-start(bf16[2,256,256]{2,1,0:T(8,128)(2,1)S(1)} %collective-permute-done.3.refs_6_), channel_id=1, source_target_pairs={{0,4},{4,0},{8,12},{12,8},{1,5},{5,1},{9,13},{13,9},{2,6},{6,2},{1... | collective-permute-start | bytes 786440 | tf_op jit(solution)/shard_map/ppermute | solution.py:32
  18.6 28.4 %copy-start.2 = (bf16[2,256,256]{2,1,0:T(8,128)(2,1)}, bf16[2,256,256]{2,1,0:T(8,128)(2,1)S(1)}, u32[]{:S(2)}) copy-start(bf16[2,256,256]{2,1,0:T(8,128)(2,1)S(1)} %collective-permute-done.6.refs_10_) | copy-start | bytes 786436
  18.6 3.6 %collective-permute-start.7 = (bf16[2,256,256]{2,1,0:T(8,128)(2,1)S(1)}, bf16[2,256,256]{2,1,0:T(8,128)(2,1)S(1)}, u32[]{:S(2)}, u32[]{:S(2)}) collective-permute-start(bf16[2,256,256]{2,1,0:T(8,128)(2,1)S(1)} %collective-permute-done.6.refs_10_), channel_id=1, source_target_pairs={{0,4},{4,0},{8,12},{12,8},{1,5},{5,1},{9,13},{13,9},{2,6},{6,2},{1... | collective-permute-start | bytes 786440 | tf_op jit(solution)/shard_map/ppermute | solution.py:32
  19.4 27.6 %copy-start.4 = (bf16[2,256,256]{2,1,0:T(8,128)(2,1)}, bf16[2,256,256]{2,1,0:T(8,128)(2,1)S(1)}, u32[]{:S(2)}) copy-start(bf16[2,256,256]{2,1,0:T(8,128)(2,1)S(1)} %collective-permute-done.2.refs_5_) | copy-start | bytes 786436
  19.4 31.2 %collective-permute-start.1 = (bf16[2,512,128]{2,1,0:T(8,128)(2,1)S(1)}, bf16[2,512,128]{2,1,0:T(8,128)(2,1)S(1)}, u32[]{:S(2)}, u32[]{:S(2)}) collective-permute-start(bf16[2,512,128]{2,1,0:T(8,128)(2,1)S(1)} %get-tuple-element.30), channel_id=1, source_target_pairs={{0,1},{1,0},{2,3},{3,2},{4,5},{5,4},{6,7},{7,6},{8,9},{9,8},{10,11... | collective-permute-start | bytes 786440 | tf_op jit(solution)/shard_map/ppermute | solution.py:32
  22.2 24.8 %copy-start.8 = (bf16[2,256,256]{2,1,0:T(8,128)(2,1)}, bf16[2,256,256]{2,1,0:T(8,128)(2,1)S(1)}, u32[]{:S(2)}) copy-start(bf16[2,256,256]{2,1,0:T(8,128)(2,1)S(1)} %collective-permute-done.4.refs_7_) | copy-start | bytes 786436
  22.2 24.8 %copy-start.6 = (bf16[2,256,256]{2,1,0:T(8,128)(2,1)}, bf16[2,256,256]{2,1,0:T(8,128)(2,1)S(1)}, u32[]{:S(2)}) copy-start(bf16[2,256,256]{2,1,0:T(8,128)(2,1)S(1)} %collective-permute-done.5.refs_9_) | copy-start | bytes 786436
  23.4 23.7 %copy-start.10 = (bf16[2,256,256]{2,1,0:T(8,128)(2,1)}, bf16[2,256,256]{2,1,0:T(8,128)(2,1)S(1)}, u32[]{:S(2)}) copy-start(bf16[2,256,256]{2,1,0:T(8,128)(2,1)S(1)} %collective-permute-done.7.refs_11_) | copy-start | bytes 786436
  47.0 32.8 %collective-permute-start.11 = (bf16[2,256,256]{2,1,0:T(8,128)(2,1)S(1)}, bf16[2,256,256]{2,1,0:T(8,128)(2,1)S(1)}, u32[]{:S(2)}, u32[]{:S(2)}) collective-permute-start(bf16[2,256,256]{2,1,0:T(8,128)(2,1)S(1)} %bitcast.14), channel_id=1, source_target_pairs={{0,4},{4,0},{8,12},{12,8},{1,5},{5,1},{9,13},{13,9},{2,6},{6,2},{1... | collective-permute-start | bytes 786440 | tf_op jit(solution)/shard_map/ppermute | solution.py:32
  47.1 32.7 %collective-permute-start.12 = (bf16[2,256,256]{2,1,0:T(8,128)(2,1)S(1)}, bf16[2,256,256]{2,1,0:T(8,128)(2,1)S(1)}, u32[]{:S(2)}, u32[]{:S(2)}) collective-permute-start(bf16[2,256,256]{2,1,0:T(8,128)(2,1)S(1)} %bitcast.13), channel_id=1, source_target_pairs={{0,8},{4,12},{8,0},{12,4},{1,9},{5,13},{9,1},{13,5},{2,10},{6,14},... | collective-permute-start | bytes 786440 | tf_op jit(solution)/shard_map/ppermute | solution.py:32
  48.1 31.8 %collective-permute-start.13 = (bf16[2,256,256]{2,1,0:T(8,128)(2,1)S(1)}, bf16[2,256,256]{2,1,0:T(8,128)(2,1)S(1)}, u32[]{:S(2)}, u32[]{:S(2)}) collective-permute-start(bf16[2,256,256]{2,1,0:T(8,128)(2,1)S(1)} %bitcast.12), channel_id=1, source_target_pairs={{0,12},{4,8},{8,4},{12,0},{1,13},{5,9},{9,5},{13,1},{2,14},{6,10},... | collective-permute-start | bytes 786440 | tf_op jit(solution)/shard_map/ppermute | solution.py:32
  49.0 30.9 %collective-permute-start.9 = (bf16[2,512,128]{2,1,0:T(8,128)(2,1)S(1)}, bf16[2,512,128]{2,1,0:T(8,128)(2,1)S(1)}, u32[]{:S(2)}, u32[]{:S(2)}) collective-permute-start(bf16[2,512,128]{2,1,0:T(8,128)(2,1)S(1)} %get-tuple-element.40), channel_id=1, source_target_pairs={{0,1},{1,0},{2,3},{3,2},{4,5},{5,4},{6,7},{7,6},{8,9},{9,8},{10,11... | collective-permute-start | bytes 786440 | tf_op jit(solution)/shard_map/ppermute | solution.py:32
  81.3 1.9 %collective-permute-start.14 = (bf16[2,2,256,256]{3,2,1,0:T(8,128)(2,1)S(1)}, bf16[2,2,256,256]{3,2,1,0:T(8,128)(2,1)S(1)}, u32[]{:S(2)}, u32[]{:S(2)}) collective-permute-start(bf16[2,2,256,256]{3,2,1,0:T(8,128)(2,1)S(1)} %get-tuple-element.48), channel_id=1, source_target_pairs={{0,4},{4,0},{8,12},{12,8},{1,5},{5,1},{9,13},{13,9},{2,6},{6,2},{1... | collective-permute-start | bytes 1572872 | tf_op jit(solution)/shard_map/ppermute | solution.py:32
  81.3 9.4 %collective-permute-start.10 = (bf16[2,512,128]{2,1,0:T(8,128)(2,1)}, bf16[2,512,128]{2,1,0:T(8,128)(2,1)S(1)}, u32[]{:S(2)}, u32[]{:S(2)}) collective-permute-start(bf16[2,512,128]{2,1,0:T(8,128)(2,1)} %copy-done.12), channel_id=1, source_target_pairs={{0,1},{1,0},{2,3},{3,2},{4,5},{5,4},{6,7},{7,6},{8,9},{9,8},{10,11... | collective-permute-start | bytes 786440 | tf_op jit(solution)/shard_map/ppermute | solution.py:32
  83.3 7.4 %copy-start.23 = (bf16[2,512,128]{2,1,0:T(8,128)(2,1)S(1)}, bf16[2,512,128]{2,1,0:T(8,128)(2,1)}, u32[]{:S(2)}) copy-start(bf16[2,512,128]{2,1,0:T(8,128)(2,1)} %copy-done.22) | copy-start | bytes 786436
  83.4 8.4 %collective-permute-start.15 = (bf16[2,256,256]{2,1,0:T(8,128)(2,1)S(1)}, bf16[2,256,256]{2,1,0:T(8,128)(2,1)S(1)}, u32[]{:S(2)}, u32[]{:S(2)}) collective-permute-start(bf16[2,256,256]{2,1,0:T(8,128)(2,1)S(1)} %fusion.1), channel_id=1, source_target_pairs={{0,8},{4,12},{8,0},{12,4},{1,9},{5,13},{9,1},{13,5},{2,10},{6,14},... | collective-permute-start | bytes 786440 | tf_op jit(solution)/shard_map/ppermute | solution.py:32
  84.1 8.9 %collective-permute-start.16 = (bf16[2,256,128]{2,1,0:T(8,128)(2,1)S(1)}, bf16[2,256,128]{2,1,0:T(8,128)(2,1)S(1)}, u32[]{:S(2)}, u32[]{:S(2)}) collective-permute-start(bf16[2,256,128]{2,1,0:T(8,128)(2,1)S(1)} %slice.42), channel_id=1, source_target_pairs={{0,1},{1,0},{2,3},{3,2},{4,5},{5,4},{6,7},{7,6},{8,9},{9,8},{10,11... | collective-permute-start | bytes 393224 | tf_op jit(solution)/shard_map/ppermute | solution.py:32
  91.9 5.0 %collective-permute-start.17 = (bf16[2,256,128]{2,1,0:T(8,128)(2,1)S(1)}, bf16[2,256,128]{2,1,0:T(8,128)(2,1)S(1)}, u32[]{:S(2)}, u32[]{:S(2)}) collective-permute-start(bf16[2,256,128]{2,1,0:T(8,128)(2,1)S(1)} %slice.41), channel_id=1, source_target_pairs={{0,1},{1,0},{2,3},{3,2},{4,5},{5,4},{6,7},{7,6},{8,9},{9,8},{10,11... | collective-permute-start | bytes 393224 | tf_op jit(solution)/shard_map/ppermute | solution.py:32
  (20 other events, 31.6 us)

commit v11 on v10

--- a/solution.py
+++ b/solution.py
@@ -16,7 +16,7 @@
 STRIP = 16
 PAIR = 2
 MASKED = -1e30
-ATTEND_VMEM = 48 * 2**20
+ATTEND_VMEM = 40 * 2**20
 PACK_VMEM = 48 * 2**20
 SCALE = HD ** (-0.5)
 

time: 98.3 us -> 101 us (1.027)
  local copies, waits for them, and re-layouts: 12 us -> 15.2 us
    unnamed x52 -> x56, local copies, waits for them, and re-layouts: 11.9 us -> 15.1 us
    pallas_call x2, Pallas kernels: 47.5 us -> 46.4 us  [attend(): pl.pallas_call(functools.partial(attend_kernel, (pieces, rows, keep, send...]
  transfers between devices with their start and end apart: 18 -> 18, of which waited for: 8 -> 8; matrix products, arithmetic and copies ran while one was open for 1% -> 1% of each run, Pallas kernels for 49% -> 47%
where the time goes in v11:
time: 101 us; the launch traced here: 100 us
  Pallas kernels  46.6 us (46%)
  waiting for transfers between devices  19.9 us (20%)
  starting transfers between devices  16.1 us (16%)
  local copies, waits for them, and re-layouts  15.2 us (15%)
  other arithmetic  1.37 us (1%)
    pallas_call x2, Pallas kernels, attend(): pl.pallas_call(functools.partial(attend_kernel, (pieces, rows, keep, send...  46.4 us
    ppermute x18, waiting for transfers between devices, swap(): lax.ppermute(block, axis, [(i, i ^ step) for i in range(lax.axis_size(axi...  19.9 us
    ppermute x18, starting transfers between devices, swap(): lax.ppermute(block, axis, [(i, i ^ step) for i in range(lax.axis_size(axi...  16.1 us
    unnamed x56, local copies, waits for them, and re-layouts  15.1 us
  transfers between devices with their start and end apart: 18, of which 8 were waited for; matrix products, arithmetic and copies ran while one was open for 1% of the time, Pallas kernels for 47%

profile of v11, /device:TPU:0, one launch (start us, length us, event | category | flops | bytes accessed | tf_op | source)
XLA Modules:
  0.0 100.0 jit_solution(537686590665838723)
XLA Ops:
  0.6 1.0 %copy-done.1 = bf16[2,256,512]{2,1,0:T(8,128)(2,1)S(1)} copy-done((bf16[2,256,512]{2,1,0:T(8,128)(2,1)S(1)}, bf16[2,256,512]{2,1,0:T(8,128)(2,1)}, u32[]{:S(2)}) %copy-start.1) | copy-done | bytes 524312
  1.7 3.1 %collective-permute-start = (bf16[2,256,256]{2,1,0:T(8,128)(2,1)S(1)}, bf16[2,256,256]{2,1,0:T(8,128)(2,1)S(1)}, u32[]{:S(2)}, u32[]{:S(2)}) collective-permute-start(bf16[2,256,256]{2,1,0:T(8,128)(2,1)S(1)} %get-tuple-element.29), channel_id=1, source_target_pairs={{0,1},{1,0},{2,3},{3,2},{4,5},{5,4},{6,7},{7,6},{8,9},{9,8},{10,11... | collective-permute-start | bytes 786440 | tf_op jit(solution)/shard_map/ppermute | solution.py:32
  4.8 1.5 %collective-permute-start.3 = (bf16[2,256,256]{2,1,0:T(8,128)(2,1)S(1)}, bf16[2,256,256]{2,1,0:T(8,128)(2,1)S(1)}, u32[]{:S(2)}, u32[]{:S(2)}) collective-permute-start(bf16[2,256,256]{2,1,0:T(8,128)(2,1)S(1)} %get-tuple-element.31.refs_4_), channel_id=1, source_target_pairs={{0,8},{4,12},{8,0},{12,4},{1,9},{5,13},{9,1},{13,5},{2,10},{6,14},... | collective-permute-start | bytes 786440 | tf_op jit(solution)/shard_map/ppermute | solution.py:32
  6.3 1.2 %copy-done = bf16[2,512,512]{2,1,0:T(8,128)(2,1)S(1)} copy-done((bf16[2,512,512]{2,1,0:T(8,128)(2,1)S(1)}, bf16[2,512,512]{2,1,0:T(8,128)(2,1)}, u32[]{:S(2)}) %copy-start) | copy-done | bytes 1048600
  7.7 3.5 %collective-permute-done.refs_8_ = bf16[2,256,256]{2,1,0:T(8,128)(2,1)S(1)} collective-permute-done((bf16[2,256,256]{2,1,0:T(8,128)(2,1)S(1)}, bf16[2,256,256]{2,1,0:T(8,128)(2,1)S(1)}, u32[]{:S(2)}, u32[]{:S(2)}) %collective-permute-start) | collective-permute-done | bytes 262176 | tf_op jit(solution)/shard_map/ppermute | solution.py:32
  11.1 1.7 %collective-permute-start.6 = (bf16[2,256,256]{2,1,0:T(8,128)(2,1)S(1)}, bf16[2,256,256]{2,1,0:T(8,128)(2,1)S(1)}, u32[]{:S(2)}, u32[]{:S(2)}) collective-permute-start(bf16[2,256,256]{2,1,0:T(8,128)(2,1)S(1)} %collective-permute-done.refs_8_), channel_id=1, source_target_pairs={{0,8},{4,12},{8,0},{12,4},{1,9},{5,13},{9,1},{13,5},{2,10},{6,14},... | collective-permute-start | bytes 786440 | tf_op jit(solution)/shard_map/ppermute | solution.py:32
  12.8 1.6 %collective-permute-start.8 = (bf16[2,512,128]{2,1,0:T(8,128)(2,1)S(1)}, bf16[2,512,128]{2,1,0:T(8,128)(2,1)S(1)}, u32[]{:S(2)}, u32[]{:S(2)}) collective-permute-start(bf16[2,512,128]{2,1,0:T(8,128)(2,1)S(1)} %get-tuple-element.33), channel_id=1, source_target_pairs={{0,1},{1,0},{2,3},{3,2},{4,5},{5,4},{6,7},{7,6},{8,9},{9,8},{10,11... | collective-permute-start | bytes 786440 | tf_op jit(solution)/shard_map/ppermute | solution.py:32
  14.9 3.7 %collective-permute-done.6.refs_10_ = bf16[2,256,256]{2,1,0:T(8,128)(2,1)S(1)} collective-permute-done((bf16[2,256,256]{2,1,0:T(8,128)(2,1)S(1)}, bf16[2,256,256]{2,1,0:T(8,128)(2,1)S(1)}, u32[]{:S(2)}, u32[]{:S(2)}) %collective-permute-start.6) | collective-permute-done | bytes 262176 | tf_op jit(solution)/shard_map/ppermute | solution.py:32
  19.4 1.4 %collective-permute-start.1 = (bf16[2,512,128]{2,1,0:T(8,128)(2,1)S(1)}, bf16[2,512,128]{2,1,0:T(8,128)(2,1)S(1)}, u32[]{:S(2)}, u32[]{:S(2)}) collective-permute-start(bf16[2,512,128]{2,1,0:T(8,128)(2,1)S(1)} %get-tuple-element.30), channel_id=1, source_target_pairs={{0,1},{1,0},{2,3},{3,2},{4,5},{5,4},{6,7},{7,6},{8,9},{9,8},{10,11... | collective-permute-start | bytes 786440 | tf_op jit(solution)/shard_map/ppermute | solution.py:32
  22.2 1.8 %copy-done.2 = bf16[2,512,1024]{2,1,0:T(8,128)(2,1)S(1)} copy-done((bf16[2,512,1024]{2,1,0:T(8,128)(2,1)S(1)}, bf16[2,512,1024]{2,1,0:T(8,128)(2,1)}, u32[]{:S(2)}) %copy-start.2) | copy-done | bytes 2097176
  24.0 1.6 %copy-done.3 = bf16[2,512,1024]{2,1,0:T(8,128)(2,1)S(1)} copy-done((bf16[2,512,1024]{2,1,0:T(8,128)(2,1)S(1)}, bf16[2,512,1024]{2,1,0:T(8,128)(2,1)}, u32[]{:S(2)}) %copy-start.3) | copy-done | bytes 2097176
  25.6 0.9 copy-done.16
  26.5 23.1 %shard_map.86 = (bf16[2,512,1024]{2,1,0:T(8,128)(2,1)}, bf16[2,512,1024]{2,1,0:T(8,128)(2,1)}, bf16[2,512,512]{2,1,0:T(8,128)(2,1)}, bf16[2,512,128]{2,1,0:T(8,1...) custom-call(s32[3]{0:T(128)S(1)} %pad_add_fusion.scalars, ...), custom_call_target="tpu_custom_call" | custom-call | flops 19327352832 | bytes 4194304 | tf_op jit(solution)/shard_map/pallas_call | solution.py:271
  49.8 1.0 collective-permute-start.12
  51.6 1.6 %collective-permute-start.9 = (bf16[2,512,128]{2,1,0:T(8,128)(2,1)S(1)}, bf16[2,512,128]{2,1,0:T(8,128)(2,1)S(1)}, u32[]{:S(2)}, u32[]{:S(2)}) collective-permute-start(bf16[2,512,128]{2,1,0:T(8,128)(2,1)S(1)} %get-tuple-element.40), channel_id=1, source_target_pairs={{0,1},{1,0},{2,3},{3,2},{4,5},{5,4},{6,7},{7,6},{8,9},{9,8},{10,11... | collective-permute-start | bytes 786440 | tf_op jit(solution)/shard_map/ppermute | solution.py:32
  53.2 0.9 copy-done.5
  54.1 0.9 copy-done.7
  56.0 0.9 copy-done.11
  57.0 0.9 copy-done.13
  57.9 23.3 %shard_map.87 = (bf16[2,512,1024]{2,1,0:T(8,128)(2,1)}, bf16[2,512,1024]{2,1,0:T(8,128)(2,1)}, bf16[2,512,512]{2,1,0:T(8,128)(2,1)}, bf16[2,512,128]{2,1,0:T(8,1...) custom-call(s32[3]{0:T(128)S(1)} %pad_add_fusion.scalars, ...), custom_call_target="tpu_custom_call", output_to_operand_aliasing={{0}: (13, {}), {1}: (14, {}), {2}: (15, {})} | custom-call | flops 19327352832 | bytes 4194304 | tf_op jit(solution)/shard_map/pallas_call | solution.py:271
  84.0 1.3 %collective-permute-done.14 = bf16[2,2,256,256]{3,2,1,0:T(8,128)(2,1)S(1)} collective-permute-done((bf16[2,2,256,256]{3,2,1,0:T(8,128)(2,1)S(1)}, bf16[2,2,256,256]{3,2,1,0:T(8,128)(2,1)S(1)}, u32[]{:S(2)}, u32[]{:S(2)}) %collective-permute-start.14) | collective-permute-done | bytes 524320 | tf_op jit(solution)/shard_map/ppermute | solution.py:32
  87.2 5.6 %collective-permute-done.10 = bf16[2,512,128]{2,1,0:T(8,128)(2,1)S(1)} collective-permute-done((bf16[2,512,128]{2,1,0:T(8,128)(2,1)}, bf16[2,512,128]{2,1,0:T(8,128)(2,1)S(1)}, u32[]{:S(2)}, u32[]{:S(2)}) %collective-permute-start.10) | collective-permute-done | bytes 262176 | tf_op jit(solution)/shard_map/ppermute | solution.py:32
  95.3 3.7 %collective-permute-done.17 = bf16[2,256,128]{2,1,0:T(8,128)(2,1)S(1)} collective-permute-done((bf16[2,256,128]{2,1,0:T(8,128)(2,1)S(1)}, bf16[2,256,128]{2,1,0:T(8,128)(2,1)S(1)}, u32[]{:S(2)}, u32[]{:S(2)}) %collective-permute-start.17) | collective-permute-done | bytes 131104 | tf_op jit(solution)/shard_map/ppermute | solution.py:32
  99.1 1.0 copy-done.17
  (85 shorter events, 11.9 us)
Async XLA Ops:
  1.7 9.4 %collective-permute-start = (bf16[2,256,256]{2,1,0:T(8,128)(2,1)S(1)}, bf16[2,256,256]{2,1,0:T(8,128)(2,1)S(1)}, u32[]{:S(2)}, u32[]{:S(2)}) collective-permute-start(bf16[2,256,256]{2,1,0:T(8,128)(2,1)S(1)} %get-tuple-element.29), channel_id=1, source_target_pairs={{0,1},{1,0},{2,3},{3,2},{4,5},{5,4},{6,7},{7,6},{8,9},{9,8},{10,11... | collective-permute-start | bytes 786440 | tf_op jit(solution)/shard_map/ppermute | solution.py:32
  4.8 9.8 %collective-permute-start.3 = (bf16[2,256,256]{2,1,0:T(8,128)(2,1)S(1)}, bf16[2,256,256]{2,1,0:T(8,128)(2,1)S(1)}, u32[]{:S(2)}, u32[]{:S(2)}) collective-permute-start(bf16[2,256,256]{2,1,0:T(8,128)(2,1)S(1)} %get-tuple-element.31.refs_4_), channel_id=1, source_target_pairs={{0,8},{4,12},{8,0},{12,4},{1,9},{5,13},{9,1},{13,5},{2,10},{6,14},... | collective-permute-start | bytes 786440 | tf_op jit(solution)/shard_map/ppermute | solution.py:32
  11.1 7.5 %collective-permute-start.6 = (bf16[2,256,256]{2,1,0:T(8,128)(2,1)S(1)}, bf16[2,256,256]{2,1,0:T(8,128)(2,1)S(1)}, u32[]{:S(2)}, u32[]{:S(2)}) collective-permute-start(bf16[2,256,256]{2,1,0:T(8,128)(2,1)S(1)} %collective-permute-done.refs_8_), channel_id=1, source_target_pairs={{0,8},{4,12},{8,0},{12,4},{1,9},{5,13},{9,1},{13,5},{2,10},{6,14},... | collective-permute-start | bytes 786440 | tf_op jit(solution)/shard_map/ppermute | solution.py:32
  12.8 6.6 %collective-permute-start.2 = (bf16[2,256,256]{2,1,0:T(8,128)(2,1)S(1)}, bf16[2,256,256]{2,1,0:T(8,128)(2,1)S(1)}, u32[]{:S(2)}, u32[]{:S(2)}) collective-permute-start(bf16[2,256,256]{2,1,0:T(8,128)(2,1)S(1)} %get-tuple-element.31.refs_4_), channel_id=1, source_target_pairs={{0,4},{4,0},{8,12},{12,8},{1,5},{5,1},{9,13},{13,9},{2,6},{6,2},{1... | collective-permute-start | bytes 786440 | tf_op jit(solution)/shard_map/ppermute | solution.py:32
  12.8 8.7 %collective-permute-start.8 = (bf16[2,512,128]{2,1,0:T(8,128)(2,1)S(1)}, bf16[2,512,128]{2,1,0:T(8,128)(2,1)S(1)}, u32[]{:S(2)}, u32[]{:S(2)}) collective-permute-start(bf16[2,512,128]{2,1,0:T(8,128)(2,1)S(1)} %get-tuple-element.33), channel_id=1, source_target_pairs={{0,1},{1,0},{2,3},{3,2},{4,5},{5,4},{6,7},{7,6},{8,9},{9,8},{10,11... | collective-permute-start | bytes 786440 | tf_op jit(solution)/shard_map/ppermute | solution.py:32
  14.3 7.9 %collective-permute-start.5 = (bf16[2,256,256]{2,1,0:T(8,128)(2,1)S(1)}, bf16[2,256,256]{2,1,0:T(8,128)(2,1)S(1)}, u32[]{:S(2)}, u32[]{:S(2)}) collective-permute-start(bf16[2,256,256]{2,1,0:T(8,128)(2,1)S(1)} %collective-permute-done.refs_8_), channel_id=1, source_target_pairs={{0,4},{4,0},{8,12},{12,8},{1,5},{5,1},{9,13},{13,9},{2,6},{6,2},{1... | collective-permute-start | bytes 786440 | tf_op jit(solution)/shard_map/ppermute | solution.py:32
  14.6 7.6 %collective-permute-start.4 = (bf16[2,256,256]{2,1,0:T(8,128)(2,1)S(1)}, bf16[2,256,256]{2,1,0:T(8,128)(2,1)S(1)}, u32[]{:S(2)}, u32[]{:S(2)}) collective-permute-start(bf16[2,256,256]{2,1,0:T(8,128)(2,1)S(1)} %collective-permute-done.3.refs_6_), channel_id=1, source_target_pairs={{0,4},{4,0},{8,12},{12,8},{1,5},{5,1},{9,13},{13,9},{2,6},{6,2},{1... | collective-permute-start | bytes 786440 | tf_op jit(solution)/shard_map/ppermute | solution.py:32
  18.6 31.0 %copy-start.4 = (bf16[2,256,256]{2,1,0:T(8,128)(2,1)}, bf16[2,256,256]{2,1,0:T(8,128)(2,1)S(1)}, u32[]{:S(2)}) copy-start(bf16[2,256,256]{2,1,0:T(8,128)(2,1)S(1)} %collective-permute-done.6.refs_10_) | copy-start | bytes 786436
  18.6 3.6 %collective-permute-start.7 = (bf16[2,256,256]{2,1,0:T(8,128)(2,1)S(1)}, bf16[2,256,256]{2,1,0:T(8,128)(2,1)S(1)}, u32[]{:S(2)}, u32[]{:S(2)}) collective-permute-start(bf16[2,256,256]{2,1,0:T(8,128)(2,1)S(1)} %collective-permute-done.6.refs_10_), channel_id=1, source_target_pairs={{0,4},{4,0},{8,12},{12,8},{1,5},{5,1},{9,13},{13,9},{2,6},{6,2},{1... | collective-permute-start | bytes 786440 | tf_op jit(solution)/shard_map/ppermute | solution.py:32
  19.4 30.3 %copy-start.6 = (bf16[2,256,256]{2,1,0:T(8,128)(2,1)}, bf16[2,256,256]{2,1,0:T(8,128)(2,1)S(1)}, u32[]{:S(2)}) copy-start(bf16[2,256,256]{2,1,0:T(8,128)(2,1)S(1)} %collective-permute-done.2.refs_5_) | copy-start | bytes 786436
  19.4 33.8 %collective-permute-start.1 = (bf16[2,512,128]{2,1,0:T(8,128)(2,1)S(1)}, bf16[2,512,128]{2,1,0:T(8,128)(2,1)S(1)}, u32[]{:S(2)}, u32[]{:S(2)}) collective-permute-start(bf16[2,512,128]{2,1,0:T(8,128)(2,1)S(1)} %get-tuple-element.30), channel_id=1, source_target_pairs={{0,1},{1,0},{2,3},{3,2},{4,5},{5,4},{6,7},{7,6},{8,9},{9,8},{10,11... | collective-permute-start | bytes 786440 | tf_op jit(solution)/shard_map/ppermute | solution.py:32
  22.2 27.5 %copy-start.10 = (bf16[2,256,256]{2,1,0:T(8,128)(2,1)}, bf16[2,256,256]{2,1,0:T(8,128)(2,1)S(1)}, u32[]{:S(2)}) copy-start(bf16[2,256,256]{2,1,0:T(8,128)(2,1)S(1)} %collective-permute-done.4.refs_7_) | copy-start | bytes 786436
  22.2 27.5 %copy-start.8 = (bf16[2,256,256]{2,1,0:T(8,128)(2,1)}, bf16[2,256,256]{2,1,0:T(8,128)(2,1)S(1)}, u32[]{:S(2)}) copy-start(bf16[2,256,256]{2,1,0:T(8,128)(2,1)S(1)} %collective-permute-done.5.refs_9_) | copy-start | bytes 786436
  26.5 23.1 %copy-start.12 = (bf16[2,256,256]{2,1,0:T(8,128)(2,1)}, bf16[2,256,256]{2,1,0:T(8,128)(2,1)S(1)}, u32[]{:S(2)}) copy-start(bf16[2,256,256]{2,1,0:T(8,128)(2,1)S(1)} %collective-permute-done.7.refs_11_) | copy-start | bytes 786436
  49.7 32.3 %collective-permute-start.11 = (bf16[2,256,256]{2,1,0:T(8,128)(2,1)S(1)}, bf16[2,256,256]{2,1,0:T(8,128)(2,1)S(1)}, u32[]{:S(2)}, u32[]{:S(2)}) collective-permute-start(bf16[2,256,256]{2,1,0:T(8,128)(2,1)S(1)} %bitcast.14), channel_id=1, source_target_pairs={{0,4},{4,0},{8,12},{12,8},{1,5},{5,1},{9,13},{13,9},{2,6},{6,2},{1... | collective-permute-start | bytes 786440 | tf_op jit(solution)/shard_map/ppermute | solution.py:32
  49.8 32.2 %collective-permute-start.12 = (bf16[2,256,256]{2,1,0:T(8,128)(2,1)S(1)}, bf16[2,256,256]{2,1,0:T(8,128)(2,1)S(1)}, u32[]{:S(2)}, u32[]{:S(2)}) collective-permute-start(bf16[2,256,256]{2,1,0:T(8,128)(2,1)S(1)} %bitcast.13), channel_id=1, source_target_pairs={{0,8},{4,12},{8,0},{12,4},{1,9},{5,13},{9,1},{13,5},{2,10},{6,14},... | collective-permute-start | bytes 786440 | tf_op jit(solution)/shard_map/ppermute | solution.py:32
  50.7 31.2 %collective-permute-start.13 = (bf16[2,256,256]{2,1,0:T(8,128)(2,1)S(1)}, bf16[2,256,256]{2,1,0:T(8,128)(2,1)S(1)}, u32[]{:S(2)}, u32[]{:S(2)}) collective-permute-start(bf16[2,256,256]{2,1,0:T(8,128)(2,1)S(1)} %bitcast.12), channel_id=1, source_target_pairs={{0,12},{4,8},{8,4},{12,0},{1,13},{5,9},{9,5},{13,1},{2,14},{6,10},... | collective-permute-start | bytes 786440 | tf_op jit(solution)/shard_map/ppermute | solution.py:32
  51.6 30.4 %collective-permute-start.9 = (bf16[2,512,128]{2,1,0:T(8,128)(2,1)S(1)}, bf16[2,512,128]{2,1,0:T(8,128)(2,1)S(1)}, u32[]{:S(2)}, u32[]{:S(2)}) collective-permute-start(bf16[2,512,128]{2,1,0:T(8,128)(2,1)S(1)} %get-tuple-element.40), channel_id=1, source_target_pairs={{0,1},{1,0},{2,3},{3,2},{4,5},{5,4},{6,7},{7,6},{8,9},{9,8},{10,11... | collective-permute-start | bytes 786440 | tf_op jit(solution)/shard_map/ppermute | solution.py:32
  83.3 1.9 %collective-permute-start.14 = (bf16[2,2,256,256]{3,2,1,0:T(8,128)(2,1)S(1)}, bf16[2,2,256,256]{3,2,1,0:T(8,128)(2,1)S(1)}, u32[]{:S(2)}, u32[]{:S(2)}) collective-permute-start(bf16[2,2,256,256]{3,2,1,0:T(8,128)(2,1)S(1)} %get-tuple-element.48), channel_id=1, source_target_pairs={{0,4},{4,0},{8,12},{12,8},{1,5},{5,1},{9,13},{13,9},{2,6},{6,2},{1... | collective-permute-start | bytes 1572872 | tf_op jit(solution)/shard_map/ppermute | solution.py:32
  83.5 9.3 %collective-permute-start.10 = (bf16[2,512,128]{2,1,0:T(8,128)(2,1)}, bf16[2,512,128]{2,1,0:T(8,128)(2,1)S(1)}, u32[]{:S(2)}, u32[]{:S(2)}) collective-permute-start(bf16[2,512,128]{2,1,0:T(8,128)(2,1)} %copy-done.14), channel_id=1, source_target_pairs={{0,1},{1,0},{2,3},{3,2},{4,5},{5,4},{6,7},{7,6},{8,9},{9,8},{10,11... | collective-permute-start | bytes 786440 | tf_op jit(solution)/shard_map/ppermute | solution.py:32
  85.4 7.5 %copy-start.25 = (bf16[2,512,128]{2,1,0:T(8,128)(2,1)S(1)}, bf16[2,512,128]{2,1,0:T(8,128)(2,1)}, u32[]{:S(2)}) copy-start(bf16[2,512,128]{2,1,0:T(8,128)(2,1)} %copy-done.24) | copy-start | bytes 786436
  85.4 8.4 %collective-permute-start.15 = (bf16[2,256,256]{2,1,0:T(8,128)(2,1)S(1)}, bf16[2,256,256]{2,1,0:T(8,128)(2,1)S(1)}, u32[]{:S(2)}, u32[]{:S(2)}) collective-permute-start(bf16[2,256,256]{2,1,0:T(8,128)(2,1)S(1)} %fusion.1), channel_id=1, source_target_pairs={{0,8},{4,12},{8,0},{12,4},{1,9},{5,13},{9,1},{13,5},{2,10},{6,14},... | collective-permute-start | bytes 786440 | tf_op jit(solution)/shard_map/ppermute | solution.py:32
  86.4 8.7 %collective-permute-start.16 = (bf16[2,256,128]{2,1,0:T(8,128)(2,1)S(1)}, bf16[2,256,128]{2,1,0:T(8,128)(2,1)S(1)}, u32[]{:S(2)}, u32[]{:S(2)}) collective-permute-start(bf16[2,256,128]{2,1,0:T(8,128)(2,1)S(1)} %slice.42), channel_id=1, source_target_pairs={{0,1},{1,0},{2,3},{3,2},{4,5},{5,4},{6,7},{7,6},{8,9},{9,8},{10,11... | collective-permute-start | bytes 393224 | tf_op jit(solution)/shard_map/ppermute | solution.py:32
  94.0 5.0 %collective-permute-start.17 = (bf16[2,256,128]{2,1,0:T(8,128)(2,1)S(1)}, bf16[2,256,128]{2,1,0:T(8,128)(2,1)S(1)}, u32[]{:S(2)}, u32[]{:S(2)}) collective-permute-start(bf16[2,256,128]{2,1,0:T(8,128)(2,1)S(1)} %slice.41), channel_id=1, source_target_pairs={{0,1},{1,0},{2,3},{3,2},{4,5},{5,4},{6,7},{7,6},{8,9},{9,8},{10,11... | collective-permute-start | bytes 393224 | tf_op jit(solution)/shard_map/ppermute | solution.py:32
  (22 other events, 35.0 us)

commit v12 on v8

--- a/solution.py
+++ b/solution.py
@@ -14,6 +14,7 @@
 GROUP = H // KVH
 BLOCK = 256
 STRIP = 16
+PAIR = 2
 MASKED = -1e30
 SCALE = HD ** (-0.5)
 
@@ -38,7 +39,7 @@
     rest = refs[4 + 2 * pieces + n_pass :]
     out_ref, dq_ref, dra_ref, drb_ref, keep_ref = rest[:5]
     send_refs = rest[5 : 5 + len(sends)]
-    k_all, v_all, q_t, do_t, scores, grad_probs, probs, dscores, acc_k, acc_v, sum_k, sum_v = rest[5 + len(sends) :]
+    k_all, v_all, q_all, do_all, q_t, do_t, scores, grad_probs, probs, dscores, acc_k, acc_v, sum_k, sum_v = rest[5 + len(sends) :]
 
     r = pl.program_id(0)
     head = pl.program_id(1)
@@ -70,37 +71,54 @@
         acc_k[...] = jnp.zeros_like(acc_k)
         acc_v[...] = jnp.zeros_like(acc_v)
 
+    size = PAIR * BLOCK
+
+    for i in range(n_blocks):
+        for j in range(PAIR):
+            at = slice(i * size + j * BLOCK, i * size + (j + 1) * BLOCK)
+            from_t, lanes = slice(i * BLOCK, (i + 1) * BLOCK), slice(j * HD, (j + 1) * HD)
+            q_all[at, :] = q_ref[0, from_t, lanes]
+            do_all[at, :] = do_ref[0, from_t, lanes]
+
+    def seeing(u):
+        return slice(max(u - n_prompt, 0) // BLOCK * size, n_blocks * size)
+
     def score(u):
-        t = slice(max(u - n_prompt, 0), n_query)
-        scores[t, u : u + BLOCK] = dot(q_ref[0, t, :], k_all[u : u + BLOCK, :], NT)
+        t = seeing(u)
+        scores[t, u : u + BLOCK] = dot(q_all[t, :], k_all[u : u + BLOCK, :], NT)
 
     def grad_prob(u):
-        t = slice(max(u - n_prompt, 0), n_query)
-        grad_probs[t, u : u + BLOCK] = dot(do_ref[0, t, :], v_all[u : u + BLOCK, :], NT)
+        t = seeing(u)
+        grad_probs[t, u : u + BLOCK] = dot(do_all[t, :], v_all[u : u + BLOCK, :], NT)
 
     def grad_value(u):
-        t = slice(max(u - n_prompt, 0), n_query)
+        t = seeing(u)
         acc_v[:, u : u + BLOCK] += dot(do_t[:, t], probs[t, u : u + BLOCK], NN)
 
     def grad_key(u):
-        t = slice(max(u - n_prompt, 0), n_query)
+        t = seeing(u)
         acc_k[:, u : u + BLOCK] += dot(q_t[:, t], dscores[t, u : u + BLOCK], NN)
 
     def turn():
-        q_t[...] = q_ref[0].T
-        do_t[...] = do_ref[0].T
+        q_t[...] = q_all[...].T
+        do_t[...] = do_all[...].T
 
     def stages(i):
         st = {}
-        t0 = i * BLOCK
-        t = slice(t0, t0 + BLOCK)
-        edge = n_prompt + t0
+        t0 = i * size
+        t = slice(t0, t0 + size)
+        edge = n_prompt + i * BLOCK
         seen = edge + BLOCK
+
+        def put(ref, rows_out):
+            for j in range(PAIR):
+                part = rows_out[j * BLOCK : (j + 1) * BLOCK].astype(jnp.bfloat16)
+                ref[0, i * BLOCK : (i + 1) * BLOCK, j * HD : (j + 1) * HD] = part
 
         def softmax(row):
             at = slice(t0 + row, t0 + row + STRIP)
             left = scores[at, :edge]
-            rows_at = lax.broadcasted_iota(jnp.int32, (STRIP, BLOCK), 0) + row
+            rows_at = lax.broadcasted_iota(jnp.int32, (STRIP, BLOCK), 0) + row % BLOCK
             columns = lax.broadcasted_iota(jnp.int32, (STRIP, BLOCK), 1)
             right = jnp.where(columns <= rows_at, scores[at, edge:seen], MASKED)
             top = jnp.maximum(jnp.max(left, axis=1, keepdims=True), jnp.max(right, axis=1, keepdims=True)) * SCALE
@@ -113,8 +131,8 @@
 
         def output():
             o = dot(probs[t, :seen], v_all[:seen, :], NN)
-            out_ref[0, t, :] = o.astype(jnp.bfloat16)
-            st["delta"] = jnp.sum(o * do_ref[0, t, :].astype(jnp.float32), axis=1, keepdims=True)
+            put(out_ref, o)
+            st["delta"] = jnp.sum(o * do_all[t, :].astype(jnp.float32), axis=1, keepdims=True)
 
         def grad_score(row):
             at = slice(t0 + row, t0 + row + STRIP)
@@ -123,9 +141,9 @@
             dscores[at, :seen] = ds.astype(jnp.bfloat16)
 
         def query():
-            dq_ref[0, t, :] = dot(dscores[t, :seen], k_all[:seen, :], NN).astype(jnp.bfloat16)
-
-        strips = range(0, BLOCK, STRIP)
+            put(dq_ref, dot(dscores[t, :seen], k_all[:seen, :], NN))
+
+        strips = range(0, size, STRIP)
         each = lambda f: [functools.partial(f, x) for x in strips]
         return {"softmax": each(softmax), "output": [output], "grad": each(grad_score), "query": [query]}
 
@@ -203,7 +221,9 @@
     def prompt_map(column):
         return lambda r, j, sc: (sc[r], 0, column(sc[n_resp]))
 
-    q_spec = pl.BlockSpec((1, n_query, HD), lambda r, j, sc: (r, 0, chunk * heads + j))
+    steps = heads // PAIR
+    n_rows = PAIR * n_query
+    q_spec = pl.BlockSpec((1, n_query, PAIR * HD), lambda r, j, sc: (r, 0, chunk * steps + j))
     in_specs = [q_spec, q_spec]
     in_specs += [pl.BlockSpec((1, n_query, HD), resp_map(c)) for _, c in (resp_a, resp_b)]
     in_specs += [pl.BlockSpec((1, rows, HD), prompt_map(c)) for _, c in (*prompt_a, *prompt_b)]
@@ -232,12 +252,14 @@
     scratch = [
         pltpu.VMEM((n_keys, HD), jnp.bfloat16),
         pltpu.VMEM((n_keys, HD), jnp.bfloat16),
-        pltpu.VMEM((HD, n_query), jnp.bfloat16),
-        pltpu.VMEM((HD, n_query), jnp.bfloat16),
-        pltpu.VMEM((n_query, n_keys), jnp.float32),
-        pltpu.VMEM((n_query, n_keys), jnp.float32),
-        pltpu.VMEM((n_query, n_keys), jnp.bfloat16),
-        pltpu.VMEM((n_query, n_keys), jnp.bfloat16),
+        pltpu.VMEM((n_rows, HD), jnp.bfloat16),
+        pltpu.VMEM((n_rows, HD), jnp.bfloat16),
+        pltpu.VMEM((HD, n_rows), jnp.bfloat16),
+        pltpu.VMEM((HD, n_rows), jnp.bfloat16),
+        pltpu.VMEM((n_rows, n_keys), jnp.float32),
+        pltpu.VMEM((n_rows, n_keys), jnp.float32),
+        pltpu.VMEM((n_rows, n_keys), jnp.bfloat16),
+        pltpu.VMEM((n_rows, n_keys), jnp.bfloat16),
         pltpu.VMEM((HD, n_keys), jnp.float32),
         pltpu.VMEM((HD, n_keys), jnp.float32),
         pltpu.VMEM((P_SIZE, n_prompt, HD), jnp.float32),
@@ -248,7 +270,7 @@
         functools.partial(attend_kernel, (pieces, rows, keep, sends, n_pass)),
         grid_spec=pltpu.PrefetchScalarGridSpec(
             num_scalar_prefetch=1,
-            grid=(n_resp, heads),
+            grid=(n_resp, steps),
             in_specs=in_specs,
             out_specs=out_specs,
             scratch_shapes=scratch,
@@ -361,7 +383,7 @@
         if final:
             (send,) = order([sends[0]], arrived)
             sums = keep + core(send).astype(jnp.float32)
-            (across,) = order([x(sums[1].astype(jnp.bfloat16))], [d_resp[-1], *[b for _, b in d_prompt]])
+            (across,) = order([x(sums[1].astype(jnp.bfloat16))], [d_resp[-1]])
             total = sums[0] + across.astype(jnp.float32)
         else:
             parts = [move(part[0]) for move, part in zip((core, x, both), sends)]

time: 96.7 us -> 94.3 us (0.975)
  waiting for transfers between devices: 15 us -> 20 us
  Pallas kernels: 51.4 us -> 47.4 us
  starting transfers between devices: 22.8 us -> 19.6 us
    ppermute x25, waiting for transfers between devices: 15 us -> 20 us  [swap(): lax.ppermute(block, axis, [(i, i ^ step) for i in range(lax.axis_size(axi...]
    pallas_call x2, Pallas kernels: 50.6 us -> 46.6 us  [attend(): pl.pallas_call(functools.partial(attend_kernel, (pieces, rows, keep, send...]
    ppermute x25, starting transfers between devices: 22.8 us -> 19.6 us  [swap(): lax.ppermute(block, axis, [(i, i ^ step) for i in range(lax.axis_size(axi...]
  transfers between devices with their start and end apart: 25 -> 25, of which waited for: 7 -> 7; matrix products, arithmetic and copies ran while one was open for 0% -> 1% of each run, Pallas kernels for 52% -> 50%
where the time goes in v12:
time: 94.3 us; the launch traced here: 94.1 us
  Pallas kernels  47.4 us (50%)
  waiting for transfers between devices  20 us (21%)
  starting transfers between devices  19.6 us (21%)
  local copies, waits for them, and re-layouts  3.97 us (4%)
  other arithmetic  2.35 us (2%)
    pallas_call x2, Pallas kernels, attend(): pl.pallas_call(functools.partial(attend_kernel, (pieces, rows, keep, send...  46.6 us
    ppermute x25, waiting for transfers between devices, swap(): lax.ppermute(block, axis, [(i, i ^ step) for i in range(lax.axis_size(axi...  20 us
    ppermute x25, starting transfers between devices, swap(): lax.ppermute(block, axis, [(i, i ^ step) for i in range(lax.axis_size(axi...  19.6 us
    unnamed x10, local copies, waits for them, and re-layouts  3.87 us
  transfers between devices with their start and end apart: 25, of which 7 were waited for; matrix products, arithmetic and copies ran while one was open for 1% of the time, Pallas kernels for 50%

profile of v12, /device:TPU:0, one launch (start us, length us, event | category | flops | bytes accessed | tf_op | source)
XLA Modules:
  0.0 94.1 jit_solution(11269891354629112362)
XLA Ops:
  0.6 0.7 pad_add_fusion.scalars
  1.4 1.2 %copy-done = bf16[2,512,512]{2,1,0:T(8,128)(2,1)S(1)} copy-done((bf16[2,512,512]{2,1,0:T(8,128)(2,1)S(1)}, bf16[2,512,512]{2,1,0:T(8,128)(2,1)}, u32[]{:S(2)}) %copy-start) | copy-done | bytes 1048600
  2.6 1.0 %copy-done.1 = bf16[2,256,512]{2,1,0:T(8,128)(2,1)S(1)} copy-done((bf16[2,256,512]{2,1,0:T(8,128)(2,1)S(1)}, bf16[2,256,512]{2,1,0:T(8,128)(2,1)}, u32[]{:S(2)}) %copy-start.1) | copy-done | bytes 524312
  3.6 0.8 shard_map.84
  4.5 3.0 %collective-permute-start.6 = (bf16[2,256,128]{2,1,0:T(8,128)(2,1)S(1)}, bf16[2,256,128]{2,1,0:T(8,128)(2,1)S(1)}, u32[]{:S(2)}, u32[]{:S(2)}) collective-permute-start(bf16[2,256,128]{2,1,0:T(8,128)(2,1)S(1)} %get-tuple-element.40.refs_4_), channel_id=1, source_target_pairs={{0,8},{4,12},{8,0},{12,4},{1,9},{5,13},{9,1},{13,5},{2,10},{6,14},... | collective-permute-start | bytes 393224 | tf_op jit(solution)/shard_map/ppermute | solution.py:30
  7.5 1.6 %collective-permute-start.5 = (bf16[2,256,128]{2,1,0:T(8,128)(2,1)S(1)}, bf16[2,256,128]{2,1,0:T(8,128)(2,1)S(1)}, u32[]{:S(2)}, u32[]{:S(2)}) collective-permute-start(bf16[2,256,128]{2,1,0:T(8,128)(2,1)S(1)} %get-tuple-element.39), channel_id=1, source_target_pairs={{0,1},{1,0},{2,3},{3,2},{4,5},{5,4},{6,7},{7,6},{8,9},{9,8},{10,11... | collective-permute-start | bytes 393224 | tf_op jit(solution)/shard_map/ppermute | solution.py:30
  9.5 1.6 %collective-permute-start.4 = (bf16[2,256,128]{2,1,0:T(8,128)(2,1)S(1)}, bf16[2,256,128]{2,1,0:T(8,128)(2,1)S(1)}, u32[]{:S(2)}, u32[]{:S(2)}) collective-permute-start(bf16[2,256,128]{2,1,0:T(8,128)(2,1)S(1)} %get-tuple-element.38), channel_id=1, source_target_pairs={{0,1},{1,0},{2,3},{3,2},{4,5},{5,4},{6,7},{7,6},{8,9},{9,8},{10,11... | collective-permute-start | bytes 393224 | tf_op jit(solution)/shard_map/ppermute | solution.py:30
  11.1 2.8 %collective-permute-done.5.refs_8_ = bf16[2,256,128]{2,1,0:T(8,128)(2,1)S(1)} collective-permute-done((bf16[2,256,128]{2,1,0:T(8,128)(2,1)S(1)}, bf16[2,256,128]{2,1,0:T(8,128)(2,1)S(1)}, u32[]{:S(2)}, u32[]{:S(2)}) %collective-permute-start.5) | collective-permute-done | bytes 131104 | tf_op jit(solution)/shard_map/ppermute | solution.py:30
  14.5 6.4 %collective-permute-done.4.refs_8_ = bf16[2,256,128]{2,1,0:T(8,128)(2,1)S(1)} collective-permute-done((bf16[2,256,128]{2,1,0:T(8,128)(2,1)S(1)}, bf16[2,256,128]{2,1,0:T(8,128)(2,1)S(1)}, u32[]{:S(2)}, u32[]{:S(2)}) %collective-permute-start.4) | collective-permute-done | bytes 131104 | tf_op jit(solution)/shard_map/ppermute | solution.py:30
  22.3 1.7 %collective-permute-start.8 = (bf16[2,256,128]{2,1,0:T(8,128)(2,1)S(1)}, bf16[2,256,128]{2,1,0:T(8,128)(2,1)S(1)}, u32[]{:S(2)}, u32[]{:S(2)}) collective-permute-start(bf16[2,256,128]{2,1,0:T(8,128)(2,1)S(1)} %collective-permute-done.4.refs_8_), channel_id=1, source_target_pairs={{0,8},{4,12},{8,0},{12,4},{1,9},{5,13},{9,1},{13,5},{2,10},{6,14},... | collective-permute-start | bytes 393224 | tf_op jit(solution)/shard_map/ppermute | solution.py:30
  23.9 1.6 %collective-permute-start.1 = (bf16[2,512,128]{2,1,0:T(8,128)(2,1)S(1)}, bf16[2,512,128]{2,1,0:T(8,128)(2,1)S(1)}, u32[]{:S(2)}, u32[]{:S(2)}) collective-permute-start(bf16[2,512,128]{2,1,0:T(8,128)(2,1)S(1)} %get-tuple-element.36), channel_id=1, source_target_pairs={{0,1},{1,0},{2,3},{3,2},{4,5},{5,4},{6,7},{7,6},{8,9},{9,8},{10,11... | collective-permute-start | bytes 786440 | tf_op jit(solution)/shard_map/ppermute | solution.py:30
  25.5 1.6 %copy-done.2 = bf16[2,512,1024]{2,1,0:T(8,128)(2,1)S(1)} copy-done((bf16[2,512,1024]{2,1,0:T(8,128)(2,1)S(1)}, bf16[2,512,1024]{2,1,0:T(8,128)(2,1)}, u32[]{:S(2)}) %copy-start.2) | copy-done | bytes 2097176
  27.1 23.2 %shard_map.85 = (bf16[2,512,1024]{2,1,0:T(8,128)(2,1)}, bf16[2,512,1024]{2,1,0:T(8,128)(2,1)}, bf16[2,512,512]{2,1,0:T(8,128)(2,1)}, bf16[2,512,128]{2,1,0:T(8,1...) custom-call(s32[3]{0:T(128)S(1)} %pad_add_fusion.scalars, ...), custom_call_target="tpu_custom_call" | custom-call | flops 19327352832 | bytes 4194304 | tf_op jit(solution)/shard_map/pallas_call | solution.py:269
  52.3 1.0 %collective-permute-start.20 = (bf16[2,256,256]{2,1,0:T(8,128)(2,1)S(1)}, bf16[2,256,256]{2,1,0:T(8,128)(2,1)S(1)}, u32[]{:S(2)}, u32[]{:S(2)}) collective-permute-start(bf16[2,256,256]{2,1,0:T(8,128)(2,1)S(1)} %bitcast.12), channel_id=1, source_target_pairs={{0,12},{4,8},{8,4},{12,0},{1,13},{5,9},{9,5},{13,1},{2,14},{6,10},... | collective-permute-start | bytes 786440 | tf_op jit(solution)/shard_map/ppermute | solution.py:30
  53.2 23.4 %shard_map.86 = (bf16[2,512,1024]{2,1,0:T(8,128)(2,1)}, bf16[2,512,1024]{2,1,0:T(8,128)(2,1)}, bf16[2,512,512]{2,1,0:T(8,128)(2,1)}, bf16[2,512,128]{2,1,0:T(8,1...) custom-call(s32[3]{0:T(128)S(1)} %pad_add_fusion.scalars, ...), custom_call_target="tpu_custom_call", output_to_operand_aliasing={{0}: (13, {}), {1}: (14, {}), {2}: (15, {})} | custom-call | flops 19327352832 | bytes 4194304 | tf_op jit(solution)/shard_map/pallas_call | solution.py:269
  76.7 0.7 collective-permute-start.21
  77.4 1.3 %collective-permute-start.17 = (bf16[2,512,128]{2,1,0:T(8,128)(2,1)S(1)}, bf16[2,512,128]{2,1,0:T(8,128)(2,1)S(1)}, u32[]{:S(2)}, u32[]{:S(2)}) collective-permute-start(bf16[2,512,128]{2,1,0:T(8,128)(2,1)S(1)} %get-tuple-element.53), channel_id=1, source_target_pairs={{0,1},{1,0},{2,3},{3,2},{4,5},{5,4},{6,7},{7,6},{8,9},{9,8},{10,11... | collective-permute-start | bytes 786440 | tf_op jit(solution)/shard_map/ppermute | solution.py:30
  79.1 0.6 collective-permute-start.22
  79.8 1.3 %collective-permute-start.23 = (bf16[2,256,128]{2,1,0:T(8,128)(2,1)S(1)}, bf16[2,256,128]{2,1,0:T(8,128)(2,1)S(1)}, u32[]{:S(2)}, u32[]{:S(2)}) collective-permute-start(bf16[2,256,128]{2,1,0:T(8,128)(2,1)S(1)} %slice.42), channel_id=1, source_target_pairs={{0,1},{1,0},{2,3},{3,2},{4,5},{5,4},{6,7},{7,6},{8,9},{9,8},{10,11... | collective-permute-start | bytes 393224 | tf_op jit(solution)/shard_map/ppermute | solution.py:30
  81.2 5.3 %collective-permute-done.17 = bf16[2,512,128]{2,1,0:T(8,128)(2,1)S(1)} collective-permute-done((bf16[2,512,128]{2,1,0:T(8,128)(2,1)S(1)}, bf16[2,512,128]{2,1,0:T(8,128)(2,1)S(1)}, u32[]{:S(2)}, u32[]{:S(2)}) %collective-permute-start.17) | collective-permute-done | bytes 262176 | tf_op jit(solution)/shard_map/ppermute | solution.py:30
  86.5 1.2 %collective-permute-done.22 = bf16[2,256,256]{2,1,0:T(8,128)(2,1)S(1)} collective-permute-done((bf16[2,256,256]{2,1,0:T(8,128)(2,1)S(1)}, bf16[2,256,256]{2,1,0:T(8,128)(2,1)S(1)}, u32[]{:S(2)}, u32[]{:S(2)}) %collective-permute-start.22) | collective-permute-done | bytes 262176 | tf_op jit(solution)/shard_map/ppermute | solution.py:30
  87.8 1.3 %collective-permute-start.24 = (bf16[2,256,128]{2,1,0:T(8,128)(2,1)S(1)}, bf16[2,256,128]{2,1,0:T(8,128)(2,1)S(1)}, u32[]{:S(2)}, u32[]{:S(2)}) collective-permute-start(bf16[2,256,128]{2,1,0:T(8,128)(2,1)S(1)} %slice.41), channel_id=1, source_target_pairs={{0,1},{1,0},{2,3},{3,2},{4,5},{5,4},{6,7},{7,6},{8,9},{9,8},{10,11... | collective-permute-start | bytes 393224 | tf_op jit(solution)/shard_map/ppermute | solution.py:30
  89.3 3.5 %collective-permute-done.24 = bf16[2,256,128]{2,1,0:T(8,128)(2,1)S(1)} collective-permute-done((bf16[2,256,128]{2,1,0:T(8,128)(2,1)S(1)}, bf16[2,256,128]{2,1,0:T(8,128)(2,1)S(1)}, u32[]{:S(2)}, u32[]{:S(2)}) %collective-permute-start.24) | collective-permute-done | bytes 131104 | tf_op jit(solution)/shard_map/ppermute | solution.py:30
  92.9 1.1 %pad_maximum_fusion = f32[2,256,512]{2,1,0:T(8,128)} fusion(f32[2,256,256]{2,1,0:T(8,128)S(1)} %get-tuple-element.63, f32[2,256,256]{2,1,0:T(8,128)S(1)} %get-tuple-element.62), kind=kLoop, calls=%fused_computation | loop fusion | flops 262144 | bytes 2097152 | tf_op jit(solution)/shard_map/concatenate | solution.py:398
  (51 shorter events, 5.3 us)
Async XLA Ops:
  4.5 6.6 %collective-permute-start.6 = (bf16[2,256,128]{2,1,0:T(8,128)(2,1)S(1)}, bf16[2,256,128]{2,1,0:T(8,128)(2,1)S(1)}, u32[]{:S(2)}, u32[]{:S(2)}) collective-permute-start(bf16[2,256,128]{2,1,0:T(8,128)(2,1)S(1)} %get-tuple-element.40.refs_4_), channel_id=1, source_target_pairs={{0,8},{4,12},{8,0},{12,4},{1,9},{5,13},{9,1},{13,5},{2,10},{6,14},... | collective-permute-start | bytes 393224 | tf_op jit(solution)/shard_map/ppermute | solution.py:30
  7.5 6.4 %collective-permute-start.5 = (bf16[2,256,128]{2,1,0:T(8,128)(2,1)S(1)}, bf16[2,256,128]{2,1,0:T(8,128)(2,1)S(1)}, u32[]{:S(2)}, u32[]{:S(2)}) collective-permute-start(bf16[2,256,128]{2,1,0:T(8,128)(2,1)S(1)} %get-tuple-element.39), channel_id=1, source_target_pairs={{0,1},{1,0},{2,3},{3,2},{4,5},{5,4},{6,7},{7,6},{8,9},{9,8},{10,11... | collective-permute-start | bytes 393224 | tf_op jit(solution)/shard_map/ppermute | solution.py:30
  9.0 12.3 %collective-permute-start = (bf16[2,512,128]{2,1,0:T(8,128)(2,1)S(1)}, bf16[2,512,128]{2,1,0:T(8,128)(2,1)S(1)}, u32[]{:S(2)}, u32[]{:S(2)}) collective-permute-start(bf16[2,512,128]{2,1,0:T(8,128)(2,1)S(1)} %get-tuple-element.35), channel_id=1, source_target_pairs={{0,1},{1,0},{2,3},{3,2},{4,5},{5,4},{6,7},{7,6},{8,9},{9,8},{10,11... | collective-permute-start | bytes 786440 | tf_op jit(solution)/shard_map/ppermute | solution.py:30
  9.5 11.4 %collective-permute-start.4 = (bf16[2,256,128]{2,1,0:T(8,128)(2,1)S(1)}, bf16[2,256,128]{2,1,0:T(8,128)(2,1)S(1)}, u32[]{:S(2)}, u32[]{:S(2)}) collective-permute-start(bf16[2,256,128]{2,1,0:T(8,128)(2,1)S(1)} %get-tuple-element.38), channel_id=1, source_target_pairs={{0,1},{1,0},{2,3},{3,2},{4,5},{5,4},{6,7},{7,6},{8,9},{9,8},{10,11... | collective-permute-start | bytes 393224 | tf_op jit(solution)/shard_map/ppermute | solution.py:30
  13.9 7.0 %collective-permute-start.7 = (bf16[2,256,128]{2,1,0:T(8,128)(2,1)S(1)}, bf16[2,256,128]{2,1,0:T(8,128)(2,1)S(1)}, u32[]{:S(2)}, u32[]{:S(2)}) collective-permute-start(bf16[2,256,128]{2,1,0:T(8,128)(2,1)S(1)} %collective-permute-done.5.refs_8_), channel_id=1, source_target_pairs={{0,8},{4,12},{8,0},{12,4},{1,9},{5,13},{9,1},{13,5},{2,10},{6,14},... | collective-permute-start | bytes 393224 | tf_op jit(solution)/shard_map/ppermute | solution.py:30
  13.9 7.8 %collective-permute-start.9 = (bf16[2,256,128]{2,1,0:T(8,128)(2,1)S(1)}, bf16[2,256,128]{2,1,0:T(8,128)(2,1)S(1)}, u32[]{:S(2)}, u32[]{:S(2)}) collective-permute-start(bf16[2,256,128]{2,1,0:T(8,128)(2,1)S(1)} %get-tuple-element.40.refs_4_), channel_id=1, source_target_pairs={{0,4},{4,0},{8,12},{12,8},{1,5},{5,1},{9,13},{13,9},{2,6},{6,2},{1... | collective-permute-start | bytes 393224 | tf_op jit(solution)/shard_map/ppermute | solution.py:30
  13.9 7.8 %collective-permute-start.10 = (bf16[2,256,128]{2,1,0:T(8,128)(2,1)S(1)}, bf16[2,256,128]{2,1,0:T(8,128)(2,1)S(1)}, u32[]{:S(2)}, u32[]{:S(2)}) collective-permute-start(bf16[2,256,128]{2,1,0:T(8,128)(2,1)S(1)} %collective-permute-done.6.refs_6_), channel_id=1, source_target_pairs={{0,4},{4,0},{8,12},{12,8},{1,5},{5,1},{9,13},{13,9},{2,6},{6,2},{1... | collective-permute-start | bytes 393224 | tf_op jit(solution)/shard_map/ppermute | solution.py:30
  20.9 3.1 %collective-permute-start.12 = (bf16[2,256,128]{2,1,0:T(8,128)(2,1)S(1)}, bf16[2,256,128]{2,1,0:T(8,128)(2,1)S(1)}, u32[]{:S(2)}, u32[]{:S(2)}) collective-permute-start(bf16[2,256,128]{2,1,0:T(8,128)(2,1)S(1)} %collective-permute-done.7.refs_10_), channel_id=1, source_target_pairs={{0,4},{4,0},{8,12},{12,8},{1,5},{5,1},{9,13},{13,9},{2,6},{6,2},{1... | collective-permute-start | bytes 393224 | tf_op jit(solution)/shard_map/ppermute | solution.py:30
  21.4 28.9 %collective-permute-start.3 = (bf16[2,256,128]{2,1,0:T(8,128)(2,1)S(1)}, bf16[2,256,128]{2,1,0:T(8,128)(2,1)S(1)}, u32[]{:S(2)}, u32[]{:S(2)}) collective-permute-start(bf16[2,256,128]{2,1,0:T(8,128)(2,1)S(1)} %get-tuple-element.37.refs_4_), channel_id=1, source_target_pairs={{0,8},{4,12},{8,0},{12,4},{1,9},{5,13},{9,1},{13,5},{2,10},{6,14},... | collective-permute-start | bytes 393224 | tf_op jit(solution)/shard_map/ppermute | solution.py:30
  21.7 29.1 %collective-permute-start.2 = (bf16[2,256,128]{2,1,0:T(8,128)(2,1)S(1)}, bf16[2,256,128]{2,1,0:T(8,128)(2,1)S(1)}, u32[]{:S(2)}, u32[]{:S(2)}) collective-permute-start(bf16[2,256,128]{2,1,0:T(8,128)(2,1)S(1)} %get-tuple-element.37.refs_4_), channel_id=1, source_target_pairs={{0,4},{4,0},{8,12},{12,8},{1,5},{5,1},{9,13},{13,9},{2,6},{6,2},{1... | collective-permute-start | bytes 393224 | tf_op jit(solution)/shard_map/ppermute | solution.py:30
  21.8 29.6 %collective-permute-start.14 = (bf16[2,256,128]{2,1,0:T(8,128)(2,1)S(1)}, bf16[2,256,128]{2,1,0:T(8,128)(2,1)S(1)}, u32[]{:S(2)}, u32[]{:S(2)}) collective-permute-start(bf16[2,256,128]{2,1,0:T(8,128)(2,1)S(1)} %collective-permute-done.4.refs_8_), channel_id=1, source_target_pairs={{0,4},{4,0},{8,12},{12,8},{1,5},{5,1},{9,13},{13,9},{2,6},{6,2},{1... | collective-permute-start | bytes 393224 | tf_op jit(solution)/shard_map/ppermute | solution.py:30
  22.3 28.0 %collective-permute-start.8 = (bf16[2,256,128]{2,1,0:T(8,128)(2,1)S(1)}, bf16[2,256,128]{2,1,0:T(8,128)(2,1)S(1)}, u32[]{:S(2)}, u32[]{:S(2)}) collective-permute-start(bf16[2,256,128]{2,1,0:T(8,128)(2,1)S(1)} %collective-permute-done.4.refs_8_), channel_id=1, source_target_pairs={{0,8},{4,12},{8,0},{12,4},{1,9},{5,13},{9,1},{13,5},{2,10},{6,14},... | collective-permute-start | bytes 393224 | tf_op jit(solution)/shard_map/ppermute | solution.py:30
  23.9 29.3 %collective-permute-start.1 = (bf16[2,512,128]{2,1,0:T(8,128)(2,1)S(1)}, bf16[2,512,128]{2,1,0:T(8,128)(2,1)S(1)}, u32[]{:S(2)}, u32[]{:S(2)}) collective-permute-start(bf16[2,512,128]{2,1,0:T(8,128)(2,1)S(1)} %get-tuple-element.36), channel_id=1, source_target_pairs={{0,1},{1,0},{2,3},{3,2},{4,5},{5,4},{6,7},{7,6},{8,9},{9,8},{10,11... | collective-permute-start | bytes 786440 | tf_op jit(solution)/shard_map/ppermute | solution.py:30
  50.3 1.4 %collective-permute-start.13 = (bf16[2,256,128]{2,1,0:T(8,128)(2,1)S(1)}, bf16[2,256,128]{2,1,0:T(8,128)(2,1)S(1)}, u32[]{:S(2)}, u32[]{:S(2)}) collective-permute-start(bf16[2,256,128]{2,1,0:T(8,128)(2,1)S(1)} %collective-permute-done.3.refs_6_), channel_id=1, source_target_pairs={{0,4},{4,0},{8,12},{12,8},{1,5},{5,1},{9,13},{13,9},{2,6},{6,2},{1... | collective-permute-start | bytes 393224 | tf_op jit(solution)/shard_map/ppermute | solution.py:30
  50.4 1.9 %collective-permute-start.15 = (bf16[2,256,128]{2,1,0:T(8,128)(2,1)S(1)}, bf16[2,256,128]{2,1,0:T(8,128)(2,1)S(1)}, u32[]{:S(2)}, u32[]{:S(2)}) collective-permute-start(bf16[2,256,128]{2,1,0:T(8,128)(2,1)S(1)} %collective-permute-done.8.refs_10_), channel_id=1, source_target_pairs={{0,4},{4,0},{8,12},{12,8},{1,5},{5,1},{9,13},{13,9},{2,6},{6,2},{1... | collective-permute-start | bytes 393224 | tf_op jit(solution)/shard_map/ppermute | solution.py:30
  50.9 25.8 %collective-permute-start.16 = (bf16[2,512,128]{2,1,0:T(8,128)(2,1)S(1)}, bf16[2,512,128]{2,1,0:T(8,128)(2,1)S(1)}, u32[]{:S(2)}, u32[]{:S(2)}) collective-permute-start(bf16[2,512,128]{2,1,0:T(8,128)(2,1)S(1)} %get-tuple-element.44), channel_id=1, source_target_pairs={{0,1},{1,0},{2,3},{3,2},{4,5},{5,4},{6,7},{7,6},{8,9},{9,8},{10,11... | collective-permute-start | bytes 786440 | tf_op jit(solution)/shard_map/ppermute | solution.py:30
  51.3 25.3 %collective-permute-start.18 = (bf16[2,256,256]{2,1,0:T(8,128)(2,1)S(1)}, bf16[2,256,256]{2,1,0:T(8,128)(2,1)S(1)}, u32[]{:S(2)}, u32[]{:S(2)}) collective-permute-start(bf16[2,256,256]{2,1,0:T(8,128)(2,1)S(1)} %bitcast.14), channel_id=1, source_target_pairs={{0,4},{4,0},{8,12},{12,8},{1,5},{5,1},{9,13},{13,9},{2,6},{6,2},{1... | collective-permute-start | bytes 786440 | tf_op jit(solution)/shard_map/ppermute | solution.py:30
  51.7 24.9 %collective-permute-start.19 = (bf16[2,256,256]{2,1,0:T(8,128)(2,1)S(1)}, bf16[2,256,256]{2,1,0:T(8,128)(2,1)S(1)}, u32[]{:S(2)}, u32[]{:S(2)}) collective-permute-start(bf16[2,256,256]{2,1,0:T(8,128)(2,1)S(1)} %bitcast.13), channel_id=1, source_target_pairs={{0,8},{4,12},{8,0},{12,4},{1,9},{5,13},{9,1},{13,5},{2,10},{6,14},... | collective-permute-start | bytes 786440 | tf_op jit(solution)/shard_map/ppermute | solution.py:30
  52.3 24.4 %collective-permute-start.20 = (bf16[2,256,256]{2,1,0:T(8,128)(2,1)S(1)}, bf16[2,256,256]{2,1,0:T(8,128)(2,1)S(1)}, u32[]{:S(2)}, u32[]{:S(2)}) collective-permute-start(bf16[2,256,256]{2,1,0:T(8,128)(2,1)S(1)} %bitcast.12), channel_id=1, source_target_pairs={{0,12},{4,8},{8,4},{12,0},{1,13},{5,9},{9,5},{13,1},{2,14},{6,10},... | collective-permute-start | bytes 786440 | tf_op jit(solution)/shard_map/ppermute | solution.py:30
  76.7 2.2 %collective-permute-start.21 = (bf16[2,2,256,256]{3,2,1,0:T(8,128)(2,1)S(1)}, bf16[2,2,256,256]{3,2,1,0:T(8,128)(2,1)S(1)}, u32[]{:S(2)}, u32[]{:S(2)}) collective-permute-start(bf16[2,2,256,256]{3,2,1,0:T(8,128)(2,1)S(1)} %get-tuple-element.60), channel_id=1, source_target_pairs={{0,4},{4,0},{8,12},{12,8},{1,5},{5,1},{9,13},{13,9},{2,6},{6,2},{1... | collective-permute-start | bytes 1572872 | tf_op jit(solution)/shard_map/ppermute | solution.py:30
  77.4 9.2 %collective-permute-start.17 = (bf16[2,512,128]{2,1,0:T(8,128)(2,1)S(1)}, bf16[2,512,128]{2,1,0:T(8,128)(2,1)S(1)}, u32[]{:S(2)}, u32[]{:S(2)}) collective-permute-start(bf16[2,512,128]{2,1,0:T(8,128)(2,1)S(1)} %get-tuple-element.53), channel_id=1, source_target_pairs={{0,1},{1,0},{2,3},{3,2},{4,5},{5,4},{6,7},{7,6},{8,9},{9,8},{10,11... | collective-permute-start | bytes 786440 | tf_op jit(solution)/shard_map/ppermute | solution.py:30
  79.1 8.7 %collective-permute-start.22 = (bf16[2,256,256]{2,1,0:T(8,128)(2,1)S(1)}, bf16[2,256,256]{2,1,0:T(8,128)(2,1)S(1)}, u32[]{:S(2)}, u32[]{:S(2)}) collective-permute-start(bf16[2,256,256]{2,1,0:T(8,128)(2,1)S(1)} %fusion.1), channel_id=1, source_target_pairs={{0,8},{4,12},{8,0},{12,4},{1,9},{5,13},{9,1},{13,5},{2,10},{6,14},... | collective-permute-start | bytes 786440 | tf_op jit(solution)/shard_map/ppermute | solution.py:30
  79.8 9.5 %collective-permute-start.23 = (bf16[2,256,128]{2,1,0:T(8,128)(2,1)S(1)}, bf16[2,256,128]{2,1,0:T(8,128)(2,1)S(1)}, u32[]{:S(2)}, u32[]{:S(2)}) collective-permute-start(bf16[2,256,128]{2,1,0:T(8,128)(2,1)S(1)} %slice.42), channel_id=1, source_target_pairs={{0,1},{1,0},{2,3},{3,2},{4,5},{5,4},{6,7},{7,6},{8,9},{9,8},{10,11... | collective-permute-start | bytes 393224 | tf_op jit(solution)/shard_map/ppermute | solution.py:30
  87.8 5.0 %collective-permute-start.24 = (bf16[2,256,128]{2,1,0:T(8,128)(2,1)S(1)}, bf16[2,256,128]{2,1,0:T(8,128)(2,1)S(1)}, u32[]{:S(2)}, u32[]{:S(2)}) collective-permute-start(bf16[2,256,128]{2,1,0:T(8,128)(2,1)S(1)} %slice.41), channel_id=1, source_target_pairs={{0,1},{1,0},{2,3},{3,2},{4,5},{5,4},{6,7},{7,6},{8,9},{9,8},{10,11... | collective-permute-start | bytes 393224 | tf_op jit(solution)/shard_map/ppermute | solution.py:30
  (6 other events, 19.5 us)

commit v13 on v12

--- a/solution.py
+++ b/solution.py
@@ -282,7 +282,7 @@
     )(scalars, *args)
 
 
-def pack_kernel(n_own, n_resp, scalars, prompt_ref, resp_ref, *outs):
+def pack_kernel(n_own, prompt_ref, resp_ref, *outs):
     width = n_own * HD
 
     def split(own):
@@ -294,29 +294,28 @@
             ):
                 outs[4 * h + k][...] = ref[:, :, lanes]
 
-    @pl.when(scalars[n_resp] == 0)
+    parity = lax.axis_index("prefix") % 2
+
+    @pl.when(parity == 0)
     def _():
         split(0)
 
-    @pl.when(scalars[n_resp] != 0)
+    @pl.when(parity != 0)
     def _():
         split(width)
 
 
-def pack(scalars, prompt_kv, resp_kv, n_own):
-    block = lambda shape: pl.BlockSpec(shape, lambda i, sc: (0, 0, 0))
+def pack(prompt_kv, resp_kv, n_own):
+    block = lambda shape: pl.BlockSpec(shape, lambda i: (0, 0, 0))
     shapes = [x.shape[:2] + (HD,) for x in (prompt_kv, prompt_kv, resp_kv, resp_kv)] * n_own
     return pl.pallas_call(
-        functools.partial(pack_kernel, n_own, resp_kv.shape[0]),
-        grid_spec=pltpu.PrefetchScalarGridSpec(
-            num_scalar_prefetch=1,
-            grid=(1,),
-            in_specs=[block(prompt_kv.shape), block(resp_kv.shape)],
-            out_specs=[block(s) for s in shapes],
-        ),
+        functools.partial(pack_kernel, n_own),
+        grid=(1,),
+        in_specs=[block(prompt_kv.shape), block(resp_kv.shape)],
+        out_specs=[block(s) for s in shapes],
         out_shape=[jax.ShapeDtypeStruct(s, prompt_kv.dtype) for s in shapes],
         compiler_params=pltpu.CompilerParams(vmem_limit_bytes=48 * 2**20),
-    )(scalars, prompt_kv, resp_kv)
+    )(prompt_kv, resp_kv)
 
 
 def per_device(queries, resp_kv, prompt_kv, prompt_of, d_out):
@@ -337,7 +336,7 @@
     def order(values, done):
         return lax.optimization_barrier((tuple(values), tuple(done)))[0]
 
-    packed = pack(scalars, prompt_kv, resp_kv, n_own)
+    packed = pack(prompt_kv, resp_kv, n_own)
     pa, pb, resp_a, resp_b = [], [], [], []
     for h in range(n_own):
         a0, b0, ra, rb = packed[4 * h : 4 * h + 4]
@@ -345,6 +344,8 @@
             (rb,) = order([rb], [resp_b[h - 1]])
         b0 = z(b0)
         a2 = x(a0)
+        if h == 0:
+            (rb,) = order([rb], [b0])
         resp_a.append(ra)
         resp_b.append(z(rb))
         if h == 0:

time: 94.3 us -> 94.1 us (level)
  starting transfers between devices: 19.6 us -> 22.2 us
  waiting for transfers between devices: 20 us -> 17.7 us
    ppermute x25, starting transfers between devices: 19.6 us -> 22.2 us  [swap(): lax.ppermute(block, axis, [(i, i ^ step) for i in range(lax.axis_size(axi...]
    ppermute x25, waiting for transfers between devices: 20 us -> 17.7 us  [swap(): lax.ppermute(block, axis, [(i, i ^ step) for i in range(lax.axis_size(axi...]
where the time goes in v13:
time: 94.1 us; the launch traced here: 93.8 us
  Pallas kernels  46.9 us (50%)
  starting transfers between devices  22.2 us (24%)
  waiting for transfers between devices  17.7 us (19%)
  local copies, waits for them, and re-layouts  3.97 us (4%)
  other arithmetic  2.35 us (2%)
    pallas_call x2, Pallas kernels, attend(): pl.pallas_call(functools.partial(attend_kernel, (pieces, rows, keep, send...  46.6 us
    ppermute x25, starting transfers between devices, swap(): lax.ppermute(block, axis, [(i, i ^ step) for i in range(lax.axis_size(axi...  22.2 us
    ppermute x25, waiting for transfers between devices, swap(): lax.ppermute(block, axis, [(i, i ^ step) for i in range(lax.axis_size(axi...  17.7 us
    unnamed x10, local copies, waits for them, and re-layouts  3.86 us
  transfers between devices with their start and end apart: 25, of which 7 were waited for; matrix products, arithmetic and copies ran while one was open for 1% of the time, Pallas kernels for 50%

profile of v13, /device:TPU:0, one launch (start us, length us, event | category | flops | bytes accessed | tf_op | source)
XLA Modules:
  0.0 93.8 jit_solution(2224721599863623900)
XLA Ops:
  0.6 1.2 %copy-done = bf16[2,512,512]{2,1,0:T(8,128)(2,1)S(1)} copy-done((bf16[2,512,512]{2,1,0:T(8,128)(2,1)S(1)}, bf16[2,512,512]{2,1,0:T(8,128)(2,1)}, u32[]{:S(2)}) %copy-start) | copy-done | bytes 1048600
  1.9 1.0 %copy-done.1 = bf16[2,256,512]{2,1,0:T(8,128)(2,1)S(1)} copy-done((bf16[2,256,512]{2,1,0:T(8,128)(2,1)S(1)}, bf16[2,256,512]{2,1,0:T(8,128)(2,1)}, u32[]{:S(2)}) %copy-start.1) | copy-done | bytes 524312
  3.2 3.1 %collective-permute-start = (bf16[2,256,128]{2,1,0:T(8,128)(2,1)S(1)}, bf16[2,256,128]{2,1,0:T(8,128)(2,1)S(1)}, u32[]{:S(2)}, u32[]{:S(2)}) collective-permute-start(bf16[2,256,128]{2,1,0:T(8,128)(2,1)S(1)} %get-tuple-element.37), channel_id=1, source_target_pairs={{0,1},{1,0},{2,3},{3,2},{4,5},{5,4},{6,7},{7,6},{8,9},{9,8},{10,11... | collective-permute-start | bytes 393224 | tf_op jit(solution)/shard_map/ppermute | solution.py:30
  6.3 1.5 %collective-permute-start.6 = (bf16[2,256,128]{2,1,0:T(8,128)(2,1)S(1)}, bf16[2,256,128]{2,1,0:T(8,128)(2,1)S(1)}, u32[]{:S(2)}, u32[]{:S(2)}) collective-permute-start(bf16[2,256,128]{2,1,0:T(8,128)(2,1)S(1)} %get-tuple-element.42.refs_4_), channel_id=1, source_target_pairs={{0,8},{4,12},{8,0},{12,4},{1,9},{5,13},{9,1},{13,5},{2,10},{6,14},... | collective-permute-start | bytes 393224 | tf_op jit(solution)/shard_map/ppermute | solution.py:30
  7.8 2.0 %collective-permute-done.refs_8_ = bf16[2,256,128]{2,1,0:T(8,128)(2,1)S(1)} collective-permute-done((bf16[2,256,128]{2,1,0:T(8,128)(2,1)S(1)}, bf16[2,256,128]{2,1,0:T(8,128)(2,1)S(1)}, u32[]{:S(2)}, u32[]{:S(2)}) %collective-permute-start) | collective-permute-done | bytes 131104 | tf_op jit(solution)/shard_map/ppermute | solution.py:30
  9.8 1.7 %collective-permute-start.1 = (bf16[2,512,128]{2,1,0:T(8,128)(2,1)S(1)}, bf16[2,512,128]{2,1,0:T(8,128)(2,1)S(1)}, u32[]{:S(2)}, u32[]{:S(2)}) collective-permute-start(bf16[2,512,128]{2,1,0:T(8,128)(2,1)S(1)} %get-tuple-element.38), channel_id=1, source_target_pairs={{0,1},{1,0},{2,3},{3,2},{4,5},{5,4},{6,7},{7,6},{8,9},{9,8},{10,11... | collective-permute-start | bytes 786440 | tf_op jit(solution)/shard_map/ppermute | solution.py:30
  11.8 1.7 %collective-permute-start.7 = (bf16[2,256,128]{2,1,0:T(8,128)(2,1)S(1)}, bf16[2,256,128]{2,1,0:T(8,128)(2,1)S(1)}, u32[]{:S(2)}, u32[]{:S(2)}) collective-permute-start(bf16[2,256,128]{2,1,0:T(8,128)(2,1)S(1)} %collective-permute-done.refs_8_), channel_id=1, source_target_pairs={{0,8},{4,12},{8,0},{12,4},{1,9},{5,13},{9,1},{13,5},{2,10},{6,14},... | collective-permute-start | bytes 393224 | tf_op jit(solution)/shard_map/ppermute | solution.py:30
  14.0 6.1 %collective-permute-done.5.refs_8_ = bf16[2,256,128]{2,1,0:T(8,128)(2,1)S(1)} collective-permute-done((bf16[2,256,128]{2,1,0:T(8,128)(2,1)S(1)}, bf16[2,256,128]{2,1,0:T(8,128)(2,1)S(1)}, u32[]{:S(2)}, u32[]{:S(2)}) %collective-permute-start.5) | collective-permute-done | bytes 131104 | tf_op jit(solution)/shard_map/ppermute | solution.py:30
  20.6 0.7 pad_add_fusion.scalars
  21.3 1.3 %collective-permute-start.4 = (bf16[2,256,128]{2,1,0:T(8,128)(2,1)S(1)}, bf16[2,256,128]{2,1,0:T(8,128)(2,1)S(1)}, u32[]{:S(2)}, u32[]{:S(2)}) collective-permute-start(bf16[2,256,128]{2,1,0:T(8,128)(2,1)S(1)} %get-tuple-element.40.refs_4_), channel_id=1, source_target_pairs={{0,8},{4,12},{8,0},{12,4},{1,9},{5,13},{9,1},{13,5},{2,10},{6,14},... | collective-permute-start | bytes 393224 | tf_op jit(solution)/shard_map/ppermute | solution.py:30
  23.2 0.7 collective-permute-start.8
  23.9 1.4 %collective-permute-start.2 = (bf16[2,512,128]{2,1,0:T(8,128)(2,1)S(1)}, bf16[2,512,128]{2,1,0:T(8,128)(2,1)S(1)}, u32[]{:S(2)}, u32[]{:S(2)}) collective-permute-start(bf16[2,512,128]{2,1,0:T(8,128)(2,1)S(1)} %get-tuple-element.39), channel_id=1, source_target_pairs={{0,1},{1,0},{2,3},{3,2},{4,5},{5,4},{6,7},{7,6},{8,9},{9,8},{10,11... | collective-permute-start | bytes 786440 | tf_op jit(solution)/shard_map/ppermute | solution.py:30
  25.3 1.6 %copy-done.2 = bf16[2,512,1024]{2,1,0:T(8,128)(2,1)S(1)} copy-done((bf16[2,512,1024]{2,1,0:T(8,128)(2,1)S(1)}, bf16[2,512,1024]{2,1,0:T(8,128)(2,1)}, u32[]{:S(2)}) %copy-start.2) | copy-done | bytes 2097176
  26.9 23.2 %shard_map.85 = (bf16[2,512,1024]{2,1,0:T(8,128)(2,1)}, bf16[2,512,1024]{2,1,0:T(8,128)(2,1)}, bf16[2,512,512]{2,1,0:T(8,128)(2,1)}, bf16[2,512,128]{2,1,0:T(8,1...) custom-call(s32[3]{0:T(128)S(1)} %pad_add_fusion.scalars, ...), custom_call_target="tpu_custom_call" | custom-call | flops 19327352832 | bytes 4194304 | tf_op jit(solution)/shard_map/pallas_call | solution.py:269
  51.5 1.5 %collective-permute-start.19 = (bf16[2,256,256]{2,1,0:T(8,128)(2,1)S(1)}, bf16[2,256,256]{2,1,0:T(8,128)(2,1)S(1)}, u32[]{:S(2)}, u32[]{:S(2)}) collective-permute-start(bf16[2,256,256]{2,1,0:T(8,128)(2,1)S(1)} %bitcast.13), channel_id=1, source_target_pairs={{0,8},{4,12},{8,0},{12,4},{1,9},{5,13},{9,1},{13,5},{2,10},{6,14},... | collective-permute-start | bytes 786440 | tf_op jit(solution)/shard_map/ppermute | solution.py:30
  53.2 23.4 %shard_map.86 = (bf16[2,512,1024]{2,1,0:T(8,128)(2,1)}, bf16[2,512,1024]{2,1,0:T(8,128)(2,1)}, bf16[2,512,512]{2,1,0:T(8,128)(2,1)}, bf16[2,512,128]{2,1,0:T(8,1...) custom-call(s32[3]{0:T(128)S(1)} %pad_add_fusion.scalars, ...), custom_call_target="tpu_custom_call", output_to_operand_aliasing={{0}: (13, {}), {1}: (14, {}), {2}: (15, {})} | custom-call | flops 19327352832 | bytes 4194304 | tf_op jit(solution)/shard_map/pallas_call | solution.py:269
  77.1 1.3 %collective-permute-start.17 = (bf16[2,512,128]{2,1,0:T(8,128)(2,1)S(1)}, bf16[2,512,128]{2,1,0:T(8,128)(2,1)S(1)}, u32[]{:S(2)}, u32[]{:S(2)}) collective-permute-start(bf16[2,512,128]{2,1,0:T(8,128)(2,1)S(1)} %get-tuple-element.55), channel_id=1, source_target_pairs={{0,1},{1,0},{2,3},{3,2},{4,5},{5,4},{6,7},{7,6},{8,9},{9,8},{10,11... | collective-permute-start | bytes 786440 | tf_op jit(solution)/shard_map/ppermute | solution.py:30
  78.9 1.6 %collective-permute-start.22 = (bf16[2,256,256]{2,1,0:T(8,128)(2,1)S(1)}, bf16[2,256,256]{2,1,0:T(8,128)(2,1)S(1)}, u32[]{:S(2)}, u32[]{:S(2)}) collective-permute-start(bf16[2,256,256]{2,1,0:T(8,128)(2,1)S(1)} %fusion.1), channel_id=1, source_target_pairs={{0,8},{4,12},{8,0},{12,4},{1,9},{5,13},{9,1},{13,5},{2,10},{6,14},... | collective-permute-start | bytes 786440 | tf_op jit(solution)/shard_map/ppermute | solution.py:30
  80.6 1.4 %collective-permute-start.23 = (bf16[2,256,128]{2,1,0:T(8,128)(2,1)S(1)}, bf16[2,256,128]{2,1,0:T(8,128)(2,1)S(1)}, u32[]{:S(2)}, u32[]{:S(2)}) collective-permute-start(bf16[2,256,128]{2,1,0:T(8,128)(2,1)S(1)} %slice.42), channel_id=1, source_target_pairs={{0,1},{1,0},{2,3},{3,2},{4,5},{5,4},{6,7},{7,6},{8,9},{9,8},{10,11... | collective-permute-start | bytes 393224 | tf_op jit(solution)/shard_map/ppermute | solution.py:30
  81.9 4.4 %collective-permute-done.17 = bf16[2,512,128]{2,1,0:T(8,128)(2,1)S(1)} collective-permute-done((bf16[2,512,128]{2,1,0:T(8,128)(2,1)S(1)}, bf16[2,512,128]{2,1,0:T(8,128)(2,1)S(1)}, u32[]{:S(2)}, u32[]{:S(2)}) %collective-permute-start.17) | collective-permute-done | bytes 262176 | tf_op jit(solution)/shard_map/ppermute | solution.py:30
  86.3 1.2 %collective-permute-done.22 = bf16[2,256,256]{2,1,0:T(8,128)(2,1)S(1)} collective-permute-done((bf16[2,256,256]{2,1,0:T(8,128)(2,1)S(1)}, bf16[2,256,256]{2,1,0:T(8,128)(2,1)S(1)}, u32[]{:S(2)}, u32[]{:S(2)}) %collective-permute-start.22) | collective-permute-done | bytes 262176 | tf_op jit(solution)/shard_map/ppermute | solution.py:30
  87.6 1.3 %collective-permute-start.24 = (bf16[2,256,128]{2,1,0:T(8,128)(2,1)S(1)}, bf16[2,256,128]{2,1,0:T(8,128)(2,1)S(1)}, u32[]{:S(2)}, u32[]{:S(2)}) collective-permute-start(bf16[2,256,128]{2,1,0:T(8,128)(2,1)S(1)} %slice.41), channel_id=1, source_target_pairs={{0,1},{1,0},{2,3},{3,2},{4,5},{5,4},{6,7},{7,6},{8,9},{9,8},{10,11... | collective-permute-start | bytes 393224 | tf_op jit(solution)/shard_map/ppermute | solution.py:30
  89.1 3.5 %collective-permute-done.24 = bf16[2,256,128]{2,1,0:T(8,128)(2,1)S(1)} collective-permute-done((bf16[2,256,128]{2,1,0:T(8,128)(2,1)S(1)}, bf16[2,256,128]{2,1,0:T(8,128)(2,1)S(1)}, u32[]{:S(2)}, u32[]{:S(2)}) %collective-permute-start.24) | collective-permute-done | bytes 131104 | tf_op jit(solution)/shard_map/ppermute | solution.py:30
  92.7 1.1 %pad_maximum_fusion = f32[2,256,512]{2,1,0:T(8,128)} fusion(f32[2,256,256]{2,1,0:T(8,128)S(1)} %get-tuple-element.65, f32[2,256,256]{2,1,0:T(8,128)S(1)} %get-tuple-element.64), kind=kLoop, calls=%fused_computation | loop fusion | flops 262144 | bytes 2097152 | tf_op jit(solution)/shard_map/concatenate | solution.py:399
  (51 shorter events, 5.1 us)
Async XLA Ops:
  3.2 6.6 %collective-permute-start = (bf16[2,256,128]{2,1,0:T(8,128)(2,1)S(1)}, bf16[2,256,128]{2,1,0:T(8,128)(2,1)S(1)}, u32[]{:S(2)}, u32[]{:S(2)}) collective-permute-start(bf16[2,256,128]{2,1,0:T(8,128)(2,1)S(1)} %get-tuple-element.37), channel_id=1, source_target_pairs={{0,1},{1,0},{2,3},{3,2},{4,5},{5,4},{6,7},{7,6},{8,9},{9,8},{10,11... | collective-permute-start | bytes 393224 | tf_op jit(solution)/shard_map/ppermute | solution.py:30
  6.3 5.5 %collective-permute-start.6 = (bf16[2,256,128]{2,1,0:T(8,128)(2,1)S(1)}, bf16[2,256,128]{2,1,0:T(8,128)(2,1)S(1)}, u32[]{:S(2)}, u32[]{:S(2)}) collective-permute-start(bf16[2,256,128]{2,1,0:T(8,128)(2,1)S(1)} %get-tuple-element.42.refs_4_), channel_id=1, source_target_pairs={{0,8},{4,12},{8,0},{12,4},{1,9},{5,13},{9,1},{13,5},{2,10},{6,14},... | collective-permute-start | bytes 393224 | tf_op jit(solution)/shard_map/ppermute | solution.py:30
  9.8 11.5 %collective-permute-start.1 = (bf16[2,512,128]{2,1,0:T(8,128)(2,1)S(1)}, bf16[2,512,128]{2,1,0:T(8,128)(2,1)S(1)}, u32[]{:S(2)}, u32[]{:S(2)}) collective-permute-start(bf16[2,512,128]{2,1,0:T(8,128)(2,1)S(1)} %get-tuple-element.38), channel_id=1, source_target_pairs={{0,1},{1,0},{2,3},{3,2},{4,5},{5,4},{6,7},{7,6},{8,9},{9,8},{10,11... | collective-permute-start | bytes 786440 | tf_op jit(solution)/shard_map/ppermute | solution.py:30
  11.5 8.6 %collective-permute-start.5 = (bf16[2,256,128]{2,1,0:T(8,128)(2,1)S(1)}, bf16[2,256,128]{2,1,0:T(8,128)(2,1)S(1)}, u32[]{:S(2)}, u32[]{:S(2)}) collective-permute-start(bf16[2,256,128]{2,1,0:T(8,128)(2,1)S(1)} %get-tuple-element.41), channel_id=1, source_target_pairs={{0,1},{1,0},{2,3},{3,2},{4,5},{5,4},{6,7},{7,6},{8,9},{9,8},{10,11... | collective-permute-start | bytes 393224 | tf_op jit(solution)/shard_map/ppermute | solution.py:30
  11.8 8.3 %collective-permute-start.7 = (bf16[2,256,128]{2,1,0:T(8,128)(2,1)S(1)}, bf16[2,256,128]{2,1,0:T(8,128)(2,1)S(1)}, u32[]{:S(2)}, u32[]{:S(2)}) collective-permute-start(bf16[2,256,128]{2,1,0:T(8,128)(2,1)S(1)} %collective-permute-done.refs_8_), channel_id=1, source_target_pairs={{0,8},{4,12},{8,0},{12,4},{1,9},{5,13},{9,1},{13,5},{2,10},{6,14},... | collective-permute-start | bytes 393224 | tf_op jit(solution)/shard_map/ppermute | solution.py:30
  13.4 9.2 %collective-permute-start.9 = (bf16[2,256,128]{2,1,0:T(8,128)(2,1)S(1)}, bf16[2,256,128]{2,1,0:T(8,128)(2,1)S(1)}, u32[]{:S(2)}, u32[]{:S(2)}) collective-permute-start(bf16[2,256,128]{2,1,0:T(8,128)(2,1)S(1)} %get-tuple-element.42.refs_4_), channel_id=1, source_target_pairs={{0,4},{4,0},{8,12},{12,8},{1,5},{5,1},{9,13},{13,9},{2,6},{6,2},{1... | collective-permute-start | bytes 393224 | tf_op jit(solution)/shard_map/ppermute | solution.py:30
  13.5 9.2 %collective-permute-start.10 = (bf16[2,256,128]{2,1,0:T(8,128)(2,1)S(1)}, bf16[2,256,128]{2,1,0:T(8,128)(2,1)S(1)}, u32[]{:S(2)}, u32[]{:S(2)}) collective-permute-start(bf16[2,256,128]{2,1,0:T(8,128)(2,1)S(1)} %collective-permute-done.6.refs_6_), channel_id=1, source_target_pairs={{0,4},{4,0},{8,12},{12,8},{1,5},{5,1},{9,13},{13,9},{2,6},{6,2},{1... | collective-permute-start | bytes 393224 | tf_op jit(solution)/shard_map/ppermute | solution.py:30
  20.1 3.1 %collective-permute-start.11 = (bf16[2,256,128]{2,1,0:T(8,128)(2,1)S(1)}, bf16[2,256,128]{2,1,0:T(8,128)(2,1)S(1)}, u32[]{:S(2)}, u32[]{:S(2)}) collective-permute-start(bf16[2,256,128]{2,1,0:T(8,128)(2,1)S(1)} %collective-permute-done.refs_8_), channel_id=1, source_target_pairs={{0,4},{4,0},{8,12},{12,8},{1,5},{5,1},{9,13},{13,9},{2,6},{6,2},{1... | collective-permute-start | bytes 393224 | tf_op jit(solution)/shard_map/ppermute | solution.py:30
  20.1 3.8 %collective-permute-start.12 = (bf16[2,256,128]{2,1,0:T(8,128)(2,1)S(1)}, bf16[2,256,128]{2,1,0:T(8,128)(2,1)S(1)}, u32[]{:S(2)}, u32[]{:S(2)}) collective-permute-start(bf16[2,256,128]{2,1,0:T(8,128)(2,1)S(1)} %collective-permute-done.7.refs_10_), channel_id=1, source_target_pairs={{0,4},{4,0},{8,12},{12,8},{1,5},{5,1},{9,13},{13,9},{2,6},{6,2},{1... | collective-permute-start | bytes 393224 | tf_op jit(solution)/shard_map/ppermute | solution.py:30
  21.3 28.8 %collective-permute-start.4 = (bf16[2,256,128]{2,1,0:T(8,128)(2,1)S(1)}, bf16[2,256,128]{2,1,0:T(8,128)(2,1)S(1)}, u32[]{:S(2)}, u32[]{:S(2)}) collective-permute-start(bf16[2,256,128]{2,1,0:T(8,128)(2,1)S(1)} %get-tuple-element.40.refs_4_), channel_id=1, source_target_pairs={{0,8},{4,12},{8,0},{12,4},{1,9},{5,13},{9,1},{13,5},{2,10},{6,14},... | collective-permute-start | bytes 393224 | tf_op jit(solution)/shard_map/ppermute | solution.py:30
  22.7 28.0 %collective-permute-start.3 = (bf16[2,256,128]{2,1,0:T(8,128)(2,1)S(1)}, bf16[2,256,128]{2,1,0:T(8,128)(2,1)S(1)}, u32[]{:S(2)}, u32[]{:S(2)}) collective-permute-start(bf16[2,256,128]{2,1,0:T(8,128)(2,1)S(1)} %get-tuple-element.40.refs_4_), channel_id=1, source_target_pairs={{0,4},{4,0},{8,12},{12,8},{1,5},{5,1},{9,13},{13,9},{2,6},{6,2},{1... | collective-permute-start | bytes 393224 | tf_op jit(solution)/shard_map/ppermute | solution.py:30
  22.7 28.6 %collective-permute-start.14 = (bf16[2,256,128]{2,1,0:T(8,128)(2,1)S(1)}, bf16[2,256,128]{2,1,0:T(8,128)(2,1)S(1)}, u32[]{:S(2)}, u32[]{:S(2)}) collective-permute-start(bf16[2,256,128]{2,1,0:T(8,128)(2,1)S(1)} %collective-permute-done.5.refs_8_), channel_id=1, source_target_pairs={{0,4},{4,0},{8,12},{12,8},{1,5},{5,1},{9,13},{13,9},{2,6},{6,2},{1... | collective-permute-start | bytes 393224 | tf_op jit(solution)/shard_map/ppermute | solution.py:30
  23.2 26.9 %collective-permute-start.8 = (bf16[2,256,128]{2,1,0:T(8,128)(2,1)S(1)}, bf16[2,256,128]{2,1,0:T(8,128)(2,1)S(1)}, u32[]{:S(2)}, u32[]{:S(2)}) collective-permute-start(bf16[2,256,128]{2,1,0:T(8,128)(2,1)S(1)} %collective-permute-done.5.refs_8_), channel_id=1, source_target_pairs={{0,8},{4,12},{8,0},{12,4},{1,9},{5,13},{9,1},{13,5},{2,10},{6,14},... | collective-permute-start | bytes 393224 | tf_op jit(solution)/shard_map/ppermute | solution.py:30
  23.9 29.3 %collective-permute-start.2 = (bf16[2,512,128]{2,1,0:T(8,128)(2,1)S(1)}, bf16[2,512,128]{2,1,0:T(8,128)(2,1)S(1)}, u32[]{:S(2)}, u32[]{:S(2)}) collective-permute-start(bf16[2,512,128]{2,1,0:T(8,128)(2,1)S(1)} %get-tuple-element.39), channel_id=1, source_target_pairs={{0,1},{1,0},{2,3},{3,2},{4,5},{5,4},{6,7},{7,6},{8,9},{9,8},{10,11... | collective-permute-start | bytes 786440 | tf_op jit(solution)/shard_map/ppermute | solution.py:30
  50.2 2.8 %collective-permute-start.15 = (bf16[2,256,128]{2,1,0:T(8,128)(2,1)S(1)}, bf16[2,256,128]{2,1,0:T(8,128)(2,1)S(1)}, u32[]{:S(2)}, u32[]{:S(2)}) collective-permute-start(bf16[2,256,128]{2,1,0:T(8,128)(2,1)S(1)} %collective-permute-done.8.refs_10_), channel_id=1, source_target_pairs={{0,4},{4,0},{8,12},{12,8},{1,5},{5,1},{9,13},{13,9},{2,6},{6,2},{1... | collective-permute-start | bytes 393224 | tf_op jit(solution)/shard_map/ppermute | solution.py:30
  50.7 25.9 %collective-permute-start.16 = (bf16[2,512,128]{2,1,0:T(8,128)(2,1)S(1)}, bf16[2,512,128]{2,1,0:T(8,128)(2,1)S(1)}, u32[]{:S(2)}, u32[]{:S(2)}) collective-permute-start(bf16[2,512,128]{2,1,0:T(8,128)(2,1)S(1)} %get-tuple-element.46), channel_id=1, source_target_pairs={{0,1},{1,0},{2,3},{3,2},{4,5},{5,4},{6,7},{7,6},{8,9},{9,8},{10,11... | collective-permute-start | bytes 786440 | tf_op jit(solution)/shard_map/ppermute | solution.py:30
  51.3 25.3 %collective-permute-start.18 = (bf16[2,256,256]{2,1,0:T(8,128)(2,1)S(1)}, bf16[2,256,256]{2,1,0:T(8,128)(2,1)S(1)}, u32[]{:S(2)}, u32[]{:S(2)}) collective-permute-start(bf16[2,256,256]{2,1,0:T(8,128)(2,1)S(1)} %bitcast.14), channel_id=1, source_target_pairs={{0,4},{4,0},{8,12},{12,8},{1,5},{5,1},{9,13},{13,9},{2,6},{6,2},{1... | collective-permute-start | bytes 786440 | tf_op jit(solution)/shard_map/ppermute | solution.py:30
  51.5 25.1 %collective-permute-start.19 = (bf16[2,256,256]{2,1,0:T(8,128)(2,1)S(1)}, bf16[2,256,256]{2,1,0:T(8,128)(2,1)S(1)}, u32[]{:S(2)}, u32[]{:S(2)}) collective-permute-start(bf16[2,256,256]{2,1,0:T(8,128)(2,1)S(1)} %bitcast.13), channel_id=1, source_target_pairs={{0,8},{4,12},{8,0},{12,4},{1,9},{5,13},{9,1},{13,5},{2,10},{6,14},... | collective-permute-start | bytes 786440 | tf_op jit(solution)/shard_map/ppermute | solution.py:30
  53.0 23.6 %collective-permute-start.20 = (bf16[2,256,256]{2,1,0:T(8,128)(2,1)S(1)}, bf16[2,256,256]{2,1,0:T(8,128)(2,1)S(1)}, u32[]{:S(2)}, u32[]{:S(2)}) collective-permute-start(bf16[2,256,256]{2,1,0:T(8,128)(2,1)S(1)} %bitcast.12), channel_id=1, source_target_pairs={{0,12},{4,8},{8,4},{12,0},{1,13},{5,9},{9,5},{13,1},{2,14},{6,10},... | collective-permute-start | bytes 786440 | tf_op jit(solution)/shard_map/ppermute | solution.py:30
  76.6 2.1 %collective-permute-start.21 = (bf16[2,2,256,256]{3,2,1,0:T(8,128)(2,1)S(1)}, bf16[2,2,256,256]{3,2,1,0:T(8,128)(2,1)S(1)}, u32[]{:S(2)}, u32[]{:S(2)}) collective-permute-start(bf16[2,2,256,256]{3,2,1,0:T(8,128)(2,1)S(1)} %get-tuple-element.62), channel_id=1, source_target_pairs={{0,4},{4,0},{8,12},{12,8},{1,5},{5,1},{9,13},{13,9},{2,6},{6,2},{1... | collective-permute-start | bytes 1572872 | tf_op jit(solution)/shard_map/ppermute | solution.py:30
  77.1 9.2 %collective-permute-start.17 = (bf16[2,512,128]{2,1,0:T(8,128)(2,1)S(1)}, bf16[2,512,128]{2,1,0:T(8,128)(2,1)S(1)}, u32[]{:S(2)}, u32[]{:S(2)}) collective-permute-start(bf16[2,512,128]{2,1,0:T(8,128)(2,1)S(1)} %get-tuple-element.55), channel_id=1, source_target_pairs={{0,1},{1,0},{2,3},{3,2},{4,5},{5,4},{6,7},{7,6},{8,9},{9,8},{10,11... | collective-permute-start | bytes 786440 | tf_op jit(solution)/shard_map/ppermute | solution.py:30
  78.9 8.7 %collective-permute-start.22 = (bf16[2,256,256]{2,1,0:T(8,128)(2,1)S(1)}, bf16[2,256,256]{2,1,0:T(8,128)(2,1)S(1)}, u32[]{:S(2)}, u32[]{:S(2)}) collective-permute-start(bf16[2,256,256]{2,1,0:T(8,128)(2,1)S(1)} %fusion.1), channel_id=1, source_target_pairs={{0,8},{4,12},{8,0},{12,4},{1,9},{5,13},{9,1},{13,5},{2,10},{6,14},... | collective-permute-start | bytes 786440 | tf_op jit(solution)/shard_map/ppermute | solution.py:30
  80.6 8.6 %collective-permute-start.23 = (bf16[2,256,128]{2,1,0:T(8,128)(2,1)S(1)}, bf16[2,256,128]{2,1,0:T(8,128)(2,1)S(1)}, u32[]{:S(2)}, u32[]{:S(2)}) collective-permute-start(bf16[2,256,128]{2,1,0:T(8,128)(2,1)S(1)} %slice.42), channel_id=1, source_target_pairs={{0,1},{1,0},{2,3},{3,2},{4,5},{5,4},{6,7},{7,6},{8,9},{9,8},{10,11... | collective-permute-start | bytes 393224 | tf_op jit(solution)/shard_map/ppermute | solution.py:30
  87.6 5.0 %collective-permute-start.24 = (bf16[2,256,128]{2,1,0:T(8,128)(2,1)S(1)}, bf16[2,256,128]{2,1,0:T(8,128)(2,1)S(1)}, u32[]{:S(2)}, u32[]{:S(2)}) collective-permute-start(bf16[2,256,128]{2,1,0:T(8,128)(2,1)S(1)} %slice.41), channel_id=1, source_target_pairs={{0,1},{1,0},{2,3},{3,2},{4,5},{5,4},{6,7},{7,6},{8,9},{9,8},{10,11... | collective-permute-start | bytes 393224 | tf_op jit(solution)/shard_map/ppermute | solution.py:30
  (6 other events, 18.6 us)

commit v14 on v13

--- a/solution.py
+++ b/solution.py
@@ -337,15 +337,16 @@
         return lax.optimization_barrier((tuple(values), tuple(done)))[0]
 
     packed = pack(prompt_kv, resp_kv, n_own)
+    others = [z(packed[4 * h + 1]) for h in range(n_own)]
     pa, pb, resp_a, resp_b = [], [], [], []
     for h in range(n_own):
-        a0, b0, ra, rb = packed[4 * h : 4 * h + 4]
+        a0, _, ra, rb = packed[4 * h : 4 * h + 4]
         if h > 0:
             (rb,) = order([rb], [resp_b[h - 1]])
-        b0 = z(b0)
+        b0 = others[h]
         a2 = x(a0)
         if h == 0:
-            (rb,) = order([rb], [b0])
+            (rb,) = order([rb], [others[-1]])
         resp_a.append(ra)
         resp_b.append(z(rb))
         if h == 0:

time: 94.1 us -> 92.5 us (0.983)
  waiting for transfers between devices: 17.7 us -> 15.8 us
    ppermute x25, waiting for transfers between devices: 17.7 us -> 15.8 us  [swap(): lax.ppermute(block, axis, [(i, i ^ step) for i in range(lax.axis_size(axi...]
  transfers between devices with their start and end apart: 25 -> 25, of which waited for: 7 -> 8; matrix products, arithmetic and copies ran while one was open for 1% -> 1% of each run, Pallas kernels for 50% -> 50%
where the time goes in v14:
time: 92.5 us; the launch traced here: 92.3 us
  Pallas kernels  46.9 us (51%)
  starting transfers between devices  22.5 us (24%)
  waiting for transfers between devices  15.8 us (17%)
  local copies, waits for them, and re-layouts  3.97 us (4%)
  other arithmetic  2.35 us (3%)
    pallas_call x2, Pallas kernels, attend(): pl.pallas_call(functools.partial(attend_kernel, (pieces, rows, keep, send...  46.6 us
    ppermute x25, starting transfers between devices, swap(): lax.ppermute(block, axis, [(i, i ^ step) for i in range(lax.axis_size(axi...  22.5 us
    ppermute x25, waiting for transfers between devices, swap(): lax.ppermute(block, axis, [(i, i ^ step) for i in range(lax.axis_size(axi...  15.8 us
    unnamed x10, local copies, waits for them, and re-layouts  3.86 us
  transfers between devices with their start and end apart: 25, of which 8 were waited for; matrix products, arithmetic and copies ran while one was open for 1% of the time, Pallas kernels for 50%

profile of v14, /device:TPU:0, one launch (start us, length us, event | category | flops | bytes accessed | tf_op | source)
XLA Modules:
  0.0 92.3 jit_solution(15636622120890752461)
XLA Ops:
  0.6 1.2 %copy-done = bf16[2,512,512]{2,1,0:T(8,128)(2,1)S(1)} copy-done((bf16[2,512,512]{2,1,0:T(8,128)(2,1)S(1)}, bf16[2,512,512]{2,1,0:T(8,128)(2,1)}, u32[]{:S(2)}) %copy-start) | copy-done | bytes 1048600
  1.9 1.0 %copy-done.1 = bf16[2,256,512]{2,1,0:T(8,128)(2,1)S(1)} copy-done((bf16[2,256,512]{2,1,0:T(8,128)(2,1)S(1)}, bf16[2,256,512]{2,1,0:T(8,128)(2,1)}, u32[]{:S(2)}) %copy-start.1) | copy-done | bytes 524312
  3.2 3.1 %collective-permute-start = (bf16[2,256,128]{2,1,0:T(8,128)(2,1)S(1)}, bf16[2,256,128]{2,1,0:T(8,128)(2,1)S(1)}, u32[]{:S(2)}, u32[]{:S(2)}) collective-permute-start(bf16[2,256,128]{2,1,0:T(8,128)(2,1)S(1)} %get-tuple-element.37), channel_id=1, source_target_pairs={{0,1},{1,0},{2,3},{3,2},{4,5},{5,4},{6,7},{7,6},{8,9},{9,8},{10,11... | collective-permute-start | bytes 393224 | tf_op jit(solution)/shard_map/ppermute | solution.py:30
  6.3 1.5 %collective-permute-start.6 = (bf16[2,256,128]{2,1,0:T(8,128)(2,1)S(1)}, bf16[2,256,128]{2,1,0:T(8,128)(2,1)S(1)}, u32[]{:S(2)}, u32[]{:S(2)}) collective-permute-start(bf16[2,256,128]{2,1,0:T(8,128)(2,1)S(1)} %get-tuple-element.42.refs_4_), channel_id=1, source_target_pairs={{0,8},{4,12},{8,0},{12,4},{1,9},{5,13},{9,1},{13,5},{2,10},{6,14},... | collective-permute-start | bytes 393224 | tf_op jit(solution)/shard_map/ppermute | solution.py:30
  8.2 2.0 %collective-permute-done.refs_8_ = bf16[2,256,128]{2,1,0:T(8,128)(2,1)S(1)} collective-permute-done((bf16[2,256,128]{2,1,0:T(8,128)(2,1)S(1)}, bf16[2,256,128]{2,1,0:T(8,128)(2,1)S(1)}, u32[]{:S(2)}, u32[]{:S(2)}) %collective-permute-start) | collective-permute-done | bytes 131104 | tf_op jit(solution)/shard_map/ppermute | solution.py:30
  10.2 2.5 %collective-permute-start.1 = (bf16[2,512,128]{2,1,0:T(8,128)(2,1)S(1)}, bf16[2,512,128]{2,1,0:T(8,128)(2,1)S(1)}, u32[]{:S(2)}, u32[]{:S(2)}) collective-permute-start(bf16[2,512,128]{2,1,0:T(8,128)(2,1)S(1)} %get-tuple-element.38), channel_id=1, source_target_pairs={{0,1},{1,0},{2,3},{3,2},{4,5},{5,4},{6,7},{7,6},{8,9},{9,8},{10,11... | collective-permute-start | bytes 786440 | tf_op jit(solution)/shard_map/ppermute | solution.py:30
  12.7 1.2 %collective-permute-done.5.refs_8_ = bf16[2,256,128]{2,1,0:T(8,128)(2,1)S(1)} collective-permute-done((bf16[2,256,128]{2,1,0:T(8,128)(2,1)S(1)}, bf16[2,256,128]{2,1,0:T(8,128)(2,1)S(1)}, u32[]{:S(2)}, u32[]{:S(2)}) %collective-permute-start.5) | collective-permute-done | bytes 131104 | tf_op jit(solution)/shard_map/ppermute | solution.py:30
  13.8 1.6 %collective-permute-start.7 = (bf16[2,256,128]{2,1,0:T(8,128)(2,1)S(1)}, bf16[2,256,128]{2,1,0:T(8,128)(2,1)S(1)}, u32[]{:S(2)}, u32[]{:S(2)}) collective-permute-start(bf16[2,256,128]{2,1,0:T(8,128)(2,1)S(1)} %collective-permute-done.5.refs_8_), channel_id=1, source_target_pairs={{0,8},{4,12},{8,0},{12,4},{1,9},{5,13},{9,1},{13,5},{2,10},{6,14},... | collective-permute-start | bytes 393224 | tf_op jit(solution)/shard_map/ppermute | solution.py:30
  15.9 2.9 %collective-permute-done.7.refs_10_ = bf16[2,256,128]{2,1,0:T(8,128)(2,1)S(1)} collective-permute-done((bf16[2,256,128]{2,1,0:T(8,128)(2,1)S(1)}, bf16[2,256,128]{2,1,0:T(8,128)(2,1)S(1)}, u32[]{:S(2)}, u32[]{:S(2)}) %collective-permute-start.7) | collective-permute-done | bytes 131104 | tf_op jit(solution)/shard_map/ppermute | solution.py:30
  18.8 0.7 pad_add_fusion.scalars
  19.5 1.6 %collective-permute-start.4 = (bf16[2,256,128]{2,1,0:T(8,128)(2,1)S(1)}, bf16[2,256,128]{2,1,0:T(8,128)(2,1)S(1)}, u32[]{:S(2)}, u32[]{:S(2)}) collective-permute-start(bf16[2,256,128]{2,1,0:T(8,128)(2,1)S(1)} %get-tuple-element.40.refs_4_), channel_id=1, source_target_pairs={{0,8},{4,12},{8,0},{12,4},{1,9},{5,13},{9,1},{13,5},{2,10},{6,14},... | collective-permute-start | bytes 393224 | tf_op jit(solution)/shard_map/ppermute | solution.py:30
  22.1 1.6 %collective-permute-start.2 = (bf16[2,512,128]{2,1,0:T(8,128)(2,1)S(1)}, bf16[2,512,128]{2,1,0:T(8,128)(2,1)S(1)}, u32[]{:S(2)}, u32[]{:S(2)}) collective-permute-start(bf16[2,512,128]{2,1,0:T(8,128)(2,1)S(1)} %get-tuple-element.39), channel_id=1, source_target_pairs={{0,1},{1,0},{2,3},{3,2},{4,5},{5,4},{6,7},{7,6},{8,9},{9,8},{10,11... | collective-permute-start | bytes 786440 | tf_op jit(solution)/shard_map/ppermute | solution.py:30
  23.7 1.6 %copy-done.2 = bf16[2,512,1024]{2,1,0:T(8,128)(2,1)S(1)} copy-done((bf16[2,512,1024]{2,1,0:T(8,128)(2,1)S(1)}, bf16[2,512,1024]{2,1,0:T(8,128)(2,1)}, u32[]{:S(2)}) %copy-start.2) | copy-done | bytes 2097176
  25.3 23.2 %shard_map.85 = (bf16[2,512,1024]{2,1,0:T(8,128)(2,1)}, bf16[2,512,1024]{2,1,0:T(8,128)(2,1)}, bf16[2,512,512]{2,1,0:T(8,128)(2,1)}, bf16[2,512,128]{2,1,0:T(8,1...) custom-call(s32[3]{0:T(128)S(1)} %pad_add_fusion.scalars, ...), custom_call_target="tpu_custom_call" | custom-call | flops 19327352832 | bytes 4194304 | tf_op jit(solution)/shard_map/pallas_call | solution.py:269
  49.9 1.5 %collective-permute-start.19 = (bf16[2,256,256]{2,1,0:T(8,128)(2,1)S(1)}, bf16[2,256,256]{2,1,0:T(8,128)(2,1)S(1)}, u32[]{:S(2)}, u32[]{:S(2)}) collective-permute-start(bf16[2,256,256]{2,1,0:T(8,128)(2,1)S(1)} %bitcast.13), channel_id=1, source_target_pairs={{0,8},{4,12},{8,0},{12,4},{1,9},{5,13},{9,1},{13,5},{2,10},{6,14},... | collective-permute-start | bytes 786440 | tf_op jit(solution)/shard_map/ppermute | solution.py:30
  51.5 23.4 %shard_map.86 = (bf16[2,512,1024]{2,1,0:T(8,128)(2,1)}, bf16[2,512,1024]{2,1,0:T(8,128)(2,1)}, bf16[2,512,512]{2,1,0:T(8,128)(2,1)}, bf16[2,512,128]{2,1,0:T(8,1...) custom-call(s32[3]{0:T(128)S(1)} %pad_add_fusion.scalars, ...), custom_call_target="tpu_custom_call", output_to_operand_aliasing={{0}: (13, {}), {1}: (14, {}), {2}: (15, {})} | custom-call | flops 19327352832 | bytes 4194304 | tf_op jit(solution)/shard_map/pallas_call | solution.py:269
  75.6 1.3 %collective-permute-start.17 = (bf16[2,512,128]{2,1,0:T(8,128)(2,1)S(1)}, bf16[2,512,128]{2,1,0:T(8,128)(2,1)S(1)}, u32[]{:S(2)}, u32[]{:S(2)}) collective-permute-start(bf16[2,512,128]{2,1,0:T(8,128)(2,1)S(1)} %get-tuple-element.55), channel_id=1, source_target_pairs={{0,1},{1,0},{2,3},{3,2},{4,5},{5,4},{6,7},{7,6},{8,9},{9,8},{10,11... | collective-permute-start | bytes 786440 | tf_op jit(solution)/shard_map/ppermute | solution.py:30
  77.3 1.6 %collective-permute-start.22 = (bf16[2,256,256]{2,1,0:T(8,128)(2,1)S(1)}, bf16[2,256,256]{2,1,0:T(8,128)(2,1)S(1)}, u32[]{:S(2)}, u32[]{:S(2)}) collective-permute-start(bf16[2,256,256]{2,1,0:T(8,128)(2,1)S(1)} %fusion.1), channel_id=1, source_target_pairs={{0,8},{4,12},{8,0},{12,4},{1,9},{5,13},{9,1},{13,5},{2,10},{6,14},... | collective-permute-start | bytes 786440 | tf_op jit(solution)/shard_map/ppermute | solution.py:30
  79.0 1.4 %collective-permute-start.23 = (bf16[2,256,128]{2,1,0:T(8,128)(2,1)S(1)}, bf16[2,256,128]{2,1,0:T(8,128)(2,1)S(1)}, u32[]{:S(2)}, u32[]{:S(2)}) collective-permute-start(bf16[2,256,128]{2,1,0:T(8,128)(2,1)S(1)} %slice.42), channel_id=1, source_target_pairs={{0,1},{1,0},{2,3},{3,2},{4,5},{5,4},{6,7},{7,6},{8,9},{9,8},{10,11... | collective-permute-start | bytes 393224 | tf_op jit(solution)/shard_map/ppermute | solution.py:30
  80.4 4.4 %collective-permute-done.17 = bf16[2,512,128]{2,1,0:T(8,128)(2,1)S(1)} collective-permute-done((bf16[2,512,128]{2,1,0:T(8,128)(2,1)S(1)}, bf16[2,512,128]{2,1,0:T(8,128)(2,1)S(1)}, u32[]{:S(2)}, u32[]{:S(2)}) %collective-permute-start.17) | collective-permute-done | bytes 262176 | tf_op jit(solution)/shard_map/ppermute | solution.py:30
  84.7 1.2 %collective-permute-done.22 = bf16[2,256,256]{2,1,0:T(8,128)(2,1)S(1)} collective-permute-done((bf16[2,256,256]{2,1,0:T(8,128)(2,1)S(1)}, bf16[2,256,256]{2,1,0:T(8,128)(2,1)S(1)}, u32[]{:S(2)}, u32[]{:S(2)}) %collective-permute-start.22) | collective-permute-done | bytes 262176 | tf_op jit(solution)/shard_map/ppermute | solution.py:30
  86.0 1.3 %collective-permute-start.24 = (bf16[2,256,128]{2,1,0:T(8,128)(2,1)S(1)}, bf16[2,256,128]{2,1,0:T(8,128)(2,1)S(1)}, u32[]{:S(2)}, u32[]{:S(2)}) collective-permute-start(bf16[2,256,128]{2,1,0:T(8,128)(2,1)S(1)} %slice.41), channel_id=1, source_target_pairs={{0,1},{1,0},{2,3},{3,2},{4,5},{5,4},{6,7},{7,6},{8,9},{9,8},{10,11... | collective-permute-start | bytes 393224 | tf_op jit(solution)/shard_map/ppermute | solution.py:30
  87.6 3.5 %collective-permute-done.24 = bf16[2,256,128]{2,1,0:T(8,128)(2,1)S(1)} collective-permute-done((bf16[2,256,128]{2,1,0:T(8,128)(2,1)S(1)}, bf16[2,256,128]{2,1,0:T(8,128)(2,1)S(1)}, u32[]{:S(2)}, u32[]{:S(2)}) %collective-permute-start.24) | collective-permute-done | bytes 131104 | tf_op jit(solution)/shard_map/ppermute | solution.py:30
  91.1 1.1 %pad_maximum_fusion = f32[2,256,512]{2,1,0:T(8,128)} fusion(f32[2,256,256]{2,1,0:T(8,128)S(1)} %get-tuple-element.65, f32[2,256,256]{2,1,0:T(8,128)S(1)} %get-tuple-element.64), kind=kLoop, calls=%fused_computation | loop fusion | flops 262144 | bytes 2097152 | tf_op jit(solution)/shard_map/concatenate | solution.py:400
  (51 shorter events, 5.2 us)
Async XLA Ops:
  3.2 7.0 %collective-permute-start = (bf16[2,256,128]{2,1,0:T(8,128)(2,1)S(1)}, bf16[2,256,128]{2,1,0:T(8,128)(2,1)S(1)}, u32[]{:S(2)}, u32[]{:S(2)}) collective-permute-start(bf16[2,256,128]{2,1,0:T(8,128)(2,1)S(1)} %get-tuple-element.37), channel_id=1, source_target_pairs={{0,1},{1,0},{2,3},{3,2},{4,5},{5,4},{6,7},{7,6},{8,9},{9,8},{10,11... | collective-permute-start | bytes 393224 | tf_op jit(solution)/shard_map/ppermute | solution.py:30
  6.3 6.4 %collective-permute-start.6 = (bf16[2,256,128]{2,1,0:T(8,128)(2,1)S(1)}, bf16[2,256,128]{2,1,0:T(8,128)(2,1)S(1)}, u32[]{:S(2)}, u32[]{:S(2)}) collective-permute-start(bf16[2,256,128]{2,1,0:T(8,128)(2,1)S(1)} %get-tuple-element.42.refs_4_), channel_id=1, source_target_pairs={{0,8},{4,12},{8,0},{12,4},{1,9},{5,13},{9,1},{13,5},{2,10},{6,14},... | collective-permute-start | bytes 393224 | tf_op jit(solution)/shard_map/ppermute | solution.py:30
  7.8 6.1 %collective-permute-start.5 = (bf16[2,256,128]{2,1,0:T(8,128)(2,1)S(1)}, bf16[2,256,128]{2,1,0:T(8,128)(2,1)S(1)}, u32[]{:S(2)}, u32[]{:S(2)}) collective-permute-start(bf16[2,256,128]{2,1,0:T(8,128)(2,1)S(1)} %get-tuple-element.41), channel_id=1, source_target_pairs={{0,1},{1,0},{2,3},{3,2},{4,5},{5,4},{6,7},{7,6},{8,9},{9,8},{10,11... | collective-permute-start | bytes 393224 | tf_op jit(solution)/shard_map/ppermute | solution.py:30
  10.2 9.3 %collective-permute-start.1 = (bf16[2,512,128]{2,1,0:T(8,128)(2,1)S(1)}, bf16[2,512,128]{2,1,0:T(8,128)(2,1)S(1)}, u32[]{:S(2)}, u32[]{:S(2)}) collective-permute-start(bf16[2,512,128]{2,1,0:T(8,128)(2,1)S(1)} %get-tuple-element.38), channel_id=1, source_target_pairs={{0,1},{1,0},{2,3},{3,2},{4,5},{5,4},{6,7},{7,6},{8,9},{9,8},{10,11... | collective-permute-start | bytes 786440 | tf_op jit(solution)/shard_map/ppermute | solution.py:30
  13.8 5.0 %collective-permute-start.7 = (bf16[2,256,128]{2,1,0:T(8,128)(2,1)S(1)}, bf16[2,256,128]{2,1,0:T(8,128)(2,1)S(1)}, u32[]{:S(2)}, u32[]{:S(2)}) collective-permute-start(bf16[2,256,128]{2,1,0:T(8,128)(2,1)S(1)} %collective-permute-done.5.refs_8_), channel_id=1, source_target_pairs={{0,8},{4,12},{8,0},{12,4},{1,9},{5,13},{9,1},{13,5},{2,10},{6,14},... | collective-permute-start | bytes 393224 | tf_op jit(solution)/shard_map/ppermute | solution.py:30
  15.4 5.7 %collective-permute-start.9 = (bf16[2,256,128]{2,1,0:T(8,128)(2,1)S(1)}, bf16[2,256,128]{2,1,0:T(8,128)(2,1)S(1)}, u32[]{:S(2)}, u32[]{:S(2)}) collective-permute-start(bf16[2,256,128]{2,1,0:T(8,128)(2,1)S(1)} %get-tuple-element.42.refs_4_), channel_id=1, source_target_pairs={{0,4},{4,0},{8,12},{12,8},{1,5},{5,1},{9,13},{13,9},{2,6},{6,2},{1... | collective-permute-start | bytes 393224 | tf_op jit(solution)/shard_map/ppermute | solution.py:30
  15.4 5.9 %collective-permute-start.10 = (bf16[2,256,128]{2,1,0:T(8,128)(2,1)S(1)}, bf16[2,256,128]{2,1,0:T(8,128)(2,1)S(1)}, u32[]{:S(2)}, u32[]{:S(2)}) collective-permute-start(bf16[2,256,128]{2,1,0:T(8,128)(2,1)S(1)} %collective-permute-done.6.refs_6_), channel_id=1, source_target_pairs={{0,4},{4,0},{8,12},{12,8},{1,5},{5,1},{9,13},{13,9},{2,6},{6,2},{1... | collective-permute-start | bytes 393224 | tf_op jit(solution)/shard_map/ppermute | solution.py:30
  15.9 5.7 %collective-permute-start.11 = (bf16[2,256,128]{2,1,0:T(8,128)(2,1)S(1)}, bf16[2,256,128]{2,1,0:T(8,128)(2,1)S(1)}, u32[]{:S(2)}, u32[]{:S(2)}) collective-permute-start(bf16[2,256,128]{2,1,0:T(8,128)(2,1)S(1)} %collective-permute-done.5.refs_8_), channel_id=1, source_target_pairs={{0,4},{4,0},{8,12},{12,8},{1,5},{5,1},{9,13},{13,9},{2,6},{6,2},{1... | collective-permute-start | bytes 393224 | tf_op jit(solution)/shard_map/ppermute | solution.py:30
  18.8 3.3 %collective-permute-start.12 = (bf16[2,256,128]{2,1,0:T(8,128)(2,1)S(1)}, bf16[2,256,128]{2,1,0:T(8,128)(2,1)S(1)}, u32[]{:S(2)}, u32[]{:S(2)}) collective-permute-start(bf16[2,256,128]{2,1,0:T(8,128)(2,1)S(1)} %collective-permute-done.7.refs_10_), channel_id=1, source_target_pairs={{0,4},{4,0},{8,12},{12,8},{1,5},{5,1},{9,13},{13,9},{2,6},{6,2},{1... | collective-permute-start | bytes 393224 | tf_op jit(solution)/shard_map/ppermute | solution.py:30
  19.5 29.0 %collective-permute-start.4 = (bf16[2,256,128]{2,1,0:T(8,128)(2,1)S(1)}, bf16[2,256,128]{2,1,0:T(8,128)(2,1)S(1)}, u32[]{:S(2)}, u32[]{:S(2)}) collective-permute-start(bf16[2,256,128]{2,1,0:T(8,128)(2,1)S(1)} %get-tuple-element.40.refs_4_), channel_id=1, source_target_pairs={{0,8},{4,12},{8,0},{12,4},{1,9},{5,13},{9,1},{13,5},{2,10},{6,14},... | collective-permute-start | bytes 393224 | tf_op jit(solution)/shard_map/ppermute | solution.py:30
  21.1 28.0 %collective-permute-start.3 = (bf16[2,256,128]{2,1,0:T(8,128)(2,1)S(1)}, bf16[2,256,128]{2,1,0:T(8,128)(2,1)S(1)}, u32[]{:S(2)}, u32[]{:S(2)}) collective-permute-start(bf16[2,256,128]{2,1,0:T(8,128)(2,1)S(1)} %get-tuple-element.40.refs_4_), channel_id=1, source_target_pairs={{0,4},{4,0},{8,12},{12,8},{1,5},{5,1},{9,13},{13,9},{2,6},{6,2},{1... | collective-permute-start | bytes 393224 | tf_op jit(solution)/shard_map/ppermute | solution.py:30
  21.3 28.2 %collective-permute-start.14 = (bf16[2,256,128]{2,1,0:T(8,128)(2,1)S(1)}, bf16[2,256,128]{2,1,0:T(8,128)(2,1)S(1)}, u32[]{:S(2)}, u32[]{:S(2)}) collective-permute-start(bf16[2,256,128]{2,1,0:T(8,128)(2,1)S(1)} %collective-permute-done.refs_8_), channel_id=1, source_target_pairs={{0,4},{4,0},{8,12},{12,8},{1,5},{5,1},{9,13},{13,9},{2,6},{6,2},{1... | collective-permute-start | bytes 393224 | tf_op jit(solution)/shard_map/ppermute | solution.py:30
  21.6 26.9 %collective-permute-start.8 = (bf16[2,256,128]{2,1,0:T(8,128)(2,1)S(1)}, bf16[2,256,128]{2,1,0:T(8,128)(2,1)S(1)}, u32[]{:S(2)}, u32[]{:S(2)}) collective-permute-start(bf16[2,256,128]{2,1,0:T(8,128)(2,1)S(1)} %collective-permute-done.refs_8_), channel_id=1, source_target_pairs={{0,8},{4,12},{8,0},{12,4},{1,9},{5,13},{9,1},{13,5},{2,10},{6,14},... | collective-permute-start | bytes 393224 | tf_op jit(solution)/shard_map/ppermute | solution.py:30
  22.1 29.5 %collective-permute-start.2 = (bf16[2,512,128]{2,1,0:T(8,128)(2,1)S(1)}, bf16[2,512,128]{2,1,0:T(8,128)(2,1)S(1)}, u32[]{:S(2)}, u32[]{:S(2)}) collective-permute-start(bf16[2,512,128]{2,1,0:T(8,128)(2,1)S(1)} %get-tuple-element.39), channel_id=1, source_target_pairs={{0,1},{1,0},{2,3},{3,2},{4,5},{5,4},{6,7},{7,6},{8,9},{9,8},{10,11... | collective-permute-start | bytes 786440 | tf_op jit(solution)/shard_map/ppermute | solution.py:30
  48.6 2.8 %collective-permute-start.15 = (bf16[2,256,128]{2,1,0:T(8,128)(2,1)S(1)}, bf16[2,256,128]{2,1,0:T(8,128)(2,1)S(1)}, u32[]{:S(2)}, u32[]{:S(2)}) collective-permute-start(bf16[2,256,128]{2,1,0:T(8,128)(2,1)S(1)} %collective-permute-done.8.refs_10_), channel_id=1, source_target_pairs={{0,4},{4,0},{8,12},{12,8},{1,5},{5,1},{9,13},{13,9},{2,6},{6,2},{1... | collective-permute-start | bytes 393224 | tf_op jit(solution)/shard_map/ppermute | solution.py:30
  49.1 25.9 %collective-permute-start.16 = (bf16[2,512,128]{2,1,0:T(8,128)(2,1)S(1)}, bf16[2,512,128]{2,1,0:T(8,128)(2,1)S(1)}, u32[]{:S(2)}, u32[]{:S(2)}) collective-permute-start(bf16[2,512,128]{2,1,0:T(8,128)(2,1)S(1)} %get-tuple-element.46), channel_id=1, source_target_pairs={{0,1},{1,0},{2,3},{3,2},{4,5},{5,4},{6,7},{7,6},{8,9},{9,8},{10,11... | collective-permute-start | bytes 786440 | tf_op jit(solution)/shard_map/ppermute | solution.py:30
  49.5 25.5 %collective-permute-start.18 = (bf16[2,256,256]{2,1,0:T(8,128)(2,1)S(1)}, bf16[2,256,256]{2,1,0:T(8,128)(2,1)S(1)}, u32[]{:S(2)}, u32[]{:S(2)}) collective-permute-start(bf16[2,256,256]{2,1,0:T(8,128)(2,1)S(1)} %bitcast.14), channel_id=1, source_target_pairs={{0,4},{4,0},{8,12},{12,8},{1,5},{5,1},{9,13},{13,9},{2,6},{6,2},{1... | collective-permute-start | bytes 786440 | tf_op jit(solution)/shard_map/ppermute | solution.py:30
  49.9 25.0 %collective-permute-start.19 = (bf16[2,256,256]{2,1,0:T(8,128)(2,1)S(1)}, bf16[2,256,256]{2,1,0:T(8,128)(2,1)S(1)}, u32[]{:S(2)}, u32[]{:S(2)}) collective-permute-start(bf16[2,256,256]{2,1,0:T(8,128)(2,1)S(1)} %bitcast.13), channel_id=1, source_target_pairs={{0,8},{4,12},{8,0},{12,4},{1,9},{5,13},{9,1},{13,5},{2,10},{6,14},... | collective-permute-start | bytes 786440 | tf_op jit(solution)/shard_map/ppermute | solution.py:30
  51.4 23.5 %collective-permute-start.20 = (bf16[2,256,256]{2,1,0:T(8,128)(2,1)S(1)}, bf16[2,256,256]{2,1,0:T(8,128)(2,1)S(1)}, u32[]{:S(2)}, u32[]{:S(2)}) collective-permute-start(bf16[2,256,256]{2,1,0:T(8,128)(2,1)S(1)} %bitcast.12), channel_id=1, source_target_pairs={{0,12},{4,8},{8,4},{12,0},{1,13},{5,9},{9,5},{13,1},{2,14},{6,10},... | collective-permute-start | bytes 786440 | tf_op jit(solution)/shard_map/ppermute | solution.py:30
  75.0 2.1 %collective-permute-start.21 = (bf16[2,2,256,256]{3,2,1,0:T(8,128)(2,1)S(1)}, bf16[2,2,256,256]{3,2,1,0:T(8,128)(2,1)S(1)}, u32[]{:S(2)}, u32[]{:S(2)}) collective-permute-start(bf16[2,2,256,256]{3,2,1,0:T(8,128)(2,1)S(1)} %get-tuple-element.62), channel_id=1, source_target_pairs={{0,4},{4,0},{8,12},{12,8},{1,5},{5,1},{9,13},{13,9},{2,6},{6,2},{1... | collective-permute-start | bytes 1572872 | tf_op jit(solution)/shard_map/ppermute | solution.py:30
  75.6 9.2 %collective-permute-start.17 = (bf16[2,512,128]{2,1,0:T(8,128)(2,1)S(1)}, bf16[2,512,128]{2,1,0:T(8,128)(2,1)S(1)}, u32[]{:S(2)}, u32[]{:S(2)}) collective-permute-start(bf16[2,512,128]{2,1,0:T(8,128)(2,1)S(1)} %get-tuple-element.55), channel_id=1, source_target_pairs={{0,1},{1,0},{2,3},{3,2},{4,5},{5,4},{6,7},{7,6},{8,9},{9,8},{10,11... | collective-permute-start | bytes 786440 | tf_op jit(solution)/shard_map/ppermute | solution.py:30
  77.3 8.7 %collective-permute-start.22 = (bf16[2,256,256]{2,1,0:T(8,128)(2,1)S(1)}, bf16[2,256,256]{2,1,0:T(8,128)(2,1)S(1)}, u32[]{:S(2)}, u32[]{:S(2)}) collective-permute-start(bf16[2,256,256]{2,1,0:T(8,128)(2,1)S(1)} %fusion.1), channel_id=1, source_target_pairs={{0,8},{4,12},{8,0},{12,4},{1,9},{5,13},{9,1},{13,5},{2,10},{6,14},... | collective-permute-start | bytes 786440 | tf_op jit(solution)/shard_map/ppermute | solution.py:30
  79.0 8.6 %collective-permute-start.23 = (bf16[2,256,128]{2,1,0:T(8,128)(2,1)S(1)}, bf16[2,256,128]{2,1,0:T(8,128)(2,1)S(1)}, u32[]{:S(2)}, u32[]{:S(2)}) collective-permute-start(bf16[2,256,128]{2,1,0:T(8,128)(2,1)S(1)} %slice.42), channel_id=1, source_target_pairs={{0,1},{1,0},{2,3},{3,2},{4,5},{5,4},{6,7},{7,6},{8,9},{9,8},{10,11... | collective-permute-start | bytes 393224 | tf_op jit(solution)/shard_map/ppermute | solution.py:30
  86.0 5.0 %collective-permute-start.24 = (bf16[2,256,128]{2,1,0:T(8,128)(2,1)S(1)}, bf16[2,256,128]{2,1,0:T(8,128)(2,1)S(1)}, u32[]{:S(2)}, u32[]{:S(2)}) collective-permute-start(bf16[2,256,128]{2,1,0:T(8,128)(2,1)S(1)} %slice.41), channel_id=1, source_target_pairs={{0,1},{1,0},{2,3},{3,2},{4,5},{5,4},{6,7},{7,6},{8,9},{9,8},{10,11... | collective-permute-start | bytes 393224 | tf_op jit(solution)/shard_map/ppermute | solution.py:30
  (6 other events, 18.6 us)
